TPU v7x, 32 devices: a whole 2x2x4 slice. The times are simulated.
32 devices in a mesh: gran: 8 (over z, x), band: 4 (over y, core).
Axes of the slice: x: 2, y: 2, z: 4, core: 2. Of those that a mesh axis runs over, the one named last changes fastest.
Arguments:
- prior_grids: float32 [128, 12, 2, 4096], P('gran', 'band'), may hold values from -1.5 to 1.5
- pif_rhs: float32 [128, 12, 2, 4096], P('gran', 'band'), may hold values from -8 to 8
- pif_diagonal: float32 [128, 12, 2, 4096], P('gran', 'band'), may hold values from 0.5 to 2
- pif_cross: float32 [128, 12, 4096], P('gran', 'band'), may hold values from -0.7 to 0.7
- pif_coupling: bfloat16 [128, 8, 12, 4096], P('gran', None, 'band'), may hold values from 0.25 to 2
- neighbour_offset: int32 [128, 8], P('gran'), may hold values from -4 to 4, as said below
- neighbour_count: int32 [128], P('gran'), may hold values from 1 to 8, as said below
- tile_route: int32 [128, 2], replicated, may hold values from 0 to 7, all different within a row; in each aligned block of 16 rows (0 to 15, 16 to 31, ...) at most 8 rows name the same one
- tile_window: int32 [128, 2, 2], replicated, may hold values from 0 to 1760
- tile_pixels: bfloat16 [8, 12, 256, 256], P('gran', 'band'), may hold values from 0.049804688 to 1
Outputs:
- balanced_grids: float32 [128, 12, 2, 4096], P('gran', 'band')
- corrected_tiles: bfloat16 [8, 12, 256, 256], P('gran', 'band')
Inputs may be any that keep to these rules, and one draw needn't show every extreme that they name: `neighbour_offset`: A granule's slots below its count hold a nonzero offset to another granule; the other slots hold 0. In every aligned block of 16 granules the granule of count 8 has an offset of magnitude 4 in its first slot. `neighbour_count`: every aligned block of 16 granules holds a granule with 8 neighbours. `tile_route`: each granule names two different tiles; every tile is named; among the 16 granules of one device no tile is named more than 8 times.
All inputs are finite; a program needn't handle non-finite values.
Results may differ from a plain program's by a relative error of at most 0.0036.
The roundings to bfloat16 on the way count: a program that leaves them out, or rounds other values in their place, can miss the bound.
Values may be sent and summed in bfloat16 or wider, within the bound.
No kernel may reach another device: no remote copies, remote signals or barrier semaphores. Data moves between devices by JAX's collectives and lax.ppermute only.
A program may use at most 128 MiB of HBM per device.

v0:
```python
import functools
import jax
import jax.numpy as jnp
from jax import lax
from jax.experimental import pallas as pl
from jax.experimental.pallas import tpu as pltpu
from jax.sharding import PartitionSpec as P

BANDS = 12
KN = 64
PATCH = 8
REACH = 4
SWEEPS = 3
SP = 32
LANES = 128
SPAN = 16

robust_scale = 0.3

ON_CHIP = pl.BlockSpec(memory_space=pltpu.VMEM)
SCALARS = pl.BlockSpec(memory_space=pltpu.SMEM)
f32 = jnp.float32
bf16 = jnp.bfloat16


def held(array):
    return pltpu.with_memory_space_constraint(array, pltpu.VMEM)


def scalars(array):
    return pltpu.with_memory_space_constraint(array, pltpu.SMEM)


def call(body, inputs, outputs, scratch=(), aliases=None, limit=24):
    operands, specs = [], []
    for kind, array in inputs:
        operands.append(scalars(array) if kind == "s" else held(array))
        specs.append(SCALARS if kind == "s" else ON_CHIP)
    return pl.pallas_call(
        body,
        in_specs=specs,
        out_specs=tuple(ON_CHIP for _ in outputs),
        out_shape=tuple(pltpu.VMEM(shape, dtype) for shape, dtype in outputs),
        scratch_shapes=list(scratch),
        input_output_aliases=aliases or {},
        compiler_params=pltpu.CompilerParams(vmem_limit_bytes=limit * 2**20),
    )(*operands)


def put_edges(side_ref, load, near_ref, far_ref, granules):
    odd = side_ref[0]
    last = granules - REACH
    for ref, base in ((near_ref, (1 - odd) * last), (far_ref, odd * last)):

        def step(g, carry, ref=ref, base=base):
            for b in range(ref.shape[1]):
                for j in range(4):
                    both = jnp.concatenate([load(base + g, b, j, 0), load(base + g, b, j, 1)], axis=0)
                    ref[g, b, 16 * j : 16 * j + 16, :] = both.astype(bf16)
            return carry

        lax.fori_loop(0, REACH, step, 0)


def first_edges(side_ref, grids_ref, near_ref, far_ref):
    def load(g, b, j, c):
        return grids_ref[g, b, pl.ds(2 * j + c, 8, stride=8), :]

    put_edges(side_ref, load, near_ref, far_ref, grids_ref.shape[0])


def arrange(grids_ref, rhs_ref, diag_ref, cross_ref, coupling_ref, ext_ref, rhs_out, diag_out, cross_out, coupling_out, wide):
    granules, bands = grids_ref.shape[:2]
    slots = coupling_out.shape[1]

    def step(i, carry):
        for b in range(bands):
            for j in range(4):
                d = []
                for c in range(2):
                    rows = pl.ds(2 * j + c, 8, stride=8)
                    to = slice(16 * j + 8 * c, 16 * j + 8 * c + 8)
                    ext_ref[i + REACH, b, to, :] = grids_ref[i, b, rows, :]
                    rhs_out[i, b, to, :] = rhs_ref[i, b, rows, :]
                    value = diag_ref[i, b, rows, :]
                    diag_out[i, b, to, :] = value
                    d.append(value)
                pick = cross_ref[b, i // 8, pl.ds(8 * j + i % 8, 8, stride=32), :]
                cross_out[i, b, 8 * j : 8 * j + 8, :] = pick * jnp.sqrt(d[0] * d[1])
            wide[b] = coupling_ref[i, b].astype(f32)
            for s in range(slots):
                for j in (0, 2):
                    pair = [wide[b, pl.ds(8 * (j + k) + s, 8, stride=32), :] for k in (0, 1)]
                    coupling_out[i, s, b, 8 * j : 8 * j + 16, :] = jnp.concatenate(pair, axis=0).astype(bf16)
        return carry

    lax.fori_loop(0, granules, step, 0)


def lane_sums():
    row = lax.broadcasted_iota(jnp.int32, (LANES, LANES), 0)
    col = lax.broadcasted_iota(jnp.int32, (LANES, LANES), 1)
    return ((row % KN) // PATCH == col % PATCH).astype(f32).astype(bf16)


def lane_spread():
    row = lax.broadcasted_iota(jnp.int32, (LANES, LANES), 0)
    col = lax.broadcasted_iota(jnp.int32, (LANES, LANES), 1)
    return ((col % KN) // PATCH == row % PATCH).astype(f32).astype(bf16)


def disparities(side_ref, offset_ref, count_ref, near_ref, far_ref, ext_in, ext_ref, out_ref, gathered):
    del ext_in
    granules = ext_ref.shape[0] - 2 * REACH
    bands = ext_ref.shape[1]
    slots = gathered.shape[0] * 8 // granules
    odd = side_ref[0]
    right = granules + REACH
    for ref, base in ((near_ref, (1 - odd) * right), (far_ref, odd * right)):

        def widen(g, carry, ref=ref, base=base):
            for b in range(bands):
                ext_ref[base + g, b] = ref[g, b].astype(f32)
            return carry

        lax.fori_loop(0, REACH, widen, 0)
    gathered[...] = jnp.zeros_like(gathered)

    def response(g):
        return [
            ext_ref[g, b, 16 * j : 16 * j + 8, :] + ext_ref[g, b, 16 * j + 8 : 16 * j + 16, :]
            for b in range(bands)
            for j in range(4)
        ]

    def granule(i, carry):
        own = response(i + REACH)
        row = pl.multiple_of((i % 8) * 8, 8)

        def slot(s, carry):
            other = response(i + REACH + offset_ref[i * slots + s])
            total = None
            for a, o in zip(own, other):
                d = a - o
                total = d * d if total is None else total + d * d
            gathered[(i // 8) * slots + s, pl.ds(row, 8), :] = total
            return carry

        lax.fori_loop(0, count_ref[i], slot, 0)
        return carry

    lax.fori_loop(0, granules, granule, 0)
    groups = gathered.shape[0]
    sums = jnp.dot(
        gathered[...].reshape(groups * 64, LANES).astype(bf16), lane_sums(), preferred_element_type=f32
    )
    lane = lax.broadcasted_iota(jnp.int32, (64, LANES), 1) // PATCH
    packed = jnp.zeros((64, LANES), f32)
    for k in range(groups):
        packed = jnp.where(lane == k, sums[64 * k : 64 * k + 64], packed)
    out_ref[...] = packed


def balance(offset_ref, count_ref, own_ref, a_ref, b_ref, c_ref, ext_ref, rhs_ref, diag_ref, cross_ref, coupling_ref, weights, store):
    granules, bands = rhs_ref.shape[:2]
    slots = coupling_ref.shape[1]
    groups = weights.shape[0]
    total = (own_ref[...] + a_ref[...]) + (b_ref[...] + c_ref[...])
    robust = 1.0 / (1.0 + total * (1.0 / (robust_scale * BANDS * PATCH * PATCH)))
    lane = lax.broadcasted_iota(jnp.int32, (64, LANES), 1) // PATCH
    high = robust.astype(bf16).astype(f32)
    low = robust - high
    both = jnp.concatenate([high, low], axis=1)
    lane = jnp.concatenate([lane, lane], axis=1)
    spread = lane_spread()
    spread = jnp.concatenate([spread, spread], axis=0)
    stacked = jnp.concatenate(
        [jnp.where(lane == k, both, 0.0).astype(bf16) for k in range(groups)], axis=0
    )
    weights[...] = jnp.dot(stacked, spread, preferred_element_type=f32).reshape(groups, 64, LANES)

    def granule(i, carry):
        row = pl.multiple_of((i % 8) * 8, 8)
        parts = [(b, j) for b in range(bands) for j in range(4)]
        rhs = tuple(
            rhs_ref[i, b, 16 * j + 8 * c : 16 * j + 8 * c + 8, :] for b, j in parts for c in range(2)
        )

        def slot(s, sums):
            sigma, drive = sums
            weight = weights[(i // 8) * slots + s, pl.ds(row, 8), :]
            n = i + REACH + offset_ref[i * slots + s]
            new_sigma, new_drive = [], []
            for b in range(bands):
                coupling = coupling_ref[i, s, b].astype(f32)
                for j in range(4):
                    k = 4 * b + j
                    effective = weight * coupling[8 * j : 8 * j + 8]
                    new_sigma.append(sigma[k] + effective)
                    for c in range(2):
                        grid = ext_ref[n, b, 16 * j + 8 * c : 16 * j + 8 * c + 8, :]
                        new_drive.append(drive[2 * k + c] + effective * grid)
            return tuple(new_sigma), tuple(new_drive)

        zero = jnp.zeros((8, LANES), f32)
        sigma, drive = lax.fori_loop(0, count_ref[i], slot, ((zero,) * len(parts), rhs))
        for k, (b, j) in enumerate(parts):
            first = diag_ref[i, b, 16 * j : 16 * j + 8, :] + sigma[k]
            second = diag_ref[i, b, 16 * j + 8 : 16 * j + 16, :] + sigma[k]
            cross = cross_ref[i, b, 8 * j : 8 * j + 8, :]
            inverse = 1.0 / (first * second - cross * cross)
            gain, offset = drive[2 * k], drive[2 * k + 1]
            store(i, b, j, 0, (second * gain - cross * offset) * inverse)
            store(i, b, j, 1, (first * offset - cross * gain) * inverse)
        return carry

    lax.fori_loop(0, granules, granule, 0)


def middle_sweep(side_ref, *refs):
    inputs, (new_ref, near_ref, far_ref, weights) = refs[:11], refs[11:]

    def store(i, b, j, c, value):
        new_ref[i + REACH, b, 16 * j + 8 * c : 16 * j + 8 * c + 8, :] = value

    def load(g, b, j, c):
        return new_ref[g + REACH, b, 16 * j + 8 * c : 16 * j + 8 * c + 8, :]

    balance(*inputs, weights, store)
    put_edges(side_ref, load, near_ref, far_ref, new_ref.shape[0] - 2 * REACH)


def last_sweep(place_ref, *refs):
    inputs, (out_ref, send_ref, weights, windows) = refs[:11], refs[11:]
    granules, bands = out_ref.shape[:2]

    def store(i, b, j, c, value):
        out_ref[i, b, pl.ds(2 * j + c, 8, stride=8), :] = value

    balance(*inputs, weights, store)
    windows[...] = jnp.zeros_like(windows)
    lane = lax.broadcasted_iota(jnp.int32, (8, LANES), 1) // SPAN

    def entry(e, carry):
        i = e // 2
        owner, rank, top, left = (place_ref[4 * e + k] for k in range(4))
        here = lane == rank
        shift = rank * SPAN - left
        turns = [lax.rem(shift - KN * half + 2 * LANES, LANES) for half in (0, 1)]
        for b in range(bands):
            for c in range(2):
                rows = out_ref[i, b, pl.ds(2 * top + c, 8, stride=2), :]
                for half in (0, 1):
                    to = slice(16 * (2 * b + c) + 8 * half, 16 * (2 * b + c) + 8 * half + 8)
                    moved = pltpu.roll(rows, turns[half], 1)
                    windows[owner, to, :] = jnp.where(here, moved, windows[owner, to, :])
        return carry

    lax.fori_loop(0, 2 * granules, entry, 0)
    send_ref[...] = windows[...].astype(bf16)


def cubic(distance):
    near = (1.5 * distance - 2.5) * distance * distance + 1.0
    far = ((2.5 - 0.5 * distance) * distance - 4.0) * distance + 2.0
    return jnp.where(distance <= 1.0, near, jnp.where(distance < 2.0, far, 0.0))


def interp_weights(table_ref, rows_out, cols_out):
    pixels, lanes = rows_out.shape

    def step(t, carry):
        at = pl.ds(pl.multiple_of(t * LANES, LANES), LANES)
        for n, ref in ((0, rows_out), (3, cols_out)):
            start, knot, beyond = (table_ref[n + k : n + k + 1, at] for k in range(3))
            for r in range(0, pixels, 16):
                pixel = (lax.broadcasted_iota(jnp.int32, (16, LANES), 0) + r).astype(f32)
                place = pixel * (1.0 / SP) + start
                value = cubic(jnp.abs(place - knot)) + cubic(jnp.abs(place - beyond))
                ref[r : r + 16, at] = value.astype(bf16)
        return carry

    lax.fori_loop(0, lanes // LANES, step, 0)


def compose(covers_ref, received_ref, row_ref, col_ref, pixels_ref, out_ref, passed):
    senders = received_ref.shape[0]
    bands = out_ref.shape[1]
    lane = lax.broadcasted_iota(jnp.int32, (16, LANES), 1) // SPAN
    masks = [(lane == r).astype(f32).astype(bf16) for r in range(LANES // SPAN)]

    def sender(n, carry):
        at = pl.ds(pl.multiple_of(n * LANES, LANES), LANES)
        blocks = []
        for k in range(2 * bands):
            window = received_ref[n, 16 * k : 16 * k + 16, :]
            blocks.append(jnp.concatenate([window * mask for mask in masks], axis=0))
        rows = jnp.dot(row_ref[:, at], jnp.concatenate(blocks, axis=1), preferred_element_type=f32)
        for k in range(2 * bands):
            passed[k, :, at] = rows[:, LANES * k : LANES * k + LANES].astype(bf16)
        return carry

    lax.fori_loop(0, senders, sender, 0)
    scale = 1.0 / covers_ref[0].astype(f32)
    for b in range(bands):
        fields = [
            lax.dot_general(
                passed[2 * b + c], col_ref[...], (((1,), (1,)), ((), ())), preferred_element_type=f32
            )
            * scale
            for c in range(2)
        ]
        pixels = pixels_ref[0, b].astype(f32)
        out_ref[0, b] = (pixels * (1.0 + fields[0]) + fields[1]).astype(bf16)


def per_device(
    prior_grids,
    pif_rhs,
    pif_diagonal,
    pif_cross,
    pif_coupling,
    neighbour_offset,
    neighbour_count,
    tile_route,
    tile_window,
    tile_pixels,
):
    granules, bands = prior_grids.shape[:2]
    slots = pif_coupling.shape[1]
    own_index = lax.axis_index("gran")
    device_total = lax.axis_size("gran")
    band_total = lax.axis_size("band")
    groups = slots * granules // 8

    def by_lane_tile(array):
        cut = array.reshape(array.shape[:2] + (array.shape[2], 32, LANES)).transpose(0, 1, 3, 2, 4)
        return cut.reshape(array.shape[:2] + (32 * array.shape[2], LANES))

    grids = by_lane_tile(prior_grids)
    rhs = by_lane_tile(pif_rhs)
    diagonal = by_lane_tile(pif_diagonal)
    cross = by_lane_tile(pif_cross.transpose(1, 0, 2).reshape(bands, granules // 8, 8, KN * KN))
    coupling = by_lane_tile(pif_coupling.transpose(0, 2, 1, 3))
    side = (own_index % 2).astype(jnp.int32).reshape(1)
    offsets = neighbour_offset.reshape(-1)
    edge = (REACH, bands, 64, LANES)
    own = (granules, bands, 64, LANES)
    ext = (granules + 2 * REACH, bands, 64, LANES)

    near_pairs = [(i, i ^ 1) for i in range(device_total)]
    far_pairs = [
        pair for i in range(1, device_total - 1, 2) for pair in ((i, i + 1), (i + 1, i))
    ]

    def exchange(near, far):
        far = lax.ppermute(far, "gran", far_pairs)
        near = lax.ppermute(near, "gran", near_pairs)
        return near, far

    near, far = call(first_edges, [("s", side), ("v", grids)], [(edge, bf16), (edge, bf16)])
    near, far = exchange(near, far)
    extended, rhs, diagonal, cross, coupling = call(
        arrange,
        [("v", grids), ("v", rhs), ("v", diagonal), ("v", cross), ("v", coupling)],
        [
            (ext, f32),
            (own, f32),
            (own, f32),
            ((granules, bands, 32, LANES), f32),
            ((granules, slots, bands, 32, LANES), bf16),
        ],
        [pltpu.VMEM((bands, 32 * slots, LANES), f32)],
    )

    entries = 2 * granules
    capacity = max(2, 4 * granules // device_total)
    route_table = tile_route.reshape(device_total, entries)
    window_table = tile_window.reshape(device_total, entries, 2)
    order = jnp.arange(entries, dtype=jnp.int32)
    same_tile = route_table[:, :, None] == route_table[:, None, :]
    ranks = jnp.sum((same_tile & (order[None, :] < order[:, None])[None]).astype(jnp.int32), axis=2)

    def first_pair(start):
        return jnp.clip(start // SP - 1, 0, KN - SPAN) // 2

    def first_knot(start):
        return jnp.clip(start // SP - 1, 0, KN - SPAN)

    my_routes = lax.dynamic_index_in_dim(route_table, own_index, 0, keepdims=False)
    my_ranks = lax.dynamic_index_in_dim(ranks, own_index, 0, keepdims=False)
    my_windows = lax.dynamic_index_in_dim(window_table, own_index, 0, keepdims=False)
    places = jnp.stack(
        [my_routes, my_ranks, first_pair(my_windows[:, 0]), first_knot(my_windows[:, 1])], axis=1
    ).reshape(-1)

    seats = LANES // SPAN
    matched = (route_table == own_index)[:, None, :] & (
        ranks[:, None, :] == jnp.arange(seats, dtype=jnp.int32)[None, :, None]
    )
    live = jnp.any(matched, axis=2)
    starts = jnp.sum(jnp.where(matched[..., None], window_table[:, None], 0), axis=2)
    step = jnp.arange(SPAN, dtype=jnp.int32)
    row_knots = 2 * (first_pair(starts[..., 0])[..., None] + step % 8) + step // 8
    col_knots = first_knot(starts[..., 1])[..., None] + step
    table = []
    for start, knots in ((starts[..., 0], row_knots), (starts[..., 1], col_knots)):
        table.append(jnp.broadcast_to(start[..., None], knots.shape).astype(f32) / SP)
        table.append(jnp.where(live[..., None], knots, 4 * KN).astype(f32))
        beyond = jnp.where(knots == 0, -1, jnp.where(knots == KN - 1, KN, 4 * KN))
        table.append(jnp.where(live[..., None], beyond, 4 * KN).astype(f32))
    table = jnp.stack(table + table[:2]).reshape(8, device_total * LANES)
    pixel_count = tile_pixels.shape[2]
    weight_shape = (pixel_count, device_total * LANES)
    row_weights, col_weights = call(
        interp_weights, [("v", table)], [(weight_shape, bf16), (weight_shape, bf16)]
    )

    for sweep in range(SWEEPS):
        extended, partial = call(
            disparities,
            [("s", side), ("s", offsets), ("s", neighbour_count), ("v", near), ("v", far), ("v", extended)],
            [(ext, f32), ((64, LANES), f32)],
            [pltpu.VMEM((groups, 64, LANES), f32)],
            aliases={5: 0},
        )
        shares = [
            lax.ppermute(partial, "band", [(i, i ^ flip) for i in range(band_total)])
            for flip in range(1, band_total)
        ]
        inputs = [("s", offsets), ("s", neighbour_count), ("v", partial)]
        inputs += [("v", share) for share in shares]
        inputs += [("v", extended), ("v", rhs), ("v", diagonal), ("v", cross), ("v", coupling)]
        weights = pltpu.VMEM((groups, 64, LANES), f32)
        if sweep < SWEEPS - 1:
            extended, near, far = call(
                middle_sweep,
                [("s", side)] + inputs,
                [(ext, f32), (edge, bf16), (edge, bf16)],
                [weights],
            )
            near, far = exchange(near, far)
        else:
            windows = (device_total, 2 * bands * SPAN, LANES)
            balanced, payload = call(
                last_sweep,
                [("s", places)] + inputs,
                [(own, f32), (windows, bf16)],
                [weights, pltpu.VMEM(windows, f32)],
            )
    received = lax.all_to_all(payload, "gran", split_axis=0, concat_axis=0, tiled=True)
    covers = jnp.sum((tile_route == own_index).astype(jnp.int32)).reshape(1)
    (corrected,) = call(
        compose,
        [("s", covers), ("v", received), ("v", row_weights), ("v", col_weights), ("v", tile_pixels)],
        [(tile_pixels.shape, bf16)],
        [pltpu.VMEM((2 * bands, pixel_count, device_total * LANES), bf16)],
    )
    balanced = balanced.reshape(granules, bands, 32, 2, LANES).transpose(0, 1, 3, 2, 4)
    return (balanced.reshape(prior_grids.shape), corrected)


def solution(mesh):
    placed = (
        P("gran", "band", None, None),
        P("gran", "band", None, None),
        P("gran", "band", None, None),
        P("gran", "band", None),
        P("gran", None, "band", None),
        P("gran", None),
        P("gran"),
        P(),
        P(),
        P("gran", "band", None, None),
    )
    return jax.shard_map(
        per_device,
        mesh=mesh,
        in_specs=placed,
        out_specs=(P("gran", "band", None, None), P("gran", "band", None, None)),
        check_vma=False,
    )
```

profile of v0, /device:TPU:0, one launch (start us, length us, event | category | flops | bytes accessed | tf_op | source)
XLA Modules:
  0.0 105.3 jit_solution(8881955774698483312)
XLA Ops:
  0.7 1.4 %copy-done.8 = f32[16,3,2,4096]{3,2,1,0:T(2,128)S(1)} copy-done((f32[16,3,2,4096]{3,2,1,0:T(2,128)S(1)}, f32[16,3,2,4096]{3,2,1,0:T(2,128)}, u32[]{:S(2)}) %copy-start.8) | copy-done | bytes 1572888
  2.1 0.9 shard_map.113
  3.0 2.9 %collective-permute-start = (bf16[4,3,64,128]{3,2,1,0:T(8,128)(2,1)}, bf16[4,3,64,128]{3,2,1,0:T(8,128)(2,1)S(1)}, u32[]{:S(2)}, u32[]{:S(2)}) collective-permute-start(bf16[4,3,64,128]{3,2,1,0:T(8,128)(2,1)} %get-tuple-element.25), channel_id=1, source_target_pairs={{0,4},{4,0},{8,12},{12,8},{16,20},{20,16},{24,28},{28,24},{1,5},{5... | collective-permute-start | bytes 589832 | tf_op jit(solution)/shard_map/ppermute | solution.py:358
  5.9 0.7 collective-permute-start.1
  7.2 0.8 copy.34
  8.0 0.8 copy.31
  9.8 0.8 copy.32
  10.8 0.8 fusion.8
  12.1 1.9 %copy-done.10 = bf16[16,8,3,4096]{3,1,2,0:T(8,128)(2,1)S(1)} copy-done((bf16[16,8,3,4096]{3,1,2,0:T(8,128)(2,1)S(1)}, bf16[16,8,3,4096]{3,1,2,0:T(8,128)(2,1)}, u32[]{:S(2)}) %copy-start.10) | copy-done | bytes 3145752
  14.0 1.4 %copy-done.11 = f32[16,3,2,4096]{3,2,1,0:T(2,128)S(1)} copy-done((f32[16,3,2,4096]{3,2,1,0:T(2,128)S(1)}, f32[16,3,2,4096]{3,2,1,0:T(2,128)}, u32[]{:S(2)}) %copy-start.11) | copy-done | bytes 1572888
  15.4 1.4 %copy-done.12 = f32[16,3,2,4096]{3,2,1,0:T(2,128)S(1)} copy-done((f32[16,3,2,4096]{3,2,1,0:T(2,128)S(1)}, f32[16,3,2,4096]{3,2,1,0:T(2,128)}, u32[]{:S(2)}) %copy-start.12) | copy-done | bytes 1572888
  16.8 1.1 %copy-done.13 = f32[16,3,4096]{2,0,1:T(8,128)S(1)} copy-done((f32[16,3,4096]{2,0,1:T(8,128)S(1)}, f32[16,3,4096]{2,0,1:T(8,128)}, u32[]{:S(2)}) %copy-start.13) | copy-done | bytes 786456
  17.9 5.2 %shard_map.114 = (f32[24,3,64,128]{3,2,1,0:T(8,128)S(1)}, f32[16,3,64,128]{3,2,1,0:T(8,128)S(1)}, f32[16,3,64,128]{3,2,1,0:T(8,128)S(1)}, f32[16,3,32,128]{3,2,1,0:T(8,128)S(1)}, bf16[16,8,3,32,128]{4,3,2,1,0:T(8,128)(2,1)S(1)}) custom-call(f32[16,3,64,128]{3,2,1,0:T(8,128)S(1)} %bitcast.49, f32[16,3,64,128]{3,2,1,0:T(8,128)S(1)} %bitcast.51, ...), custom_call_target="tpu_custom_call" | custom-call | tf_op jit(solution)/shard_map/pallas_call | solution.py:39
  23.2 0.8 multiply_add_fusion
  24.0 1.9 %shard_map.115 = (f32[24,3,64,128]{3,2,1,0:T(8,128)S(1)}, f32[64,128]{1,0:T(8,128)S(1)}) custom-call(s32[1]{0:T(128)} %bitcast.3.side_ref, s32[128]{0:T(128)S(1)} %reshape.342.offset_ref.refs_0_, s32[16]{0:T(128)S(1)} %copy-done.15, bf16[4,3,64,128]{3,2,1,0:T(8,128)(2,1)S(1)} %collective-permute-done.near_ref, ...), custom_call_target="tpu_custom_call", output_to_operand_aliasing={{0}: (5, {})} | custom-call | tf_op jit(solution)/shard_map/pallas_call | solution.py:39
  26.0 1.6 %collective-permute-start.3 = (f32[64,128]{1,0:T(8,128)S(1)}, f32[64,128]{1,0:T(8,128)S(1)}, u32[]{:S(2)}, u32[]{:S(2)}) collective-permute-start(f32[64,128]{1,0:T(8,128)S(1)} %get-tuple-element.28.refs_2_), channel_id=1, source_target_pairs={{0,2},{1,3},{2,0},{3,1},{4,6},{5,7},{6,4},{7,5},{8,10},{9,11},{10,... | collective-permute-start | bytes 98312 | tf_op jit(solution)/shard_map/ppermute | solution.py:428
  27.9 0.7 fusion.6
  28.6 1.4 %collective-permute-done.3.refs_4_ = f32[64,128]{1,0:T(8,128)S(1)} collective-permute-done((f32[64,128]{1,0:T(8,128)S(1)}, f32[64,128]{1,0:T(8,128)S(1)}, u32[]{:S(2)}, u32[]{:S(2)}) %collective-permute-start.3) | collective-permute-done | bytes 32800 | tf_op jit(solution)/shard_map/ppermute | solution.py:428
  30.0 0.9 collective-permute-done.4.refs_5_
  31.0 2.6 %shard_map.116 = (f32[24,3,64,128]{3,2,1,0:T(8,128)S(1)}, bf16[4,3,64,128]{3,2,1,0:T(8,128)(2,1)S(1)}, bf16[4,3,64,128]{3,2,1,0:T(8,128)(2,1)S(1)}) custom-call(s32[1]{0:T(128)} %bitcast.3.side_ref, s32[128]{0:T(128)S(1)} %reshape.342.offset_ref.refs_0_, s32[16]{0:T(128)S(1)} %copy-done.15, f32[64,128]{1,0:T(8,128)S(1)} %get-tuple-element.28.refs_2_, ...), custom_call_target="tpu_custom_call" | custom-call | tf_op jit(solution)/shard_map/pallas_call | solution.py:39
  33.6 3.9 %collective-permute-start.5 = (bf16[4,3,64,128]{3,2,1,0:T(8,128)(2,1)S(1)}, bf16[4,3,64,128]{3,2,1,0:T(8,128)(2,1)S(1)}, u32[]{:S(2)}, u32[]{:S(2)}) collective-permute-start(bf16[4,3,64,128]{3,2,1,0:T(8,128)(2,1)S(1)} %get-tuple-element.34), channel_id=1, source_target_pairs={{0,4},{4,0},{8,12},{12,8},{16,20},{20,16},{24,28},{28,24},{1,5},{5... | collective-permute-start | bytes 589832 | tf_op jit(solution)/shard_map/ppermute | solution.py:358
  37.5 0.7 collective-permute-start.6
  38.2 0.7 iota_add_fusion
  38.9 7.3 %collective-permute-done.5.near_ref = bf16[4,3,64,128]{3,2,1,0:T(8,128)(2,1)S(1)} collective-permute-done((bf16[4,3,64,128]{3,2,1,0:T(8,128)(2,1)S(1)}, bf16[4,3,64,128]{3,2,1,0:T(8,128)(2,1)S(1)}, u32[]{:S(2)}, u32[]{:S(2)}) %collective-permute-start.5) | collective-permute-done | bytes 196640 | tf_op jit(solution)/shard_map/ppermute | solution.py:358
  46.2 1.9 %shard_map.117 = (f32[24,3,64,128]{3,2,1,0:T(8,128)S(1)}, f32[64,128]{1,0:T(8,128)S(1)}) custom-call(s32[1]{0:T(128)} %bitcast.3.side_ref, s32[128]{0:T(128)S(1)} %reshape.342.offset_ref.refs_0_, s32[16]{0:T(128)S(1)} %copy-done.15, bf16[4,3,64,128]{3,2,1,0:T(8,128)(2,1)S(1)} %collective-permute-done.5.near_ref, ...), custom_call_target="tpu_custom_call", output_to_operand_aliasing={{0}: (5, {})} | custom-call | tf_op jit(solution)/shard_map/pallas_call | solution.py:39
  48.2 0.9 collective-permute-start.8
  49.2 0.9 collective-permute-start.9
  50.1 0.7 constant_dynamic-slice_fusion
  50.8 1.5 %collective-permute-done.8.refs_4_ = f32[64,128]{1,0:T(8,128)S(1)} collective-permute-done((f32[64,128]{1,0:T(8,128)S(1)}, f32[64,128]{1,0:T(8,128)S(1)}, u32[]{:S(2)}, u32[]{:S(2)}) %collective-permute-start.8) | collective-permute-done | bytes 32800 | tf_op jit(solution)/shard_map/ppermute | solution.py:428
  52.6 2.6 %shard_map.118 = (f32[24,3,64,128]{3,2,1,0:T(8,128)S(1)}, bf16[4,3,64,128]{3,2,1,0:T(8,128)(2,1)S(1)}, bf16[4,3,64,128]{3,2,1,0:T(8,128)(2,1)S(1)}) custom-call(s32[1]{0:T(128)} %bitcast.3.side_ref, s32[128]{0:T(128)S(1)} %reshape.342.offset_ref.refs_0_, s32[16]{0:T(128)S(1)} %copy-done.15, f32[64,128]{1,0:T(8,128)S(1)} %get-tuple-element.37.refs_2_, ...), custom_call_target="tpu_custom_call" | custom-call | tf_op jit(solution)/shard_map/pallas_call | solution.py:39
  55.3 2.1 %collective-permute-start.10 = (bf16[4,3,64,128]{3,2,1,0:T(8,128)(2,1)S(1)}, bf16[4,3,64,128]{3,2,1,0:T(8,128)(2,1)S(1)}, u32[]{:S(2)}, u32[]{:S(2)}) collective-permute-start(bf16[4,3,64,128]{3,2,1,0:T(8,128)(2,1)S(1)} %get-tuple-element.39), channel_id=1, source_target_pairs={{0,4},{4,0},{8,12},{12,8},{16,20},{20,16},{24,28},{28,24},{1,5},{5... | collective-permute-start | bytes 589832 | tf_op jit(solution)/shard_map/ppermute | solution.py:358
  58.1 8.0 %collective-permute-done.10.near_ref = bf16[4,3,64,128]{3,2,1,0:T(8,128)(2,1)S(1)} collective-permute-done((bf16[4,3,64,128]{3,2,1,0:T(8,128)(2,1)S(1)}, bf16[4,3,64,128]{3,2,1,0:T(8,128)(2,1)S(1)}, u32[]{:S(2)}, u32[]{:S(2)}) %collective-permute-start.10) | collective-permute-done | bytes 196640 | tf_op jit(solution)/shard_map/ppermute | solution.py:358
  66.1 1.9 %shard_map.119 = (f32[24,3,64,128]{3,2,1,0:T(8,128)S(1)}, f32[64,128]{1,0:T(8,128)S(1)}) custom-call(s32[1]{0:T(128)} %bitcast.3.side_ref, s32[128]{0:T(128)S(1)} %reshape.342.offset_ref.refs_0_, s32[16]{0:T(128)S(1)} %copy-done.15, bf16[4,3,64,128]{3,2,1,0:T(8,128)(2,1)S(1)} %collective-permute-done.10.near_ref, ...), custom_call_target="tpu_custom_call", output_to_operand_aliasing={{0}: (5, {})} | custom-call | tf_op jit(solution)/shard_map/pallas_call | solution.py:39
  68.0 1.4 %copy-done.4 = f32[24,3,64,128]{3,2,1,0:T(8,128)} copy-done((f32[24,3,64,128]{3,2,1,0:T(8,128)}, f32[24,3,64,128]{3,2,1,0:T(8,128)S(1)}, u32[]{:S(2)}) %copy-start.4) | copy-done | bytes 2359320
  69.4 1.1 %collective-permute-start.13 = (f32[64,128]{1,0:T(8,128)S(1)}, f32[64,128]{1,0:T(8,128)S(1)}, u32[]{:S(2)}, u32[]{:S(2)}) collective-permute-start(f32[64,128]{1,0:T(8,128)S(1)} %get-tuple-element.42.refs_2_), channel_id=1, source_target_pairs={{0,2},{1,3},{2,0},{3,1},{4,6},{5,7},{6,4},{7,5},{8,10},{9,11},{10,... | collective-permute-start | bytes 98312 | tf_op jit(solution)/shard_map/ppermute | solution.py:428
  70.5 0.8 collective-permute-start.14
  71.5 1.8 %collective-permute-done.13.refs_4_ = f32[64,128]{1,0:T(8,128)S(1)} collective-permute-done((f32[64,128]{1,0:T(8,128)S(1)}, f32[64,128]{1,0:T(8,128)S(1)}, u32[]{:S(2)}, u32[]{:S(2)}) %collective-permute-start.13) | collective-permute-done | bytes 32800 | tf_op jit(solution)/shard_map/ppermute | solution.py:428
  73.9 1.9 %copy-done.1 = bf16[16,8,3,32,128]{4,3,2,1,0:T(8,128)(2,1)S(1)} copy-done((bf16[16,8,3,32,128]{4,3,2,1,0:T(8,128)(2,1)S(1)}, bf16[16,8,3,32,128]{4,3,2,1,0:T(8,128)(2,1)}, u32[]{:S(2)}) %copy-start.1) | copy-done | bytes 3145752
  75.8 1.4 %copy-done.3 = f32[16,3,64,128]{3,2,1,0:T(8,128)S(1)} copy-done((f32[16,3,64,128]{3,2,1,0:T(8,128)S(1)}, f32[16,3,64,128]{3,2,1,0:T(8,128)}, u32[]{:S(2)}) %copy-start.3) | copy-done | bytes 1572888
  77.2 1.7 %copy-done.5 = f32[24,3,64,128]{3,2,1,0:T(8,128)S(1)} copy-done((f32[24,3,64,128]{3,2,1,0:T(8,128)S(1)}, f32[24,3,64,128]{3,2,1,0:T(8,128)}, u32[]{:S(2)}) %copy-start.5) | copy-done | bytes 2359320
  78.8 1.1 %copy-done.7 = f32[16,3,32,128]{3,2,1,0:T(8,128)S(1)} copy-done((f32[16,3,32,128]{3,2,1,0:T(8,128)S(1)}, f32[16,3,32,128]{3,2,1,0:T(8,128)}, u32[]{:S(2)}) %copy-start.7) | copy-done | bytes 786456
  80.0 5.9 %shard_map.120 = (f32[16,3,64,128]{3,2,1,0:T(8,128)S(1)}, bf16[8,96,128]{2,1,0:T(8,128)(2,1)}) custom-call(s32[128]{0:T(128)S(1)} %reshape.341.place_ref, s32[128]{0:T(128)S(1)} %reshape.342.offset_ref.refs_0_, s32[16]{0:T(128)S(1)} %copy-done.15, f32[64,128]{1,0:T(8,128)S(1)} %get-tuple-element.42.refs_2_, f32[64,128]{1,0:T(8,128)S(1)} %collective-permute-done.12.refs_3_, ...), custom_call_target="tpu_custom_call" | custom-call | tf_op jit(solution)/shard_map/pallas_call | solution.py:39
  85.8 6.7 %all-to-all-start = ((bf16[8,96,128]{2,1,0:T(8,128)(2,1)}), bf16[8,96,128]{2,1,0:T(8,128)(2,1)S(1)}, u32[]{:S(2)}, u32[]{:S(2)}) async-start(bf16[8,96,128]{2,1,0:T(8,128)(2,1)} %get-tuple-element.45), calls=%async_computation | async-start | bytes 393216 | tf_op jit(solution)/shard_map/all_to_all | solution.py:451
  93.3 2.7 %shard_map.121 = (bf16[256,1024]{1,0:T(8,128)(2,1)S(1)}, bf16[256,1024]{1,0:T(8,128)(2,1)S(1)}) custom-call(f32[8,1024]{1,0:T(8,128)S(1)} %stack.11.table_ref), custom_call_target="tpu_custom_call" | custom-call | tf_op jit(solution)/shard_map/pallas_call | solution.py:39
  96.6 1.1 %copy.43 = f32[16,3,2,4096]{3,2,1,0:T(2,128)} copy(f32[16,3,2,4096]{3,2,1,0:T(2,128)S(1)} %bitcast.47) | data formatting | bytes 3145728
  97.8 3.1 %all-to-all-done.received_ref = bf16[8,96,128]{2,1,0:T(8,128)(2,1)S(1)} async-done(((bf16[8,96,128]{2,1,0:T(8,128)(2,1)}), bf16[8,96,128]{2,1,0:T(8,128)(2,1)S(1)}, u32[]{:S(2)}, u32[]{:S(2)}) %all-to-all-start) | async-done | bytes 196640 | tf_op jit(solution)/shard_map/all_to_all | solution.py:451
  100.9 3.7 %shard_map.122 = bf16[1,3,256,256]{3,2,1,0:T(8,128)(2,1)S(1)} custom-call(s32[1]{0:T(128)} %bitcast.26.covers_ref, bf16[8,96,128]{2,1,0:T(8,128)(2,1)S(1)} %all-to-all-done.received_ref, bf16[256,1024]{1,0:T(8,128)(2,1)S(1)} %get-tuple-element.46.row_ref, bf16[256,1024]{1,0:T(8,128)(2,1)S(1)} %get-tuple-element.47.col_ref, ...), custom_call_target="tpu_custom_call" | custom-call | tf_op jit(solution)/shard_map/pallas_call | solution.py:39
  104.6 0.7 copy.44
  (80 shorter events, 5.8 us)
Async XLA Ops:
  0.6 1.4 %copy-start.8 = (f32[16,3,2,4096]{3,2,1,0:T(2,128)S(1)}, f32[16,3,2,4096]{3,2,1,0:T(2,128)}, u32[]{:S(2)}) copy-start(f32[16,3,2,4096]{3,2,1,0:T(2,128)} %param.10) | copy-start | bytes 4718596
  2.0 10.0 %copy-start.9 = (f32[16,3,2,4096]{3,2,1,0:T(2,128)S(1)}, f32[16,3,2,4096]{3,2,1,0:T(2,128)}, u32[]{:S(2)}) copy-start(f32[16,3,2,4096]{3,2,1,0:T(2,128)} %param.10) | copy-start | bytes 4718596
  3.0 21.1 %collective-permute-start = (bf16[4,3,64,128]{3,2,1,0:T(8,128)(2,1)}, bf16[4,3,64,128]{3,2,1,0:T(8,128)(2,1)S(1)}, u32[]{:S(2)}, u32[]{:S(2)}) collective-permute-start(bf16[4,3,64,128]{3,2,1,0:T(8,128)(2,1)} %get-tuple-element.25), channel_id=1, source_target_pairs={{0,4},{4,0},{8,12},{12,8},{16,20},{20,16},{24,28},{28,24},{1,5},{5... | collective-permute-start | bytes 589832 | tf_op jit(solution)/shard_map/ppermute | solution.py:358
  5.9 18.1 %collective-permute-start.1 = (bf16[4,3,64,128]{3,2,1,0:T(8,128)(2,1)}, bf16[4,3,64,128]{3,2,1,0:T(8,128)(2,1)S(1)}, u32[]{:S(2)}, u32[]{:S(2)}) collective-permute-start(bf16[4,3,64,128]{3,2,1,0:T(8,128)(2,1)} %get-tuple-element.26), channel_id=1, source_target_pairs={{4,8},{8,4},{12,16},{16,12},{20,24},{24,20},{5,9},{9,5},{13,17},{1... | collective-permute-start | bytes 589832 | tf_op jit(solution)/shard_map/ppermute | solution.py:357
  8.9 0.6 copy-start.18
  9.8 2.2 %copy-start.20 = (s32[8,32]{1,0:T(8,128)}, s32[8,32]{1,0:T(8,128)S(1)}, u32[]{:S(2)}) copy-start(s32[8,32]{1,0:T(8,128)S(1)} %convert_reduce_fusion) | copy-start | bytes 3076
  10.7 1.3 %copy-start.19 = (s32[8,32,2]{1,0,2:T(8,128)}, s32[8,32,2]{1,0,2:T(8,128)S(1)}, u32[]{:S(2)}) copy-start(s32[8,32,2]{1,0,2:T(8,128)S(1)} %reshape.340) | copy-start | bytes 6148
  12.1 1.9 %copy-start.10 = (bf16[16,8,3,4096]{3,1,2,0:T(8,128)(2,1)S(1)}, bf16[16,8,3,4096]{3,1,2,0:T(8,128)(2,1)}, u32[]{:S(2)}) copy-start(bf16[16,8,3,4096]{3,1,2,0:T(8,128)(2,1)} %param.14) | copy-start | bytes 9437188
  14.0 1.4 %copy-start.11 = (f32[16,3,2,4096]{3,2,1,0:T(2,128)S(1)}, f32[16,3,2,4096]{3,2,1,0:T(2,128)}, u32[]{:S(2)}) copy-start(f32[16,3,2,4096]{3,2,1,0:T(2,128)} %param.11) | copy-start | bytes 4718596
  15.4 1.4 %copy-start.12 = (f32[16,3,2,4096]{3,2,1,0:T(2,128)S(1)}, f32[16,3,2,4096]{3,2,1,0:T(2,128)}, u32[]{:S(2)}) copy-start(f32[16,3,2,4096]{3,2,1,0:T(2,128)} %param.12) | copy-start | bytes 4718596
  16.8 1.1 %copy-start.13 = (f32[16,3,4096]{2,0,1:T(8,128)S(1)}, f32[16,3,4096]{2,0,1:T(8,128)}, u32[]{:S(2)}) copy-start(f32[16,3,4096]{2,0,1:T(8,128)} %param.13) | copy-start | bytes 2359300
  17.9 5.3 %copy-start.23 = (s32[16]{0:T(128)S(1)}, s32[16]{0:T(128)}, u32[]{:S(2)}) copy-start(s32[16]{0:T(128)} %get-tuple-element.62) | copy-start | bytes 196
  17.9 5.3 %copy-start.24 = (s32[16]{0:T(128)S(1)}, s32[16]{0:T(128)}, u32[]{:S(2)}) copy-start(s32[16]{0:T(128)} %get-tuple-element.63) | copy-start | bytes 196
  17.9 6.1 %copy-start.15 = (s32[16]{0:T(128)S(1)}, s32[16]{0:T(128)}, u32[]{:S(2)}) copy-start(s32[16]{0:T(128)} %refs_1_.5) | copy-start | bytes 196
  23.1 29.5 %copy-start = (bf16[16,8,3,32,128]{4,3,2,1,0:T(8,128)(2,1)}, bf16[16,8,3,32,128]{4,3,2,1,0:T(8,128)(2,1)S(1)}, u32[]{:S(2)}) copy-start(bf16[16,8,3,32,128]{4,3,2,1,0:T(8,128)(2,1)S(1)} %get-tuple-element.33.refs_10_) | copy-start | bytes 9437188
  23.1 29.5 %copy-start.2 = (f32[16,3,64,128]{3,2,1,0:T(8,128)}, f32[16,3,64,128]{3,2,1,0:T(8,128)S(1)}, u32[]{:S(2)}) copy-start(f32[16,3,64,128]{3,2,1,0:T(8,128)S(1)} %get-tuple-element.31.refs_8_) | copy-start | bytes 4718596
  23.2 29.5 %copy-start.6 = (f32[16,3,32,128]{3,2,1,0:T(8,128)}, f32[16,3,32,128]{3,2,1,0:T(8,128)S(1)}, u32[]{:S(2)}) copy-start(f32[16,3,32,128]{3,2,1,0:T(8,128)S(1)} %get-tuple-element.32.refs_9_) | copy-start | bytes 2359300
  25.9 2.6 %collective-permute-start.2 = (f32[64,128]{1,0:T(8,128)S(1)}, f32[64,128]{1,0:T(8,128)S(1)}, u32[]{:S(2)}, u32[]{:S(2)}) collective-permute-start(f32[64,128]{1,0:T(8,128)S(1)} %get-tuple-element.28.refs_2_), channel_id=1, source_target_pairs={{0,1},{1,0},{2,3},{3,2},{4,5},{5,4},{6,7},{7,6},{8,9},{9,8},{10,11... | collective-permute-start | bytes 98312 | tf_op jit(solution)/shard_map/ppermute | solution.py:428
  26.0 4.0 %collective-permute-start.3 = (f32[64,128]{1,0:T(8,128)S(1)}, f32[64,128]{1,0:T(8,128)S(1)}, u32[]{:S(2)}, u32[]{:S(2)}) collective-permute-start(f32[64,128]{1,0:T(8,128)S(1)} %get-tuple-element.28.refs_2_), channel_id=1, source_target_pairs={{0,2},{1,3},{2,0},{3,1},{4,6},{5,7},{6,4},{7,5},{8,10},{9,11},{10,... | collective-permute-start | bytes 98312 | tf_op jit(solution)/shard_map/ppermute | solution.py:428
  27.6 3.3 %collective-permute-start.4 = (f32[64,128]{1,0:T(8,128)S(1)}, f32[64,128]{1,0:T(8,128)S(1)}, u32[]{:S(2)}, u32[]{:S(2)}) collective-permute-start(f32[64,128]{1,0:T(8,128)S(1)} %get-tuple-element.28.refs_2_), channel_id=1, source_target_pairs={{0,3},{1,2},{2,1},{3,0},{4,7},{5,6},{6,5},{7,4},{8,11},{9,10},{10,... | collective-permute-start | bytes 98312 | tf_op jit(solution)/shard_map/ppermute | solution.py:428
  33.6 12.6 %collective-permute-start.5 = (bf16[4,3,64,128]{3,2,1,0:T(8,128)(2,1)S(1)}, bf16[4,3,64,128]{3,2,1,0:T(8,128)(2,1)S(1)}, u32[]{:S(2)}, u32[]{:S(2)}) collective-permute-start(bf16[4,3,64,128]{3,2,1,0:T(8,128)(2,1)S(1)} %get-tuple-element.34), channel_id=1, source_target_pairs={{0,4},{4,0},{8,12},{12,8},{16,20},{20,16},{24,28},{28,24},{1,5},{5... | collective-permute-start | bytes 589832 | tf_op jit(solution)/shard_map/ppermute | solution.py:358
  37.5 8.7 %collective-permute-start.6 = (bf16[4,3,64,128]{3,2,1,0:T(8,128)(2,1)S(1)}, bf16[4,3,64,128]{3,2,1,0:T(8,128)(2,1)S(1)}, u32[]{:S(2)}, u32[]{:S(2)}) collective-permute-start(bf16[4,3,64,128]{3,2,1,0:T(8,128)(2,1)S(1)} %get-tuple-element.35), channel_id=1, source_target_pairs={{4,8},{8,4},{12,16},{16,12},{20,24},{24,20},{5,9},{9,5},{13,17},{1... | collective-permute-start | bytes 589832 | tf_op jit(solution)/shard_map/ppermute | solution.py:357
  48.1 2.6 %collective-permute-start.7 = (f32[64,128]{1,0:T(8,128)S(1)}, f32[64,128]{1,0:T(8,128)S(1)}, u32[]{:S(2)}, u32[]{:S(2)}) collective-permute-start(f32[64,128]{1,0:T(8,128)S(1)} %get-tuple-element.37.refs_2_), channel_id=1, source_target_pairs={{0,1},{1,0},{2,3},{3,2},{4,5},{5,4},{6,7},{7,6},{8,9},{9,8},{10,11... | collective-permute-start | bytes 98312 | tf_op jit(solution)/shard_map/ppermute | solution.py:428
  48.2 4.0 %collective-permute-start.8 = (f32[64,128]{1,0:T(8,128)S(1)}, f32[64,128]{1,0:T(8,128)S(1)}, u32[]{:S(2)}, u32[]{:S(2)}) collective-permute-start(f32[64,128]{1,0:T(8,128)S(1)} %get-tuple-element.37.refs_2_), channel_id=1, source_target_pairs={{0,2},{1,3},{2,0},{3,1},{4,6},{5,7},{6,4},{7,5},{8,10},{9,11},{10,... | collective-permute-start | bytes 98312 | tf_op jit(solution)/shard_map/ppermute | solution.py:428
  49.2 3.5 %collective-permute-start.9 = (f32[64,128]{1,0:T(8,128)S(1)}, f32[64,128]{1,0:T(8,128)S(1)}, u32[]{:S(2)}, u32[]{:S(2)}) collective-permute-start(f32[64,128]{1,0:T(8,128)S(1)} %get-tuple-element.37.refs_2_), channel_id=1, source_target_pairs={{0,3},{1,2},{2,1},{3,0},{4,7},{5,6},{6,5},{7,4},{8,11},{9,10},{10,... | collective-permute-start | bytes 98312 | tf_op jit(solution)/shard_map/ppermute | solution.py:428
  55.3 10.8 %collective-permute-start.10 = (bf16[4,3,64,128]{3,2,1,0:T(8,128)(2,1)S(1)}, bf16[4,3,64,128]{3,2,1,0:T(8,128)(2,1)S(1)}, u32[]{:S(2)}, u32[]{:S(2)}) collective-permute-start(bf16[4,3,64,128]{3,2,1,0:T(8,128)(2,1)S(1)} %get-tuple-element.39), channel_id=1, source_target_pairs={{0,4},{4,0},{8,12},{12,8},{16,20},{20,16},{24,28},{28,24},{1,5},{5... | collective-permute-start | bytes 589832 | tf_op jit(solution)/shard_map/ppermute | solution.py:358
  57.4 8.7 %collective-permute-start.11 = (bf16[4,3,64,128]{3,2,1,0:T(8,128)(2,1)S(1)}, bf16[4,3,64,128]{3,2,1,0:T(8,128)(2,1)S(1)}, u32[]{:S(2)}, u32[]{:S(2)}) collective-permute-start(bf16[4,3,64,128]{3,2,1,0:T(8,128)(2,1)S(1)} %get-tuple-element.40), channel_id=1, source_target_pairs={{4,8},{8,4},{12,16},{16,12},{20,24},{24,20},{5,9},{9,5},{13,17},{1... | collective-permute-start | bytes 589832 | tf_op jit(solution)/shard_map/ppermute | solution.py:357
  68.0 1.4 %copy-start.4 = (f32[24,3,64,128]{3,2,1,0:T(8,128)}, f32[24,3,64,128]{3,2,1,0:T(8,128)S(1)}, u32[]{:S(2)}) copy-start(f32[24,3,64,128]{3,2,1,0:T(8,128)S(1)} %get-tuple-element.43.refs_6_) | copy-start | bytes 7077892
  69.4 2.1 %collective-permute-start.12 = (f32[64,128]{1,0:T(8,128)S(1)}, f32[64,128]{1,0:T(8,128)S(1)}, u32[]{:S(2)}, u32[]{:S(2)}) collective-permute-start(f32[64,128]{1,0:T(8,128)S(1)} %get-tuple-element.42.refs_2_), channel_id=1, source_target_pairs={{0,1},{1,0},{2,3},{3,2},{4,5},{5,4},{6,7},{7,6},{8,9},{9,8},{10,11... | collective-permute-start | bytes 98312 | tf_op jit(solution)/shard_map/ppermute | solution.py:428
  69.4 3.9 %collective-permute-start.13 = (f32[64,128]{1,0:T(8,128)S(1)}, f32[64,128]{1,0:T(8,128)S(1)}, u32[]{:S(2)}, u32[]{:S(2)}) collective-permute-start(f32[64,128]{1,0:T(8,128)S(1)} %get-tuple-element.42.refs_2_), channel_id=1, source_target_pairs={{0,2},{1,3},{2,0},{3,1},{4,6},{5,7},{6,4},{7,5},{8,10},{9,11},{10,... | collective-permute-start | bytes 98312 | tf_op jit(solution)/shard_map/ppermute | solution.py:428
  70.5 3.3 %collective-permute-start.14 = (f32[64,128]{1,0:T(8,128)S(1)}, f32[64,128]{1,0:T(8,128)S(1)}, u32[]{:S(2)}, u32[]{:S(2)}) collective-permute-start(f32[64,128]{1,0:T(8,128)S(1)} %get-tuple-element.42.refs_2_), channel_id=1, source_target_pairs={{0,3},{1,2},{2,1},{3,0},{4,7},{5,6},{6,5},{7,4},{8,11},{9,10},{10,... | collective-permute-start | bytes 98312 | tf_op jit(solution)/shard_map/ppermute | solution.py:428
  73.9 1.9 %copy-start.1 = (bf16[16,8,3,32,128]{4,3,2,1,0:T(8,128)(2,1)S(1)}, bf16[16,8,3,32,128]{4,3,2,1,0:T(8,128)(2,1)}, u32[]{:S(2)}) copy-start(bf16[16,8,3,32,128]{4,3,2,1,0:T(8,128)(2,1)} %copy-done) | copy-start | bytes 9437188
  75.7 1.4 %copy-start.3 = (f32[16,3,64,128]{3,2,1,0:T(8,128)S(1)}, f32[16,3,64,128]{3,2,1,0:T(8,128)}, u32[]{:S(2)}) copy-start(f32[16,3,64,128]{3,2,1,0:T(8,128)} %copy-done.2) | copy-start | bytes 4718596
  77.2 1.7 %copy-start.5 = (f32[24,3,64,128]{3,2,1,0:T(8,128)S(1)}, f32[24,3,64,128]{3,2,1,0:T(8,128)}, u32[]{:S(2)}) copy-start(f32[24,3,64,128]{3,2,1,0:T(8,128)} %copy-done.4) | copy-start | bytes 7077892
  78.8 1.1 %copy-start.7 = (f32[16,3,32,128]{3,2,1,0:T(8,128)S(1)}, f32[16,3,32,128]{3,2,1,0:T(8,128)}, u32[]{:S(2)}) copy-start(f32[16,3,32,128]{3,2,1,0:T(8,128)} %copy-done.6) | copy-start | bytes 2359300
  80.0 12.6 %copy-start.16 = (s32[8,8,16]{2,1,0:T(8,128)S(1)}, s32[8,8,16]{2,1,0:T(8,128)}, u32[]{:S(2)}) copy-start(s32[8,8,16]{2,1,0:T(8,128)} %multiply_add_fusion) | copy-start | bytes 12292
  80.0 12.7 %copy-start.17 = (s32[8,8,16]{2,1,0:T(8,128)S(1)}, s32[8,8,16]{2,1,0:T(8,128)}, u32[]{:S(2)}) copy-start(s32[8,8,16]{2,1,0:T(8,128)} %iota_add_fusion) | copy-start | bytes 12292
  80.0 12.8 %copy-start.22 = (pred[8,8]{1,0:T(8,128)(4,1)S(1)}, pred[8,8]{1,0:T(8,128)(4,1)}, u32[]{:S(2)}) copy-start(pred[8,8]{1,0:T(8,128)(4,1)} %get-tuple-element.56) | copy-start | bytes 196
  80.0 16.1 %copy-start.21 = (s32[128,2]{0,1:T(2,128)S(1)}, s32[128,2]{0,1:T(2,128)}, u32[]{:S(2)}) copy-start(s32[128,2]{0,1:T(2,128)} %param.17) | copy-start | bytes 3076
  85.8 15.1 %copy-start.14 = (bf16[1,3,256,256]{3,2,1,0:T(8,128)(2,1)S(1)}, bf16[1,3,256,256]{3,2,1,0:T(8,128)(2,1)}, u32[]{:S(2)}) copy-start(bf16[1,3,256,256]{3,2,1,0:T(8,128)(2,1)} %pixels_ref.1) | copy-start | bytes 1179652
  85.8 15.0 %all-to-all-start = ((bf16[8,96,128]{2,1,0:T(8,128)(2,1)}), bf16[8,96,128]{2,1,0:T(8,128)(2,1)S(1)}, u32[]{:S(2)}, u32[]{:S(2)}) async-start(bf16[8,96,128]{2,1,0:T(8,128)(2,1)} %get-tuple-element.45), calls=%async_computation | async-start | bytes 393216 | tf_op jit(solution)/shard_map/all_to_all | solution.py:451
where the time goes:
time: 106 us; the launch traced here: 105 us
  Pallas kernels  29.4 us (28%)
  waiting for transfers between devices  25 us (24%)
  starting transfers between devices  23.4 us (22%)
  local copies, waits for them, and re-layouts  22.2 us (21%)
  other arithmetic  4.35 us (4%)
    pallas_call x10, Pallas kernels, call(): pl.pallas_call(body, in_specs=specs, out_specs=tuple((ON_CHIP for _ in ou...  29.4 us
    unnamed x55, local copies, waits for them, and re-layouts  19.6 us
    ppermute x3, waiting for transfers between devices, exchange(): near = lax.ppermute(near, 'gran', near_pairs)  15.3 us
    ppermute x3, starting transfers between devices, exchange(): near = lax.ppermute(near, 'gran', near_pairs)  9.01 us
    all_to_all x1, starting transfers between devices, per_device(): lax.all_to_all(payload, 'gran', split_axis=0, concat_axis=0, tiled=True)  6.69 us
    ppermute x9, waiting for transfers between devices, per_device(): lax.ppermute(partial, 'band', [(i, i ^ flip) for i in range(band_total)])  6.57 us
    ppermute x9, starting transfers between devices, per_device(): lax.ppermute(partial, 'band', [(i, i ^ flip) for i in range(band_total)])  5.73 us
    all_to_all x1, waiting for transfers between devices, per_device(): lax.all_to_all(payload, 'gran', split_axis=0, concat_axis=0, tiled=True)  3.12 us
  transfers between devices with their start and end apart: 16, of which 9 were waited for; matrix products, arithmetic and copies ran while one was open for 10% of the time, Pallas kernels for 7%

commit v1 on v0

v1 whole, which is shorter than its diff:
```python
import functools
import jax
import jax.numpy as jnp
from jax import lax
from jax.experimental import pallas as pl
from jax.experimental.pallas import tpu as pltpu
from jax.sharding import PartitionSpec as P

BANDS = 12
KN = 64
PATCH = 8
REACH = 4
SWEEPS = 3
SP = 32
LANES = 128
SPAN = 16

robust_scale = 0.3

ON_CHIP = pl.BlockSpec(memory_space=pltpu.VMEM)
ANYWHERE = pl.BlockSpec(memory_space=pl.ANY)
f32 = jnp.float32
bf16 = jnp.bfloat16


def call(body, inputs, outputs, scratch=(), aliases=None, limit=16):
    operands = [
        pltpu.with_memory_space_constraint(array, pltpu.VMEM) if kind == "v" else array
        for kind, array in inputs
    ]
    return pl.pallas_call(
        body,
        in_specs=[ON_CHIP if kind == "v" else ANYWHERE for kind, _ in inputs],
        out_specs=tuple(ON_CHIP if kind == "v" else ANYWHERE for kind, _, _ in outputs),
        out_shape=tuple(
            pltpu.VMEM(shape, dtype) if kind == "v" else jax.ShapeDtypeStruct(shape, dtype)
            for kind, shape, dtype in outputs
        ),
        scratch_shapes=list(scratch),
        input_output_aliases=aliases or {},
        compiler_params=pltpu.CompilerParams(vmem_limit_bytes=limit * 2**20),
    )(*operands)


def parity():
    return lax.rem(lax.axis_index("gran"), 2)


def first_edges(grids_ref, near_ref, far_ref, raw, sems):
    odd = parity()
    last = grids_ref.shape[0] - REACH
    sides = ((far_ref, odd * last), (near_ref, (1 - odd) * last))
    copies = [
        pltpu.make_async_copy(grids_ref.at[pl.ds(base, REACH)], raw.at[k], sems.at[k])
        for k, (_, base) in enumerate(sides)
    ]
    for copy in copies:
        copy.start()
    for k, (ref, _) in enumerate(sides):
        copies[k].wait()
        for g in range(REACH):
            for b in range(ref.shape[1]):
                for j in range(4):
                    both = [raw[k, g, b, pl.ds(2 * j + c, 8, stride=8), :] for c in range(2)]
                    ref[g, b, 16 * j : 16 * j + 16, :] = jnp.concatenate(both, axis=0).astype(bf16)


def arrange(grids_ref, rhs_ref, diag_ref, cross_ref, coupling_ref, ext_ref, rhs_out, diag_out, cross_out, coupling_out, grids_raw, cross_raw, coupling_raw, wide, sems):
    granules, bands = grids_ref.shape[:2]
    slots = coupling_out.shape[1]
    chunks = sems.shape[1]
    size = granules // chunks
    whole = pltpu.make_async_copy(cross_ref, cross_raw, sems.at[4, 0])
    whole.start()
    copies = []
    for n in range(chunks):
        part = pl.ds(n * size, size)
        moves = ((coupling_ref, coupling_raw), (diag_ref, diag_out), (grids_ref, grids_raw), (rhs_ref, rhs_out))
        copies.append(
            [
                pltpu.make_async_copy(source.at[part], target.at[part], sems.at[k, n])
                for k, (source, target) in enumerate(moves)
            ]
        )
        for copy in copies[n]:
            copy.start()
    whole.wait()

    def step(i, carry):
        for b in range(bands):
            wide[b] = coupling_raw[i, b].astype(f32)
        for b in range(bands):
            for j in range(4):
                d = []
                for c in range(2):
                    rows = pl.ds(2 * j + c, 8, stride=8)
                    to = slice(16 * j + 8 * c, 16 * j + 8 * c + 8)
                    ext_ref[i + REACH, b, to, :] = grids_raw[i, b, rows, :]
                    d.append(diag_out[i, b, rows, :])
                pick = cross_raw[b, i // 8, pl.ds(8 * j + i % 8, 8, stride=32), :]
                cross_out[i, b, 8 * j : 8 * j + 8, :] = pick * jnp.sqrt(d[0] * d[1])
        for b in range(bands):
            for s in range(slots):
                for j in (0, 2):
                    pair = [wide[b, pl.ds(8 * (j + k) + s, 8, stride=32), :] for k in (0, 1)]
                    coupling_out[i, s, b, 8 * j : 8 * j + 16, :] = jnp.concatenate(pair, axis=0).astype(bf16)
        return carry

    for n in range(chunks):
        for copy in copies[n]:
            copy.wait()
        lax.fori_loop(n * size, (n + 1) * size, step, 0)


def lane_sums():
    row = lax.broadcasted_iota(jnp.int32, (LANES, LANES), 0)
    col = lax.broadcasted_iota(jnp.int32, (LANES, LANES), 1)
    return ((row % KN) // PATCH == col % PATCH).astype(f32).astype(bf16)


def lane_spread():
    row = lax.broadcasted_iota(jnp.int32, (LANES, LANES), 0)
    col = lax.broadcasted_iota(jnp.int32, (LANES, LANES), 1)
    return ((col % KN) // PATCH == row % PATCH).astype(f32).astype(bf16)


def read_graph(offset_ref, count_ref, graph):
    slots, granules = offset_ref.shape
    slot = lax.broadcasted_iota(jnp.int32, offset_ref.shape, 0)
    codes = jnp.sum(jnp.left_shift(offset_ref[...] + REACH, 4 * slot), axis=0, keepdims=True)
    counts = count_ref[...]
    for i in range(granules):
        graph[0, i] = codes[0, i]
        graph[1, i] = counts[0, i]


def neighbour(graph, i, s):
    return i + jnp.bitwise_and(jnp.right_shift(graph[0, i], 4 * s), 15)


def group_mask(interior, slots):
    row = lax.broadcasted_iota(jnp.int32, (64, LANES), 0) // 32
    lane = lax.broadcasted_iota(jnp.int32, (64, LANES), 1) // PATCH
    return lane - slots * (1 - row if interior else row)


def disparities(interior, offset_ref, count_ref, ext_ref, gathered, graph):
    bands = ext_ref.shape[1]
    granules = ext_ref.shape[0] - 2 * REACH
    slots = gathered.shape[0]
    gathered[...] = jnp.zeros_like(gathered)
    read_graph(offset_ref, count_ref, graph)

    def response(g):
        return [
            ext_ref[g, b, 16 * j : 16 * j + 8, :] + ext_ref[g, b, 16 * j + 8 : 16 * j + 16, :]
            for b in range(bands)
            for j in range(4)
        ]

    for i in range(granules):
        if (REACH <= i < granules - REACH) != interior:
            continue
        own = response(i + REACH)

        def slot(s, carry, i=i, own=own):
            total = None
            for a, o in zip(own, response(neighbour(graph, i, s))):
                d = a - o
                total = d * d if total is None else total + d * d
            gathered[s, 8 * (i % 8) : 8 * (i % 8) + 8, :] = total
            return carry

        lax.fori_loop(0, graph[1, i], slot, 0)
    sums = jnp.dot(
        gathered[...].reshape(slots * 64, LANES).astype(bf16), lane_sums(), preferred_element_type=f32
    )
    place = group_mask(interior, slots)
    packed = jnp.zeros((64, LANES), f32)
    for s in range(slots):
        packed = jnp.where(place == s, sums[64 * s : 64 * s + 64], packed)
    return packed


def interior_disparities(offset_ref, count_ref, ext_ref, out_ref, gathered, graph):
    out_ref[...] = disparities(True, offset_ref, count_ref, ext_ref, gathered, graph)


def edge_disparities(offset_ref, count_ref, near_ref, far_ref, inner_ref, ext_in, ext_ref, out_ref, gathered, graph):
    del ext_in
    odd = parity()
    right = ext_ref.shape[0] - REACH
    for ref, base in ((near_ref, (1 - odd) * right), (far_ref, odd * right)):
        for g in range(REACH):
            for b in range(ref.shape[1]):
                ext_ref[base + g, b] = ref[g, b].astype(f32)
    out_ref[...] = inner_ref[...] + disparities(False, offset_ref, count_ref, ext_ref, gathered, graph)


def spread_weights(shares, interior, weights):
    slots = weights.shape[0]
    total = (shares[0][...] + shares[1][...]) + (shares[2][...] + shares[3][...])
    robust = 1.0 / (1.0 + total * (1.0 / (robust_scale * BANDS * PATCH * PATCH)))
    high = robust.astype(bf16).astype(f32)
    both = jnp.concatenate([high, robust - high], axis=1)
    place = group_mask(interior, slots)
    place = jnp.concatenate([place, place], axis=1)
    spread = lane_spread()
    spread = jnp.concatenate([spread, spread], axis=0)
    stacked = jnp.concatenate(
        [jnp.where(place == s, both, 0.0).astype(bf16) for s in range(slots)], axis=0
    )
    weights[...] = jnp.dot(stacked, spread, preferred_element_type=f32).reshape(slots, 64, LANES)


def balance(i, ext_ref, rhs_ref, diag_ref, cross_ref, coupling_ref, weights, graph, store):
    bands = rhs_ref.shape[1]
    row = pl.multiple_of(lax.rem(i, 8) * 8, 8)
    parts = [(b, j) for b in range(bands) for j in range(4)]
    rhs = tuple(rhs_ref[i, b, pl.ds(2 * j + c, 8, stride=8), :] for b, j in parts for c in range(2))

    def slot(s, sums):
        sigma, drive = sums
        weight = weights[s, pl.ds(row, 8), :]
        n = neighbour(graph, i, s)
        new_sigma, new_drive = [], []
        for b in range(bands):
            coupling = coupling_ref[i, s, b].astype(f32)
            for j in range(4):
                k = 4 * b + j
                effective = weight * coupling[8 * j : 8 * j + 8]
                new_sigma.append(sigma[k] + effective)
                for c in range(2):
                    grid = ext_ref[n, b, 16 * j + 8 * c : 16 * j + 8 * c + 8, :]
                    new_drive.append(drive[2 * k + c] + effective * grid)
        return tuple(new_sigma), tuple(new_drive)

    zero = jnp.zeros((8, LANES), f32)
    sigma, drive = lax.fori_loop(0, graph[1, i], slot, ((zero,) * len(parts), rhs))
    for k, (b, j) in enumerate(parts):
        first, second = (
            diag_ref[i, b, pl.ds(2 * j + c, 8, stride=8), :] + sigma[k] for c in range(2)
        )
        cross = cross_ref[i, b, 8 * j : 8 * j + 8, :]
        inverse = 1.0 / (first * second - cross * cross)
        gain, offset = drive[2 * k], drive[2 * k + 1]
        store(
            b,
            j,
            (second * gain - cross * offset) * inverse,
            (first * offset - cross * gain) * inverse,
        )


def edge_sweep(offset_ref, count_ref, *refs):
    shares, state, (new_ref, near_ref, far_ref, weights, graph) = refs[:4], refs[4:9], refs[9:]
    read_graph(offset_ref, count_ref, graph)
    spread_weights(shares, False, weights)
    odd = parity()
    last = new_ref.shape[0] - 3 * REACH
    for ref, base in ((far_ref, odd * last), (near_ref, (1 - odd) * last)):

        def step(g, carry, ref=ref, base=base):
            def store(b, j, gain, offset):
                both = jnp.concatenate([gain, offset], axis=0)
                new_ref[base + g + REACH, b, 16 * j : 16 * j + 16, :] = both
                ref[g, b, 16 * j : 16 * j + 16, :] = both.astype(bf16)

            balance(base + g, *state, weights, graph, store)
            return carry

        lax.fori_loop(0, REACH, step, 0)


def interior_sweep(offset_ref, count_ref, *refs):
    shares, state, (_, new_ref, weights, graph) = refs[:4], refs[4:9], refs[9:]
    read_graph(offset_ref, count_ref, graph)
    spread_weights(shares, True, weights)

    def step(i, carry):
        def store(b, j, gain, offset):
            both = jnp.concatenate([gain, offset], axis=0)
            new_ref[i + REACH, b, 16 * j : 16 * j + 16, :] = both

        balance(i, *state, weights, graph, store)
        return carry

    lax.fori_loop(REACH, new_ref.shape[0] - 3 * REACH, step, 0)


def own_columns(ref, at, granules):
    first = lax.axis_index("gran") * granules
    base = pl.multiple_of((first // LANES) * LANES, LANES)
    turn = jnp.bitwise_and(LANES - lax.rem(first, LANES), LANES - 1)
    return pltpu.roll(ref[at + (pl.ds(base, LANES),)], turn, 1)


def last_sweep(offset_ref, count_ref, *refs):
    shares, state, (route_ref, window_ref) = refs[:4], refs[4:9], refs[9:11]
    out_ref, send_ref, solved, windows, weights, graph, ranks, sems = refs[11:]
    granules, bands = solved.shape[:2]
    read_graph(offset_ref, count_ref, graph)
    windows[...] = jnp.zeros_like(windows)
    for owner in range(windows.shape[0]):
        ranks[owner] = 0
    chunks = sems.shape[0]
    size = granules // chunks
    copies = []
    for interior in (True, False):
        spread_weights(shares, interior, weights)

        def step(t, carry, interior=interior):
            i = t if interior else jnp.where(t < REACH, t, t + granules - 2 * REACH)

            def store(b, j, gain, offset):
                solved[i, b, pl.ds(2 * j, 8, stride=8), :] = gain
                solved[i, b, pl.ds(2 * j + 1, 8, stride=8), :] = offset

            balance(i, *state, weights, graph, store)
            return carry

        lax.fori_loop(*((REACH, granules - REACH) if interior else (0, 2 * REACH)), step, 0)
        for n in range(chunks):
            if (REACH <= n * size < granules - REACH) == interior:
                part = pl.ds(n * size, size)
                copies.append(pltpu.make_async_copy(solved.at[part], out_ref.at[part], sems.at[n]))
                copies[-1].start()
    lane = lax.broadcasted_iota(jnp.int32, (8, LANES), 1) // SPAN
    routes = own_columns(route_ref, (slice(None),), granules)
    tops, lefts = [], []
    for r in range(2):
        starts = own_columns(window_ref, (r, slice(None)), granules)
        knots = jnp.clip(jnp.right_shift(starts, 5) - 1, 0, KN - SPAN)
        tops.append(jnp.right_shift(knots, 1))
        lefts.append(knots)
    for i in range(granules):
        for r in range(2):
            owner = routes[r, i]
            rank = ranks[owner]
            ranks[owner] = rank + 1
            top = tops[r][0, i]
            turn = rank * SPAN - lefts[r][1, i] + LANES
            here = lane == rank
            for b in range(bands):
                for c in range(2):
                    rows = solved[i, b, pl.ds(2 * top + c, 8, stride=2), :]
                    for half in (0, 1):
                        at = 16 * (2 * b + c) + 8 * half
                        moved = pltpu.roll(rows, jnp.bitwise_and(turn + KN * half, LANES - 1), 1)
                        pltpu.store(windows.at[owner, at : at + 8, :], moved, mask=here)
    send_ref[...] = windows[...].astype(bf16)
    for copy in copies:
        copy.wait()


def cubic(distance):
    near = (1.5 * distance - 2.5) * distance * distance + 1.0
    far = ((2.5 - 0.5 * distance) * distance - 4.0) * distance + 2.0
    return jnp.where(distance <= 1.0, near, jnp.where(distance < 2.0, far, 0.0))


def interp_weights(route_ref, window_ref, rows_out, cols_out):
    pixels, lanes = rows_out.shape
    senders = lanes // LANES
    granules = route_ref.shape[1] // senders
    own = lax.axis_index("gran")
    lane = lax.broadcasted_iota(jnp.int32, (8, LANES), 1)
    seat, step = lane // SPAN, lane % SPAN

    def sender(n, carry):
        first = n * granules
        base = pl.multiple_of((first // LANES) * LANES, LANES)
        turn = jnp.bitwise_and(LANES - lax.rem(first, LANES), LANES - 1)
        at = pl.ds(base, LANES)
        routes = pltpu.roll(route_ref[:, at], turn, 1)
        starts = [pltpu.roll(window_ref[r, :, at], turn, 1) for r in range(2)]
        rank = jnp.int32(0)
        place = [jnp.full((8, LANES), -1, jnp.int32) for _ in range(2)]
        for i in range(granules):
            for r in range(2):
                hit = routes[r, i] == own
                here = seat == jnp.where(hit, rank, -1)
                rank = rank + hit.astype(jnp.int32)
                for k in range(2):
                    place[k] = jnp.where(here, starts[r][k, i], place[k])
        to = pl.ds(pl.multiple_of(n * LANES, LANES), LANES)
        for k, ref in ((0, rows_out), (1, cols_out)):
            first_knot = jnp.clip(jnp.right_shift(place[k], 5) - 1, 0, KN - SPAN)
            if k == 0:
                knot = 2 * jnp.right_shift(first_knot, 1) + 2 * (step % 8) + step // 8
            else:
                knot = first_knot + step
            beyond = jnp.where(knot == 0, -1, jnp.where(knot == KN - 1, KN, 4 * KN))
            dead = place[k] < 0
            knot = jnp.where(dead, 4 * KN, knot).astype(f32)
            beyond = jnp.where(dead, 4 * KN, beyond).astype(f32)
            start = place[k].astype(f32) * (1.0 / SP)
            knot, beyond = start - knot, start - beyond
            pixel = lax.broadcasted_iota(jnp.int32, (8, LANES), 0).astype(f32) * (1.0 / SP)
            for r in range(0, pixels, 16):
                values = []
                for q in (r, r + 8):
                    at_pixel = pixel + q * (1.0 / SP)
                    values.append(cubic(jnp.abs(at_pixel + knot)) + cubic(jnp.abs(at_pixel + beyond)))
                ref[r : r + 16, to] = jnp.concatenate(values, axis=0).astype(bf16)
        return carry

    lax.fori_loop(0, senders, sender, 0)


def compose(route_ref, received_ref, row_ref, col_ref, pixels_ref, out_ref, passed, result, sems):
    senders = received_ref.shape[0]
    bands = result.shape[0]
    lane = lax.broadcasted_iota(jnp.int32, (16, LANES), 1) // SPAN
    masks = [(lane == r).astype(f32).astype(bf16) for r in range(LANES // SPAN)]
    named = (route_ref[...] == lax.axis_index("gran")).astype(f32)
    scale = 1.0 / jnp.sum(named, keepdims=True)

    def sender(n, carry):
        at = pl.ds(pl.multiple_of(n * LANES, LANES), LANES)
        blocks = []
        for k in range(2 * bands):
            window = received_ref[n, 16 * k : 16 * k + 16, :]
            blocks.append(jnp.concatenate([window * mask for mask in masks], axis=0))
        rows = jnp.dot(row_ref[:, at], jnp.concatenate(blocks, axis=1), preferred_element_type=f32)
        for k in range(2 * bands):
            passed[k, :, at] = rows[:, LANES * k : LANES * k + LANES].astype(bf16)
        return carry

    lax.fori_loop(0, senders, sender, 0)
    copies = []
    for b in range(bands):
        fields = [
            lax.dot_general(
                passed[2 * b + c], col_ref[...], (((1,), (1,)), ((), ())), preferred_element_type=f32
            )
            * scale
            for c in range(2)
        ]
        pixels = pixels_ref[0, b].astype(f32)
        result[b] = (pixels * (1.0 + fields[0]) + fields[1]).astype(bf16)
        copies.append(pltpu.make_async_copy(result.at[b], out_ref.at[0, b], sems.at[b]))
        copies[b].start()
    for copy in copies:
        copy.wait()


def per_device(
    prior_grids,
    pif_rhs,
    pif_diagonal,
    pif_cross,
    pif_coupling,
    neighbour_offset,
    neighbour_count,
    tile_route,
    tile_window,
    tile_pixels,
):
    granules, bands = prior_grids.shape[:2]
    slots = pif_coupling.shape[1]
    pixel_count = tile_pixels.shape[2]
    device_total = lax.axis_size("gran")
    band_total = lax.axis_size("band")

    def by_lane_tile(array):
        cut = array.reshape(array.shape[:2] + (array.shape[2], 32, LANES)).transpose(0, 1, 3, 2, 4)
        return cut.reshape(array.shape[:2] + (32 * array.shape[2], LANES))

    grids = by_lane_tile(prior_grids)
    rhs = by_lane_tile(pif_rhs)
    diagonal = by_lane_tile(pif_diagonal)
    cross = by_lane_tile(pif_cross.transpose(1, 0, 2).reshape(bands, granules // 8, 8, KN * KN))
    coupling = by_lane_tile(pif_coupling.transpose(0, 2, 1, 3))
    graph = [("v", neighbour_offset.T), ("v", neighbour_count[None, :])]
    tiles = [("v", tile_route.T), ("v", tile_window.transpose(1, 2, 0))]
    edge = (REACH, bands, 64, LANES)
    own = (granules, bands, 64, LANES)
    ext = (granules + 2 * REACH, bands, 64, LANES)
    packed = ("v", (64, LANES), f32)
    chunks = 4

    near_pairs = [(i, i ^ 1) for i in range(device_total)]
    far_pairs = [
        pair for i in range(1, device_total - 1, 2) for pair in ((i, i + 1), (i + 1, i))
    ]

    def exchange(near, far):
        far = lax.ppermute(far, "gran", far_pairs)
        near = lax.ppermute(near, "gran", near_pairs)
        return near, far

    near, far = call(
        first_edges,
        [("a", grids)],
        [("v", edge, bf16), ("v", edge, bf16)],
        [pltpu.VMEM((2,) + edge, f32), pltpu.SemaphoreType.DMA((2,))],
    )
    near, far = exchange(near, far)
    extended, rhs, diagonal, cross, coupling = call(
        arrange,
        [("a", grids), ("a", rhs), ("a", diagonal), ("a", cross), ("a", coupling)],
        [
            ("v", ext, f32),
            ("v", own, f32),
            ("v", own, f32),
            ("v", (granules, bands, 32, LANES), f32),
            ("v", (granules, slots, bands, 32, LANES), bf16),
        ],
        [
            pltpu.VMEM(own, f32),
            pltpu.VMEM(cross.shape, f32),
            pltpu.VMEM(coupling.shape, bf16),
            pltpu.VMEM((bands, 32 * slots, LANES), f32),
            pltpu.SemaphoreType.DMA((5, chunks)),
        ],
    )
    gathered = pltpu.VMEM((slots, 64, LANES), f32)
    weights = pltpu.VMEM((slots, 64, LANES), f32)
    scalars = pltpu.SMEM((2, granules), jnp.int32)

    for sweep in range(SWEEPS):
        (inner,) = call(
            interior_disparities, graph + [("v", extended)], [packed], [gathered, scalars]
        )
        if sweep == 1:
            weight_shape = (pixel_count, device_total * LANES)
            row_weights, col_weights = call(
                interp_weights, tiles, [("v", weight_shape, bf16), ("v", weight_shape, bf16)]
            )
        extended, partial = call(
            edge_disparities,
            graph + [("v", near), ("v", far), ("v", inner), ("v", extended)],
            [("v", ext, f32), packed],
            [gathered, scalars],
            aliases={5: 0},
        )
        shares = [partial] + [
            lax.ppermute(partial, "band", [(i, i ^ flip) for i in range(band_total)])
            for flip in range(1, band_total)
        ]
        inputs = graph + [("v", share) for share in shares]
        inputs += [("v", extended), ("v", rhs), ("v", diagonal), ("v", cross), ("v", coupling)]
        if sweep < SWEEPS - 1:
            updated, near, far = call(
                edge_sweep,
                inputs,
                [("v", ext, f32), ("v", edge, bf16), ("v", edge, bf16)],
                [weights, scalars],
            )
            near, far = exchange(near, far)
            (extended,) = call(
                interior_sweep,
                inputs + [("v", updated)],
                [("v", ext, f32)],
                [weights, scalars],
                aliases={len(inputs): 0},
            )
        else:
            windows = (device_total, 2 * bands * SPAN, LANES)
            balanced, payload = call(
                last_sweep,
                inputs + tiles,
                [("a", own, f32), ("v", windows, bf16)],
                [
                    pltpu.VMEM(own, f32),
                    pltpu.VMEM(windows, f32),
                    weights,
                    scalars,
                    pltpu.SMEM((device_total,), jnp.int32),
                    pltpu.SemaphoreType.DMA((chunks,)),
                ],
            )
    received = lax.all_to_all(payload, "gran", split_axis=0, concat_axis=0, tiled=True)
    (corrected,) = call(
        compose,
        [tiles[0], ("v", received), ("v", row_weights), ("v", col_weights), ("v", tile_pixels)],
        [("a", tile_pixels.shape, bf16)],
        [
            pltpu.VMEM((2 * bands, pixel_count, device_total * LANES), bf16),
            pltpu.VMEM(tile_pixels.shape[1:], bf16),
            pltpu.SemaphoreType.DMA((bands,)),
        ],
        limit=32,
    )
    balanced = balanced.reshape(granules, bands, 32, 2, LANES).transpose(0, 1, 3, 2, 4)
    return (balanced.reshape(prior_grids.shape), corrected)


def solution(mesh):
    placed = (
        P("gran", "band", None, None),
        P("gran", "band", None, None),
        P("gran", "band", None, None),
        P("gran", "band", None),
        P("gran", None, "band", None),
        P("gran", None),
        P("gran"),
        P(),
        P(),
        P("gran", "band", None, None),
    )
    return jax.shard_map(
        per_device,
        mesh=mesh,
        in_specs=placed,
        out_specs=(P("gran", "band", None, None), P("gran", "band", None, None)),
        check_vma=False,
    )
```

time: 106 us -> 86.3 us (0.81)
  local copies, waits for them, and re-layouts: 22.2 us -> 5.85 us
  other arithmetic: 4.35 us -> 0 us
  Pallas kernels: 29.4 us -> 32.2 us
  waiting for transfers between devices: 25 us -> 23.1 us
    unnamed x55 -> x20, local copies, waits for them, and re-layouts: 19.6 us -> 5.85 us
    ppermute x3, waiting for transfers between devices: 15.3 us -> 11.8 us  [exchange(): near = lax.ppermute(near, 'gran', near_pairs)]
    pallas_call x10 -> x15, Pallas kernels: 29.4 us -> 32.2 us  [call(): pl.pallas_call(body, in_specs=[ON_CHIP if kind == 'v' else ANYWHERE for k...]
    ppermute x9, waiting for transfers between devices: 6.57 us -> 8.24 us  [per_device(): lax.ppermute(partial, 'band', [(i, i ^ flip) for i in range(band_total)])]
    add x2 -> x0, other arithmetic: 1.53 us -> none  [the longest x1 0.84 us: per_device(): 2 * (first_pair(starts[..., 0])[..., None] + step % 8) + step // 8]
    reduce_sum x3 -> x0, other arithmetic: 1.26 us -> none  [the longest x1 0.6 us: per_device(): covers = jnp.sum((tile_route == own_index).astype(jnp.int32)).reshape(1)]
    ppermute x3, starting transfers between devices: 9.01 us -> 10.1 us  [exchange(): near = lax.ppermute(near, 'gran', near_pairs)]
  transfers between devices with their start and end apart: 16 -> 16, of which waited for: 9 -> 9; matrix products, arithmetic and copies ran while one was open for 10% -> 0% of each run, Pallas kernels for 7% -> 21%
where the time goes in v1:
time: 86.3 us; the launch traced here: 86 us
  Pallas kernels  32.2 us (37%)
  starting transfers between devices  24 us (28%)
  waiting for transfers between devices  23.1 us (27%)
  local copies, waits for them, and re-layouts  5.85 us (7%)
    pallas_call x15, Pallas kernels, call(): pl.pallas_call(body, in_specs=[ON_CHIP if kind == 'v' else ANYWHERE for k...  32.2 us
    ppermute x3, waiting for transfers between devices, exchange(): near = lax.ppermute(near, 'gran', near_pairs)  11.8 us
    ppermute x3, starting transfers between devices, exchange(): near = lax.ppermute(near, 'gran', near_pairs)  10.1 us
    ppermute x9, waiting for transfers between devices, per_device(): lax.ppermute(partial, 'band', [(i, i ^ flip) for i in range(band_total)])  8.24 us
    all_to_all x1, starting transfers between devices, per_device(): lax.all_to_all(payload, 'gran', split_axis=0, concat_axis=0, tiled=True)  6.08 us
    unnamed x20, local copies, waits for them, and re-layouts  5.85 us
    ppermute x9, starting transfers between devices, per_device(): lax.ppermute(partial, 'band', [(i, i ^ flip) for i in range(band_total)])  5.8 us
    all_to_all x1, waiting for transfers between devices, per_device(): lax.all_to_all(payload, 'gran', split_axis=0, concat_axis=0, tiled=True)  3.08 us
  transfers between devices with their start and end apart: 16, of which 9 were waited for; matrix products, arithmetic and copies ran while one was open for 0% of the time, Pallas kernels for 21%

profile of v1, /device:TPU:0, one launch (start us, length us, event | category | flops | bytes accessed | tf_op | source)
XLA Modules:
  0.0 86.0 jit_solution(9777799206225301984)
XLA Ops:
  0.6 1.4 %copy-done = f32[16,3,2,4096]{3,2,1,0:T(2,128)S(1)} copy-done((f32[16,3,2,4096]{3,2,1,0:T(2,128)S(1)}, f32[16,3,2,4096]{3,2,1,0:T(2,128)}, u32[]{:S(2)}) %copy-start) | copy-done | bytes 1572888
  2.0 0.5 shard_map.113
  2.6 3.0 %collective-permute-start = (bf16[4,3,64,128]{3,2,1,0:T(8,128)(2,1)S(1)}, bf16[4,3,64,128]{3,2,1,0:T(8,128)(2,1)S(1)}, u32[]{:S(2)}, u32[]{:S(2)}) collective-permute-start(bf16[4,3,64,128]{3,2,1,0:T(8,128)(2,1)S(1)} %get-tuple-element.25), channel_id=1, source_target_pairs={{0,4},{4,0},{8,12},{12,8},{16,20},{20,16},{24,28},{28,24},{1,5},{5... | collective-permute-start | bytes 589832 | tf_op jit(solution)/shard_map/ppermute | solution.py:490
  5.6 0.7 collective-permute-start.1
  6.3 0.0 copy-start.1
  6.3 1.9 %copy-done.1 = bf16[16,8,3,4096]{3,1,2,0:T(8,128)(2,1)S(1)} copy-done((bf16[16,8,3,4096]{3,1,2,0:T(8,128)(2,1)S(1)}, bf16[16,8,3,4096]{3,1,2,0:T(8,128)(2,1)}, u32[]{:S(2)}) %copy-start.1) | copy-done | bytes 3145752
  8.1 1.4 %copy-done.3 = f32[16,3,2,4096]{3,2,1,0:T(2,128)S(1)} copy-done((f32[16,3,2,4096]{3,2,1,0:T(2,128)S(1)}, f32[16,3,2,4096]{3,2,1,0:T(2,128)}, u32[]{:S(2)}) %copy-start.3) | copy-done | bytes 1572888
  9.6 1.1 %copy-done.4 = f32[16,3,4096]{2,0,1:T(8,128)S(1)} copy-done((f32[16,3,4096]{2,0,1:T(8,128)S(1)}, f32[16,3,4096]{2,0,1:T(8,128)}, u32[]{:S(2)}) %copy-start.4) | copy-done | bytes 786456
  10.7 7.5 %shard_map.114 = (f32[24,3,64,128]{3,2,1,0:T(8,128)S(1)}, f32[16,3,64,128]{3,2,1,0:T(8,128)S(1)}, f32[16,3,64,128]{3,2,1,0:T(8,128)S(1)}, f32[16,3,32,128]{3,2,1,0:T(8,128)S(1)}, bf16[16,8,3,32,128]{4,3,2,1,0:T(8,128)(2,1)S(1)}) custom-call(f32[16,3,64,128]{3,2,1,0:T(8,128)S(1)} %bitcast.39, f32[16,3,64,128]{3,2,1,0:T(8,128)S(1)} %bitcast.41, ...), custom_call_target="tpu_custom_call" | custom-call | tf_op jit(solution)/shard_map/pallas_call | solution.py:31
  18.3 0.8 shard_map.115.inner_ref
  19.1 0.0 collective-permute-done.near_ref
  19.1 0.7 shard_map.116
  19.9 0.1 collective-permute-start.2
  19.9 1.6 %collective-permute-start.3 = (f32[64,128]{1,0:T(8,128)S(1)}, f32[64,128]{1,0:T(8,128)S(1)}, u32[]{:S(2)}, u32[]{:S(2)}) collective-permute-start(f32[64,128]{1,0:T(8,128)S(1)} %get-tuple-element.28.refs_0_), channel_id=1, source_target_pairs={{0,2},{1,3},{2,0},{3,1},{4,6},{5,7},{6,4},{7,5},{8,10},{9,11},{10,... | collective-permute-start | bytes 98312 | tf_op jit(solution)/shard_map/ppermute | solution.py:539
  21.5 0.3 collective-permute-start.4
  21.8 2.1 %collective-permute-done.3.refs_2_ = f32[64,128]{1,0:T(8,128)S(1)} collective-permute-done((f32[64,128]{1,0:T(8,128)S(1)}, f32[64,128]{1,0:T(8,128)S(1)}, u32[]{:S(2)}, u32[]{:S(2)}) %collective-permute-start.3) | collective-permute-done | bytes 32800 | tf_op jit(solution)/shard_map/ppermute | solution.py:539
  23.9 0.9 %collective-permute-done.4.refs_3_ = f32[64,128]{1,0:T(8,128)S(1)} collective-permute-done((f32[64,128]{1,0:T(8,128)S(1)}, f32[64,128]{1,0:T(8,128)S(1)}, u32[]{:S(2)}, u32[]{:S(2)}) %collective-permute-start.4) | collective-permute-done | bytes 32800 | tf_op jit(solution)/shard_map/ppermute | solution.py:539
  24.9 1.1 %shard_map.117 = (f32[24,3,64,128]{3,2,1,0:T(8,128)S(1)}, bf16[4,3,64,128]{3,2,1,0:T(8,128)(2,1)S(1)}, bf16[4,3,64,128]{3,2,1,0:T(8,128)(2,1)S(1)}) custom-call(s32[8,16]{1,0:T(8,128)S(1)} %bitcast.46, s32[1,16]{1,0:T(1,128)S(1)} %bitcast.57, f32[64,128]{1,0:T(8,128)S(1)} %get-tuple-element.28.refs_0_, f32[64,128]{1,0:T(8,128)S(1)} %collective-permute-done.2.refs_1_, ...), custom_call_target="tpu_custom_call" | custom-call | tf_op jit(solution)/shard_map/pallas_call | solution.py:31
  26.0 4.4 %collective-permute-start.5 = (bf16[4,3,64,128]{3,2,1,0:T(8,128)(2,1)S(1)}, bf16[4,3,64,128]{3,2,1,0:T(8,128)(2,1)S(1)}, u32[]{:S(2)}, u32[]{:S(2)}) collective-permute-start(bf16[4,3,64,128]{3,2,1,0:T(8,128)(2,1)S(1)} %get-tuple-element.34), channel_id=1, source_target_pairs={{0,4},{4,0},{8,12},{12,8},{16,20},{20,16},{24,28},{28,24},{1,5},{5... | collective-permute-start | bytes 589832 | tf_op jit(solution)/shard_map/ppermute | solution.py:490
  30.4 0.7 collective-permute-start.6
  31.0 1.2 %shard_map.118.ext_ref.ext_in = f32[24,3,64,128]{3,2,1,0:T(8,128)S(1)} custom-call(s32[8,16]{1,0:T(8,128)S(1)} %bitcast.47, s32[1,16]{1,0:T(1,128)S(1)} %bitcast.58, f32[64,128]{1,0:T(8,128)S(1)} %get-tuple-element.28.refs_0_, f32[64,128]{1,0:T(8,128)S(1)} %collective-permute-done.2.refs_1_, ...), custom_call_target="tpu_custom_call", output_to_operand_aliasing={{}: (11, {})} | custom-call | tf_op jit(solution)/shard_map/pallas_call | solution.py:31
  32.3 0.8 shard_map.119.inner_ref
  33.1 5.9 %collective-permute-done.5.near_ref = bf16[4,3,64,128]{3,2,1,0:T(8,128)(2,1)S(1)} collective-permute-done((bf16[4,3,64,128]{3,2,1,0:T(8,128)(2,1)S(1)}, bf16[4,3,64,128]{3,2,1,0:T(8,128)(2,1)S(1)}, u32[]{:S(2)}, u32[]{:S(2)}) %collective-permute-start.5) | collective-permute-done | bytes 196640 | tf_op jit(solution)/shard_map/ppermute | solution.py:490
  39.1 0.7 shard_map.120
  39.8 0.1 collective-permute-start.7
  39.9 0.9 %collective-permute-start.8 = (f32[64,128]{1,0:T(8,128)S(1)}, f32[64,128]{1,0:T(8,128)S(1)}, u32[]{:S(2)}, u32[]{:S(2)}) collective-permute-start(f32[64,128]{1,0:T(8,128)S(1)} %get-tuple-element.37.refs_0_), channel_id=1, source_target_pairs={{0,2},{1,3},{2,0},{3,1},{4,6},{5,7},{6,4},{7,5},{8,10},{9,11},{10,... | collective-permute-start | bytes 98312 | tf_op jit(solution)/shard_map/ppermute | solution.py:539
  40.8 0.9 %collective-permute-start.9 = (f32[64,128]{1,0:T(8,128)S(1)}, f32[64,128]{1,0:T(8,128)S(1)}, u32[]{:S(2)}, u32[]{:S(2)}) collective-permute-start(f32[64,128]{1,0:T(8,128)S(1)} %get-tuple-element.37.refs_0_), channel_id=1, source_target_pairs={{0,3},{1,2},{2,1},{3,0},{4,7},{5,6},{6,5},{7,4},{8,11},{9,10},{10,... | collective-permute-start | bytes 98312 | tf_op jit(solution)/shard_map/ppermute | solution.py:539
  41.8 2.2 %collective-permute-done.8.refs_2_ = f32[64,128]{1,0:T(8,128)S(1)} collective-permute-done((f32[64,128]{1,0:T(8,128)S(1)}, f32[64,128]{1,0:T(8,128)S(1)}, u32[]{:S(2)}, u32[]{:S(2)}) %collective-permute-start.8) | collective-permute-done | bytes 32800 | tf_op jit(solution)/shard_map/ppermute | solution.py:539
  43.9 0.4 collective-permute-done.9.refs_3_
  44.3 1.1 %shard_map.121 = (f32[24,3,64,128]{3,2,1,0:T(8,128)S(1)}, bf16[4,3,64,128]{3,2,1,0:T(8,128)(2,1)S(1)}, bf16[4,3,64,128]{3,2,1,0:T(8,128)(2,1)S(1)}) custom-call(s32[8,16]{1,0:T(8,128)S(1)} %bitcast.50, s32[1,16]{1,0:T(1,128)S(1)} %bitcast.61, f32[64,128]{1,0:T(8,128)S(1)} %get-tuple-element.37.refs_0_, f32[64,128]{1,0:T(8,128)S(1)} %collective-permute-done.7.refs_1_, ...), custom_call_target="tpu_custom_call" | custom-call | tf_op jit(solution)/shard_map/pallas_call | solution.py:31
  45.4 2.7 %collective-permute-start.10 = (bf16[4,3,64,128]{3,2,1,0:T(8,128)(2,1)S(1)}, bf16[4,3,64,128]{3,2,1,0:T(8,128)(2,1)S(1)}, u32[]{:S(2)}, u32[]{:S(2)}) collective-permute-start(bf16[4,3,64,128]{3,2,1,0:T(8,128)(2,1)S(1)} %get-tuple-element.39), channel_id=1, source_target_pairs={{0,4},{4,0},{8,12},{12,8},{16,20},{20,16},{24,28},{28,24},{1,5},{5... | collective-permute-start | bytes 589832 | tf_op jit(solution)/shard_map/ppermute | solution.py:490
  48.1 0.7 collective-permute-start.11
  48.8 1.2 %shard_map.122.ext_ref.ext_in = f32[24,3,64,128]{3,2,1,0:T(8,128)S(1)} custom-call(s32[8,16]{1,0:T(8,128)S(1)} %bitcast.51, s32[1,16]{1,0:T(1,128)S(1)} %bitcast.62, f32[64,128]{1,0:T(8,128)S(1)} %get-tuple-element.37.refs_0_, f32[64,128]{1,0:T(8,128)S(1)} %collective-permute-done.7.refs_1_, ...), custom_call_target="tpu_custom_call", output_to_operand_aliasing={{}: (11, {})} | custom-call | tf_op jit(solution)/shard_map/pallas_call | solution.py:31
  50.0 0.0 copy-start.8
  50.0 0.0 copy-start.9
  50.1 0.8 shard_map.123.inner_ref
  50.9 5.9 %collective-permute-done.10.near_ref = bf16[4,3,64,128]{3,2,1,0:T(8,128)(2,1)S(1)} collective-permute-done((bf16[4,3,64,128]{3,2,1,0:T(8,128)(2,1)S(1)}, bf16[4,3,64,128]{3,2,1,0:T(8,128)(2,1)S(1)}, u32[]{:S(2)}, u32[]{:S(2)}) %collective-permute-start.10) | collective-permute-done | bytes 196640 | tf_op jit(solution)/shard_map/ppermute | solution.py:490
  56.8 0.7 shard_map.124
  57.5 0.1 collective-permute-start.12
  57.6 1.1 %collective-permute-start.13 = (f32[64,128]{1,0:T(8,128)S(1)}, f32[64,128]{1,0:T(8,128)S(1)}, u32[]{:S(2)}, u32[]{:S(2)}) collective-permute-start(f32[64,128]{1,0:T(8,128)S(1)} %get-tuple-element.42.refs_0_), channel_id=1, source_target_pairs={{0,2},{1,3},{2,0},{3,1},{4,6},{5,7},{6,4},{7,5},{8,10},{9,11},{10,... | collective-permute-start | bytes 98312 | tf_op jit(solution)/shard_map/ppermute | solution.py:539
  58.7 0.7 collective-permute-start.14
  59.5 2.1 %collective-permute-done.13.refs_2_ = f32[64,128]{1,0:T(8,128)S(1)} collective-permute-done((f32[64,128]{1,0:T(8,128)S(1)}, f32[64,128]{1,0:T(8,128)S(1)}, u32[]{:S(2)}, u32[]{:S(2)}) %collective-permute-start.13) | collective-permute-done | bytes 32800 | tf_op jit(solution)/shard_map/ppermute | solution.py:539
  61.6 0.5 collective-permute-done.14.refs_3_
  62.1 5.6 %shard_map.125 = (f32[16,3,64,128]{3,2,1,0:T(8,128)}, bf16[8,96,128]{2,1,0:T(8,128)(2,1)}) custom-call(s32[8,16]{1,0:T(8,128)S(1)} %bitcast.54, s32[1,16]{1,0:T(1,128)S(1)} %bitcast.65, f32[64,128]{1,0:T(8,128)S(1)} %get-tuple-element.42.refs_0_, f32[64,128]{1,0:T(8,128)S(1)} %collective-permute-done.12.refs_1_, ...), custom_call_target="tpu_custom_call" | custom-call | tf_op jit(solution)/shard_map/pallas_call | solution.py:31
  67.7 6.1 %all-to-all-start = ((bf16[8,96,128]{2,1,0:T(8,128)(2,1)}), bf16[8,96,128]{2,1,0:T(8,128)(2,1)S(1)}, u32[]{:S(2)}, u32[]{:S(2)}) async-start(bf16[8,96,128]{2,1,0:T(8,128)(2,1)} %get-tuple-element.45), calls=%async_computation | async-start | bytes 393216 | tf_op jit(solution)/shard_map/all_to_all | solution.py:574
  73.8 5.2 %shard_map.126 = (bf16[256,1024]{1,0:T(8,128)(2,1)S(1)}, bf16[256,1024]{1,0:T(8,128)(2,1)S(1)}) custom-call(s32[2,128]{1,0:T(2,128)S(1)} %bitcast.67, s32[2,2,128]{2,1,0:T(2,128)S(1)} %bitcast.70), custom_call_target="tpu_custom_call" | custom-call | tf_op jit(solution)/shard_map/pallas_call | solution.py:31
  79.0 3.1 %all-to-all-done.received_ref = bf16[8,96,128]{2,1,0:T(8,128)(2,1)S(1)} async-done(((bf16[8,96,128]{2,1,0:T(8,128)(2,1)}), bf16[8,96,128]{2,1,0:T(8,128)(2,1)S(1)}, u32[]{:S(2)}, u32[]{:S(2)}) %all-to-all-start) | async-done | bytes 196640 | tf_op jit(solution)/shard_map/all_to_all | solution.py:574
  82.1 3.9 %shard_map.127 = bf16[1,3,256,256]{3,2,1,0:T(8,128)(2,1)} custom-call(s32[2,128]{1,0:T(2,128)S(1)} %bitcast.68, bf16[8,96,128]{2,1,0:T(8,128)(2,1)S(1)} %all-to-all-done.received_ref, bf16[256,1024]{1,0:T(8,128)(2,1)S(1)} %get-tuple-element.46.row_ref, bf16[256,1024]{1,0:T(8,128)(2,1)S(1)} %get-tuple-element.47.col_ref, bf16[1,3,256,256]{3,2,1,0:T(8,128)(2,1)S(1)} %copy-done.6), custom_call_target="tpu_custom_call" | custom-call | tf_op jit(solution)/shard_map/pallas_call | solution.py:31
  (19 shorter events, 0.0 us)
Async XLA Ops:
  0.6 1.4 %copy-start = (f32[16,3,2,4096]{3,2,1,0:T(2,128)S(1)}, f32[16,3,2,4096]{3,2,1,0:T(2,128)}, u32[]{:S(2)}) copy-start(f32[16,3,2,4096]{3,2,1,0:T(2,128)} %param.10) | copy-start | bytes 4718596
  2.0 4.2 %copy-start.2 = (f32[16,3,2,4096]{3,2,1,0:T(2,128)S(1)}, f32[16,3,2,4096]{3,2,1,0:T(2,128)}, u32[]{:S(2)}) copy-start(f32[16,3,2,4096]{3,2,1,0:T(2,128)} %param.11) | copy-start | bytes 4718596
  2.6 16.5 %collective-permute-start = (bf16[4,3,64,128]{3,2,1,0:T(8,128)(2,1)S(1)}, bf16[4,3,64,128]{3,2,1,0:T(8,128)(2,1)S(1)}, u32[]{:S(2)}, u32[]{:S(2)}) collective-permute-start(bf16[4,3,64,128]{3,2,1,0:T(8,128)(2,1)S(1)} %get-tuple-element.25), channel_id=1, source_target_pairs={{0,4},{4,0},{8,12},{12,8},{16,20},{20,16},{24,28},{28,24},{1,5},{5... | collective-permute-start | bytes 589832 | tf_op jit(solution)/shard_map/ppermute | solution.py:490
  5.6 13.5 %collective-permute-start.1 = (bf16[4,3,64,128]{3,2,1,0:T(8,128)(2,1)S(1)}, bf16[4,3,64,128]{3,2,1,0:T(8,128)(2,1)S(1)}, u32[]{:S(2)}, u32[]{:S(2)}) collective-permute-start(bf16[4,3,64,128]{3,2,1,0:T(8,128)(2,1)S(1)} %get-tuple-element.26), channel_id=1, source_target_pairs={{4,8},{8,4},{12,16},{16,12},{20,24},{24,20},{5,9},{9,5},{13,17},{1... | collective-permute-start | bytes 589832 | tf_op jit(solution)/shard_map/ppermute | solution.py:489
  6.3 1.9 %copy-start.1 = (bf16[16,8,3,4096]{3,1,2,0:T(8,128)(2,1)S(1)}, bf16[16,8,3,4096]{3,1,2,0:T(8,128)(2,1)}, u32[]{:S(2)}) copy-start(bf16[16,8,3,4096]{3,1,2,0:T(8,128)(2,1)} %param.14) | copy-start | bytes 9437188
  8.1 1.4 %copy-start.3 = (f32[16,3,2,4096]{3,2,1,0:T(2,128)S(1)}, f32[16,3,2,4096]{3,2,1,0:T(2,128)}, u32[]{:S(2)}) copy-start(f32[16,3,2,4096]{3,2,1,0:T(2,128)} %param.12) | copy-start | bytes 4718596
  9.6 1.1 %copy-start.4 = (f32[16,3,4096]{2,0,1:T(8,128)S(1)}, f32[16,3,4096]{2,0,1:T(8,128)}, u32[]{:S(2)}) copy-start(f32[16,3,4096]{2,0,1:T(8,128)} %param.13) | copy-start | bytes 2359300
  10.7 7.6 %copy-start.5 = (s32[16,8]{0,1:T(8,128)S(1)}, s32[16,8]{0,1:T(8,128)}, u32[]{:S(2)}) copy-start(s32[16,8]{0,1:T(8,128)} %param.15) | copy-start | bytes 1540
  10.7 7.6 %copy-start.7 = (s32[16]{0:T(128)S(1)}, s32[16]{0:T(128)}, u32[]{:S(2)}) copy-start(s32[16]{0:T(128)} %param.16) | copy-start | bytes 196
  19.9 1.9 %collective-permute-start.2 = (f32[64,128]{1,0:T(8,128)S(1)}, f32[64,128]{1,0:T(8,128)S(1)}, u32[]{:S(2)}, u32[]{:S(2)}) collective-permute-start(f32[64,128]{1,0:T(8,128)S(1)} %get-tuple-element.28.refs_0_), channel_id=1, source_target_pairs={{0,1},{1,0},{2,3},{3,2},{4,5},{5,4},{6,7},{7,6},{8,9},{9,8},{10,11... | collective-permute-start | bytes 98312 | tf_op jit(solution)/shard_map/ppermute | solution.py:539
  19.9 4.0 %collective-permute-start.3 = (f32[64,128]{1,0:T(8,128)S(1)}, f32[64,128]{1,0:T(8,128)S(1)}, u32[]{:S(2)}, u32[]{:S(2)}) collective-permute-start(f32[64,128]{1,0:T(8,128)S(1)} %get-tuple-element.28.refs_0_), channel_id=1, source_target_pairs={{0,2},{1,3},{2,0},{3,1},{4,6},{5,7},{6,4},{7,5},{8,10},{9,11},{10,... | collective-permute-start | bytes 98312 | tf_op jit(solution)/shard_map/ppermute | solution.py:539
  21.5 3.3 %collective-permute-start.4 = (f32[64,128]{1,0:T(8,128)S(1)}, f32[64,128]{1,0:T(8,128)S(1)}, u32[]{:S(2)}, u32[]{:S(2)}) collective-permute-start(f32[64,128]{1,0:T(8,128)S(1)} %get-tuple-element.28.refs_0_), channel_id=1, source_target_pairs={{0,3},{1,2},{2,1},{3,0},{4,7},{5,6},{6,5},{7,4},{8,11},{9,10},{10,... | collective-permute-start | bytes 98312 | tf_op jit(solution)/shard_map/ppermute | solution.py:539
  26.0 13.1 %collective-permute-start.5 = (bf16[4,3,64,128]{3,2,1,0:T(8,128)(2,1)S(1)}, bf16[4,3,64,128]{3,2,1,0:T(8,128)(2,1)S(1)}, u32[]{:S(2)}, u32[]{:S(2)}) collective-permute-start(bf16[4,3,64,128]{3,2,1,0:T(8,128)(2,1)S(1)} %get-tuple-element.34), channel_id=1, source_target_pairs={{0,4},{4,0},{8,12},{12,8},{16,20},{20,16},{24,28},{28,24},{1,5},{5... | collective-permute-start | bytes 589832 | tf_op jit(solution)/shard_map/ppermute | solution.py:490
  30.4 8.7 %collective-permute-start.6 = (bf16[4,3,64,128]{3,2,1,0:T(8,128)(2,1)S(1)}, bf16[4,3,64,128]{3,2,1,0:T(8,128)(2,1)S(1)}, u32[]{:S(2)}, u32[]{:S(2)}) collective-permute-start(bf16[4,3,64,128]{3,2,1,0:T(8,128)(2,1)S(1)} %get-tuple-element.35), channel_id=1, source_target_pairs={{4,8},{8,4},{12,16},{16,12},{20,24},{24,20},{5,9},{9,5},{13,17},{1... | collective-permute-start | bytes 589832 | tf_op jit(solution)/shard_map/ppermute | solution.py:489
  39.8 1.9 %collective-permute-start.7 = (f32[64,128]{1,0:T(8,128)S(1)}, f32[64,128]{1,0:T(8,128)S(1)}, u32[]{:S(2)}, u32[]{:S(2)}) collective-permute-start(f32[64,128]{1,0:T(8,128)S(1)} %get-tuple-element.37.refs_0_), channel_id=1, source_target_pairs={{0,1},{1,0},{2,3},{3,2},{4,5},{5,4},{6,7},{7,6},{8,9},{9,8},{10,11... | collective-permute-start | bytes 98312 | tf_op jit(solution)/shard_map/ppermute | solution.py:539
  39.9 4.0 %collective-permute-start.8 = (f32[64,128]{1,0:T(8,128)S(1)}, f32[64,128]{1,0:T(8,128)S(1)}, u32[]{:S(2)}, u32[]{:S(2)}) collective-permute-start(f32[64,128]{1,0:T(8,128)S(1)} %get-tuple-element.37.refs_0_), channel_id=1, source_target_pairs={{0,2},{1,3},{2,0},{3,1},{4,6},{5,7},{6,4},{7,5},{8,10},{9,11},{10,... | collective-permute-start | bytes 98312 | tf_op jit(solution)/shard_map/ppermute | solution.py:539
  40.8 3.5 %collective-permute-start.9 = (f32[64,128]{1,0:T(8,128)S(1)}, f32[64,128]{1,0:T(8,128)S(1)}, u32[]{:S(2)}, u32[]{:S(2)}) collective-permute-start(f32[64,128]{1,0:T(8,128)S(1)} %get-tuple-element.37.refs_0_), channel_id=1, source_target_pairs={{0,3},{1,2},{2,1},{3,0},{4,7},{5,6},{6,5},{7,4},{8,11},{9,10},{10,... | collective-permute-start | bytes 98312 | tf_op jit(solution)/shard_map/ppermute | solution.py:539
  45.4 11.4 %collective-permute-start.10 = (bf16[4,3,64,128]{3,2,1,0:T(8,128)(2,1)S(1)}, bf16[4,3,64,128]{3,2,1,0:T(8,128)(2,1)S(1)}, u32[]{:S(2)}, u32[]{:S(2)}) collective-permute-start(bf16[4,3,64,128]{3,2,1,0:T(8,128)(2,1)S(1)} %get-tuple-element.39), channel_id=1, source_target_pairs={{0,4},{4,0},{8,12},{12,8},{16,20},{20,16},{24,28},{28,24},{1,5},{5... | collective-permute-start | bytes 589832 | tf_op jit(solution)/shard_map/ppermute | solution.py:490
  48.1 8.7 %collective-permute-start.11 = (bf16[4,3,64,128]{3,2,1,0:T(8,128)(2,1)S(1)}, bf16[4,3,64,128]{3,2,1,0:T(8,128)(2,1)S(1)}, u32[]{:S(2)}, u32[]{:S(2)}) collective-permute-start(bf16[4,3,64,128]{3,2,1,0:T(8,128)(2,1)S(1)} %get-tuple-element.40), channel_id=1, source_target_pairs={{4,8},{8,4},{12,16},{16,12},{20,24},{24,20},{5,9},{9,5},{13,17},{1... | collective-permute-start | bytes 589832 | tf_op jit(solution)/shard_map/ppermute | solution.py:489
  50.0 12.0 %copy-start.8 = (s32[128,2]{0,1:T(2,128)S(1)}, s32[128,2]{0,1:T(2,128)}, u32[]{:S(2)}) copy-start(s32[128,2]{0,1:T(2,128)} %param.17) | copy-start | bytes 3076
  50.0 12.0 %copy-start.9 = (s32[128,2,2]{0,2,1:T(2,128)S(1)}, s32[128,2,2]{0,2,1:T(2,128)}, u32[]{:S(2)}) copy-start(s32[128,2,2]{0,2,1:T(2,128)} %param.18) | copy-start | bytes 6148
  57.5 1.9 %collective-permute-start.12 = (f32[64,128]{1,0:T(8,128)S(1)}, f32[64,128]{1,0:T(8,128)S(1)}, u32[]{:S(2)}, u32[]{:S(2)}) collective-permute-start(f32[64,128]{1,0:T(8,128)S(1)} %get-tuple-element.42.refs_0_), channel_id=1, source_target_pairs={{0,1},{1,0},{2,3},{3,2},{4,5},{5,4},{6,7},{7,6},{8,9},{9,8},{10,11... | collective-permute-start | bytes 98312 | tf_op jit(solution)/shard_map/ppermute | solution.py:539
  57.6 4.0 %collective-permute-start.13 = (f32[64,128]{1,0:T(8,128)S(1)}, f32[64,128]{1,0:T(8,128)S(1)}, u32[]{:S(2)}, u32[]{:S(2)}) collective-permute-start(f32[64,128]{1,0:T(8,128)S(1)} %get-tuple-element.42.refs_0_), channel_id=1, source_target_pairs={{0,2},{1,3},{2,0},{3,1},{4,6},{5,7},{6,4},{7,5},{8,10},{9,11},{10,... | collective-permute-start | bytes 98312 | tf_op jit(solution)/shard_map/ppermute | solution.py:539
  58.7 3.3 %collective-permute-start.14 = (f32[64,128]{1,0:T(8,128)S(1)}, f32[64,128]{1,0:T(8,128)S(1)}, u32[]{:S(2)}, u32[]{:S(2)}) collective-permute-start(f32[64,128]{1,0:T(8,128)S(1)} %get-tuple-element.42.refs_0_), channel_id=1, source_target_pairs={{0,3},{1,2},{2,1},{3,0},{4,7},{5,6},{6,5},{7,4},{8,11},{9,10},{10,... | collective-permute-start | bytes 98312 | tf_op jit(solution)/shard_map/ppermute | solution.py:539
  62.1 20.0 %copy-start.6 = (bf16[1,3,256,256]{3,2,1,0:T(8,128)(2,1)S(1)}, bf16[1,3,256,256]{3,2,1,0:T(8,128)(2,1)}, u32[]{:S(2)}) copy-start(bf16[1,3,256,256]{3,2,1,0:T(8,128)(2,1)} %pixels_ref.1) | copy-start | bytes 1179652
  67.7 14.4 %all-to-all-start = ((bf16[8,96,128]{2,1,0:T(8,128)(2,1)}), bf16[8,96,128]{2,1,0:T(8,128)(2,1)S(1)}, u32[]{:S(2)}, u32[]{:S(2)}) async-start(bf16[8,96,128]{2,1,0:T(8,128)(2,1)} %get-tuple-element.45), calls=%async_computation | async-start | bytes 393216 | tf_op jit(solution)/shard_map/all_to_all | solution.py:574

commit v2 on v1

--- a/solution.py
+++ b/solution.py
@@ -25,7 +25,7 @@
 
 def call(body, inputs, outputs, scratch=(), aliases=None, limit=16):
     operands = [
-        pltpu.with_memory_space_constraint(array, pltpu.VMEM) if kind == "v" else array
+        pltpu.with_memory_space_constraint(array, pltpu.VMEM if kind == "v" else pltpu.HBM)
         for kind, array in inputs
     ]
     return pl.pallas_call(
@@ -33,7 +33,7 @@
         in_specs=[ON_CHIP if kind == "v" else ANYWHERE for kind, _ in inputs],
         out_specs=tuple(ON_CHIP if kind == "v" else ANYWHERE for kind, _, _ in outputs),
         out_shape=tuple(
-            pltpu.VMEM(shape, dtype) if kind == "v" else jax.ShapeDtypeStruct(shape, dtype)
+            (pltpu.VMEM if kind == "v" else pltpu.HBM)(shape, dtype)
             for kind, shape, dtype in outputs
         ),
         scratch_shapes=list(scratch),
@@ -65,17 +65,36 @@
                     ref[g, b, 16 * j : 16 * j + 16, :] = jnp.concatenate(both, axis=0).astype(bf16)
 
 
-def arrange(grids_ref, rhs_ref, diag_ref, cross_ref, coupling_ref, ext_ref, rhs_out, diag_out, cross_out, coupling_out, grids_raw, cross_raw, coupling_raw, wide, sems):
+def arrange_grids(grids_ref, ext_ref, raw, sems):
     granules, bands = grids_ref.shape[:2]
+    chunks = sems.shape[0]
+    size = granules // chunks
+    copies = []
+    for n in range(chunks):
+        part = pl.ds(n * size, size)
+        copies.append(pltpu.make_async_copy(grids_ref.at[part], raw.at[part], sems.at[n]))
+        copies[n].start()
+
+    def step(i, carry):
+        for b in range(bands):
+            for q in range(8):
+                ext_ref[i + REACH, b, 8 * q : 8 * q + 8, :] = raw[i, b, pl.ds(q, 8, stride=8), :]
+        return carry
+
+    for n in range(chunks):
+        copies[n].wait()
+        lax.fori_loop(n * size, (n + 1) * size, step, 0)
+
+
+def arrange(rhs_ref, diag_ref, cross_ref, coupling_ref, rhs_out, diag_out, cross_out, coupling_out, cross_raw, coupling_raw, wide, sems):
+    granules, bands = rhs_ref.shape[:2]
     slots = coupling_out.shape[1]
     chunks = sems.shape[1]
     size = granules // chunks
-    whole = pltpu.make_async_copy(cross_ref, cross_raw, sems.at[4, 0])
-    whole.start()
     copies = []
     for n in range(chunks):
         part = pl.ds(n * size, size)
-        moves = ((coupling_ref, coupling_raw), (diag_ref, diag_out), (grids_ref, grids_raw), (rhs_ref, rhs_out))
+        moves = ((coupling_ref, coupling_raw), (diag_ref, diag_out))
         copies.append(
             [
                 pltpu.make_async_copy(source.at[part], target.at[part], sems.at[k, n])
@@ -84,19 +103,18 @@
         )
         for copy in copies[n]:
             copy.start()
-    whole.wait()
+        if n == 0:
+            whole = pltpu.make_async_copy(cross_ref, cross_raw, sems.at[2, 0])
+            whole.start()
+    rest = pltpu.make_async_copy(rhs_ref, rhs_out, sems.at[2, 1])
+    rest.start()
 
     def step(i, carry):
         for b in range(bands):
             wide[b] = coupling_raw[i, b].astype(f32)
         for b in range(bands):
             for j in range(4):
-                d = []
-                for c in range(2):
-                    rows = pl.ds(2 * j + c, 8, stride=8)
-                    to = slice(16 * j + 8 * c, 16 * j + 8 * c + 8)
-                    ext_ref[i + REACH, b, to, :] = grids_raw[i, b, rows, :]
-                    d.append(diag_out[i, b, rows, :])
+                d = [diag_out[i, b, pl.ds(2 * j + c, 8, stride=8), :] for c in range(2)]
                 pick = cross_raw[b, i // 8, pl.ds(8 * j + i % 8, 8, stride=32), :]
                 cross_out[i, b, 8 * j : 8 * j + 8, :] = pick * jnp.sqrt(d[0] * d[1])
         for b in range(bands):
@@ -109,7 +127,10 @@
     for n in range(chunks):
         for copy in copies[n]:
             copy.wait()
+        if n == 0:
+            whole.wait()
         lax.fori_loop(n * size, (n + 1) * size, step, 0)
+    rest.wait()
 
 
 def lane_sums():
@@ -186,15 +207,16 @@
     out_ref[...] = disparities(True, offset_ref, count_ref, ext_ref, gathered, graph)
 
 
-def edge_disparities(offset_ref, count_ref, near_ref, far_ref, inner_ref, ext_in, ext_ref, out_ref, gathered, graph):
-    del ext_in
+def edge_disparities(offset_ref, count_ref, near_ref, far_ref, *refs):
+    ext_ref, out_ref, gathered, graph = refs[-4:]
     odd = parity()
     right = ext_ref.shape[0] - REACH
     for ref, base in ((near_ref, (1 - odd) * right), (far_ref, odd * right)):
         for g in range(REACH):
             for b in range(ref.shape[1]):
                 ext_ref[base + g, b] = ref[g, b].astype(f32)
-    out_ref[...] = inner_ref[...] + disparities(False, offset_ref, count_ref, ext_ref, gathered, graph)
+    packed = disparities(False, offset_ref, count_ref, ext_ref, gathered, graph)
+    out_ref[...] = packed + refs[1][...] if len(refs) == 6 else packed
 
 
 def spread_weights(shares, interior, weights):
@@ -295,45 +317,58 @@
     return pltpu.roll(ref[at + (pl.ds(base, LANES),)], turn, 1)
 
 
-def last_sweep(offset_ref, count_ref, *refs):
+def visits(granules, interior):
+    inner = list(range(REACH, granules - REACH))
+    return inner if interior else [i for i in range(granules) if i not in inner]
+
+
+def last_sweep(interior, offset_ref, count_ref, *refs):
     shares, state, (route_ref, window_ref) = refs[:4], refs[4:9], refs[9:11]
-    out_ref, send_ref, solved, windows, weights, graph, ranks, sems = refs[11:]
+    weights, graph, ranks, solved, sems = refs[-5:]
+    if interior:
+        out_ref, windows = refs[11:13]
+    else:
+        out_ref, send_ref, windows = refs[13:16]
     granules, bands = solved.shape[:2]
+    inner = visits(granules, True)
     read_graph(offset_ref, count_ref, graph)
-    windows[...] = jnp.zeros_like(windows)
+    if interior:
+        windows[...] = jnp.zeros_like(windows)
     for owner in range(windows.shape[0]):
         ranks[owner] = 0
-    chunks = sems.shape[0]
-    size = granules // chunks
+    spread_weights(shares, interior, weights)
+
+    def step(t, carry):
+        i = t if interior else jnp.where(t < REACH, t, t + granules - 2 * REACH)
+
+        def store(b, j, gain, offset):
+            solved[i, b, pl.ds(2 * j, 8, stride=8), :] = gain
+            solved[i, b, pl.ds(2 * j + 1, 8, stride=8), :] = offset
+
+        balance(i, *state, weights, graph, store)
+        return carry
+
+    lax.fori_loop(*((REACH, granules - REACH) if interior else (0, 2 * REACH)), step, 0)
+    parts = ((REACH, granules - 2 * REACH),) if interior else ((0, REACH), (granules - REACH, REACH))
     copies = []
-    for interior in (True, False):
-        spread_weights(shares, interior, weights)
-
-        def step(t, carry, interior=interior):
-            i = t if interior else jnp.where(t < REACH, t, t + granules - 2 * REACH)
-
-            def store(b, j, gain, offset):
-                solved[i, b, pl.ds(2 * j, 8, stride=8), :] = gain
-                solved[i, b, pl.ds(2 * j + 1, 8, stride=8), :] = offset
-
-            balance(i, *state, weights, graph, store)
-            return carry
-
-        lax.fori_loop(*((REACH, granules - REACH) if interior else (0, 2 * REACH)), step, 0)
-        for n in range(chunks):
-            if (REACH <= n * size < granules - REACH) == interior:
-                part = pl.ds(n * size, size)
-                copies.append(pltpu.make_async_copy(solved.at[part], out_ref.at[part], sems.at[n]))
-                copies[-1].start()
+    for n, (first, size) in enumerate(parts):
+        part = pl.ds(first, size)
+        copies.append(pltpu.make_async_copy(solved.at[part], out_ref.at[part], sems.at[n]))
+        copies[n].start()
     lane = lax.broadcasted_iota(jnp.int32, (8, LANES), 1) // SPAN
     routes = own_columns(route_ref, (slice(None),), granules)
+    if not interior:
+        for i in inner:
+            for r in range(2):
+                owner = routes[r, i]
+                ranks[owner] = ranks[owner] + 1
     tops, lefts = [], []
     for r in range(2):
         starts = own_columns(window_ref, (r, slice(None)), granules)
         knots = jnp.clip(jnp.right_shift(starts, 5) - 1, 0, KN - SPAN)
         tops.append(jnp.right_shift(knots, 1))
         lefts.append(knots)
-    for i in range(granules):
+    for i in visits(granules, interior):
         for r in range(2):
             owner = routes[r, i]
             rank = ranks[owner]
@@ -348,7 +383,8 @@
                         at = 16 * (2 * b + c) + 8 * half
                         moved = pltpu.roll(rows, jnp.bitwise_and(turn + KN * half, LANES - 1), 1)
                         pltpu.store(windows.at[owner, at : at + 8, :], moved, mask=here)
-    send_ref[...] = windows[...].astype(bf16)
+    if not interior:
+        send_ref[...] = windows[...].astype(bf16)
     for copy in copies:
         copy.wait()
 
@@ -376,7 +412,7 @@
         starts = [pltpu.roll(window_ref[r, :, at], turn, 1) for r in range(2)]
         rank = jnp.int32(0)
         place = [jnp.full((8, LANES), -1, jnp.int32) for _ in range(2)]
-        for i in range(granules):
+        for i in visits(granules, True) + visits(granules, False):
             for r in range(2):
                 hit = routes[r, i] == own
                 here = seat == jnp.where(hit, rank, -1)
@@ -492,56 +528,74 @@
 
     near, far = call(
         first_edges,
-        [("a", grids)],
+        [("h", grids)],
         [("v", edge, bf16), ("v", edge, bf16)],
         [pltpu.VMEM((2,) + edge, f32), pltpu.SemaphoreType.DMA((2,))],
     )
     near, far = exchange(near, far)
-    extended, rhs, diagonal, cross, coupling = call(
+    (extended,) = call(
+        arrange_grids,
+        [("h", grids)],
+        [("v", ext, f32)],
+        [pltpu.VMEM(own, f32), pltpu.SemaphoreType.DMA((chunks,))],
+    )
+    rhs, diagonal, cross, coupling = call(
         arrange,
-        [("a", grids), ("a", rhs), ("a", diagonal), ("a", cross), ("a", coupling)],
+        [("h", rhs), ("h", diagonal), ("h", cross), ("h", coupling)],
         [
-            ("v", ext, f32),
             ("v", own, f32),
             ("v", own, f32),
             ("v", (granules, bands, 32, LANES), f32),
             ("v", (granules, slots, bands, 32, LANES), bf16),
         ],
         [
-            pltpu.VMEM(own, f32),
             pltpu.VMEM(cross.shape, f32),
             pltpu.VMEM(coupling.shape, bf16),
             pltpu.VMEM((bands, 32 * slots, LANES), f32),
-            pltpu.SemaphoreType.DMA((5, chunks)),
+            pltpu.SemaphoreType.DMA((3, chunks)),
         ],
     )
     gathered = pltpu.VMEM((slots, 64, LANES), f32)
     weights = pltpu.VMEM((slots, 64, LANES), f32)
     scalars = pltpu.SMEM((2, granules), jnp.int32)
 
+    def over_band(partial):
+        return [("v", partial)] + [
+            ("v", lax.ppermute(partial, "band", [(i, i ^ flip) for i in range(band_total)]))
+            for flip in range(1, band_total)
+        ]
+
     for sweep in range(SWEEPS):
+        last = sweep == SWEEPS - 1
         (inner,) = call(
             interior_disparities, graph + [("v", extended)], [packed], [gathered, scalars]
         )
+        if last:
+            inner_shares = over_band(inner)
         if sweep == 1:
             weight_shape = (pixel_count, device_total * LANES)
+            routes, starts, _ = lax.optimization_barrier((tiles[0][1], tiles[1][1], inner))
             row_weights, col_weights = call(
-                interp_weights, tiles, [("v", weight_shape, bf16), ("v", weight_shape, bf16)]
+                interp_weights,
+                [("v", routes), ("v", starts)],
+                [("v", weight_shape, bf16), ("v", weight_shape, bf16)],
             )
+            inner, row_weights, col_weights = lax.optimization_barrier(
+                (inner, row_weights, col_weights)
+            )
+        inputs = graph + [("v", near), ("v", far), ("v", extended)]
+        inputs += [] if last else [("v", inner)]
         extended, partial = call(
             edge_disparities,
-            graph + [("v", near), ("v", far), ("v", inner), ("v", extended)],
+            inputs,
             [("v", ext, f32), packed],
             [gathered, scalars],
-            aliases={5: 0},
+            aliases={4: 0},
         )
-        shares = [partial] + [
-            lax.ppermute(partial, "band", [(i, i ^ flip) for i in range(band_total)])
-            for flip in range(1, band_total)
-        ]
-        inputs = graph + [("v", share) for share in shares]
-        inputs += [("v", extended), ("v", rhs), ("v", diagonal), ("v", cross), ("v", coupling)]
-        if sweep < SWEEPS - 1:
+        shares = over_band(partial)
+        state = [("v", extended), ("v", rhs), ("v", diagonal), ("v", cross), ("v", coupling)]
+        if not last:
+            inputs = graph + shares + state
             updated, near, far = call(
                 edge_sweep,
                 inputs,
@@ -556,26 +610,34 @@
                 [weights, scalars],
                 aliases={len(inputs): 0},
             )
-        else:
-            windows = (device_total, 2 * bands * SPAN, LANES)
-            balanced, payload = call(
-                last_sweep,
-                inputs + tiles,
-                [("a", own, f32), ("v", windows, bf16)],
-                [
-                    pltpu.VMEM(own, f32),
-                    pltpu.VMEM(windows, f32),
-                    weights,
-                    scalars,
-                    pltpu.SMEM((device_total,), jnp.int32),
-                    pltpu.SemaphoreType.DMA((chunks,)),
-                ],
-            )
+    windows = (device_total, 2 * bands * SPAN, LANES)
+    scratch = [
+        weights,
+        scalars,
+        pltpu.SMEM((device_total,), jnp.int32),
+        pltpu.VMEM(own, f32),
+        pltpu.SemaphoreType.DMA((2,)),
+    ]
+    inputs = graph + inner_shares + state + tiles
+    balanced, gathered_windows = call(
+        functools.partial(last_sweep, True),
+        inputs,
+        [("h", own, f32), ("v", windows, f32)],
+        scratch,
+    )
+    inputs = graph + shares + state + tiles + [("h", balanced), ("v", gathered_windows)]
+    balanced, payload, _ = call(
+        functools.partial(last_sweep, False),
+        inputs,
+        [("h", own, f32), ("v", windows, bf16), ("v", windows, f32)],
+        scratch,
+        aliases={len(inputs) - 2: 0, len(inputs) - 1: 2},
+    )
     received = lax.all_to_all(payload, "gran", split_axis=0, concat_axis=0, tiled=True)
     (corrected,) = call(
         compose,
         [tiles[0], ("v", received), ("v", row_weights), ("v", col_weights), ("v", tile_pixels)],
-        [("a", tile_pixels.shape, bf16)],
+        [("h", tile_pixels.shape, bf16)],
         [
             pltpu.VMEM((2 * bands, pixel_count, device_total * LANES), bf16),
             pltpu.VMEM(tile_pixels.shape[1:], bf16),

time: 86.3 us -> 78 us (0.904)
  blocking collectives: 0 us -> 13 us
  waiting for transfers between devices: 23.1 us -> 12.7 us
  local copies, waits for them, and re-layouts: 5.85 us -> 0.03 us
  starting transfers between devices: 24 us -> 19.5 us
    all_to_all x0 -> x1, blocking collectives: none -> 13 us  [per_device(): lax.all_to_all(payload, 'gran', split_axis=0, concat_axis=0, tiled=True)]
    all_to_all x1 -> x0, starting transfers between devices: 6.08 us -> none  [per_device(): lax.all_to_all(payload, 'gran', split_axis=0, concat_axis=0, tiled=True)]
    ppermute x9 -> x12, waiting for transfers between devices: 8.24 us -> 2.16 us  [over_band(): lax.ppermute(partial, 'band', [(i, i ^ flip) for i in range(band_total)])]
    unnamed x20 -> x10, local copies, waits for them, and re-layouts: 5.85 us -> 0.03 us
    all_to_all x1 -> x0, waiting for transfers between devices: 3.08 us -> none  [per_device(): lax.all_to_all(payload, 'gran', split_axis=0, concat_axis=0, tiled=True)]
    ppermute x9 -> x12, starting transfers between devices: 5.8 us -> 7.68 us  [over_band(): lax.ppermute(partial, 'band', [(i, i ^ flip) for i in range(band_total)])]
    ppermute x3, waiting for transfers between devices: 11.8 us -> 10.5 us  [exchange(): near = lax.ppermute(near, 'gran', near_pairs)]
    pallas_call x15 -> x17, Pallas kernels: 32.2 us -> 31.6 us  [call(): pl.pallas_call(body, in_specs=[ON_CHIP if kind == 'v' else ANYWHERE for k...]
  transfers between devices with their start and end apart: 16 -> 18, of which waited for: 9 -> 5; matrix products, arithmetic and copies ran while one was open for 0% -> 0% of each run, Pallas kernels for 21% -> 26%
where the time goes in v2:
time: 78 us; the launch traced here: 77.7 us
  Pallas kernels  31.6 us (41%)
  starting transfers between devices  19.5 us (25%)
  blocking collectives  13 us (17%)
  waiting for transfers between devices  12.7 us (16%)
  between operations  0.93 us (1%)
    pallas_call x17, Pallas kernels, call(): pl.pallas_call(body, in_specs=[ON_CHIP if kind == 'v' else ANYWHERE for k...  31.6 us
    all_to_all x1, blocking collectives, per_device(): lax.all_to_all(payload, 'gran', split_axis=0, concat_axis=0, tiled=True)  13 us
    ppermute x3, waiting for transfers between devices, exchange(): near = lax.ppermute(near, 'gran', near_pairs)  10.5 us
    ppermute x3, starting transfers between devices, exchange(): near = lax.ppermute(near, 'gran', near_pairs)  9.8 us
    ppermute x12, starting transfers between devices, over_band(): lax.ppermute(partial, 'band', [(i, i ^ flip) for i in range(band_total)])  7.68 us
    ppermute x12, waiting for transfers between devices, over_band(): lax.ppermute(partial, 'band', [(i, i ^ flip) for i in range(band_total)])  2.16 us
    ppermute x3, starting transfers between devices, exchange(): far = lax.ppermute(far, 'gran', far_pairs)  1.98 us
  transfers between devices with their start and end apart: 18, of which 5 were waited for; matrix products, arithmetic and copies ran while one was open for 0% of the time, Pallas kernels for 26%

profile of v2, /device:TPU:0, one launch (start us, length us, event | category | flops | bytes accessed | tf_op | source)
XLA Modules:
  0.0 77.7 jit_solution(15086610751335868942)
XLA Ops:
  0.6 1.2 %shard_map.113 = (bf16[4,3,64,128]{3,2,1,0:T(8,128)(2,1)S(1)}, bf16[4,3,64,128]{3,2,1,0:T(8,128)(2,1)S(1)}) custom-call(f32[16,3,64,128]{3,2,1,0:T(8,128)} %bitcast.69), custom_call_target="tpu_custom_call" | custom-call | tf_op jit(solution)/shard_map/pallas_call | solution.py:31
  1.8 0.0 copy-start
  1.9 0.0 copy-start.2
  1.9 3.0 %collective-permute-start = (bf16[4,3,64,128]{3,2,1,0:T(8,128)(2,1)S(1)}, bf16[4,3,64,128]{3,2,1,0:T(8,128)(2,1)S(1)}, u32[]{:S(2)}, u32[]{:S(2)}) collective-permute-start(bf16[4,3,64,128]{3,2,1,0:T(8,128)(2,1)S(1)} %get-tuple-element.31), channel_id=1, source_target_pairs={{0,4},{4,0},{8,12},{12,8},{16,20},{20,16},{24,28},{28,24},{1,5},{5... | collective-permute-start | bytes 589832 | tf_op jit(solution)/shard_map/ppermute | solution.py:526
  4.9 0.7 collective-permute-start.1
  5.5 1.5 %shard_map.114.ext_ref.refs_0_ = f32[24,3,64,128]{3,2,1,0:T(8,128)S(1)} custom-call(f32[16,3,64,128]{3,2,1,0:T(8,128)} %bitcast.70), custom_call_target="tpu_custom_call" | custom-call | tf_op jit(solution)/shard_map/pallas_call | solution.py:31
  7.0 0.8 shard_map.115.refs_1_
  7.8 5.4 %collective-permute-done.near_ref = bf16[4,3,64,128]{3,2,1,0:T(8,128)(2,1)S(1)} collective-permute-done((bf16[4,3,64,128]{3,2,1,0:T(8,128)(2,1)S(1)}, bf16[4,3,64,128]{3,2,1,0:T(8,128)(2,1)S(1)}, u32[]{:S(2)}, u32[]{:S(2)}) %collective-permute-start) | collective-permute-done | bytes 196640 | tf_op jit(solution)/shard_map/ppermute | solution.py:526
  13.3 0.7 shard_map.116
  13.9 0.1 collective-permute-start.4
  14.0 1.6 %collective-permute-start.3 = (f32[64,128]{1,0:T(8,128)S(1)}, f32[64,128]{1,0:T(8,128)S(1)}, u32[]{:S(2)}, u32[]{:S(2)}) collective-permute-start(f32[64,128]{1,0:T(8,128)S(1)} %get-tuple-element.33.refs_0_), channel_id=1, source_target_pairs={{0,2},{1,3},{2,0},{3,1},{4,6},{5,7},{6,4},{7,5},{8,10},{9,11},{10,... | collective-permute-start | bytes 98312 | tf_op jit(solution)/shard_map/ppermute | solution.py:564
  15.6 0.3 collective-permute-start.2
  15.9 6.1 %shard_map.117 = (f32[16,3,64,128]{3,2,1,0:T(8,128)S(1)}, f32[16,3,64,128]{3,2,1,0:T(8,128)S(1)}, f32[16,3,32,128]{3,2,1,0:T(8,128)S(1)}, bf16[16,8,3,32,128]{4,3,2,1,0:T(8,128)(2,1)S(1)}) custom-call(f32[16,3,64,128]{3,2,1,0:T(8,128)} %bitcast.72, f32[16,3,64,128]{3,2,1,0:T(8,128)} %bitcast.73, f32[3,2,256,128]{3,2,1,0:T(8,128)} %bitcast.75, ...), custom_call_target="tpu_custom_call" | custom-call | tf_op jit(solution)/shard_map/pallas_call | solution.py:31
  22.0 0.0 collective-permute-done.4.refs_3_
  22.0 1.1 %shard_map.118 = (f32[24,3,64,128]{3,2,1,0:T(8,128)S(1)}, bf16[4,3,64,128]{3,2,1,0:T(8,128)(2,1)S(1)}, bf16[4,3,64,128]{3,2,1,0:T(8,128)(2,1)S(1)}) custom-call(s32[8,16]{1,0:T(8,128)S(1)} %bitcast.40, s32[1,16]{1,0:T(1,128)S(1)} %bitcast.52, f32[64,128]{1,0:T(8,128)S(1)} %get-tuple-element.33.refs_0_, f32[64,128]{1,0:T(8,128)S(1)} %collective-permute-done.2.refs_1_, ...), custom_call_target="tpu_custom_call" | custom-call | tf_op jit(solution)/shard_map/pallas_call | solution.py:31
  23.1 2.8 %collective-permute-start.5 = (bf16[4,3,64,128]{3,2,1,0:T(8,128)(2,1)S(1)}, bf16[4,3,64,128]{3,2,1,0:T(8,128)(2,1)S(1)}, u32[]{:S(2)}, u32[]{:S(2)}) collective-permute-start(bf16[4,3,64,128]{3,2,1,0:T(8,128)(2,1)S(1)} %get-tuple-element.39), channel_id=1, source_target_pairs={{0,4},{4,0},{8,12},{12,8},{16,20},{20,16},{24,28},{28,24},{1,5},{5... | collective-permute-start | bytes 589832 | tf_op jit(solution)/shard_map/ppermute | solution.py:526
  25.9 0.7 collective-permute-start.6
  26.6 1.2 %shard_map.119.ext_ref.refs_0_ = f32[24,3,64,128]{3,2,1,0:T(8,128)S(1)} custom-call(s32[8,16]{1,0:T(8,128)S(1)} %bitcast.41, s32[1,16]{1,0:T(1,128)S(1)} %bitcast.53, f32[64,128]{1,0:T(8,128)S(1)} %get-tuple-element.33.refs_0_, f32[64,128]{1,0:T(8,128)S(1)} %collective-permute-done.2.refs_1_, ...), custom_call_target="tpu_custom_call", output_to_operand_aliasing={{}: (11, {})} | custom-call | tf_op jit(solution)/shard_map/pallas_call | solution.py:31
  27.7 0.0 copy-start.3
  27.7 0.0 copy-start.4
  27.7 0.8 shard_map.120.refs_1_
  28.5 5.2 %shard_map.121 = (bf16[256,1024]{1,0:T(8,128)(2,1)S(1)}, bf16[256,1024]{1,0:T(8,128)(2,1)S(1)}) custom-call(s32[2,128]{1,0:T(2,128)S(1)} %bitcast.65, s32[2,2,128]{2,1,0:T(2,128)S(1)} %bitcast.62), custom_call_target="tpu_custom_call" | custom-call | tf_op jit(solution)/shard_map/pallas_call | solution.py:31
  33.7 0.9 %collective-permute-done.5.near_ref = bf16[4,3,64,128]{3,2,1,0:T(8,128)(2,1)S(1)} collective-permute-done((bf16[4,3,64,128]{3,2,1,0:T(8,128)(2,1)S(1)}, bf16[4,3,64,128]{3,2,1,0:T(8,128)(2,1)S(1)}, u32[]{:S(2)}, u32[]{:S(2)}) %collective-permute-start.5) | collective-permute-done | bytes 196640 | tf_op jit(solution)/shard_map/ppermute | solution.py:526
  34.7 0.7 shard_map.122
  35.4 0.1 collective-permute-start.9
  35.4 1.3 %collective-permute-start.8 = (f32[64,128]{1,0:T(8,128)S(1)}, f32[64,128]{1,0:T(8,128)S(1)}, u32[]{:S(2)}, u32[]{:S(2)}) collective-permute-start(f32[64,128]{1,0:T(8,128)S(1)} %get-tuple-element.47.refs_0_), channel_id=1, source_target_pairs={{0,2},{1,3},{2,0},{3,1},{4,6},{5,7},{6,4},{7,5},{8,10},{9,11},{10,... | collective-permute-start | bytes 98312 | tf_op jit(solution)/shard_map/ppermute | solution.py:564
  36.8 0.5 collective-permute-start.7
  37.3 1.7 %collective-permute-done.9.refs_3_ = f32[64,128]{1,0:T(8,128)S(1)} collective-permute-done((f32[64,128]{1,0:T(8,128)S(1)}, f32[64,128]{1,0:T(8,128)S(1)}, u32[]{:S(2)}, u32[]{:S(2)}) %collective-permute-start.9) | collective-permute-done | bytes 32800 | tf_op jit(solution)/shard_map/ppermute | solution.py:564
  38.9 0.5 collective-permute-done.8.refs_2_
  39.4 0.0 collective-permute-done.7.refs_1_
  39.4 1.1 %shard_map.123 = (f32[24,3,64,128]{3,2,1,0:T(8,128)S(1)}, bf16[4,3,64,128]{3,2,1,0:T(8,128)(2,1)S(1)}, bf16[4,3,64,128]{3,2,1,0:T(8,128)(2,1)S(1)}) custom-call(s32[8,16]{1,0:T(8,128)S(1)} %bitcast.44, s32[1,16]{1,0:T(1,128)S(1)} %bitcast.56, f32[64,128]{1,0:T(8,128)S(1)} %get-tuple-element.47.refs_0_, f32[64,128]{1,0:T(8,128)S(1)} %collective-permute-done.7.refs_1_, ...), custom_call_target="tpu_custom_call" | custom-call | tf_op jit(solution)/shard_map/pallas_call | solution.py:31
  40.5 4.0 %collective-permute-start.10 = (bf16[4,3,64,128]{3,2,1,0:T(8,128)(2,1)S(1)}, bf16[4,3,64,128]{3,2,1,0:T(8,128)(2,1)S(1)}, u32[]{:S(2)}, u32[]{:S(2)}) collective-permute-start(bf16[4,3,64,128]{3,2,1,0:T(8,128)(2,1)S(1)} %get-tuple-element.49), channel_id=1, source_target_pairs={{0,4},{4,0},{8,12},{12,8},{16,20},{20,16},{24,28},{28,24},{1,5},{5... | collective-permute-start | bytes 589832 | tf_op jit(solution)/shard_map/ppermute | solution.py:526
  44.5 0.7 collective-permute-start.11
  45.2 1.2 %shard_map.124.refs_0_.ext_ref = f32[24,3,64,128]{3,2,1,0:T(8,128)S(1)} custom-call(s32[8,16]{1,0:T(8,128)S(1)} %bitcast.45, s32[1,16]{1,0:T(1,128)S(1)} %bitcast.57, f32[64,128]{1,0:T(8,128)S(1)} %get-tuple-element.47.refs_0_, f32[64,128]{1,0:T(8,128)S(1)} %collective-permute-done.7.refs_1_, ...), custom_call_target="tpu_custom_call", output_to_operand_aliasing={{}: (11, {})} | custom-call | tf_op jit(solution)/shard_map/pallas_call | solution.py:31
  46.4 0.8 shard_map.126.refs_0_
  47.1 0.1 collective-permute-start.17
  47.2 1.4 %collective-permute-start.16 = (f32[64,128]{1,0:T(8,128)S(1)}, f32[64,128]{1,0:T(8,128)S(1)}, u32[]{:S(2)}, u32[]{:S(2)}) collective-permute-start(f32[64,128]{1,0:T(8,128)S(1)} %shard_map.126.refs_0_), channel_id=1, source_target_pairs={{0,2},{1,3},{2,0},{3,1},{4,6},{5,7},{6,4},{7,5},{8,10},{9,11},{10,... | collective-permute-start | bytes 98312 | tf_op jit(solution)/shard_map/ppermute | solution.py:564
  48.7 0.4 collective-permute-start.15
  49.1 4.1 %collective-permute-done.10.near_ref = bf16[4,3,64,128]{3,2,1,0:T(8,128)(2,1)S(1)} collective-permute-done((bf16[4,3,64,128]{3,2,1,0:T(8,128)(2,1)S(1)}, bf16[4,3,64,128]{3,2,1,0:T(8,128)(2,1)S(1)}, u32[]{:S(2)}, u32[]{:S(2)}) %collective-permute-start.10) | collective-permute-done | bytes 196640 | tf_op jit(solution)/shard_map/ppermute | solution.py:526
  53.2 0.7 shard_map.125
  53.9 0.1 collective-permute-start.14
  54.0 0.6 collective-permute-start.13
  54.6 1.2 %collective-permute-start.12 = (f32[64,128]{1,0:T(8,128)S(1)}, f32[64,128]{1,0:T(8,128)S(1)}, u32[]{:S(2)}, u32[]{:S(2)}) collective-permute-start(f32[64,128]{1,0:T(8,128)S(1)} %get-tuple-element.52.refs_0_), channel_id=1, source_target_pairs={{0,1},{1,0},{2,3},{3,2},{4,5},{5,4},{6,7},{7,6},{8,9},{9,8},{10,11... | collective-permute-start | bytes 98312 | tf_op jit(solution)/shard_map/ppermute | solution.py:564
  55.8 2.5 %shard_map.127 = (f32[16,3,64,128]{3,2,1,0:T(8,128)}, f32[8,96,128]{2,1,0:T(8,128)S(1)}) custom-call(s32[8,16]{1,0:T(8,128)S(1)} %bitcast.48, s32[1,16]{1,0:T(1,128)S(1)} %bitcast.60, f32[64,128]{1,0:T(8,128)S(1)} %shard_map.126.refs_0_, f32[64,128]{1,0:T(8,128)S(1)} %collective-permute-done.15.refs_1_, f32[64,128]{1,0:T(8,128)S(1)} %collective-permute-done.16.refs_2_, ...), custom_call_target="tpu_custom_call" | custom-call | tf_op jit(solution)/shard_map/pallas_call | solution.py:31
  58.3 0.0 copy-start.1
  58.3 2.4 %shard_map.128 = (f32[16,3,64,128]{3,2,1,0:T(8,128)}, bf16[8,96,128]{2,1,0:T(8,128)(2,1)S(1)}, f32[8,96,128]{2,1,0:T(8,128)S(1)}) custom-call(s32[8,16]{1,0:T(8,128)S(1)} %bitcast.49, s32[1,16]{1,0:T(1,128)S(1)} %bitcast.61, f32[64,128]{1,0:T(8,128)S(1)} %get-tuple-element.52.refs_0_, ...), custom_call_target="tpu_custom_call", output_to_operand_aliasing={{0}: (13, {}), {2}: (14, {})} | custom-call | tf_op jit(solution)/shard_map/pallas_call | solution.py:31
  60.8 13.0 %all_to_all.5.received_ref = bf16[8,96,128]{2,1,0:T(8,128)(2,1)S(1)} all-to-all(bf16[8,96,128]{2,1,0:T(8,128)(2,1)S(1)} %get-tuple-element.57), channel_id=1, replica_groups=mesh['gran'=8,'band'=4] {'gran'}, dimensions={0} | all-to-all | bytes 393216 | tf_op jit(solution)/shard_map/all_to_all | solution.py:636
  73.8 3.9 %shard_map.129 = bf16[1,3,256,256]{3,2,1,0:T(8,128)(2,1)} custom-call(s32[2,128]{1,0:T(2,128)S(1)} %bitcast.68, bf16[8,96,128]{2,1,0:T(8,128)(2,1)S(1)} %all_to_all.5.received_ref, bf16[256,1024]{1,0:T(8,128)(2,1)S(1)} %get-tuple-element.58.row_ref, bf16[256,1024]{1,0:T(8,128)(2,1)S(1)} %get-tuple-element.59.col_ref, bf16[1,3,256,256]{3,2,1,0:T(8,128)(2,1)S(1)} %copy-done.1), custom_call_target="tpu_custom_call" | custom-call | tf_op jit(solution)/shard_map/pallas_call | solution.py:31
  (16 shorter events, 0.0 us)
Async XLA Ops:
  1.8 5.2 %copy-start = (s32[16,8]{0,1:T(8,128)S(1)}, s32[16,8]{0,1:T(8,128)}, u32[]{:S(2)}) copy-start(s32[16,8]{0,1:T(8,128)} %param.15) | copy-start | bytes 1540
  1.9 5.2 %copy-start.2 = (s32[16]{0:T(128)S(1)}, s32[16]{0:T(128)}, u32[]{:S(2)}) copy-start(s32[16]{0:T(128)} %param.16) | copy-start | bytes 196
  1.9 11.4 %collective-permute-start = (bf16[4,3,64,128]{3,2,1,0:T(8,128)(2,1)S(1)}, bf16[4,3,64,128]{3,2,1,0:T(8,128)(2,1)S(1)}, u32[]{:S(2)}, u32[]{:S(2)}) collective-permute-start(bf16[4,3,64,128]{3,2,1,0:T(8,128)(2,1)S(1)} %get-tuple-element.31), channel_id=1, source_target_pairs={{0,4},{4,0},{8,12},{12,8},{16,20},{20,16},{24,28},{28,24},{1,5},{5... | collective-permute-start | bytes 589832 | tf_op jit(solution)/shard_map/ppermute | solution.py:526
  4.9 8.4 %collective-permute-start.1 = (bf16[4,3,64,128]{3,2,1,0:T(8,128)(2,1)S(1)}, bf16[4,3,64,128]{3,2,1,0:T(8,128)(2,1)S(1)}, u32[]{:S(2)}, u32[]{:S(2)}) collective-permute-start(bf16[4,3,64,128]{3,2,1,0:T(8,128)(2,1)S(1)} %get-tuple-element.32), channel_id=1, source_target_pairs={{4,8},{8,4},{12,16},{16,12},{20,24},{24,20},{5,9},{9,5},{13,17},{1... | collective-permute-start | bytes 589832 | tf_op jit(solution)/shard_map/ppermute | solution.py:525
  13.9 8.1 %collective-permute-start.4 = (f32[64,128]{1,0:T(8,128)S(1)}, f32[64,128]{1,0:T(8,128)S(1)}, u32[]{:S(2)}, u32[]{:S(2)}) collective-permute-start(f32[64,128]{1,0:T(8,128)S(1)} %get-tuple-element.33.refs_0_), channel_id=1, source_target_pairs={{0,3},{1,2},{2,1},{3,0},{4,7},{5,6},{6,5},{7,4},{8,11},{9,10},{10,... | collective-permute-start | bytes 98312 | tf_op jit(solution)/shard_map/ppermute | solution.py:564
  14.0 8.0 %collective-permute-start.3 = (f32[64,128]{1,0:T(8,128)S(1)}, f32[64,128]{1,0:T(8,128)S(1)}, u32[]{:S(2)}, u32[]{:S(2)}) collective-permute-start(f32[64,128]{1,0:T(8,128)S(1)} %get-tuple-element.33.refs_0_), channel_id=1, source_target_pairs={{0,2},{1,3},{2,0},{3,1},{4,6},{5,7},{6,4},{7,5},{8,10},{9,11},{10,... | collective-permute-start | bytes 98312 | tf_op jit(solution)/shard_map/ppermute | solution.py:564
  15.6 6.4 %collective-permute-start.2 = (f32[64,128]{1,0:T(8,128)S(1)}, f32[64,128]{1,0:T(8,128)S(1)}, u32[]{:S(2)}, u32[]{:S(2)}) collective-permute-start(f32[64,128]{1,0:T(8,128)S(1)} %get-tuple-element.33.refs_0_), channel_id=1, source_target_pairs={{0,1},{1,0},{2,3},{3,2},{4,5},{5,4},{6,7},{7,6},{8,9},{9,8},{10,11... | collective-permute-start | bytes 98312 | tf_op jit(solution)/shard_map/ppermute | solution.py:564
  23.1 11.5 %collective-permute-start.5 = (bf16[4,3,64,128]{3,2,1,0:T(8,128)(2,1)S(1)}, bf16[4,3,64,128]{3,2,1,0:T(8,128)(2,1)S(1)}, u32[]{:S(2)}, u32[]{:S(2)}) collective-permute-start(bf16[4,3,64,128]{3,2,1,0:T(8,128)(2,1)S(1)} %get-tuple-element.39), channel_id=1, source_target_pairs={{0,4},{4,0},{8,12},{12,8},{16,20},{20,16},{24,28},{28,24},{1,5},{5... | collective-permute-start | bytes 589832 | tf_op jit(solution)/shard_map/ppermute | solution.py:526
  25.9 8.8 %collective-permute-start.6 = (bf16[4,3,64,128]{3,2,1,0:T(8,128)(2,1)S(1)}, bf16[4,3,64,128]{3,2,1,0:T(8,128)(2,1)S(1)}, u32[]{:S(2)}, u32[]{:S(2)}) collective-permute-start(bf16[4,3,64,128]{3,2,1,0:T(8,128)(2,1)S(1)} %get-tuple-element.40), channel_id=1, source_target_pairs={{4,8},{8,4},{12,16},{16,12},{20,24},{24,20},{5,9},{9,5},{13,17},{1... | collective-permute-start | bytes 589832 | tf_op jit(solution)/shard_map/ppermute | solution.py:525
  27.7 0.8 %copy-start.3 = (s32[128,2,2]{0,2,1:T(2,128)S(1)}, s32[128,2,2]{0,2,1:T(2,128)}, u32[]{:S(2)}) copy-start(s32[128,2,2]{0,2,1:T(2,128)} %param.18) | copy-start | bytes 6148
  27.7 0.8 %copy-start.4 = (s32[128,2]{0,1:T(2,128)S(1)}, s32[128,2]{0,1:T(2,128)}, u32[]{:S(2)}) copy-start(s32[128,2]{0,1:T(2,128)} %param.17) | copy-start | bytes 3076
  35.4 3.6 %collective-permute-start.9 = (f32[64,128]{1,0:T(8,128)S(1)}, f32[64,128]{1,0:T(8,128)S(1)}, u32[]{:S(2)}, u32[]{:S(2)}) collective-permute-start(f32[64,128]{1,0:T(8,128)S(1)} %get-tuple-element.47.refs_0_), channel_id=1, source_target_pairs={{0,3},{1,2},{2,1},{3,0},{4,7},{5,6},{6,5},{7,4},{8,11},{9,10},{10,... | collective-permute-start | bytes 98312 | tf_op jit(solution)/shard_map/ppermute | solution.py:564
  35.4 4.0 %collective-permute-start.8 = (f32[64,128]{1,0:T(8,128)S(1)}, f32[64,128]{1,0:T(8,128)S(1)}, u32[]{:S(2)}, u32[]{:S(2)}) collective-permute-start(f32[64,128]{1,0:T(8,128)S(1)} %get-tuple-element.47.refs_0_), channel_id=1, source_target_pairs={{0,2},{1,3},{2,0},{3,1},{4,6},{5,7},{6,4},{7,5},{8,10},{9,11},{10,... | collective-permute-start | bytes 98312 | tf_op jit(solution)/shard_map/ppermute | solution.py:564
  36.8 2.6 %collective-permute-start.7 = (f32[64,128]{1,0:T(8,128)S(1)}, f32[64,128]{1,0:T(8,128)S(1)}, u32[]{:S(2)}, u32[]{:S(2)}) collective-permute-start(f32[64,128]{1,0:T(8,128)S(1)} %get-tuple-element.47.refs_0_), channel_id=1, source_target_pairs={{0,1},{1,0},{2,3},{3,2},{4,5},{5,4},{6,7},{7,6},{8,9},{9,8},{10,11... | collective-permute-start | bytes 98312 | tf_op jit(solution)/shard_map/ppermute | solution.py:564
  40.5 12.7 %collective-permute-start.10 = (bf16[4,3,64,128]{3,2,1,0:T(8,128)(2,1)S(1)}, bf16[4,3,64,128]{3,2,1,0:T(8,128)(2,1)S(1)}, u32[]{:S(2)}, u32[]{:S(2)}) collective-permute-start(bf16[4,3,64,128]{3,2,1,0:T(8,128)(2,1)S(1)} %get-tuple-element.49), channel_id=1, source_target_pairs={{0,4},{4,0},{8,12},{12,8},{16,20},{20,16},{24,28},{28,24},{1,5},{5... | collective-permute-start | bytes 589832 | tf_op jit(solution)/shard_map/ppermute | solution.py:526
  44.5 8.7 %collective-permute-start.11 = (bf16[4,3,64,128]{3,2,1,0:T(8,128)(2,1)S(1)}, bf16[4,3,64,128]{3,2,1,0:T(8,128)(2,1)S(1)}, u32[]{:S(2)}, u32[]{:S(2)}) collective-permute-start(bf16[4,3,64,128]{3,2,1,0:T(8,128)(2,1)S(1)} %get-tuple-element.50), channel_id=1, source_target_pairs={{4,8},{8,4},{12,16},{16,12},{20,24},{24,20},{5,9},{9,5},{13,17},{1... | collective-permute-start | bytes 589832 | tf_op jit(solution)/shard_map/ppermute | solution.py:525
  47.1 7.4 %collective-permute-start.17 = (f32[64,128]{1,0:T(8,128)S(1)}, f32[64,128]{1,0:T(8,128)S(1)}, u32[]{:S(2)}, u32[]{:S(2)}) collective-permute-start(f32[64,128]{1,0:T(8,128)S(1)} %shard_map.126.refs_0_), channel_id=1, source_target_pairs={{0,3},{1,2},{2,1},{3,0},{4,7},{5,6},{6,5},{7,4},{8,11},{9,10},{10,... | collective-permute-start | bytes 98312 | tf_op jit(solution)/shard_map/ppermute | solution.py:564
  47.2 8.6 %collective-permute-start.16 = (f32[64,128]{1,0:T(8,128)S(1)}, f32[64,128]{1,0:T(8,128)S(1)}, u32[]{:S(2)}, u32[]{:S(2)}) collective-permute-start(f32[64,128]{1,0:T(8,128)S(1)} %shard_map.126.refs_0_), channel_id=1, source_target_pairs={{0,2},{1,3},{2,0},{3,1},{4,6},{5,7},{6,4},{7,5},{8,10},{9,11},{10,... | collective-permute-start | bytes 98312 | tf_op jit(solution)/shard_map/ppermute | solution.py:564
  48.7 7.2 %collective-permute-start.15 = (f32[64,128]{1,0:T(8,128)S(1)}, f32[64,128]{1,0:T(8,128)S(1)}, u32[]{:S(2)}, u32[]{:S(2)}) collective-permute-start(f32[64,128]{1,0:T(8,128)S(1)} %shard_map.126.refs_0_), channel_id=1, source_target_pairs={{0,1},{1,0},{2,3},{3,2},{4,5},{5,4},{6,7},{7,6},{8,9},{9,8},{10,11... | collective-permute-start | bytes 98312 | tf_op jit(solution)/shard_map/ppermute | solution.py:564
  53.9 4.4 %collective-permute-start.14 = (f32[64,128]{1,0:T(8,128)S(1)}, f32[64,128]{1,0:T(8,128)S(1)}, u32[]{:S(2)}, u32[]{:S(2)}) collective-permute-start(f32[64,128]{1,0:T(8,128)S(1)} %get-tuple-element.52.refs_0_), channel_id=1, source_target_pairs={{0,3},{1,2},{2,1},{3,0},{4,7},{5,6},{6,5},{7,4},{8,11},{9,10},{10,... | collective-permute-start | bytes 98312 | tf_op jit(solution)/shard_map/ppermute | solution.py:564
  54.0 4.3 %collective-permute-start.13 = (f32[64,128]{1,0:T(8,128)S(1)}, f32[64,128]{1,0:T(8,128)S(1)}, u32[]{:S(2)}, u32[]{:S(2)}) collective-permute-start(f32[64,128]{1,0:T(8,128)S(1)} %get-tuple-element.52.refs_0_), channel_id=1, source_target_pairs={{0,2},{1,3},{2,0},{3,1},{4,6},{5,7},{6,4},{7,5},{8,10},{9,11},{10,... | collective-permute-start | bytes 98312 | tf_op jit(solution)/shard_map/ppermute | solution.py:564
  54.6 3.7 %collective-permute-start.12 = (f32[64,128]{1,0:T(8,128)S(1)}, f32[64,128]{1,0:T(8,128)S(1)}, u32[]{:S(2)}, u32[]{:S(2)}) collective-permute-start(f32[64,128]{1,0:T(8,128)S(1)} %get-tuple-element.52.refs_0_), channel_id=1, source_target_pairs={{0,1},{1,0},{2,3},{3,2},{4,5},{5,4},{6,7},{7,6},{8,9},{9,8},{10,11... | collective-permute-start | bytes 98312 | tf_op jit(solution)/shard_map/ppermute | solution.py:564
  58.3 15.4 %copy-start.1 = (bf16[1,3,256,256]{3,2,1,0:T(8,128)(2,1)S(1)}, bf16[1,3,256,256]{3,2,1,0:T(8,128)(2,1)}, u32[]{:S(2)}) copy-start(bf16[1,3,256,256]{3,2,1,0:T(8,128)(2,1)} %pixels_ref.1) | copy-start | bytes 1179652

commit v3 on v2

--- a/solution.py
+++ b/solution.py
@@ -51,14 +51,14 @@
     last = grids_ref.shape[0] - REACH
     sides = ((far_ref, odd * last), (near_ref, (1 - odd) * last))
     copies = [
-        pltpu.make_async_copy(grids_ref.at[pl.ds(base, REACH)], raw.at[k], sems.at[k])
+        [pltpu.make_async_copy(grids_ref.at[base + g], raw.at[k, g], sems.at[k, g]) for g in range(REACH)]
         for k, (_, base) in enumerate(sides)
     ]
-    for copy in copies:
+    for copy in copies[0] + copies[1]:
         copy.start()
     for k, (ref, _) in enumerate(sides):
-        copies[k].wait()
         for g in range(REACH):
+            copies[k][g].wait()
             for b in range(ref.shape[1]):
                 for j in range(4):
                     both = [raw[k, g, b, pl.ds(2 * j + c, 8, stride=8), :] for c in range(2)]
@@ -86,51 +86,60 @@
         lax.fori_loop(n * size, (n + 1) * size, step, 0)
 
 
-def arrange(rhs_ref, diag_ref, cross_ref, coupling_ref, rhs_out, diag_out, cross_out, coupling_out, cross_raw, coupling_raw, wide, sems):
+def visits(granules, interior):
+    inner = list(range(REACH, granules - REACH))
+    return inner if interior else [i for i in range(granules) if i not in inner]
+
+
+def arrange(interior, rhs_ref, diag_ref, cross_ref, coupling_ref, rhs_out, diag_out, cross_out, coupling_out, cross_raw, coupling_raw, wide, sems):
     granules, bands = rhs_ref.shape[:2]
     slots = coupling_out.shape[1]
-    chunks = sems.shape[1]
-    size = granules // chunks
+    own = visits(granules, interior)
+    size = REACH
+    chunks = len(own) // size
     copies = []
     for n in range(chunks):
-        part = pl.ds(n * size, size)
-        moves = ((coupling_ref, coupling_raw), (diag_ref, diag_out))
+        source, target = pl.ds(own[n * size], size), pl.ds(n * size, size)
+        moves = ((coupling_ref, coupling_raw), (diag_ref, diag_out), (rhs_ref, rhs_out))
         copies.append(
             [
-                pltpu.make_async_copy(source.at[part], target.at[part], sems.at[k, n])
-                for k, (source, target) in enumerate(moves)
+                pltpu.make_async_copy(here.at[source], there.at[target], sems.at[k, n])
+                for k, (here, there) in enumerate(moves)
             ]
         )
-        for copy in copies[n]:
+        for copy in copies[n][:2]:
             copy.start()
         if n == 0:
-            whole = pltpu.make_async_copy(cross_ref, cross_raw, sems.at[2, 0])
+            whole = pltpu.make_async_copy(cross_ref, cross_raw, sems.at[3, 0])
             whole.start()
-    rest = pltpu.make_async_copy(rhs_ref, rhs_out, sems.at[2, 1])
-    rest.start()
-
-    def step(i, carry):
-        for b in range(bands):
-            wide[b] = coupling_raw[i, b].astype(f32)
-        for b in range(bands):
-            for j in range(4):
-                d = [diag_out[i, b, pl.ds(2 * j + c, 8, stride=8), :] for c in range(2)]
-                pick = cross_raw[b, i // 8, pl.ds(8 * j + i % 8, 8, stride=32), :]
-                cross_out[i, b, 8 * j : 8 * j + 8, :] = pick * jnp.sqrt(d[0] * d[1])
-        for b in range(bands):
-            for s in range(slots):
-                for j in (0, 2):
-                    pair = [wide[b, pl.ds(8 * (j + k) + s, 8, stride=32), :] for k in (0, 1)]
-                    coupling_out[i, s, b, 8 * j : 8 * j + 16, :] = jnp.concatenate(pair, axis=0).astype(bf16)
-        return carry
-
     for n in range(chunks):
-        for copy in copies[n]:
+        copies[n][2].start()
+    for n in range(chunks):
+        for copy in copies[n][:2]:
             copy.wait()
         if n == 0:
             whole.wait()
-        lax.fori_loop(n * size, (n + 1) * size, step, 0)
-    rest.wait()
+
+        def step(g, carry, n=n):
+            at = n * size + g
+            i = own[n * size] + g
+            for b in range(bands):
+                wide[b] = coupling_raw[at, b].astype(f32)
+            for b in range(bands):
+                for j in range(4):
+                    d = [diag_out[at, b, pl.ds(2 * j + c, 8, stride=8), :] for c in range(2)]
+                    pick = cross_raw[b, i // 8, pl.ds(8 * j + i % 8, 8, stride=32), :]
+                    cross_out[at, b, 8 * j : 8 * j + 8, :] = pick * jnp.sqrt(d[0] * d[1])
+            for b in range(bands):
+                for s in range(slots):
+                    for j in (0, 2):
+                        pair = [wide[b, pl.ds(8 * (j + k) + s, 8, stride=32), :] for k in (0, 1)]
+                        coupling_out[at, s, b, 8 * j : 8 * j + 16, :] = jnp.concatenate(pair, axis=0).astype(bf16)
+            return carry
+
+        lax.fori_loop(0, size, step, 0)
+    for n in range(chunks):
+        copies[n][2].wait()
 
 
 def lane_sums():
@@ -235,11 +244,11 @@
     weights[...] = jnp.dot(stacked, spread, preferred_element_type=f32).reshape(slots, 64, LANES)
 
 
-def balance(i, ext_ref, rhs_ref, diag_ref, cross_ref, coupling_ref, weights, graph, store):
+def balance(i, at, ext_ref, rhs_ref, diag_ref, cross_ref, coupling_ref, weights, graph, store):
     bands = rhs_ref.shape[1]
     row = pl.multiple_of(lax.rem(i, 8) * 8, 8)
     parts = [(b, j) for b in range(bands) for j in range(4)]
-    rhs = tuple(rhs_ref[i, b, pl.ds(2 * j + c, 8, stride=8), :] for b, j in parts for c in range(2))
+    rhs = tuple(rhs_ref[at, b, pl.ds(2 * j + c, 8, stride=8), :] for b, j in parts for c in range(2))
 
     def slot(s, sums):
         sigma, drive = sums
@@ -247,7 +256,7 @@
         n = neighbour(graph, i, s)
         new_sigma, new_drive = [], []
         for b in range(bands):
-            coupling = coupling_ref[i, s, b].astype(f32)
+            coupling = coupling_ref[at, s, b].astype(f32)
             for j in range(4):
                 k = 4 * b + j
                 effective = weight * coupling[8 * j : 8 * j + 8]
@@ -261,9 +270,9 @@
     sigma, drive = lax.fori_loop(0, graph[1, i], slot, ((zero,) * len(parts), rhs))
     for k, (b, j) in enumerate(parts):
         first, second = (
-            diag_ref[i, b, pl.ds(2 * j + c, 8, stride=8), :] + sigma[k] for c in range(2)
+            diag_ref[at, b, pl.ds(2 * j + c, 8, stride=8), :] + sigma[k] for c in range(2)
         )
-        cross = cross_ref[i, b, 8 * j : 8 * j + 8, :]
+        cross = cross_ref[at, b, 8 * j : 8 * j + 8, :]
         inverse = 1.0 / (first * second - cross * cross)
         gain, offset = drive[2 * k], drive[2 * k + 1]
         store(
@@ -288,7 +297,7 @@
                 new_ref[base + g + REACH, b, 16 * j : 16 * j + 16, :] = both
                 ref[g, b, 16 * j : 16 * j + 16, :] = both.astype(bf16)
 
-            balance(base + g, *state, weights, graph, store)
+            balance(base + g, lax.div(base, 2 * REACH) * REACH + g, *state, weights, graph, store)
             return carry
 
         lax.fori_loop(0, REACH, step, 0)
@@ -304,7 +313,7 @@
             both = jnp.concatenate([gain, offset], axis=0)
             new_ref[i + REACH, b, 16 * j : 16 * j + 16, :] = both
 
-        balance(i, *state, weights, graph, store)
+        balance(i, i - REACH, *state, weights, graph, store)
         return carry
 
     lax.fori_loop(REACH, new_ref.shape[0] - 3 * REACH, step, 0)
@@ -315,11 +324,6 @@
     base = pl.multiple_of((first // LANES) * LANES, LANES)
     turn = jnp.bitwise_and(LANES - lax.rem(first, LANES), LANES - 1)
     return pltpu.roll(ref[at + (pl.ds(base, LANES),)], turn, 1)
-
-
-def visits(granules, interior):
-    inner = list(range(REACH, granules - REACH))
-    return inner if interior else [i for i in range(granules) if i not in inner]
 
 
 def last_sweep(interior, offset_ref, count_ref, *refs):
@@ -345,7 +349,7 @@
             solved[i, b, pl.ds(2 * j, 8, stride=8), :] = gain
             solved[i, b, pl.ds(2 * j + 1, 8, stride=8), :] = offset
 
-        balance(i, *state, weights, graph, store)
+        balance(i, t - REACH if interior else t, *state, weights, graph, store)
         return carry
 
     lax.fori_loop(*((REACH, granules - REACH) if interior else (0, 2 * REACH)), step, 0)
@@ -395,8 +399,8 @@
     return jnp.where(distance <= 1.0, near, jnp.where(distance < 2.0, far, 0.0))
 
 
-def interp_weights(route_ref, window_ref, rows_out, cols_out):
-    pixels, lanes = rows_out.shape
+def interp_weights(axis, route_ref, window_ref, out_ref):
+    pixels, lanes = out_ref.shape
     senders = lanes // LANES
     granules = route_ref.shape[1] // senders
     own = lax.axis_index("gran")
@@ -411,34 +415,32 @@
         routes = pltpu.roll(route_ref[:, at], turn, 1)
         starts = [pltpu.roll(window_ref[r, :, at], turn, 1) for r in range(2)]
         rank = jnp.int32(0)
-        place = [jnp.full((8, LANES), -1, jnp.int32) for _ in range(2)]
+        place = jnp.full((8, LANES), -1, jnp.int32)
         for i in visits(granules, True) + visits(granules, False):
             for r in range(2):
                 hit = routes[r, i] == own
                 here = seat == jnp.where(hit, rank, -1)
                 rank = rank + hit.astype(jnp.int32)
-                for k in range(2):
-                    place[k] = jnp.where(here, starts[r][k, i], place[k])
+                place = jnp.where(here, starts[r][axis, i], place)
         to = pl.ds(pl.multiple_of(n * LANES, LANES), LANES)
-        for k, ref in ((0, rows_out), (1, cols_out)):
-            first_knot = jnp.clip(jnp.right_shift(place[k], 5) - 1, 0, KN - SPAN)
-            if k == 0:
-                knot = 2 * jnp.right_shift(first_knot, 1) + 2 * (step % 8) + step // 8
-            else:
-                knot = first_knot + step
-            beyond = jnp.where(knot == 0, -1, jnp.where(knot == KN - 1, KN, 4 * KN))
-            dead = place[k] < 0
-            knot = jnp.where(dead, 4 * KN, knot).astype(f32)
-            beyond = jnp.where(dead, 4 * KN, beyond).astype(f32)
-            start = place[k].astype(f32) * (1.0 / SP)
-            knot, beyond = start - knot, start - beyond
-            pixel = lax.broadcasted_iota(jnp.int32, (8, LANES), 0).astype(f32) * (1.0 / SP)
-            for r in range(0, pixels, 16):
-                values = []
-                for q in (r, r + 8):
-                    at_pixel = pixel + q * (1.0 / SP)
-                    values.append(cubic(jnp.abs(at_pixel + knot)) + cubic(jnp.abs(at_pixel + beyond)))
-                ref[r : r + 16, to] = jnp.concatenate(values, axis=0).astype(bf16)
+        first_knot = jnp.clip(jnp.right_shift(place, 5) - 1, 0, KN - SPAN)
+        if axis == 0:
+            knot = 2 * jnp.right_shift(first_knot, 1) + 2 * (step % 8) + step // 8
+        else:
+            knot = first_knot + step
+        beyond = jnp.where(knot == 0, -1, jnp.where(knot == KN - 1, KN, 4 * KN))
+        dead = place < 0
+        knot = jnp.where(dead, 4 * KN, knot).astype(f32)
+        beyond = jnp.where(dead, 4 * KN, beyond).astype(f32)
+        start = place.astype(f32) * (1.0 / SP)
+        knot, beyond = start - knot, start - beyond
+        pixel = lax.broadcasted_iota(jnp.int32, (8, LANES), 0).astype(f32) * (1.0 / SP)
+        for r in range(0, pixels, 16):
+            values = []
+            for q in (r, r + 8):
+                at_pixel = pixel + q * (1.0 / SP)
+                values.append(cubic(jnp.abs(at_pixel + knot)) + cubic(jnp.abs(at_pixel + beyond)))
+            out_ref[r : r + 16, to] = jnp.concatenate(values, axis=0).astype(bf16)
         return carry
 
     lax.fori_loop(0, senders, sender, 0)
@@ -463,7 +465,14 @@
             passed[k, :, at] = rows[:, LANES * k : LANES * k + LANES].astype(bf16)
         return carry
 
-    lax.fori_loop(0, senders, sender, 0)
+    steps = min(8, senders)
+
+    def several(n, carry):
+        for k in range(steps):
+            sender(n * steps + k, carry)
+        return carry
+
+    lax.fori_loop(0, senders // steps, several, 0)
     copies = []
     for b in range(bands):
         fields = [
@@ -530,7 +539,7 @@
         first_edges,
         [("h", grids)],
         [("v", edge, bf16), ("v", edge, bf16)],
-        [pltpu.VMEM((2,) + edge, f32), pltpu.SemaphoreType.DMA((2,))],
+        [pltpu.VMEM((2,) + edge, f32), pltpu.SemaphoreType.DMA((2, REACH))],
     )
     near, far = exchange(near, far)
     (extended,) = call(
@@ -539,22 +548,37 @@
         [("v", ext, f32)],
         [pltpu.VMEM(own, f32), pltpu.SemaphoreType.DMA((chunks,))],
     )
-    rhs, diagonal, cross, coupling = call(
-        arrange,
-        [("h", rhs), ("h", diagonal), ("h", cross), ("h", coupling)],
-        [
-            ("v", own, f32),
-            ("v", own, f32),
-            ("v", (granules, bands, 32, LANES), f32),
-            ("v", (granules, slots, bands, 32, LANES), bf16),
-        ],
-        [
-            pltpu.VMEM(cross.shape, f32),
-            pltpu.VMEM(coupling.shape, bf16),
-            pltpu.VMEM((bands, 32 * slots, LANES), f32),
-            pltpu.SemaphoreType.DMA((3, chunks)),
-        ],
-    )
+    sources = [rhs, diagonal, cross, coupling]
+
+    def arranged(interior, sources):
+        part = len(visits(granules, interior))
+        some = (part, bands, 64, LANES)
+        return call(
+            functools.partial(arrange, interior),
+            [("h", source) for source in sources],
+            [
+                ("v", some, f32),
+                ("v", some, f32),
+                ("v", (part, bands, 32, LANES), f32),
+                ("v", (part, slots, bands, 32, LANES), bf16),
+            ],
+            [
+                pltpu.VMEM(cross.shape, f32),
+                pltpu.VMEM((part,) + coupling.shape[1:], bf16),
+                pltpu.VMEM((bands, 32 * slots, LANES), f32),
+                pltpu.SemaphoreType.DMA((4, chunks)),
+            ],
+        )
+
+    def interpolation(axis, after):
+        weight_shape = (pixel_count, device_total * LANES)
+        routes, starts, _ = lax.optimization_barrier((tiles[0][1], tiles[1][1], after))
+        return call(
+            functools.partial(interp_weights, axis),
+            [("v", routes), ("v", starts)],
+            [("v", weight_shape, bf16)],
+        )[0]
+
     gathered = pltpu.VMEM((slots, 64, LANES), f32)
     weights = pltpu.VMEM((slots, 64, LANES), f32)
     scalars = pltpu.SMEM((2, granules), jnp.int32)
@@ -570,19 +594,12 @@
         (inner,) = call(
             interior_disparities, graph + [("v", extended)], [packed], [gathered, scalars]
         )
+        if sweep == 0:
+            inner, *edge_state = lax.optimization_barrier((inner, *arranged(False, sources)))
+        if sweep == 1:
+            inner, row_weights = lax.optimization_barrier((inner, interpolation(0, inner)))
         if last:
             inner_shares = over_band(inner)
-        if sweep == 1:
-            weight_shape = (pixel_count, device_total * LANES)
-            routes, starts, _ = lax.optimization_barrier((tiles[0][1], tiles[1][1], inner))
-            row_weights, col_weights = call(
-                interp_weights,
-                [("v", routes), ("v", starts)],
-                [("v", weight_shape, bf16), ("v", weight_shape, bf16)],
-            )
-            inner, row_weights, col_weights = lax.optimization_barrier(
-                (inner, row_weights, col_weights)
-            )
         inputs = graph + [("v", near), ("v", far), ("v", extended)]
         inputs += [] if last else [("v", inner)]
         extended, partial = call(
@@ -593,9 +610,17 @@
             aliases={4: 0},
         )
         shares = over_band(partial)
-        state = [("v", extended), ("v", rhs), ("v", diagonal), ("v", cross), ("v", coupling)]
+        if sweep == 0:
+            *later, _ = lax.optimization_barrier((*sources, partial))
+            partial, *inner_state = lax.optimization_barrier((partial, *arranged(True, later)))
+            shares[0] = ("v", partial)
+        if sweep == 1:
+            partial, col_weights = lax.optimization_barrier((partial, interpolation(1, partial)))
+            shares[0] = ("v", partial)
+        edge_state_now = [("v", extended)] + [("v", array) for array in edge_state]
+        inner_state_now = [("v", extended)] + [("v", array) for array in inner_state]
         if not last:
-            inputs = graph + shares + state
+            inputs = graph + shares + edge_state_now
             updated, near, far = call(
                 edge_sweep,
                 inputs,
@@ -603,6 +628,7 @@
                 [weights, scalars],
             )
             near, far = exchange(near, far)
+            inputs = graph + shares + inner_state_now
             (extended,) = call(
                 interior_sweep,
                 inputs + [("v", updated)],
@@ -618,14 +644,14 @@
         pltpu.VMEM(own, f32),
         pltpu.SemaphoreType.DMA((2,)),
     ]
-    inputs = graph + inner_shares + state + tiles
+    inputs = graph + inner_shares + inner_state_now + tiles
     balanced, gathered_windows = call(
         functools.partial(last_sweep, True),
         inputs,
         [("h", own, f32), ("v", windows, f32)],
         scratch,
     )
-    inputs = graph + shares + state + tiles + [("h", balanced), ("v", gathered_windows)]
+    inputs = graph + shares + edge_state_now + tiles + [("h", balanced), ("v", gathered_windows)]
     balanced, payload, _ = call(
         functools.partial(last_sweep, False),
         inputs,

time: 78 us -> 76.2 us (0.977)
  waiting for transfers between devices: 12.7 us -> 8.06 us
  Pallas kernels: 31.6 us -> 34 us
  blocking collectives: 13 us -> 14.3 us
  starting transfers between devices: 19.5 us -> 18.4 us
    ppermute x3, waiting for transfers between devices: 10.5 us -> 8.02 us  [exchange(): near = lax.ppermute(near, 'gran', near_pairs)]
    pallas_call x17 -> x19, Pallas kernels: 31.6 us -> 34 us  [call(): pl.pallas_call(body, in_specs=[ON_CHIP if kind == 'v' else ANYWHERE for k...]
    ppermute x12, waiting for transfers between devices: 2.16 us -> 0.03 us  [over_band(): lax.ppermute(partial, 'band', [(i, i ^ flip) for i in range(band_total)])]
    all_to_all x1, blocking collectives: 13 us -> 14.3 us  [per_device(): lax.all_to_all(payload, 'gran', split_axis=0, concat_axis=0, tiled=True)]
    ppermute x3, starting transfers between devices: 9.8 us -> 8.78 us  [exchange(): near = lax.ppermute(near, 'gran', near_pairs)]
  transfers between devices with their start and end apart: 18 -> 18, of which waited for: 5 -> 3; matrix products, arithmetic and copies ran while one was open for 0% -> 0% of each run, Pallas kernels for 26% -> 32%
where the time goes in v3:
time: 76.2 us; the launch traced here: 75.8 us
  Pallas kernels  34 us (45%)
  starting transfers between devices  18.4 us (24%)
  blocking collectives  14.3 us (19%)
  waiting for transfers between devices  8.06 us (11%)
  between operations  0.96 us (1%)
    pallas_call x19, Pallas kernels, call(): pl.pallas_call(body, in_specs=[ON_CHIP if kind == 'v' else ANYWHERE for k...  34 us
    all_to_all x1, blocking collectives, per_device(): lax.all_to_all(payload, 'gran', split_axis=0, concat_axis=0, tiled=True)  14.3 us
    ppermute x3, starting transfers between devices, exchange(): near = lax.ppermute(near, 'gran', near_pairs)  8.78 us
    ppermute x3, waiting for transfers between devices, exchange(): near = lax.ppermute(near, 'gran', near_pairs)  8.02 us
    ppermute x12, starting transfers between devices, over_band(): lax.ppermute(partial, 'band', [(i, i ^ flip) for i in range(band_total)])  7.68 us
    ppermute x3, starting transfers between devices, exchange(): far = lax.ppermute(far, 'gran', far_pairs)  1.98 us
  transfers between devices with their start and end apart: 18, of which 3 were waited for; matrix products, arithmetic and copies ran while one was open for 0% of the time, Pallas kernels for 32%

profile of v3, /device:TPU:0, one launch (start us, length us, event | category | flops | bytes accessed | tf_op | source)
XLA Modules:
  0.0 75.8 jit_solution(16468065629149321307)
XLA Ops:
  0.6 1.3 %shard_map.113 = (bf16[4,3,64,128]{3,2,1,0:T(8,128)(2,1)S(1)}, bf16[4,3,64,128]{3,2,1,0:T(8,128)(2,1)S(1)}) custom-call(f32[16,3,64,128]{3,2,1,0:T(8,128)} %bitcast.77), custom_call_target="tpu_custom_call" | custom-call | tf_op jit(solution)/shard_map/pallas_call | solution.py:31
  1.9 0.0 copy-start
  2.0 0.0 copy-start.2
  2.0 3.0 %collective-permute-start = (bf16[4,3,64,128]{3,2,1,0:T(8,128)(2,1)S(1)}, bf16[4,3,64,128]{3,2,1,0:T(8,128)(2,1)S(1)}, u32[]{:S(2)}, u32[]{:S(2)}) collective-permute-start(bf16[4,3,64,128]{3,2,1,0:T(8,128)(2,1)S(1)} %get-tuple-element.50), channel_id=1, source_target_pairs={{0,4},{4,0},{8,12},{12,8},{16,20},{20,16},{24,28},{28,24},{1,5},{5... | collective-permute-start | bytes 589832 | tf_op jit(solution)/shard_map/ppermute | solution.py:535
  5.0 0.7 collective-permute-start.1
  5.6 1.5 %shard_map.114.ext_ref.refs_0_ = f32[24,3,64,128]{3,2,1,0:T(8,128)S(1)} custom-call(f32[16,3,64,128]{3,2,1,0:T(8,128)} %bitcast.78), custom_call_target="tpu_custom_call" | custom-call | tf_op jit(solution)/shard_map/pallas_call | solution.py:31
  7.1 0.8 %shard_map.115.refs_1_ = f32[64,128]{1,0:T(8,128)S(1)} custom-call(s32[8,16]{1,0:T(8,128)S(1)} %bitcast.38, s32[1,16]{1,0:T(1,128)S(1)} %bitcast.50, f32[24,3,64,128]{3,2,1,0:T(8,128)S(1)} %shard_map.114.ext_ref.refs_0_), custom_call_target="tpu_custom_call" | custom-call | tf_op jit(solution)/shard_map/pallas_call | solution.py:31
  7.9 3.9 %shard_map.116 = (f32[8,3,64,128]{3,2,1,0:T(8,128)S(1)}, f32[8,3,64,128]{3,2,1,0:T(8,128)S(1)}, f32[8,3,32,128]{3,2,1,0:T(8,128)S(1)}, bf16[8,8,3,32,128]{4,3,2,1,0:T(8,128)(2,1)S(1)}) custom-call(f32[16,3,64,128]{3,2,1,0:T(8,128)} %bitcast.73, f32[16,3,64,128]{3,2,1,0:T(8,128)} %bitcast.75, f32[3,2,256,128]{3,2,1,0:T(8,128)} %bitcast.79, ...), custom_call_target="tpu_custom_call" | custom-call | tf_op jit(solution)/shard_map/pallas_call | solution.py:31
  11.8 1.5 %collective-permute-done.near_ref = bf16[4,3,64,128]{3,2,1,0:T(8,128)(2,1)S(1)} collective-permute-done((bf16[4,3,64,128]{3,2,1,0:T(8,128)(2,1)S(1)}, bf16[4,3,64,128]{3,2,1,0:T(8,128)(2,1)S(1)}, u32[]{:S(2)}, u32[]{:S(2)}) %collective-permute-start) | collective-permute-done | bytes 196640 | tf_op jit(solution)/shard_map/ppermute | solution.py:535
  13.4 0.6 shard_map.117
  14.0 0.1 collective-permute-start.4
  14.1 1.6 %collective-permute-start.3 = (f32[64,128]{1,0:T(8,128)S(1)}, f32[64,128]{1,0:T(8,128)S(1)}, u32[]{:S(2)}, u32[]{:S(2)}) collective-permute-start(f32[64,128]{1,0:T(8,128)S(1)} %get-tuple-element.66.refs_0_), channel_id=1, source_target_pairs={{0,2},{1,3},{2,0},{3,1},{4,6},{5,7},{6,4},{7,5},{8,10},{9,11},{10,... | collective-permute-start | bytes 98312 | tf_op jit(solution)/shard_map/ppermute | solution.py:588
  15.7 0.3 collective-permute-start.2
  15.9 3.9 %shard_map.118 = (f32[8,3,64,128]{3,2,1,0:T(8,128)S(1)}, f32[8,3,64,128]{3,2,1,0:T(8,128)S(1)}, f32[8,3,32,128]{3,2,1,0:T(8,128)S(1)}, bf16[8,8,3,32,128]{4,3,2,1,0:T(8,128)(2,1)S(1)}) custom-call(f32[16,3,64,128]{3,2,1,0:T(8,128)} %bitcast.74, f32[16,3,64,128]{3,2,1,0:T(8,128)} %bitcast.76, f32[3,2,256,128]{3,2,1,0:T(8,128)} %bitcast.80, ...), custom_call_target="tpu_custom_call" | custom-call | tf_op jit(solution)/shard_map/pallas_call | solution.py:31
  19.8 0.0 collective-permute-done.4.refs_3_
  19.9 0.0 collective-permute-done.3.refs_2_
  19.9 1.0 %shard_map.119 = (f32[24,3,64,128]{3,2,1,0:T(8,128)S(1)}, bf16[4,3,64,128]{3,2,1,0:T(8,128)(2,1)S(1)}, bf16[4,3,64,128]{3,2,1,0:T(8,128)(2,1)S(1)}) custom-call(s32[8,16]{1,0:T(8,128)S(1)} %bitcast.40, s32[1,16]{1,0:T(1,128)S(1)} %bitcast.52, f32[64,128]{1,0:T(8,128)S(1)} %get-tuple-element.66.refs_0_, f32[64,128]{1,0:T(8,128)S(1)} %collective-permute-done.2.refs_1_, ...), custom_call_target="tpu_custom_call" | custom-call | tf_op jit(solution)/shard_map/pallas_call | solution.py:31
  20.9 3.0 %collective-permute-start.5 = (bf16[4,3,64,128]{3,2,1,0:T(8,128)(2,1)S(1)}, bf16[4,3,64,128]{3,2,1,0:T(8,128)(2,1)S(1)}, u32[]{:S(2)}, u32[]{:S(2)}) collective-permute-start(bf16[4,3,64,128]{3,2,1,0:T(8,128)(2,1)S(1)} %get-tuple-element.72), channel_id=1, source_target_pairs={{0,4},{4,0},{8,12},{12,8},{16,20},{20,16},{24,28},{28,24},{1,5},{5... | collective-permute-start | bytes 589832 | tf_op jit(solution)/shard_map/ppermute | solution.py:535
  24.0 0.7 collective-permute-start.6
  24.6 1.2 %shard_map.120.ext_ref.refs_0_ = f32[24,3,64,128]{3,2,1,0:T(8,128)S(1)} custom-call(s32[8,16]{1,0:T(8,128)S(1)} %bitcast.41, s32[1,16]{1,0:T(1,128)S(1)} %bitcast.53, f32[64,128]{1,0:T(8,128)S(1)} %get-tuple-element.66.refs_0_, f32[64,128]{1,0:T(8,128)S(1)} %collective-permute-done.2.refs_1_, ...), custom_call_target="tpu_custom_call", output_to_operand_aliasing={{}: (11, {})} | custom-call | tf_op jit(solution)/shard_map/pallas_call | solution.py:31
  25.8 0.0 copy-start.3
  25.8 0.0 copy-start.4
  25.8 0.8 %shard_map.121.refs_1_ = f32[64,128]{1,0:T(8,128)S(1)} custom-call(s32[8,16]{1,0:T(8,128)S(1)} %bitcast.42, s32[1,16]{1,0:T(1,128)S(1)} %bitcast.54, f32[24,3,64,128]{3,2,1,0:T(8,128)S(1)} %shard_map.120.ext_ref.refs_0_), custom_call_target="tpu_custom_call" | custom-call | tf_op jit(solution)/shard_map/pallas_call | solution.py:31
  26.6 3.7 %shard_map.122.row_ref = bf16[256,1024]{1,0:T(8,128)(2,1)S(1)} custom-call(s32[2,128]{1,0:T(2,128)S(1)} %bitcast.66, s32[2,2,128]{2,1,0:T(2,128)S(1)} %bitcast.62), custom_call_target="tpu_custom_call" | custom-call | tf_op jit(solution)/shard_map/pallas_call | solution.py:31
  30.3 2.5 %collective-permute-done.5.near_ref = bf16[4,3,64,128]{3,2,1,0:T(8,128)(2,1)S(1)} collective-permute-done((bf16[4,3,64,128]{3,2,1,0:T(8,128)(2,1)S(1)}, bf16[4,3,64,128]{3,2,1,0:T(8,128)(2,1)S(1)}, u32[]{:S(2)}, u32[]{:S(2)}) %collective-permute-start.5) | collective-permute-done | bytes 196640 | tf_op jit(solution)/shard_map/ppermute | solution.py:535
  32.7 0.6 shard_map.123
  33.4 0.1 collective-permute-start.9
  33.5 1.3 %collective-permute-start.8 = (f32[64,128]{1,0:T(8,128)S(1)}, f32[64,128]{1,0:T(8,128)S(1)}, u32[]{:S(2)}, u32[]{:S(2)}) collective-permute-start(f32[64,128]{1,0:T(8,128)S(1)} %get-tuple-element.85.refs_0_), channel_id=1, source_target_pairs={{0,2},{1,3},{2,0},{3,1},{4,6},{5,7},{6,4},{7,5},{8,10},{9,11},{10,... | collective-permute-start | bytes 98312 | tf_op jit(solution)/shard_map/ppermute | solution.py:588
  34.8 0.5 collective-permute-start.7
  35.3 3.6 %shard_map.124.col_ref = bf16[256,1024]{1,0:T(8,128)(2,1)S(1)} custom-call(s32[2,128]{1,0:T(2,128)S(1)} %bitcast.67, s32[2,2,128]{2,1,0:T(2,128)S(1)} %bitcast.63), custom_call_target="tpu_custom_call" | custom-call | tf_op jit(solution)/shard_map/pallas_call | solution.py:31
  39.0 1.0 %shard_map.125 = (f32[24,3,64,128]{3,2,1,0:T(8,128)S(1)}, bf16[4,3,64,128]{3,2,1,0:T(8,128)(2,1)S(1)}, bf16[4,3,64,128]{3,2,1,0:T(8,128)(2,1)S(1)}) custom-call(s32[8,16]{1,0:T(8,128)S(1)} %bitcast.44, s32[1,16]{1,0:T(1,128)S(1)} %bitcast.56, f32[64,128]{1,0:T(8,128)S(1)} %get-tuple-element.85.refs_0_, f32[64,128]{1,0:T(8,128)S(1)} %collective-permute-done.7.refs_1_, ...), custom_call_target="tpu_custom_call" | custom-call | tf_op jit(solution)/shard_map/pallas_call | solution.py:31
  40.0 2.8 %collective-permute-start.10 = (bf16[4,3,64,128]{3,2,1,0:T(8,128)(2,1)S(1)}, bf16[4,3,64,128]{3,2,1,0:T(8,128)(2,1)S(1)}, u32[]{:S(2)}, u32[]{:S(2)}) collective-permute-start(bf16[4,3,64,128]{3,2,1,0:T(8,128)(2,1)S(1)} %get-tuple-element.87), channel_id=1, source_target_pairs={{0,4},{4,0},{8,12},{12,8},{16,20},{20,16},{24,28},{28,24},{1,5},{5... | collective-permute-start | bytes 589832 | tf_op jit(solution)/shard_map/ppermute | solution.py:535
  42.8 0.7 collective-permute-start.11
  43.5 1.2 %shard_map.126.refs_0_.ext_ref = f32[24,3,64,128]{3,2,1,0:T(8,128)S(1)} custom-call(s32[8,16]{1,0:T(8,128)S(1)} %bitcast.45, s32[1,16]{1,0:T(1,128)S(1)} %bitcast.57, f32[64,128]{1,0:T(8,128)S(1)} %get-tuple-element.85.refs_0_, f32[64,128]{1,0:T(8,128)S(1)} %collective-permute-done.7.refs_1_, ...), custom_call_target="tpu_custom_call", output_to_operand_aliasing={{}: (11, {})} | custom-call | tf_op jit(solution)/shard_map/pallas_call | solution.py:31
  44.6 0.8 %shard_map.128.refs_0_ = f32[64,128]{1,0:T(8,128)S(1)} custom-call(s32[8,16]{1,0:T(8,128)S(1)} %bitcast.46, s32[1,16]{1,0:T(1,128)S(1)} %bitcast.58, f32[24,3,64,128]{3,2,1,0:T(8,128)S(1)} %shard_map.126.refs_0_.ext_ref), custom_call_target="tpu_custom_call" | custom-call | tf_op jit(solution)/shard_map/pallas_call | solution.py:31
  45.4 0.7 collective-permute-start.17
  46.1 0.8 collective-permute-start.16
  46.8 0.5 collective-permute-start.15
  47.3 4.0 %collective-permute-done.10.near_ref = bf16[4,3,64,128]{3,2,1,0:T(8,128)(2,1)S(1)} collective-permute-done((bf16[4,3,64,128]{3,2,1,0:T(8,128)(2,1)S(1)}, bf16[4,3,64,128]{3,2,1,0:T(8,128)(2,1)S(1)}, u32[]{:S(2)}, u32[]{:S(2)}) %collective-permute-start.10) | collective-permute-done | bytes 196640 | tf_op jit(solution)/shard_map/ppermute | solution.py:535
  51.3 0.6 shard_map.127
  52.0 0.1 collective-permute-start.14
  52.1 1.3 %collective-permute-start.13 = (f32[64,128]{1,0:T(8,128)S(1)}, f32[64,128]{1,0:T(8,128)S(1)}, u32[]{:S(2)}, u32[]{:S(2)}) collective-permute-start(f32[64,128]{1,0:T(8,128)S(1)} %get-tuple-element.90.refs_0_), channel_id=1, source_target_pairs={{0,2},{1,3},{2,0},{3,1},{4,6},{5,7},{6,4},{7,5},{8,10},{9,11},{10,... | collective-permute-start | bytes 98312 | tf_op jit(solution)/shard_map/ppermute | solution.py:588
  53.4 0.5 collective-permute-start.12
  53.9 2.5 %shard_map.129 = (f32[16,3,64,128]{3,2,1,0:T(8,128)}, f32[8,96,128]{2,1,0:T(8,128)S(1)}) custom-call(s32[8,16]{1,0:T(8,128)S(1)} %bitcast.48, s32[1,16]{1,0:T(1,128)S(1)} %bitcast.60, f32[64,128]{1,0:T(8,128)S(1)} %shard_map.128.refs_0_, f32[64,128]{1,0:T(8,128)S(1)} %collective-permute-done.15.refs_1_, f32[64,128]{1,0:T(8,128)S(1)} %collective-permute-done.16.refs_2_, ...), custom_call_target="tpu_custom_call" | custom-call | tf_op jit(solution)/shard_map/pallas_call | solution.py:31
  56.4 0.0 copy-start.1
  56.5 2.4 %shard_map.130 = (f32[16,3,64,128]{3,2,1,0:T(8,128)}, bf16[8,96,128]{2,1,0:T(8,128)(2,1)S(1)}, f32[8,96,128]{2,1,0:T(8,128)S(1)}) custom-call(s32[8,16]{1,0:T(8,128)S(1)} %bitcast.49, s32[1,16]{1,0:T(1,128)S(1)} %bitcast.61, f32[64,128]{1,0:T(8,128)S(1)} %get-tuple-element.90.refs_0_, ...), custom_call_target="tpu_custom_call", output_to_operand_aliasing={{0}: (13, {}), {2}: (14, {})} | custom-call | tf_op jit(solution)/shard_map/pallas_call | solution.py:31
  58.8 14.3 %all_to_all.5.received_ref = bf16[8,96,128]{2,1,0:T(8,128)(2,1)S(1)} all-to-all(bf16[8,96,128]{2,1,0:T(8,128)(2,1)S(1)} %get-tuple-element.95), channel_id=1, replica_groups=mesh['gran'=8,'band'=4] {'gran'}, dimensions={0} | all-to-all | bytes 393216 | tf_op jit(solution)/shard_map/all_to_all | solution.py:662
  73.1 2.6 %shard_map.131 = bf16[1,3,256,256]{3,2,1,0:T(8,128)(2,1)} custom-call(s32[2,128]{1,0:T(2,128)S(1)} %bitcast.70, bf16[8,96,128]{2,1,0:T(8,128)(2,1)S(1)} %all_to_all.5.received_ref, bf16[256,1024]{1,0:T(8,128)(2,1)S(1)} %shard_map.122.row_ref, bf16[256,1024]{1,0:T(8,128)(2,1)S(1)} %shard_map.124.col_ref, bf16[1,3,256,256]{3,2,1,0:T(8,128)(2,1)S(1)} %copy-done.1), custom_call_target="tpu_custom_call" | custom-call | tf_op jit(solution)/shard_map/pallas_call | solution.py:31
  (18 shorter events, 0.0 us)
Async XLA Ops:
  1.9 5.2 %copy-start = (s32[16,8]{0,1:T(8,128)S(1)}, s32[16,8]{0,1:T(8,128)}, u32[]{:S(2)}) copy-start(s32[16,8]{0,1:T(8,128)} %param.15) | copy-start | bytes 1540
  2.0 5.2 %copy-start.2 = (s32[16]{0:T(128)S(1)}, s32[16]{0:T(128)}, u32[]{:S(2)}) copy-start(s32[16]{0:T(128)} %param.16) | copy-start | bytes 196
  2.0 11.4 %collective-permute-start = (bf16[4,3,64,128]{3,2,1,0:T(8,128)(2,1)S(1)}, bf16[4,3,64,128]{3,2,1,0:T(8,128)(2,1)S(1)}, u32[]{:S(2)}, u32[]{:S(2)}) collective-permute-start(bf16[4,3,64,128]{3,2,1,0:T(8,128)(2,1)S(1)} %get-tuple-element.50), channel_id=1, source_target_pairs={{0,4},{4,0},{8,12},{12,8},{16,20},{20,16},{24,28},{28,24},{1,5},{5... | collective-permute-start | bytes 589832 | tf_op jit(solution)/shard_map/ppermute | solution.py:535
  5.0 8.4 %collective-permute-start.1 = (bf16[4,3,64,128]{3,2,1,0:T(8,128)(2,1)S(1)}, bf16[4,3,64,128]{3,2,1,0:T(8,128)(2,1)S(1)}, u32[]{:S(2)}, u32[]{:S(2)}) collective-permute-start(bf16[4,3,64,128]{3,2,1,0:T(8,128)(2,1)S(1)} %get-tuple-element.51), channel_id=1, source_target_pairs={{4,8},{8,4},{12,16},{16,12},{20,24},{24,20},{5,9},{9,5},{13,17},{1... | collective-permute-start | bytes 589832 | tf_op jit(solution)/shard_map/ppermute | solution.py:534
  14.0 5.8 %collective-permute-start.4 = (f32[64,128]{1,0:T(8,128)S(1)}, f32[64,128]{1,0:T(8,128)S(1)}, u32[]{:S(2)}, u32[]{:S(2)}) collective-permute-start(f32[64,128]{1,0:T(8,128)S(1)} %get-tuple-element.66.refs_0_), channel_id=1, source_target_pairs={{0,3},{1,2},{2,1},{3,0},{4,7},{5,6},{6,5},{7,4},{8,11},{9,10},{10,... | collective-permute-start | bytes 98312 | tf_op jit(solution)/shard_map/ppermute | solution.py:588
  14.1 5.8 %collective-permute-start.3 = (f32[64,128]{1,0:T(8,128)S(1)}, f32[64,128]{1,0:T(8,128)S(1)}, u32[]{:S(2)}, u32[]{:S(2)}) collective-permute-start(f32[64,128]{1,0:T(8,128)S(1)} %get-tuple-element.66.refs_0_), channel_id=1, source_target_pairs={{0,2},{1,3},{2,0},{3,1},{4,6},{5,7},{6,4},{7,5},{8,10},{9,11},{10,... | collective-permute-start | bytes 98312 | tf_op jit(solution)/shard_map/ppermute | solution.py:588
  15.7 4.2 %collective-permute-start.2 = (f32[64,128]{1,0:T(8,128)S(1)}, f32[64,128]{1,0:T(8,128)S(1)}, u32[]{:S(2)}, u32[]{:S(2)}) collective-permute-start(f32[64,128]{1,0:T(8,128)S(1)} %get-tuple-element.66.refs_0_), channel_id=1, source_target_pairs={{0,1},{1,0},{2,3},{3,2},{4,5},{5,4},{6,7},{7,6},{8,9},{9,8},{10,11... | collective-permute-start | bytes 98312 | tf_op jit(solution)/shard_map/ppermute | solution.py:588
  20.9 11.8 %collective-permute-start.5 = (bf16[4,3,64,128]{3,2,1,0:T(8,128)(2,1)S(1)}, bf16[4,3,64,128]{3,2,1,0:T(8,128)(2,1)S(1)}, u32[]{:S(2)}, u32[]{:S(2)}) collective-permute-start(bf16[4,3,64,128]{3,2,1,0:T(8,128)(2,1)S(1)} %get-tuple-element.72), channel_id=1, source_target_pairs={{0,4},{4,0},{8,12},{12,8},{16,20},{20,16},{24,28},{28,24},{1,5},{5... | collective-permute-start | bytes 589832 | tf_op jit(solution)/shard_map/ppermute | solution.py:535
  24.0 8.8 %collective-permute-start.6 = (bf16[4,3,64,128]{3,2,1,0:T(8,128)(2,1)S(1)}, bf16[4,3,64,128]{3,2,1,0:T(8,128)(2,1)S(1)}, u32[]{:S(2)}, u32[]{:S(2)}) collective-permute-start(bf16[4,3,64,128]{3,2,1,0:T(8,128)(2,1)S(1)} %get-tuple-element.73), channel_id=1, source_target_pairs={{4,8},{8,4},{12,16},{16,12},{20,24},{24,20},{5,9},{9,5},{13,17},{1... | collective-permute-start | bytes 589832 | tf_op jit(solution)/shard_map/ppermute | solution.py:534
  25.8 0.8 %copy-start.3 = (s32[128,2,2]{0,2,1:T(2,128)S(1)}, s32[128,2,2]{0,2,1:T(2,128)}, u32[]{:S(2)}) copy-start(s32[128,2,2]{0,2,1:T(2,128)} %param.18) | copy-start | bytes 6148
  25.8 0.8 %copy-start.4 = (s32[128,2]{0,1:T(2,128)S(1)}, s32[128,2]{0,1:T(2,128)}, u32[]{:S(2)}) copy-start(s32[128,2]{0,1:T(2,128)} %param.17) | copy-start | bytes 3076
  33.4 5.6 %collective-permute-start.9 = (f32[64,128]{1,0:T(8,128)S(1)}, f32[64,128]{1,0:T(8,128)S(1)}, u32[]{:S(2)}, u32[]{:S(2)}) collective-permute-start(f32[64,128]{1,0:T(8,128)S(1)} %get-tuple-element.85.refs_0_), channel_id=1, source_target_pairs={{0,3},{1,2},{2,1},{3,0},{4,7},{5,6},{6,5},{7,4},{8,11},{9,10},{10,... | collective-permute-start | bytes 98312 | tf_op jit(solution)/shard_map/ppermute | solution.py:588
  33.5 5.5 %collective-permute-start.8 = (f32[64,128]{1,0:T(8,128)S(1)}, f32[64,128]{1,0:T(8,128)S(1)}, u32[]{:S(2)}, u32[]{:S(2)}) collective-permute-start(f32[64,128]{1,0:T(8,128)S(1)} %get-tuple-element.85.refs_0_), channel_id=1, source_target_pairs={{0,2},{1,3},{2,0},{3,1},{4,6},{5,7},{6,4},{7,5},{8,10},{9,11},{10,... | collective-permute-start | bytes 98312 | tf_op jit(solution)/shard_map/ppermute | solution.py:588
  34.8 4.2 %collective-permute-start.7 = (f32[64,128]{1,0:T(8,128)S(1)}, f32[64,128]{1,0:T(8,128)S(1)}, u32[]{:S(2)}, u32[]{:S(2)}) collective-permute-start(f32[64,128]{1,0:T(8,128)S(1)} %get-tuple-element.85.refs_0_), channel_id=1, source_target_pairs={{0,1},{1,0},{2,3},{3,2},{4,5},{5,4},{6,7},{7,6},{8,9},{9,8},{10,11... | collective-permute-start | bytes 98312 | tf_op jit(solution)/shard_map/ppermute | solution.py:588
  40.0 11.3 %collective-permute-start.10 = (bf16[4,3,64,128]{3,2,1,0:T(8,128)(2,1)S(1)}, bf16[4,3,64,128]{3,2,1,0:T(8,128)(2,1)S(1)}, u32[]{:S(2)}, u32[]{:S(2)}) collective-permute-start(bf16[4,3,64,128]{3,2,1,0:T(8,128)(2,1)S(1)} %get-tuple-element.87), channel_id=1, source_target_pairs={{0,4},{4,0},{8,12},{12,8},{16,20},{20,16},{24,28},{28,24},{1,5},{5... | collective-permute-start | bytes 589832 | tf_op jit(solution)/shard_map/ppermute | solution.py:535
  42.8 8.5 %collective-permute-start.11 = (bf16[4,3,64,128]{3,2,1,0:T(8,128)(2,1)S(1)}, bf16[4,3,64,128]{3,2,1,0:T(8,128)(2,1)S(1)}, u32[]{:S(2)}, u32[]{:S(2)}) collective-permute-start(bf16[4,3,64,128]{3,2,1,0:T(8,128)(2,1)S(1)} %get-tuple-element.88), channel_id=1, source_target_pairs={{4,8},{8,4},{12,16},{16,12},{20,24},{24,20},{5,9},{9,5},{13,17},{1... | collective-permute-start | bytes 589832 | tf_op jit(solution)/shard_map/ppermute | solution.py:534
  45.4 8.0 %collective-permute-start.17 = (f32[64,128]{1,0:T(8,128)S(1)}, f32[64,128]{1,0:T(8,128)S(1)}, u32[]{:S(2)}, u32[]{:S(2)}) collective-permute-start(f32[64,128]{1,0:T(8,128)S(1)} %shard_map.128.refs_0_), channel_id=1, source_target_pairs={{0,3},{1,2},{2,1},{3,0},{4,7},{5,6},{6,5},{7,4},{8,11},{9,10},{10,... | collective-permute-start | bytes 98312 | tf_op jit(solution)/shard_map/ppermute | solution.py:588
  46.1 7.9 %collective-permute-start.16 = (f32[64,128]{1,0:T(8,128)S(1)}, f32[64,128]{1,0:T(8,128)S(1)}, u32[]{:S(2)}, u32[]{:S(2)}) collective-permute-start(f32[64,128]{1,0:T(8,128)S(1)} %shard_map.128.refs_0_), channel_id=1, source_target_pairs={{0,2},{1,3},{2,0},{3,1},{4,6},{5,7},{6,4},{7,5},{8,10},{9,11},{10,... | collective-permute-start | bytes 98312 | tf_op jit(solution)/shard_map/ppermute | solution.py:588
  46.8 7.1 %collective-permute-start.15 = (f32[64,128]{1,0:T(8,128)S(1)}, f32[64,128]{1,0:T(8,128)S(1)}, u32[]{:S(2)}, u32[]{:S(2)}) collective-permute-start(f32[64,128]{1,0:T(8,128)S(1)} %shard_map.128.refs_0_), channel_id=1, source_target_pairs={{0,1},{1,0},{2,3},{3,2},{4,5},{5,4},{6,7},{7,6},{8,9},{9,8},{10,11... | collective-permute-start | bytes 98312 | tf_op jit(solution)/shard_map/ppermute | solution.py:588
  52.0 4.4 %collective-permute-start.14 = (f32[64,128]{1,0:T(8,128)S(1)}, f32[64,128]{1,0:T(8,128)S(1)}, u32[]{:S(2)}, u32[]{:S(2)}) collective-permute-start(f32[64,128]{1,0:T(8,128)S(1)} %get-tuple-element.90.refs_0_), channel_id=1, source_target_pairs={{0,3},{1,2},{2,1},{3,0},{4,7},{5,6},{6,5},{7,4},{8,11},{9,10},{10,... | collective-permute-start | bytes 98312 | tf_op jit(solution)/shard_map/ppermute | solution.py:588
  52.1 4.4 %collective-permute-start.13 = (f32[64,128]{1,0:T(8,128)S(1)}, f32[64,128]{1,0:T(8,128)S(1)}, u32[]{:S(2)}, u32[]{:S(2)}) collective-permute-start(f32[64,128]{1,0:T(8,128)S(1)} %get-tuple-element.90.refs_0_), channel_id=1, source_target_pairs={{0,2},{1,3},{2,0},{3,1},{4,6},{5,7},{6,4},{7,5},{8,10},{9,11},{10,... | collective-permute-start | bytes 98312 | tf_op jit(solution)/shard_map/ppermute | solution.py:588
  53.4 3.0 %collective-permute-start.12 = (f32[64,128]{1,0:T(8,128)S(1)}, f32[64,128]{1,0:T(8,128)S(1)}, u32[]{:S(2)}, u32[]{:S(2)}) collective-permute-start(f32[64,128]{1,0:T(8,128)S(1)} %get-tuple-element.90.refs_0_), channel_id=1, source_target_pairs={{0,1},{1,0},{2,3},{3,2},{4,5},{5,4},{6,7},{7,6},{8,9},{9,8},{10,11... | collective-permute-start | bytes 98312 | tf_op jit(solution)/shard_map/ppermute | solution.py:588
  56.4 16.7 %copy-start.1 = (bf16[1,3,256,256]{3,2,1,0:T(8,128)(2,1)S(1)}, bf16[1,3,256,256]{3,2,1,0:T(8,128)(2,1)}, u32[]{:S(2)}) copy-start(bf16[1,3,256,256]{3,2,1,0:T(8,128)(2,1)} %pixels_ref.1) | copy-start | bytes 1179652

commit v4 on v3

--- a/solution.py
+++ b/solution.py
@@ -91,9 +91,8 @@
     return inner if interior else [i for i in range(granules) if i not in inner]
 
 
-def arrange(interior, rhs_ref, diag_ref, cross_ref, coupling_ref, rhs_out, diag_out, cross_out, coupling_out, cross_raw, coupling_raw, wide, sems):
+def arrange(interior, rhs_ref, diag_ref, cross_ref, coupling_ref, rhs_out, diag_out, cross_out, coupling_out, cross_raw, coupling_raw, sems):
     granules, bands = rhs_ref.shape[:2]
-    slots = coupling_out.shape[1]
     own = visits(granules, interior)
     size = REACH
     chunks = len(own) // size
@@ -124,17 +123,11 @@
             at = n * size + g
             i = own[n * size] + g
             for b in range(bands):
-                wide[b] = coupling_raw[at, b].astype(f32)
-            for b in range(bands):
+                coupling_out[at, b] = coupling_raw[at, b].astype(f32)
                 for j in range(4):
                     d = [diag_out[at, b, pl.ds(2 * j + c, 8, stride=8), :] for c in range(2)]
                     pick = cross_raw[b, i // 8, pl.ds(8 * j + i % 8, 8, stride=32), :]
                     cross_out[at, b, 8 * j : 8 * j + 8, :] = pick * jnp.sqrt(d[0] * d[1])
-            for b in range(bands):
-                for s in range(slots):
-                    for j in (0, 2):
-                        pair = [wide[b, pl.ds(8 * (j + k) + s, 8, stride=32), :] for k in (0, 1)]
-                        coupling_out[at, s, b, 8 * j : 8 * j + 16, :] = jnp.concatenate(pair, axis=0).astype(bf16)
             return carry
 
         lax.fori_loop(0, size, step, 0)
@@ -256,10 +249,9 @@
         n = neighbour(graph, i, s)
         new_sigma, new_drive = [], []
         for b in range(bands):
-            coupling = coupling_ref[at, s, b].astype(f32)
             for j in range(4):
                 k = 4 * b + j
-                effective = weight * coupling[8 * j : 8 * j + 8]
+                effective = weight * coupling_ref[at, b, pl.ds(8 * j + s, 8, stride=32), :]
                 new_sigma.append(sigma[k] + effective)
                 for c in range(2):
                     grid = ext_ref[n, b, 16 * j + 8 * c : 16 * j + 8 * c + 8, :]
@@ -327,19 +319,16 @@
 
 
 def last_sweep(interior, offset_ref, count_ref, *refs):
-    shares, state, (route_ref, window_ref) = refs[:4], refs[4:9], refs[9:11]
-    weights, graph, ranks, solved, sems = refs[-5:]
+    shares, state, place_ref = refs[:4], refs[4:9], refs[9]
+    weights, graph, solved, sems = refs[-4:]
     if interior:
-        out_ref, windows = refs[11:13]
+        out_ref, windows = refs[10:12]
     else:
-        out_ref, send_ref, windows = refs[13:16]
+        out_ref, send_ref, windows = refs[12:15]
     granules, bands = solved.shape[:2]
-    inner = visits(granules, True)
     read_graph(offset_ref, count_ref, graph)
     if interior:
         windows[...] = jnp.zeros_like(windows)
-    for owner in range(windows.shape[0]):
-        ranks[owner] = 0
     spread_weights(shares, interior, weights)
 
     def step(t, carry):
@@ -360,25 +349,10 @@
         copies.append(pltpu.make_async_copy(solved.at[part], out_ref.at[part], sems.at[n]))
         copies[n].start()
     lane = lax.broadcasted_iota(jnp.int32, (8, LANES), 1) // SPAN
-    routes = own_columns(route_ref, (slice(None),), granules)
-    if not interior:
-        for i in inner:
-            for r in range(2):
-                owner = routes[r, i]
-                ranks[owner] = ranks[owner] + 1
-    tops, lefts = [], []
-    for r in range(2):
-        starts = own_columns(window_ref, (r, slice(None)), granules)
-        knots = jnp.clip(jnp.right_shift(starts, 5) - 1, 0, KN - SPAN)
-        tops.append(jnp.right_shift(knots, 1))
-        lefts.append(knots)
+    places = place_ref[...]
     for i in visits(granules, interior):
         for r in range(2):
-            owner = routes[r, i]
-            rank = ranks[owner]
-            ranks[owner] = rank + 1
-            top = tops[r][0, i]
-            turn = rank * SPAN - lefts[r][1, i] + LANES
+            owner, rank, top, turn = (places[k, r * granules + i] for k in range(4))
             here = lane == rank
             for b in range(bands):
                 for c in range(2):
@@ -393,57 +367,107 @@
         copy.wait()
 
 
-def cubic(distance):
-    near = (1.5 * distance - 2.5) * distance * distance + 1.0
-    far = ((2.5 - 0.5 * distance) * distance - 4.0) * distance + 2.0
-    return jnp.where(distance <= 1.0, near, jnp.where(distance < 2.0, far, 0.0))
-
-
-def interp_weights(axis, route_ref, window_ref, out_ref):
-    pixels, lanes = out_ref.shape
+def earlier(first, second, granules):
+    def edge(i):
+        return ((i < REACH) | (i >= granules - REACH)).astype(jnp.int32)
+
+    def rank(entry):
+        return (edge(entry[1]) * 2 + entry[0]) * granules + entry[1]
+
+    return rank(first) < rank(second)
+
+
+def spread_columns(row):
+    return jnp.transpose(jnp.broadcast_to(row, (LANES, LANES)))
+
+
+def tile_places(route_ref, window_ref, rows_out, cols_out, place_ref):
+    pixels, lanes = rows_out.shape
     senders = lanes // LANES
     granules = route_ref.shape[1] // senders
     own = lax.axis_index("gran")
+    lane_row = lax.broadcasted_iota(jnp.int32, (1, LANES), 1)
+
+    def both_routes(rows):
+        return jnp.where(lane_row < granules, rows[0:1], pltpu.roll(rows, granules, 1)[1:2])
+
+    routes = own_columns(route_ref, (slice(None),), granules)
+    starts = [own_columns(window_ref, (r, slice(None)), granules) for r in range(2)]
+    named = both_routes(routes).astype(f32)
+    col = lax.broadcasted_iota(jnp.int32, (LANES, LANES), 1)
+    row = lax.broadcasted_iota(jnp.int32, (LANES, LANES), 0)
+    before = earlier((row // granules, row % granules), (col // granules, col % granules), granules)
+    before = before & (row < 2 * granules) & (spread_columns(named) == named)
+    rank = jnp.sum(before.astype(f32), axis=0, keepdims=True).astype(jnp.int32)
+    knots = [
+        jnp.clip(jnp.right_shift(both_routes(jnp.concatenate([s[k : k + 1] for s in starts])), 5) - 1, 0, KN - SPAN)
+        for k in range(2)
+    ]
+    turn = rank * SPAN - knots[1] + LANES
+    place_ref[...] = jnp.concatenate(
+        [named.astype(jnp.int32), rank, jnp.right_shift(knots[0], 1), turn] * 2, axis=0
+    )
+
+    wide = 2 * LANES
+    col = lax.broadcasted_iota(jnp.int32, (wide, wide), 1)
+    row = lax.broadcasted_iota(jnp.int32, (wide, wide), 0)
+    route = [at // LANES for at in (row, col)]
+    place = [at % LANES for at in (row, col)]
+    before = earlier((route[0], place[0] % granules), (route[1], place[1] % granules), granules)
+    before = before & (place[0] // granules == place[1] // granules)
+    before = before.astype(f32).astype(bf16)
+    seat = (lax.broadcasted_iota(jnp.int32, (LANES, LANES), 1) // SPAN).astype(f32)
     lane = lax.broadcasted_iota(jnp.int32, (8, LANES), 1)
-    seat, step = lane // SPAN, lane % SPAN
-
-    def sender(n, carry):
-        first = n * granules
-        base = pl.multiple_of((first // LANES) * LANES, LANES)
-        turn = jnp.bitwise_and(LANES - lax.rem(first, LANES), LANES - 1)
-        at = pl.ds(base, LANES)
-        routes = pltpu.roll(route_ref[:, at], turn, 1)
-        starts = [pltpu.roll(window_ref[r, :, at], turn, 1) for r in range(2)]
-        rank = jnp.int32(0)
-        place = jnp.full((8, LANES), -1, jnp.int32)
-        for i in visits(granules, True) + visits(granules, False):
-            for r in range(2):
-                hit = routes[r, i] == own
-                here = seat == jnp.where(hit, rank, -1)
-                rank = rank + hit.astype(jnp.int32)
-                place = jnp.where(here, starts[r][axis, i], place)
-        to = pl.ds(pl.multiple_of(n * LANES, LANES), LANES)
-        first_knot = jnp.clip(jnp.right_shift(place, 5) - 1, 0, KN - SPAN)
-        if axis == 0:
-            knot = 2 * jnp.right_shift(first_knot, 1) + 2 * (step % 8) + step // 8
-        else:
-            knot = first_knot + step
-        beyond = jnp.where(knot == 0, -1, jnp.where(knot == KN - 1, KN, 4 * KN))
-        dead = place < 0
-        knot = jnp.where(dead, 4 * KN, knot).astype(f32)
-        beyond = jnp.where(dead, 4 * KN, beyond).astype(f32)
-        start = place.astype(f32) * (1.0 / SP)
-        knot, beyond = start - knot, start - beyond
-        pixel = lax.broadcasted_iota(jnp.int32, (8, LANES), 0).astype(f32) * (1.0 / SP)
-        for r in range(0, pixels, 16):
-            values = []
-            for q in (r, r + 8):
-                at_pixel = pixel + q * (1.0 / SP)
-                values.append(cubic(jnp.abs(at_pixel + knot)) + cubic(jnp.abs(at_pixel + beyond)))
-            out_ref[r : r + 16, to] = jnp.concatenate(values, axis=0).astype(bf16)
-        return carry
-
-    lax.fori_loop(0, senders, sender, 0)
+    step = lane % SPAN
+    pixel = lax.broadcasted_iota(jnp.int32, (8, LANES), 0).astype(f32) * (1.0 / SP)
+    part = LANES // granules
+    for t in range(route_ref.shape[1] // LANES):
+        at = slice(t * LANES, (t + 1) * LANES)
+        hits = [(route_ref[r : r + 1, at] == own).astype(f32) for r in range(2)]
+        hits = jnp.broadcast_to(jnp.concatenate(hits, axis=1), (8, wide))
+        ranks = jnp.dot(hits.astype(bf16), before, preferred_element_type=f32)
+        ranks = jnp.where(hits > 0.5, ranks, -1.0)
+        chosen, values = [], []
+        for r in range(2):
+            chosen.append((spread_columns(ranks[0:1, r * LANES : (r + 1) * LANES]) == seat).astype(f32).astype(bf16))
+            sender = lax.broadcasted_iota(jnp.int32, (part, LANES), 0)
+            within = lax.broadcasted_iota(jnp.int32, (part, LANES), 1) // granules == sender
+            kinds = []
+            for k in range(2):
+                start = window_ref[r, k : k + 1, at]
+                kinds += [jnp.right_shift(start, 5), jnp.bitwise_and(start, SP - 1)]
+            kinds.append(jnp.ones((1, LANES), jnp.int32))
+            values.append(jnp.concatenate([jnp.where(within, kind, 0).astype(f32) for kind in kinds], axis=0))
+        found = jnp.dot(
+            jnp.concatenate(values, axis=1).astype(bf16),
+            jnp.concatenate(chosen, axis=0),
+            preferred_element_type=f32,
+        )
+        for n in range(part):
+            live = found[4 * part + n : 4 * part + n + 1] > 0.5
+            for k, ref in ((0, rows_out), (1, cols_out)):
+                base = found[2 * k * part + n : 2 * k * part + n + 1]
+                rest = found[(2 * k + 1) * part + n : (2 * k + 1) * part + n + 1]
+                first = jnp.clip(base.astype(jnp.int32) - 1, 0, KN - SPAN)
+                if k == 0:
+                    knot = 2 * jnp.right_shift(first, 1) + 2 * (step % 8) + step // 8
+                else:
+                    knot = first + step
+                border = (knot == 0) | (knot == KN - 1)
+                cube = jnp.where(border, 1.0, 1.5)
+                square = jnp.where(border, -1.5, -2.5)
+                single = jnp.where(border, -0.5, 0.0)
+                away = jnp.where(live, base + rest * (1.0 / SP) - knot.astype(f32), 4.0 * KN)
+                away = away + pixel
+                to = pl.ds((t * part + n) * LANES, LANES)
+                for q in range(0, pixels, 16):
+                    pair = []
+                    for p in (q, q + 8):
+                        d = jnp.abs(away + p * (1.0 / SP))
+                        near = ((cube * d + square) * d + single) * d + 1.0
+                        far = ((2.5 - 0.5 * d) * d - 4.0) * d + 2.0
+                        pair.append(jnp.where(d <= 1.0, near, jnp.where(d < 2.0, far, 0.0)))
+                    ref[q : q + 16, to] = jnp.concatenate(pair, axis=0).astype(bf16)
 
 
 def compose(route_ref, received_ref, row_ref, col_ref, pixels_ref, out_ref, passed, result, sems):
@@ -560,24 +584,14 @@
                 ("v", some, f32),
                 ("v", some, f32),
                 ("v", (part, bands, 32, LANES), f32),
-                ("v", (part, slots, bands, 32, LANES), bf16),
+                ("v", (part,) + coupling.shape[1:], f32),
             ],
             [
                 pltpu.VMEM(cross.shape, f32),
                 pltpu.VMEM((part,) + coupling.shape[1:], bf16),
-                pltpu.VMEM((bands, 32 * slots, LANES), f32),
                 pltpu.SemaphoreType.DMA((4, chunks)),
             ],
         )
-
-    def interpolation(axis, after):
-        weight_shape = (pixel_count, device_total * LANES)
-        routes, starts, _ = lax.optimization_barrier((tiles[0][1], tiles[1][1], after))
-        return call(
-            functools.partial(interp_weights, axis),
-            [("v", routes), ("v", starts)],
-            [("v", weight_shape, bf16)],
-        )[0]
 
     gathered = pltpu.VMEM((slots, 64, LANES), f32)
     weights = pltpu.VMEM((slots, 64, LANES), f32)
@@ -597,7 +611,14 @@
         if sweep == 0:
             inner, *edge_state = lax.optimization_barrier((inner, *arranged(False, sources)))
         if sweep == 1:
-            inner, row_weights = lax.optimization_barrier((inner, interpolation(0, inner)))
+            routes, starts, _ = lax.optimization_barrier((tiles[0][1], tiles[1][1], inner))
+            weight_shape = ("v", (pixel_count, device_total * LANES), bf16)
+            made = call(
+                tile_places,
+                [("v", routes), ("v", starts)],
+                [weight_shape, weight_shape, ("v", (8, LANES), jnp.int32)],
+            )
+            inner, row_weights, col_weights, places = lax.optimization_barrier((inner, *made))
         if last:
             inner_shares = over_band(inner)
         inputs = graph + [("v", near), ("v", far), ("v", extended)]
@@ -613,9 +634,6 @@
         if sweep == 0:
             *later, _ = lax.optimization_barrier((*sources, partial))
             partial, *inner_state = lax.optimization_barrier((partial, *arranged(True, later)))
-            shares[0] = ("v", partial)
-        if sweep == 1:
-            partial, col_weights = lax.optimization_barrier((partial, interpolation(1, partial)))
             shares[0] = ("v", partial)
         edge_state_now = [("v", extended)] + [("v", array) for array in edge_state]
         inner_state_now = [("v", extended)] + [("v", array) for array in inner_state]
@@ -640,18 +658,17 @@
     scratch = [
         weights,
         scalars,
-        pltpu.SMEM((device_total,), jnp.int32),
         pltpu.VMEM(own, f32),
         pltpu.SemaphoreType.DMA((2,)),
     ]
-    inputs = graph + inner_shares + inner_state_now + tiles
+    inputs = graph + inner_shares + inner_state_now + [("v", places)]
     balanced, gathered_windows = call(
         functools.partial(last_sweep, True),
         inputs,
         [("h", own, f32), ("v", windows, f32)],
         scratch,
     )
-    inputs = graph + shares + edge_state_now + tiles + [("h", balanced), ("v", gathered_windows)]
+    inputs = graph + shares + edge_state_now + [("v", places)] + [("h", balanced), ("v", gathered_windows)]
     balanced, payload, _ = call(
         functools.partial(last_sweep, False),
         inputs,

time: 76.2 us -> 75.2 us (0.987)
  Pallas kernels: 34 us -> 28.6 us
  blocking collectives: 14.3 us -> 17.9 us
  waiting for transfers between devices: 8.06 us -> 9.56 us
  starting transfers between devices: 18.4 us -> 17.6 us
    pallas_call x19 -> x18, Pallas kernels: 34 us -> 28.6 us  [call(): pl.pallas_call(body, in_specs=[ON_CHIP if kind == 'v' else ANYWHERE for k...]
    all_to_all x1, blocking collectives: 14.3 us -> 17.9 us  [per_device(): lax.all_to_all(payload, 'gran', split_axis=0, concat_axis=0, tiled=True)]
    ppermute x12, waiting for transfers between devices: 0.03 us -> 2.33 us  [over_band(): lax.ppermute(partial, 'band', [(i, i ^ flip) for i in range(band_total)])]
    ppermute x3, starting transfers between devices: 8.78 us -> 7.95 us  [exchange(): near = lax.ppermute(near, 'gran', near_pairs)]
    ppermute x3, waiting for transfers between devices: 8.02 us -> 7.22 us  [exchange(): near = lax.ppermute(near, 'gran', near_pairs)]
  transfers between devices with their start and end apart: 18 -> 18, of which waited for: 3 -> 6; matrix products, arithmetic and copies ran while one was open for 0% -> 0% of each run, Pallas kernels for 32% -> 23%
where the time goes in v4:
time: 75.2 us; the launch traced here: 74.6 us
  Pallas kernels  28.6 us (38%)
  blocking collectives  17.9 us (24%)
  starting transfers between devices  17.6 us (23%)
  waiting for transfers between devices  9.56 us (13%)
  between operations  0.92 us (1%)
    pallas_call x18, Pallas kernels, call(): pl.pallas_call(body, in_specs=[ON_CHIP if kind == 'v' else ANYWHERE for k...  28.6 us
    all_to_all x1, blocking collectives, per_device(): lax.all_to_all(payload, 'gran', split_axis=0, concat_axis=0, tiled=True)  17.9 us
    ppermute x3, starting transfers between devices, exchange(): near = lax.ppermute(near, 'gran', near_pairs)  7.95 us
    ppermute x12, starting transfers between devices, over_band(): lax.ppermute(partial, 'band', [(i, i ^ flip) for i in range(band_total)])  7.69 us
    ppermute x3, waiting for transfers between devices, exchange(): near = lax.ppermute(near, 'gran', near_pairs)  7.22 us
    ppermute x12, waiting for transfers between devices, over_band(): lax.ppermute(partial, 'band', [(i, i ^ flip) for i in range(band_total)])  2.33 us
    ppermute x3, starting transfers between devices, exchange(): far = lax.ppermute(far, 'gran', far_pairs)  1.98 us
  transfers between devices with their start and end apart: 18, of which 6 were waited for; matrix products, arithmetic and copies ran while one was open for 0% of the time, Pallas kernels for 23%

profile of v4, /device:TPU:0, one launch (start us, length us, event | category | flops | bytes accessed | tf_op | source)
XLA Modules:
  0.0 74.6 jit_solution(6628908556057014960)
XLA Ops:
  0.6 1.3 %shard_map.113 = (bf16[4,3,64,128]{3,2,1,0:T(8,128)(2,1)S(1)}, bf16[4,3,64,128]{3,2,1,0:T(8,128)(2,1)S(1)}) custom-call(f32[16,3,64,128]{3,2,1,0:T(8,128)} %bitcast.71), custom_call_target="tpu_custom_call" | custom-call | tf_op jit(solution)/shard_map/pallas_call | solution.py:31
  1.9 0.0 copy-start
  2.0 0.0 copy-start.2
  2.0 3.0 %collective-permute-start = (bf16[4,3,64,128]{3,2,1,0:T(8,128)(2,1)S(1)}, bf16[4,3,64,128]{3,2,1,0:T(8,128)(2,1)S(1)}, u32[]{:S(2)}, u32[]{:S(2)}) collective-permute-start(bf16[4,3,64,128]{3,2,1,0:T(8,128)(2,1)S(1)} %get-tuple-element.51), channel_id=1, source_target_pairs={{0,4},{4,0},{8,12},{12,8},{16,20},{20,16},{24,28},{28,24},{1,5},{5... | collective-permute-start | bytes 589832 | tf_op jit(solution)/shard_map/ppermute | solution.py:559
  5.0 0.7 collective-permute-start.1
  5.6 1.5 %shard_map.114.ext_ref.refs_0_ = f32[24,3,64,128]{3,2,1,0:T(8,128)S(1)} custom-call(f32[16,3,64,128]{3,2,1,0:T(8,128)} %bitcast.72), custom_call_target="tpu_custom_call" | custom-call | tf_op jit(solution)/shard_map/pallas_call | solution.py:31
  7.1 0.8 %shard_map.115.refs_1_ = f32[64,128]{1,0:T(8,128)S(1)} custom-call(s32[8,16]{1,0:T(8,128)S(1)} %bitcast.38, s32[1,16]{1,0:T(1,128)S(1)} %bitcast.50, f32[24,3,64,128]{3,2,1,0:T(8,128)S(1)} %shard_map.114.ext_ref.refs_0_), custom_call_target="tpu_custom_call" | custom-call | tf_op jit(solution)/shard_map/pallas_call | solution.py:31
  7.9 2.2 %shard_map.116 = (f32[8,3,64,128]{3,2,1,0:T(8,128)S(1)}, f32[8,3,64,128]{3,2,1,0:T(8,128)S(1)}, f32[8,3,32,128]{3,2,1,0:T(8,128)S(1)}, f32[8,3,256,128]{3,2,1,0:T(8,128)S(1)}) custom-call(f32[16,3,64,128]{3,2,1,0:T(8,128)} %bitcast.67, f32[16,3,64,128]{3,2,1,0:T(8,128)} %bitcast.69, f32[3,2,256,128]{3,2,1,0:T(8,128)} %bitcast.73, ...), custom_call_target="tpu_custom_call" | custom-call | tf_op jit(solution)/shard_map/pallas_call | solution.py:31
  10.2 3.1 %collective-permute-done.near_ref = bf16[4,3,64,128]{3,2,1,0:T(8,128)(2,1)S(1)} collective-permute-done((bf16[4,3,64,128]{3,2,1,0:T(8,128)(2,1)S(1)}, bf16[4,3,64,128]{3,2,1,0:T(8,128)(2,1)S(1)}, u32[]{:S(2)}, u32[]{:S(2)}) %collective-permute-start) | collective-permute-done | bytes 196640 | tf_op jit(solution)/shard_map/ppermute | solution.py:559
  13.4 0.7 shard_map.117
  14.1 0.1 collective-permute-start.4
  14.1 1.6 %collective-permute-start.3 = (f32[64,128]{1,0:T(8,128)S(1)}, f32[64,128]{1,0:T(8,128)S(1)}, u32[]{:S(2)}, u32[]{:S(2)}) collective-permute-start(f32[64,128]{1,0:T(8,128)S(1)} %get-tuple-element.67.refs_0_), channel_id=1, source_target_pairs={{0,2},{1,3},{2,0},{3,1},{4,6},{5,7},{6,4},{7,5},{8,10},{9,11},{10,... | collective-permute-start | bytes 98312 | tf_op jit(solution)/shard_map/ppermute | solution.py:602
  15.7 0.3 collective-permute-start.2
  16.0 2.2 %shard_map.118 = (f32[8,3,64,128]{3,2,1,0:T(8,128)S(1)}, f32[8,3,64,128]{3,2,1,0:T(8,128)S(1)}, f32[8,3,32,128]{3,2,1,0:T(8,128)S(1)}, f32[8,3,256,128]{3,2,1,0:T(8,128)S(1)}) custom-call(f32[16,3,64,128]{3,2,1,0:T(8,128)} %bitcast.68, f32[16,3,64,128]{3,2,1,0:T(8,128)} %bitcast.70, f32[3,2,256,128]{3,2,1,0:T(8,128)} %bitcast.74, ...), custom_call_target="tpu_custom_call" | custom-call | tf_op jit(solution)/shard_map/pallas_call | solution.py:31
  18.3 1.4 %shard_map.119 = (f32[24,3,64,128]{3,2,1,0:T(8,128)S(1)}, bf16[4,3,64,128]{3,2,1,0:T(8,128)(2,1)S(1)}, bf16[4,3,64,128]{3,2,1,0:T(8,128)(2,1)S(1)}) custom-call(s32[8,16]{1,0:T(8,128)S(1)} %bitcast.40, s32[1,16]{1,0:T(1,128)S(1)} %bitcast.52, f32[64,128]{1,0:T(8,128)S(1)} %get-tuple-element.67.refs_0_, f32[64,128]{1,0:T(8,128)S(1)} %collective-permute-done.2.refs_1_, ...), custom_call_target="tpu_custom_call" | custom-call | tf_op jit(solution)/shard_map/pallas_call | solution.py:31
  19.7 2.5 %collective-permute-start.5 = (bf16[4,3,64,128]{3,2,1,0:T(8,128)(2,1)S(1)}, bf16[4,3,64,128]{3,2,1,0:T(8,128)(2,1)S(1)}, u32[]{:S(2)}, u32[]{:S(2)}) collective-permute-start(bf16[4,3,64,128]{3,2,1,0:T(8,128)(2,1)S(1)} %get-tuple-element.73), channel_id=1, source_target_pairs={{0,4},{4,0},{8,12},{12,8},{16,20},{20,16},{24,28},{28,24},{1,5},{5... | collective-permute-start | bytes 589832 | tf_op jit(solution)/shard_map/ppermute | solution.py:559
  22.2 0.7 collective-permute-start.6
  22.8 1.6 %shard_map.120.ext_ref.refs_0_ = f32[24,3,64,128]{3,2,1,0:T(8,128)S(1)} custom-call(s32[8,16]{1,0:T(8,128)S(1)} %bitcast.41, s32[1,16]{1,0:T(1,128)S(1)} %bitcast.53, f32[64,128]{1,0:T(8,128)S(1)} %get-tuple-element.67.refs_0_, f32[64,128]{1,0:T(8,128)S(1)} %collective-permute-done.2.refs_1_, ...), custom_call_target="tpu_custom_call", output_to_operand_aliasing={{}: (11, {})} | custom-call | tf_op jit(solution)/shard_map/pallas_call | solution.py:31
  24.5 0.0 copy-start.3
  24.5 0.0 copy-start.4
  24.5 0.8 %shard_map.121.refs_1_ = f32[64,128]{1,0:T(8,128)S(1)} custom-call(s32[8,16]{1,0:T(8,128)S(1)} %bitcast.42, s32[1,16]{1,0:T(1,128)S(1)} %bitcast.54, f32[24,3,64,128]{3,2,1,0:T(8,128)S(1)} %shard_map.120.ext_ref.refs_0_), custom_call_target="tpu_custom_call" | custom-call | tf_op jit(solution)/shard_map/pallas_call | solution.py:31
  25.3 1.8 %shard_map.122 = (bf16[256,1024]{1,0:T(8,128)(2,1)S(1)}, bf16[256,1024]{1,0:T(8,128)(2,1)S(1)}, s32[8,128]{1,0:T(8,128)S(1)}) custom-call(s32[2,128]{1,0:T(2,128)S(1)} %bitcast.62, s32[2,2,128]{2,1,0:T(2,128)S(1)} %bitcast.64), custom_call_target="tpu_custom_call" | custom-call | tf_op jit(solution)/shard_map/pallas_call | solution.py:31
  27.1 3.9 %collective-permute-done.5.near_ref = bf16[4,3,64,128]{3,2,1,0:T(8,128)(2,1)S(1)} collective-permute-done((bf16[4,3,64,128]{3,2,1,0:T(8,128)(2,1)S(1)}, bf16[4,3,64,128]{3,2,1,0:T(8,128)(2,1)S(1)}, u32[]{:S(2)}, u32[]{:S(2)}) %collective-permute-start.5) | collective-permute-done | bytes 196640 | tf_op jit(solution)/shard_map/ppermute | solution.py:559
  31.0 0.7 shard_map.123
  31.7 0.1 collective-permute-start.9
  31.8 1.3 %collective-permute-start.8 = (f32[64,128]{1,0:T(8,128)S(1)}, f32[64,128]{1,0:T(8,128)S(1)}, u32[]{:S(2)}, u32[]{:S(2)}) collective-permute-start(f32[64,128]{1,0:T(8,128)S(1)} %get-tuple-element.86.refs_0_), channel_id=1, source_target_pairs={{0,2},{1,3},{2,0},{3,1},{4,6},{5,7},{6,4},{7,5},{8,10},{9,11},{10,... | collective-permute-start | bytes 98312 | tf_op jit(solution)/shard_map/ppermute | solution.py:602
  33.1 0.5 collective-permute-start.7
  33.6 1.6 %collective-permute-done.9.refs_3_ = f32[64,128]{1,0:T(8,128)S(1)} collective-permute-done((f32[64,128]{1,0:T(8,128)S(1)}, f32[64,128]{1,0:T(8,128)S(1)}, u32[]{:S(2)}, u32[]{:S(2)}) %collective-permute-start.9) | collective-permute-done | bytes 32800 | tf_op jit(solution)/shard_map/ppermute | solution.py:602
  35.3 0.5 collective-permute-done.8.refs_2_
  35.8 1.4 %shard_map.124 = (f32[24,3,64,128]{3,2,1,0:T(8,128)S(1)}, bf16[4,3,64,128]{3,2,1,0:T(8,128)(2,1)S(1)}, bf16[4,3,64,128]{3,2,1,0:T(8,128)(2,1)S(1)}) custom-call(s32[8,16]{1,0:T(8,128)S(1)} %bitcast.44, s32[1,16]{1,0:T(1,128)S(1)} %bitcast.56, f32[64,128]{1,0:T(8,128)S(1)} %get-tuple-element.86.refs_0_, f32[64,128]{1,0:T(8,128)S(1)} %collective-permute-done.7.refs_1_, ...), custom_call_target="tpu_custom_call" | custom-call | tf_op jit(solution)/shard_map/pallas_call | solution.py:31
  37.2 2.5 %collective-permute-start.10 = (bf16[4,3,64,128]{3,2,1,0:T(8,128)(2,1)S(1)}, bf16[4,3,64,128]{3,2,1,0:T(8,128)(2,1)S(1)}, u32[]{:S(2)}, u32[]{:S(2)}) collective-permute-start(bf16[4,3,64,128]{3,2,1,0:T(8,128)(2,1)S(1)} %get-tuple-element.88), channel_id=1, source_target_pairs={{0,4},{4,0},{8,12},{12,8},{16,20},{20,16},{24,28},{28,24},{1,5},{5... | collective-permute-start | bytes 589832 | tf_op jit(solution)/shard_map/ppermute | solution.py:559
  39.6 0.7 collective-permute-start.11
  40.3 1.6 %shard_map.125.refs_0_.ext_ref = f32[24,3,64,128]{3,2,1,0:T(8,128)S(1)} custom-call(s32[8,16]{1,0:T(8,128)S(1)} %bitcast.45, s32[1,16]{1,0:T(1,128)S(1)} %bitcast.57, f32[64,128]{1,0:T(8,128)S(1)} %get-tuple-element.86.refs_0_, f32[64,128]{1,0:T(8,128)S(1)} %collective-permute-done.7.refs_1_, ...), custom_call_target="tpu_custom_call", output_to_operand_aliasing={{}: (11, {})} | custom-call | tf_op jit(solution)/shard_map/pallas_call | solution.py:31
  41.9 0.8 %shard_map.127.refs_0_ = f32[64,128]{1,0:T(8,128)S(1)} custom-call(s32[8,16]{1,0:T(8,128)S(1)} %bitcast.46, s32[1,16]{1,0:T(1,128)S(1)} %bitcast.58, f32[24,3,64,128]{3,2,1,0:T(8,128)S(1)} %shard_map.125.refs_0_.ext_ref), custom_call_target="tpu_custom_call" | custom-call | tf_op jit(solution)/shard_map/pallas_call | solution.py:31
  42.7 0.8 %collective-permute-start.17 = (f32[64,128]{1,0:T(8,128)S(1)}, f32[64,128]{1,0:T(8,128)S(1)}, u32[]{:S(2)}, u32[]{:S(2)}) collective-permute-start(f32[64,128]{1,0:T(8,128)S(1)} %shard_map.127.refs_0_), channel_id=1, source_target_pairs={{0,3},{1,2},{2,1},{3,0},{4,7},{5,6},{6,5},{7,4},{8,11},{9,10},{10,... | collective-permute-start | bytes 98312 | tf_op jit(solution)/shard_map/ppermute | solution.py:602
  43.5 0.8 %collective-permute-start.16 = (f32[64,128]{1,0:T(8,128)S(1)}, f32[64,128]{1,0:T(8,128)S(1)}, u32[]{:S(2)}, u32[]{:S(2)}) collective-permute-start(f32[64,128]{1,0:T(8,128)S(1)} %shard_map.127.refs_0_), channel_id=1, source_target_pairs={{0,2},{1,3},{2,0},{3,1},{4,6},{5,7},{6,4},{7,5},{8,10},{9,11},{10,... | collective-permute-start | bytes 98312 | tf_op jit(solution)/shard_map/ppermute | solution.py:602
  44.3 0.4 collective-permute-start.15
  44.7 0.2 collective-permute-done.10.near_ref
  44.9 0.7 shard_map.126
  45.6 0.9 %collective-permute-start.14 = (f32[64,128]{1,0:T(8,128)S(1)}, f32[64,128]{1,0:T(8,128)S(1)}, u32[]{:S(2)}, u32[]{:S(2)}) collective-permute-start(f32[64,128]{1,0:T(8,128)S(1)} %get-tuple-element.91.refs_0_), channel_id=1, source_target_pairs={{0,3},{1,2},{2,1},{3,0},{4,7},{5,6},{6,5},{7,4},{8,11},{9,10},{10,... | collective-permute-start | bytes 98312 | tf_op jit(solution)/shard_map/ppermute | solution.py:602
  46.5 0.7 %collective-permute-start.13 = (f32[64,128]{1,0:T(8,128)S(1)}, f32[64,128]{1,0:T(8,128)S(1)}, u32[]{:S(2)}, u32[]{:S(2)}) collective-permute-start(f32[64,128]{1,0:T(8,128)S(1)} %get-tuple-element.91.refs_0_), channel_id=1, source_target_pairs={{0,2},{1,3},{2,0},{3,1},{4,6},{5,7},{6,4},{7,5},{8,10},{9,11},{10,... | collective-permute-start | bytes 98312 | tf_op jit(solution)/shard_map/ppermute | solution.py:602
  47.2 0.3 collective-permute-start.12
  47.5 0.2 collective-permute-done.16.refs_2_
  47.7 3.3 %shard_map.128 = (f32[16,3,64,128]{3,2,1,0:T(8,128)}, f32[8,96,128]{2,1,0:T(8,128)S(1)}) custom-call(s32[8,16]{1,0:T(8,128)S(1)} %bitcast.48, s32[1,16]{1,0:T(1,128)S(1)} %bitcast.60, f32[64,128]{1,0:T(8,128)S(1)} %shard_map.127.refs_0_, f32[64,128]{1,0:T(8,128)S(1)} %collective-permute-done.15.refs_1_, f32[64,128]{1,0:T(8,128)S(1)} %collective-permute-done.16.refs_2_, ...), custom_call_target="tpu_custom_call" | custom-call | tf_op jit(solution)/shard_map/pallas_call | solution.py:31
  51.0 0.0 copy-start.1
  51.0 3.0 %shard_map.129 = (f32[16,3,64,128]{3,2,1,0:T(8,128)}, bf16[8,96,128]{2,1,0:T(8,128)(2,1)S(1)}, f32[8,96,128]{2,1,0:T(8,128)S(1)}) custom-call(s32[8,16]{1,0:T(8,128)S(1)} %bitcast.49, s32[1,16]{1,0:T(1,128)S(1)} %bitcast.61, f32[64,128]{1,0:T(8,128)S(1)} %get-tuple-element.91.refs_0_, ...), custom_call_target="tpu_custom_call", output_to_operand_aliasing={{0}: (12, {}), {2}: (13, {})} | custom-call | tf_op jit(solution)/shard_map/pallas_call | solution.py:31
  54.1 17.9 %all_to_all.5.received_ref = bf16[8,96,128]{2,1,0:T(8,128)(2,1)S(1)} all-to-all(bf16[8,96,128]{2,1,0:T(8,128)(2,1)S(1)} %get-tuple-element.97), channel_id=1, replica_groups=mesh['gran'=8,'band'=4] {'gran'}, dimensions={0} | all-to-all | bytes 393216 | tf_op jit(solution)/shard_map/all_to_all | solution.py:679
  72.0 2.6 %shard_map.130 = bf16[1,3,256,256]{3,2,1,0:T(8,128)(2,1)} custom-call(s32[2,128]{1,0:T(2,128)S(1)} %bitcast.63, bf16[8,96,128]{2,1,0:T(8,128)(2,1)S(1)} %all_to_all.5.received_ref, bf16[256,1024]{1,0:T(8,128)(2,1)S(1)} %get-tuple-element.98.row_ref, bf16[256,1024]{1,0:T(8,128)(2,1)S(1)} %get-tuple-element.99.col_ref, bf16[1,3,256,256]{3,2,1,0:T(8,128)(2,1)S(1)} %copy-done.1), custom_call_target="tpu_custom_call" | custom-call | tf_op jit(solution)/shard_map/pallas_call | solution.py:31
  (17 shorter events, 0.0 us)
Async XLA Ops:
  1.9 5.2 %copy-start = (s32[16,8]{0,1:T(8,128)S(1)}, s32[16,8]{0,1:T(8,128)}, u32[]{:S(2)}) copy-start(s32[16,8]{0,1:T(8,128)} %param.15) | copy-start | bytes 1540
  2.0 5.2 %copy-start.2 = (s32[16]{0:T(128)S(1)}, s32[16]{0:T(128)}, u32[]{:S(2)}) copy-start(s32[16]{0:T(128)} %param.16) | copy-start | bytes 196
  2.0 11.4 %collective-permute-start = (bf16[4,3,64,128]{3,2,1,0:T(8,128)(2,1)S(1)}, bf16[4,3,64,128]{3,2,1,0:T(8,128)(2,1)S(1)}, u32[]{:S(2)}, u32[]{:S(2)}) collective-permute-start(bf16[4,3,64,128]{3,2,1,0:T(8,128)(2,1)S(1)} %get-tuple-element.51), channel_id=1, source_target_pairs={{0,4},{4,0},{8,12},{12,8},{16,20},{20,16},{24,28},{28,24},{1,5},{5... | collective-permute-start | bytes 589832 | tf_op jit(solution)/shard_map/ppermute | solution.py:559
  5.0 8.4 %collective-permute-start.1 = (bf16[4,3,64,128]{3,2,1,0:T(8,128)(2,1)S(1)}, bf16[4,3,64,128]{3,2,1,0:T(8,128)(2,1)S(1)}, u32[]{:S(2)}, u32[]{:S(2)}) collective-permute-start(bf16[4,3,64,128]{3,2,1,0:T(8,128)(2,1)S(1)} %get-tuple-element.52), channel_id=1, source_target_pairs={{4,8},{8,4},{12,16},{16,12},{20,24},{24,20},{5,9},{9,5},{13,17},{1... | collective-permute-start | bytes 589832 | tf_op jit(solution)/shard_map/ppermute | solution.py:558
  14.1 4.2 %collective-permute-start.4 = (f32[64,128]{1,0:T(8,128)S(1)}, f32[64,128]{1,0:T(8,128)S(1)}, u32[]{:S(2)}, u32[]{:S(2)}) collective-permute-start(f32[64,128]{1,0:T(8,128)S(1)} %get-tuple-element.67.refs_0_), channel_id=1, source_target_pairs={{0,3},{1,2},{2,1},{3,0},{4,7},{5,6},{6,5},{7,4},{8,11},{9,10},{10,... | collective-permute-start | bytes 98312 | tf_op jit(solution)/shard_map/ppermute | solution.py:602
  14.1 4.1 %collective-permute-start.3 = (f32[64,128]{1,0:T(8,128)S(1)}, f32[64,128]{1,0:T(8,128)S(1)}, u32[]{:S(2)}, u32[]{:S(2)}) collective-permute-start(f32[64,128]{1,0:T(8,128)S(1)} %get-tuple-element.67.refs_0_), channel_id=1, source_target_pairs={{0,2},{1,3},{2,0},{3,1},{4,6},{5,7},{6,4},{7,5},{8,10},{9,11},{10,... | collective-permute-start | bytes 98312 | tf_op jit(solution)/shard_map/ppermute | solution.py:602
  15.7 2.5 %collective-permute-start.2 = (f32[64,128]{1,0:T(8,128)S(1)}, f32[64,128]{1,0:T(8,128)S(1)}, u32[]{:S(2)}, u32[]{:S(2)}) collective-permute-start(f32[64,128]{1,0:T(8,128)S(1)} %get-tuple-element.67.refs_0_), channel_id=1, source_target_pairs={{0,1},{1,0},{2,3},{3,2},{4,5},{5,4},{6,7},{7,6},{8,9},{9,8},{10,11... | collective-permute-start | bytes 98312 | tf_op jit(solution)/shard_map/ppermute | solution.py:602
  19.7 11.3 %collective-permute-start.5 = (bf16[4,3,64,128]{3,2,1,0:T(8,128)(2,1)S(1)}, bf16[4,3,64,128]{3,2,1,0:T(8,128)(2,1)S(1)}, u32[]{:S(2)}, u32[]{:S(2)}) collective-permute-start(bf16[4,3,64,128]{3,2,1,0:T(8,128)(2,1)S(1)} %get-tuple-element.73), channel_id=1, source_target_pairs={{0,4},{4,0},{8,12},{12,8},{16,20},{20,16},{24,28},{28,24},{1,5},{5... | collective-permute-start | bytes 589832 | tf_op jit(solution)/shard_map/ppermute | solution.py:559
  22.2 8.8 %collective-permute-start.6 = (bf16[4,3,64,128]{3,2,1,0:T(8,128)(2,1)S(1)}, bf16[4,3,64,128]{3,2,1,0:T(8,128)(2,1)S(1)}, u32[]{:S(2)}, u32[]{:S(2)}) collective-permute-start(bf16[4,3,64,128]{3,2,1,0:T(8,128)(2,1)S(1)} %get-tuple-element.74), channel_id=1, source_target_pairs={{4,8},{8,4},{12,16},{16,12},{20,24},{24,20},{5,9},{9,5},{13,17},{1... | collective-permute-start | bytes 589832 | tf_op jit(solution)/shard_map/ppermute | solution.py:558
  24.5 0.8 %copy-start.3 = (s32[128,2]{0,1:T(2,128)S(1)}, s32[128,2]{0,1:T(2,128)}, u32[]{:S(2)}) copy-start(s32[128,2]{0,1:T(2,128)} %param.17) | copy-start | bytes 3076
  24.5 0.8 %copy-start.4 = (s32[128,2,2]{0,2,1:T(2,128)S(1)}, s32[128,2,2]{0,2,1:T(2,128)}, u32[]{:S(2)}) copy-start(s32[128,2,2]{0,2,1:T(2,128)} %param.18) | copy-start | bytes 6148
  31.7 3.6 %collective-permute-start.9 = (f32[64,128]{1,0:T(8,128)S(1)}, f32[64,128]{1,0:T(8,128)S(1)}, u32[]{:S(2)}, u32[]{:S(2)}) collective-permute-start(f32[64,128]{1,0:T(8,128)S(1)} %get-tuple-element.86.refs_0_), channel_id=1, source_target_pairs={{0,3},{1,2},{2,1},{3,0},{4,7},{5,6},{6,5},{7,4},{8,11},{9,10},{10,... | collective-permute-start | bytes 98312 | tf_op jit(solution)/shard_map/ppermute | solution.py:602
  31.8 4.0 %collective-permute-start.8 = (f32[64,128]{1,0:T(8,128)S(1)}, f32[64,128]{1,0:T(8,128)S(1)}, u32[]{:S(2)}, u32[]{:S(2)}) collective-permute-start(f32[64,128]{1,0:T(8,128)S(1)} %get-tuple-element.86.refs_0_), channel_id=1, source_target_pairs={{0,2},{1,3},{2,0},{3,1},{4,6},{5,7},{6,4},{7,5},{8,10},{9,11},{10,... | collective-permute-start | bytes 98312 | tf_op jit(solution)/shard_map/ppermute | solution.py:602
  33.1 2.7 %collective-permute-start.7 = (f32[64,128]{1,0:T(8,128)S(1)}, f32[64,128]{1,0:T(8,128)S(1)}, u32[]{:S(2)}, u32[]{:S(2)}) collective-permute-start(f32[64,128]{1,0:T(8,128)S(1)} %get-tuple-element.86.refs_0_), channel_id=1, source_target_pairs={{0,1},{1,0},{2,3},{3,2},{4,5},{5,4},{6,7},{7,6},{8,9},{9,8},{10,11... | collective-permute-start | bytes 98312 | tf_op jit(solution)/shard_map/ppermute | solution.py:602
  37.2 7.7 %collective-permute-start.10 = (bf16[4,3,64,128]{3,2,1,0:T(8,128)(2,1)S(1)}, bf16[4,3,64,128]{3,2,1,0:T(8,128)(2,1)S(1)}, u32[]{:S(2)}, u32[]{:S(2)}) collective-permute-start(bf16[4,3,64,128]{3,2,1,0:T(8,128)(2,1)S(1)} %get-tuple-element.88), channel_id=1, source_target_pairs={{0,4},{4,0},{8,12},{12,8},{16,20},{20,16},{24,28},{28,24},{1,5},{5... | collective-permute-start | bytes 589832 | tf_op jit(solution)/shard_map/ppermute | solution.py:559
  39.6 5.2 %collective-permute-start.11 = (bf16[4,3,64,128]{3,2,1,0:T(8,128)(2,1)S(1)}, bf16[4,3,64,128]{3,2,1,0:T(8,128)(2,1)S(1)}, u32[]{:S(2)}, u32[]{:S(2)}) collective-permute-start(bf16[4,3,64,128]{3,2,1,0:T(8,128)(2,1)S(1)} %get-tuple-element.89), channel_id=1, source_target_pairs={{4,8},{8,4},{12,16},{16,12},{20,24},{24,20},{5,9},{9,5},{13,17},{1... | collective-permute-start | bytes 589832 | tf_op jit(solution)/shard_map/ppermute | solution.py:558
  42.7 4.5 %collective-permute-start.17 = (f32[64,128]{1,0:T(8,128)S(1)}, f32[64,128]{1,0:T(8,128)S(1)}, u32[]{:S(2)}, u32[]{:S(2)}) collective-permute-start(f32[64,128]{1,0:T(8,128)S(1)} %shard_map.127.refs_0_), channel_id=1, source_target_pairs={{0,3},{1,2},{2,1},{3,0},{4,7},{5,6},{6,5},{7,4},{8,11},{9,10},{10,... | collective-permute-start | bytes 98312 | tf_op jit(solution)/shard_map/ppermute | solution.py:602
  43.5 4.1 %collective-permute-start.16 = (f32[64,128]{1,0:T(8,128)S(1)}, f32[64,128]{1,0:T(8,128)S(1)}, u32[]{:S(2)}, u32[]{:S(2)}) collective-permute-start(f32[64,128]{1,0:T(8,128)S(1)} %shard_map.127.refs_0_), channel_id=1, source_target_pairs={{0,2},{1,3},{2,0},{3,1},{4,6},{5,7},{6,4},{7,5},{8,10},{9,11},{10,... | collective-permute-start | bytes 98312 | tf_op jit(solution)/shard_map/ppermute | solution.py:602
  44.3 3.3 %collective-permute-start.15 = (f32[64,128]{1,0:T(8,128)S(1)}, f32[64,128]{1,0:T(8,128)S(1)}, u32[]{:S(2)}, u32[]{:S(2)}) collective-permute-start(f32[64,128]{1,0:T(8,128)S(1)} %shard_map.127.refs_0_), channel_id=1, source_target_pairs={{0,1},{1,0},{2,3},{3,2},{4,5},{5,4},{6,7},{7,6},{8,9},{9,8},{10,11... | collective-permute-start | bytes 98312 | tf_op jit(solution)/shard_map/ppermute | solution.py:602
  45.6 5.4 %collective-permute-start.14 = (f32[64,128]{1,0:T(8,128)S(1)}, f32[64,128]{1,0:T(8,128)S(1)}, u32[]{:S(2)}, u32[]{:S(2)}) collective-permute-start(f32[64,128]{1,0:T(8,128)S(1)} %get-tuple-element.91.refs_0_), channel_id=1, source_target_pairs={{0,3},{1,2},{2,1},{3,0},{4,7},{5,6},{6,5},{7,4},{8,11},{9,10},{10,... | collective-permute-start | bytes 98312 | tf_op jit(solution)/shard_map/ppermute | solution.py:602
  46.5 4.5 %collective-permute-start.13 = (f32[64,128]{1,0:T(8,128)S(1)}, f32[64,128]{1,0:T(8,128)S(1)}, u32[]{:S(2)}, u32[]{:S(2)}) collective-permute-start(f32[64,128]{1,0:T(8,128)S(1)} %get-tuple-element.91.refs_0_), channel_id=1, source_target_pairs={{0,2},{1,3},{2,0},{3,1},{4,6},{5,7},{6,4},{7,5},{8,10},{9,11},{10,... | collective-permute-start | bytes 98312 | tf_op jit(solution)/shard_map/ppermute | solution.py:602
  47.2 3.8 %collective-permute-start.12 = (f32[64,128]{1,0:T(8,128)S(1)}, f32[64,128]{1,0:T(8,128)S(1)}, u32[]{:S(2)}, u32[]{:S(2)}) collective-permute-start(f32[64,128]{1,0:T(8,128)S(1)} %get-tuple-element.91.refs_0_), channel_id=1, source_target_pairs={{0,1},{1,0},{2,3},{3,2},{4,5},{5,4},{6,7},{7,6},{8,9},{9,8},{10,11... | collective-permute-start | bytes 98312 | tf_op jit(solution)/shard_map/ppermute | solution.py:602
  51.0 21.0 %copy-start.1 = (bf16[1,3,256,256]{3,2,1,0:T(8,128)(2,1)S(1)}, bf16[1,3,256,256]{3,2,1,0:T(8,128)(2,1)}, u32[]{:S(2)}) copy-start(bf16[1,3,256,256]{3,2,1,0:T(8,128)(2,1)} %pixels_ref.1) | copy-start | bytes 1179652

commit v5 on v4

--- a/solution.py
+++ b/solution.py
@@ -91,7 +91,7 @@
     return inner if interior else [i for i in range(granules) if i not in inner]
 
 
-def arrange(interior, rhs_ref, diag_ref, cross_ref, coupling_ref, rhs_out, diag_out, cross_out, coupling_out, cross_raw, coupling_raw, sems):
+def arrange(interior, offset_ref, count_ref, rhs_ref, diag_ref, cross_ref, coupling_ref, rhs_out, diag_out, cross_out, coupling_out, cross_raw, coupling_raw, wide, graph, sems):
     granules, bands = rhs_ref.shape[:2]
     own = visits(granules, interior)
     size = REACH
@@ -113,6 +113,7 @@
             whole.start()
     for n in range(chunks):
         copies[n][2].start()
+    read_graph(offset_ref, count_ref, graph)
     for n in range(chunks):
         for copy in copies[n][:2]:
             copy.wait()
@@ -123,12 +124,20 @@
             at = n * size + g
             i = own[n * size] + g
             for b in range(bands):
-                coupling_out[at, b] = coupling_raw[at, b].astype(f32)
+                wide[b] = coupling_raw[at, b].astype(f32)
                 for j in range(4):
                     d = [diag_out[at, b, pl.ds(2 * j + c, 8, stride=8), :] for c in range(2)]
                     pick = cross_raw[b, i // 8, pl.ds(8 * j + i % 8, 8, stride=32), :]
                     cross_out[at, b, 8 * j : 8 * j + 8, :] = pick * jnp.sqrt(d[0] * d[1])
-            return carry
+
+            def slot(s, carry):
+                for b in range(bands):
+                    for j in range(4):
+                        pick = wide[b, pl.ds(8 * j + s, 8, stride=32), :]
+                        coupling_out[at, s, b, 8 * j : 8 * j + 8, :] = pick
+                return carry
+
+            return lax.fori_loop(0, graph[1, i], slot, carry)
 
         lax.fori_loop(0, size, step, 0)
     for n in range(chunks):
@@ -251,7 +260,7 @@
         for b in range(bands):
             for j in range(4):
                 k = 4 * b + j
-                effective = weight * coupling_ref[at, b, pl.ds(8 * j + s, 8, stride=32), :]
+                effective = weight * coupling_ref[at, s, b, 8 * j : 8 * j + 8, :]
                 new_sigma.append(sigma[k] + effective)
                 for c in range(2):
                     grid = ext_ref[n, b, 16 * j + 8 * c : 16 * j + 8 * c + 8, :]
@@ -579,16 +588,18 @@
         some = (part, bands, 64, LANES)
         return call(
             functools.partial(arrange, interior),
-            [("h", source) for source in sources],
+            graph + [("h", source) for source in sources],
             [
                 ("v", some, f32),
                 ("v", some, f32),
                 ("v", (part, bands, 32, LANES), f32),
-                ("v", (part,) + coupling.shape[1:], f32),
+                ("v", (part, slots, bands, 32, LANES), f32),
             ],
             [
                 pltpu.VMEM(cross.shape, f32),
                 pltpu.VMEM((part,) + coupling.shape[1:], bf16),
+                pltpu.VMEM(coupling.shape[1:], f32),
+                pltpu.SMEM((2, granules), jnp.int32),
                 pltpu.SemaphoreType.DMA((4, chunks)),
             ],
         )
@@ -610,15 +621,6 @@
         )
         if sweep == 0:
             inner, *edge_state = lax.optimization_barrier((inner, *arranged(False, sources)))
-        if sweep == 1:
-            routes, starts, _ = lax.optimization_barrier((tiles[0][1], tiles[1][1], inner))
-            weight_shape = ("v", (pixel_count, device_total * LANES), bf16)
-            made = call(
-                tile_places,
-                [("v", routes), ("v", starts)],
-                [weight_shape, weight_shape, ("v", (8, LANES), jnp.int32)],
-            )
-            inner, row_weights, col_weights, places = lax.optimization_barrier((inner, *made))
         if last:
             inner_shares = over_band(inner)
         inputs = graph + [("v", near), ("v", far), ("v", extended)]
@@ -631,12 +633,17 @@
             aliases={4: 0},
         )
         shares = over_band(partial)
-        if sweep == 0:
-            *later, _ = lax.optimization_barrier((*sources, partial))
-            partial, *inner_state = lax.optimization_barrier((partial, *arranged(True, later)))
+        if sweep == 1:
+            routes, starts, _ = lax.optimization_barrier((tiles[0][1], tiles[1][1], partial))
+            weight_shape = ("v", (pixel_count, device_total * LANES), bf16)
+            made = call(
+                tile_places,
+                [("v", routes), ("v", starts)],
+                [weight_shape, weight_shape, ("v", (8, LANES), jnp.int32)],
+            )
+            partial, row_weights, col_weights, places = lax.optimization_barrier((partial, *made))
             shares[0] = ("v", partial)
         edge_state_now = [("v", extended)] + [("v", array) for array in edge_state]
-        inner_state_now = [("v", extended)] + [("v", array) for array in inner_state]
         if not last:
             inputs = graph + shares + edge_state_now
             updated, near, far = call(
@@ -646,7 +653,10 @@
                 [weights, scalars],
             )
             near, far = exchange(near, far)
-            inputs = graph + shares + inner_state_now
+            if sweep == 0:
+                *later, updated = lax.optimization_barrier((*sources, updated))
+                inner_state = [("v", array) for array in arranged(True, later)]
+            inputs = graph + shares + [("v", extended)] + inner_state
             (extended,) = call(
                 interior_sweep,
                 inputs + [("v", updated)],
@@ -661,7 +671,7 @@
         pltpu.VMEM(own, f32),
         pltpu.SemaphoreType.DMA((2,)),
     ]
-    inputs = graph + inner_shares + inner_state_now + [("v", places)]
+    inputs = graph + inner_shares + [("v", extended)] + inner_state + [("v", places)]
     balanced, gathered_windows = call(
         functools.partial(last_sweep, True),
         inputs,

time: 75.2 us -> 73.4 us (0.976); the launches traced: 74.6 us -> 73.6 us
  blocking collectives: 17.9 us -> 14.1 us
  waiting for transfers between devices: 9.56 us -> 13.2 us
    all_to_all x1, blocking collectives: 17.9 us -> 14.1 us  [per_device(): lax.all_to_all(payload, 'gran', split_axis=0, concat_axis=0, tiled=True)]
    ppermute x3, waiting for transfers between devices: 7.22 us -> 10.4 us  [exchange(): near = lax.ppermute(near, 'gran', near_pairs)]
where the time goes in v5:
time: 73.4 us; the launch traced here: 73.6 us
  Pallas kernels  28 us (38%)
  starting transfers between devices  17.4 us (24%)
  blocking collectives  14.1 us (19%)
  waiting for transfers between devices  13.2 us (18%)
  between operations  0.9 us (1%)
    pallas_call x18, Pallas kernels, call(): pl.pallas_call(body, in_specs=[ON_CHIP if kind == 'v' else ANYWHERE for k...  28 us
    all_to_all x1, blocking collectives, per_device(): lax.all_to_all(payload, 'gran', split_axis=0, concat_axis=0, tiled=True)  14.1 us
    ppermute x3, waiting for transfers between devices, exchange(): near = lax.ppermute(near, 'gran', near_pairs)  10.4 us
    ppermute x3, starting transfers between devices, exchange(): near = lax.ppermute(near, 'gran', near_pairs)  7.78 us
    ppermute x12, starting transfers between devices, over_band(): lax.ppermute(partial, 'band', [(i, i ^ flip) for i in range(band_total)])  7.68 us
    ppermute x12, waiting for transfers between devices, over_band(): lax.ppermute(partial, 'band', [(i, i ^ flip) for i in range(band_total)])  2.79 us
    ppermute x3, starting transfers between devices, exchange(): far = lax.ppermute(far, 'gran', far_pairs)  1.98 us
  transfers between devices with their start and end apart: 18, of which 6 were waited for; matrix products, arithmetic and copies ran while one was open for 0% of the time, Pallas kernels for 23%

profile of v5, /device:TPU:0, one launch (start us, length us, event | category | flops | bytes accessed | tf_op | source)
XLA Modules:
  0.0 73.6 jit_solution(9901427487775276302)
XLA Ops:
  0.6 1.3 %shard_map.113 = (bf16[4,3,64,128]{3,2,1,0:T(8,128)(2,1)S(1)}, bf16[4,3,64,128]{3,2,1,0:T(8,128)(2,1)S(1)}) custom-call(f32[16,3,64,128]{3,2,1,0:T(8,128)} %bitcast.71), custom_call_target="tpu_custom_call" | custom-call | tf_op jit(solution)/shard_map/pallas_call | solution.py:31
  1.9 0.0 copy-start
  2.0 0.0 copy-start.2
  2.0 3.0 %collective-permute-start = (bf16[4,3,64,128]{3,2,1,0:T(8,128)(2,1)S(1)}, bf16[4,3,64,128]{3,2,1,0:T(8,128)(2,1)S(1)}, u32[]{:S(2)}, u32[]{:S(2)}) collective-permute-start(bf16[4,3,64,128]{3,2,1,0:T(8,128)(2,1)S(1)} %get-tuple-element.47), channel_id=1, source_target_pairs={{0,4},{4,0},{8,12},{12,8},{16,20},{20,16},{24,28},{28,24},{1,5},{5... | collective-permute-start | bytes 589832 | tf_op jit(solution)/shard_map/ppermute | solution.py:568
  5.0 0.7 collective-permute-start.1
  5.6 1.5 %shard_map.114.ext_ref.refs_0_ = f32[24,3,64,128]{3,2,1,0:T(8,128)S(1)} custom-call(f32[16,3,64,128]{3,2,1,0:T(8,128)} %bitcast.72), custom_call_target="tpu_custom_call" | custom-call | tf_op jit(solution)/shard_map/pallas_call | solution.py:31
  7.1 0.7 shard_map.115.refs_1_
  7.8 3.0 %shard_map.116 = (f32[8,3,64,128]{3,2,1,0:T(8,128)S(1)}, f32[8,3,64,128]{3,2,1,0:T(8,128)S(1)}, f32[8,3,32,128]{3,2,1,0:T(8,128)S(1)}, f32[8,8,3,32,128]{4,3,2,1,0:T(8,128)S(1)}) custom-call(s32[8,16]{1,0:T(8,128)S(1)} %bitcast.39, s32[1,16]{1,0:T(1,128)S(1)} %bitcast.53, f32[16,3,64,128]{3,2,1,0:T(8,128)} %bitcast.73, f32[16,3,64,128]{3,2,1,0:T(8,128)} %bitcast.75, ...), custom_call_target="tpu_custom_call" | custom-call | tf_op jit(solution)/shard_map/pallas_call | solution.py:31
  10.9 2.5 %collective-permute-done.near_ref = bf16[4,3,64,128]{3,2,1,0:T(8,128)(2,1)S(1)} collective-permute-done((bf16[4,3,64,128]{3,2,1,0:T(8,128)(2,1)S(1)}, bf16[4,3,64,128]{3,2,1,0:T(8,128)(2,1)S(1)}, u32[]{:S(2)}, u32[]{:S(2)}) %collective-permute-start) | collective-permute-done | bytes 196640 | tf_op jit(solution)/shard_map/ppermute | solution.py:568
  13.4 0.9 %shard_map.117 = (f32[24,3,64,128]{3,2,1,0:T(8,128)S(1)}, f32[64,128]{1,0:T(8,128)S(1)}) custom-call(s32[8,16]{1,0:T(8,128)S(1)} %bitcast.40, s32[1,16]{1,0:T(1,128)S(1)} %bitcast.54, bf16[4,3,64,128]{3,2,1,0:T(8,128)(2,1)S(1)} %collective-permute-done.near_ref, ...), custom_call_target="tpu_custom_call", output_to_operand_aliasing={{0}: (4, {})} | custom-call | tf_op jit(solution)/shard_map/pallas_call | solution.py:31
  14.2 0.1 collective-permute-start.4
  14.3 1.6 %collective-permute-start.3 = (f32[64,128]{1,0:T(8,128)S(1)}, f32[64,128]{1,0:T(8,128)S(1)}, u32[]{:S(2)}, u32[]{:S(2)}) collective-permute-start(f32[64,128]{1,0:T(8,128)S(1)} %get-tuple-element.54.refs_0_), channel_id=1, source_target_pairs={{0,2},{1,3},{2,0},{3,1},{4,6},{5,7},{6,4},{7,5},{8,10},{9,11},{10,... | collective-permute-start | bytes 98312 | tf_op jit(solution)/shard_map/ppermute | solution.py:613
  15.9 0.3 collective-permute-start.2
  16.1 1.8 %collective-permute-done.4.refs_3_ = f32[64,128]{1,0:T(8,128)S(1)} collective-permute-done((f32[64,128]{1,0:T(8,128)S(1)}, f32[64,128]{1,0:T(8,128)S(1)}, u32[]{:S(2)}, u32[]{:S(2)}) %collective-permute-start.4) | collective-permute-done | bytes 32800 | tf_op jit(solution)/shard_map/ppermute | solution.py:613
  17.9 0.4 collective-permute-done.3.refs_2_
  18.3 1.3 %shard_map.118 = (f32[24,3,64,128]{3,2,1,0:T(8,128)S(1)}, bf16[4,3,64,128]{3,2,1,0:T(8,128)(2,1)S(1)}, bf16[4,3,64,128]{3,2,1,0:T(8,128)(2,1)S(1)}) custom-call(s32[8,16]{1,0:T(8,128)S(1)} %bitcast.41, s32[1,16]{1,0:T(1,128)S(1)} %bitcast.55, f32[64,128]{1,0:T(8,128)S(1)} %get-tuple-element.54.refs_0_, f32[64,128]{1,0:T(8,128)S(1)} %collective-permute-done.2.refs_1_, ...), custom_call_target="tpu_custom_call" | custom-call | tf_op jit(solution)/shard_map/pallas_call | solution.py:31
  19.6 2.4 %collective-permute-start.5 = (bf16[4,3,64,128]{3,2,1,0:T(8,128)(2,1)S(1)}, bf16[4,3,64,128]{3,2,1,0:T(8,128)(2,1)S(1)}, u32[]{:S(2)}, u32[]{:S(2)}) collective-permute-start(bf16[4,3,64,128]{3,2,1,0:T(8,128)(2,1)S(1)} %get-tuple-element.60), channel_id=1, source_target_pairs={{0,4},{4,0},{8,12},{12,8},{16,20},{20,16},{24,28},{28,24},{1,5},{5... | collective-permute-start | bytes 589832 | tf_op jit(solution)/shard_map/ppermute | solution.py:568
  22.0 0.7 collective-permute-start.6
  22.7 2.8 %shard_map.119 = (f32[8,3,64,128]{3,2,1,0:T(8,128)S(1)}, f32[8,3,64,128]{3,2,1,0:T(8,128)S(1)}, f32[8,3,32,128]{3,2,1,0:T(8,128)S(1)}, f32[8,8,3,32,128]{4,3,2,1,0:T(8,128)S(1)}) custom-call(s32[8,16]{1,0:T(8,128)S(1)} %bitcast.42, s32[1,16]{1,0:T(1,128)S(1)} %bitcast.56, f32[16,3,64,128]{3,2,1,0:T(8,128)} %bitcast.74, f32[16,3,64,128]{3,2,1,0:T(8,128)} %bitcast.76, ...), custom_call_target="tpu_custom_call" | custom-call | tf_op jit(solution)/shard_map/pallas_call | solution.py:31
  25.4 1.1 %shard_map.120.ext_ref.refs_0_ = f32[24,3,64,128]{3,2,1,0:T(8,128)S(1)} custom-call(s32[8,16]{1,0:T(8,128)S(1)} %bitcast.43, s32[1,16]{1,0:T(1,128)S(1)} %bitcast.57, f32[64,128]{1,0:T(8,128)S(1)} %get-tuple-element.54.refs_0_, f32[64,128]{1,0:T(8,128)S(1)} %collective-permute-done.2.refs_1_, ...), custom_call_target="tpu_custom_call", output_to_operand_aliasing={{}: (11, {})} | custom-call | tf_op jit(solution)/shard_map/pallas_call | solution.py:31
  26.5 0.0 copy-start.3
  26.5 0.0 copy-start.4
  26.5 0.7 shard_map.121.refs_1_
  27.2 3.6 %collective-permute-done.5.near_ref = bf16[4,3,64,128]{3,2,1,0:T(8,128)(2,1)S(1)} collective-permute-done((bf16[4,3,64,128]{3,2,1,0:T(8,128)(2,1)S(1)}, bf16[4,3,64,128]{3,2,1,0:T(8,128)(2,1)S(1)}, u32[]{:S(2)}, u32[]{:S(2)}) %collective-permute-start.5) | collective-permute-done | bytes 196640 | tf_op jit(solution)/shard_map/ppermute | solution.py:568
  30.9 0.9 %shard_map.122 = (f32[24,3,64,128]{3,2,1,0:T(8,128)S(1)}, f32[64,128]{1,0:T(8,128)S(1)}) custom-call(s32[8,16]{1,0:T(8,128)S(1)} %bitcast.45, s32[1,16]{1,0:T(1,128)S(1)} %bitcast.59, bf16[4,3,64,128]{3,2,1,0:T(8,128)(2,1)S(1)} %collective-permute-done.5.near_ref, ...), custom_call_target="tpu_custom_call", output_to_operand_aliasing={{0}: (4, {})} | custom-call | tf_op jit(solution)/shard_map/pallas_call | solution.py:31
  31.7 0.1 collective-permute-start.9
  31.8 1.1 %collective-permute-start.8 = (f32[64,128]{1,0:T(8,128)S(1)}, f32[64,128]{1,0:T(8,128)S(1)}, u32[]{:S(2)}, u32[]{:S(2)}) collective-permute-start(f32[64,128]{1,0:T(8,128)S(1)} %get-tuple-element.78.refs_0_), channel_id=1, source_target_pairs={{0,2},{1,3},{2,0},{3,1},{4,6},{5,7},{6,4},{7,5},{8,10},{9,11},{10,... | collective-permute-start | bytes 98312 | tf_op jit(solution)/shard_map/ppermute | solution.py:613
  32.9 0.8 %collective-permute-start.7 = (f32[64,128]{1,0:T(8,128)S(1)}, f32[64,128]{1,0:T(8,128)S(1)}, u32[]{:S(2)}, u32[]{:S(2)}) collective-permute-start(f32[64,128]{1,0:T(8,128)S(1)} %get-tuple-element.78.refs_0_), channel_id=1, source_target_pairs={{0,1},{1,0},{2,3},{3,2},{4,5},{5,4},{6,7},{7,6},{8,9},{9,8},{10,11... | collective-permute-start | bytes 98312 | tf_op jit(solution)/shard_map/ppermute | solution.py:613
  33.7 1.8 %shard_map.123 = (bf16[256,1024]{1,0:T(8,128)(2,1)S(1)}, bf16[256,1024]{1,0:T(8,128)(2,1)S(1)}, s32[8,128]{1,0:T(8,128)S(1)}) custom-call(s32[2,128]{1,0:T(2,128)S(1)} %bitcast.66, s32[2,2,128]{2,1,0:T(2,128)S(1)} %bitcast.68), custom_call_target="tpu_custom_call" | custom-call | tf_op jit(solution)/shard_map/pallas_call | solution.py:31
  35.5 0.6 collective-permute-done.8.refs_2_
  36.1 1.3 %shard_map.124 = (f32[24,3,64,128]{3,2,1,0:T(8,128)S(1)}, bf16[4,3,64,128]{3,2,1,0:T(8,128)(2,1)S(1)}, bf16[4,3,64,128]{3,2,1,0:T(8,128)(2,1)S(1)}) custom-call(s32[8,16]{1,0:T(8,128)S(1)} %bitcast.46, s32[1,16]{1,0:T(1,128)S(1)} %bitcast.60, f32[64,128]{1,0:T(8,128)S(1)} %get-tuple-element.78.refs_0_, f32[64,128]{1,0:T(8,128)S(1)} %collective-permute-done.7.refs_1_, ...), custom_call_target="tpu_custom_call" | custom-call | tf_op jit(solution)/shard_map/pallas_call | solution.py:31
  37.4 2.4 %collective-permute-start.10 = (bf16[4,3,64,128]{3,2,1,0:T(8,128)(2,1)S(1)}, bf16[4,3,64,128]{3,2,1,0:T(8,128)(2,1)S(1)}, u32[]{:S(2)}, u32[]{:S(2)}) collective-permute-start(bf16[4,3,64,128]{3,2,1,0:T(8,128)(2,1)S(1)} %get-tuple-element.80), channel_id=1, source_target_pairs={{0,4},{4,0},{8,12},{12,8},{16,20},{20,16},{24,28},{28,24},{1,5},{5... | collective-permute-start | bytes 589832 | tf_op jit(solution)/shard_map/ppermute | solution.py:568
  39.7 0.7 collective-permute-start.11
  40.4 1.1 %shard_map.125.refs_0_.ext_ref = f32[24,3,64,128]{3,2,1,0:T(8,128)S(1)} custom-call(s32[8,16]{1,0:T(8,128)S(1)} %bitcast.47, s32[1,16]{1,0:T(1,128)S(1)} %bitcast.61, f32[64,128]{1,0:T(8,128)S(1)} %get-tuple-element.78.refs_0_, f32[64,128]{1,0:T(8,128)S(1)} %collective-permute-done.7.refs_1_, ...), custom_call_target="tpu_custom_call", output_to_operand_aliasing={{}: (11, {})} | custom-call | tf_op jit(solution)/shard_map/pallas_call | solution.py:31
  41.5 0.7 shard_map.127.refs_0_
  42.2 0.7 collective-permute-start.17
  42.8 0.9 %collective-permute-start.16 = (f32[64,128]{1,0:T(8,128)S(1)}, f32[64,128]{1,0:T(8,128)S(1)}, u32[]{:S(2)}, u32[]{:S(2)}) collective-permute-start(f32[64,128]{1,0:T(8,128)S(1)} %shard_map.127.refs_0_), channel_id=1, source_target_pairs={{0,2},{1,3},{2,0},{3,1},{4,6},{5,7},{6,4},{7,5},{8,10},{9,11},{10,... | collective-permute-start | bytes 98312 | tf_op jit(solution)/shard_map/ppermute | solution.py:613
  43.7 0.4 collective-permute-start.15
  44.1 4.3 %collective-permute-done.10.near_ref = bf16[4,3,64,128]{3,2,1,0:T(8,128)(2,1)S(1)} collective-permute-done((bf16[4,3,64,128]{3,2,1,0:T(8,128)(2,1)S(1)}, bf16[4,3,64,128]{3,2,1,0:T(8,128)(2,1)S(1)}, u32[]{:S(2)}, u32[]{:S(2)}) %collective-permute-start.10) | collective-permute-done | bytes 196640 | tf_op jit(solution)/shard_map/ppermute | solution.py:568
  48.4 0.8 %shard_map.126 = (f32[24,3,64,128]{3,2,1,0:T(8,128)S(1)}, f32[64,128]{1,0:T(8,128)S(1)}) custom-call(s32[8,16]{1,0:T(8,128)S(1)} %bitcast.49, s32[1,16]{1,0:T(1,128)S(1)} %bitcast.63, bf16[4,3,64,128]{3,2,1,0:T(8,128)(2,1)S(1)} %collective-permute-done.10.near_ref, ...), custom_call_target="tpu_custom_call", output_to_operand_aliasing={{0}: (4, {})} | custom-call | tf_op jit(solution)/shard_map/pallas_call | solution.py:31
  49.2 0.1 collective-permute-start.14
  49.3 1.2 %collective-permute-start.13 = (f32[64,128]{1,0:T(8,128)S(1)}, f32[64,128]{1,0:T(8,128)S(1)}, u32[]{:S(2)}, u32[]{:S(2)}) collective-permute-start(f32[64,128]{1,0:T(8,128)S(1)} %get-tuple-element.83.refs_0_), channel_id=1, source_target_pairs={{0,2},{1,3},{2,0},{3,1},{4,6},{5,7},{6,4},{7,5},{8,10},{9,11},{10,... | collective-permute-start | bytes 98312 | tf_op jit(solution)/shard_map/ppermute | solution.py:613
  50.6 0.6 collective-permute-start.12
  51.2 2.8 %shard_map.128 = (f32[16,3,64,128]{3,2,1,0:T(8,128)}, f32[8,96,128]{2,1,0:T(8,128)S(1)}) custom-call(s32[8,16]{1,0:T(8,128)S(1)} %bitcast.50, s32[1,16]{1,0:T(1,128)S(1)} %bitcast.64, f32[64,128]{1,0:T(8,128)S(1)} %shard_map.127.refs_0_, f32[64,128]{1,0:T(8,128)S(1)} %collective-permute-done.15.refs_1_, f32[64,128]{1,0:T(8,128)S(1)} %collective-permute-done.16.refs_2_, ...), custom_call_target="tpu_custom_call" | custom-call | tf_op jit(solution)/shard_map/pallas_call | solution.py:31
  54.0 0.0 copy-start.1
  54.0 2.9 %shard_map.129 = (f32[16,3,64,128]{3,2,1,0:T(8,128)}, bf16[8,96,128]{2,1,0:T(8,128)(2,1)S(1)}, f32[8,96,128]{2,1,0:T(8,128)S(1)}) custom-call(s32[8,16]{1,0:T(8,128)S(1)} %bitcast.51, s32[1,16]{1,0:T(1,128)S(1)} %bitcast.65, f32[64,128]{1,0:T(8,128)S(1)} %get-tuple-element.83.refs_0_, ...), custom_call_target="tpu_custom_call", output_to_operand_aliasing={{0}: (12, {}), {2}: (13, {})} | custom-call | tf_op jit(solution)/shard_map/pallas_call | solution.py:31
  56.9 14.1 %all_to_all.5.received_ref = bf16[8,96,128]{2,1,0:T(8,128)(2,1)S(1)} all-to-all(bf16[8,96,128]{2,1,0:T(8,128)(2,1)S(1)} %get-tuple-element.89), channel_id=1, replica_groups=mesh['gran'=8,'band'=4] {'gran'}, dimensions={0} | all-to-all | bytes 393216 | tf_op jit(solution)/shard_map/all_to_all | solution.py:689
  71.0 2.6 %shard_map.130 = bf16[1,3,256,256]{3,2,1,0:T(8,128)(2,1)} custom-call(s32[2,128]{1,0:T(2,128)S(1)} %bitcast.67, bf16[8,96,128]{2,1,0:T(8,128)(2,1)S(1)} %all_to_all.5.received_ref, bf16[256,1024]{1,0:T(8,128)(2,1)S(1)} %get-tuple-element.90.row_ref, bf16[256,1024]{1,0:T(8,128)(2,1)S(1)} %get-tuple-element.91.col_ref, bf16[1,3,256,256]{3,2,1,0:T(8,128)(2,1)S(1)} %copy-done.1), custom_call_target="tpu_custom_call" | custom-call | tf_op jit(solution)/shard_map/pallas_call | solution.py:31
  (17 shorter events, 0.0 us)
Async XLA Ops:
  1.9 5.2 %copy-start = (s32[16,8]{0,1:T(8,128)S(1)}, s32[16,8]{0,1:T(8,128)}, u32[]{:S(2)}) copy-start(s32[16,8]{0,1:T(8,128)} %param.15) | copy-start | bytes 1540
  2.0 5.2 %copy-start.2 = (s32[16]{0:T(128)S(1)}, s32[16]{0:T(128)}, u32[]{:S(2)}) copy-start(s32[16]{0:T(128)} %param.16) | copy-start | bytes 196
  2.0 11.4 %collective-permute-start = (bf16[4,3,64,128]{3,2,1,0:T(8,128)(2,1)S(1)}, bf16[4,3,64,128]{3,2,1,0:T(8,128)(2,1)S(1)}, u32[]{:S(2)}, u32[]{:S(2)}) collective-permute-start(bf16[4,3,64,128]{3,2,1,0:T(8,128)(2,1)S(1)} %get-tuple-element.47), channel_id=1, source_target_pairs={{0,4},{4,0},{8,12},{12,8},{16,20},{20,16},{24,28},{28,24},{1,5},{5... | collective-permute-start | bytes 589832 | tf_op jit(solution)/shard_map/ppermute | solution.py:568
  5.0 8.4 %collective-permute-start.1 = (bf16[4,3,64,128]{3,2,1,0:T(8,128)(2,1)S(1)}, bf16[4,3,64,128]{3,2,1,0:T(8,128)(2,1)S(1)}, u32[]{:S(2)}, u32[]{:S(2)}) collective-permute-start(bf16[4,3,64,128]{3,2,1,0:T(8,128)(2,1)S(1)} %get-tuple-element.48), channel_id=1, source_target_pairs={{4,8},{8,4},{12,16},{16,12},{20,24},{24,20},{5,9},{9,5},{13,17},{1... | collective-permute-start | bytes 589832 | tf_op jit(solution)/shard_map/ppermute | solution.py:567
  14.2 3.7 %collective-permute-start.4 = (f32[64,128]{1,0:T(8,128)S(1)}, f32[64,128]{1,0:T(8,128)S(1)}, u32[]{:S(2)}, u32[]{:S(2)}) collective-permute-start(f32[64,128]{1,0:T(8,128)S(1)} %get-tuple-element.54.refs_0_), channel_id=1, source_target_pairs={{0,3},{1,2},{2,1},{3,0},{4,7},{5,6},{6,5},{7,4},{8,11},{9,10},{10,... | collective-permute-start | bytes 98312 | tf_op jit(solution)/shard_map/ppermute | solution.py:613
  14.3 4.0 %collective-permute-start.3 = (f32[64,128]{1,0:T(8,128)S(1)}, f32[64,128]{1,0:T(8,128)S(1)}, u32[]{:S(2)}, u32[]{:S(2)}) collective-permute-start(f32[64,128]{1,0:T(8,128)S(1)} %get-tuple-element.54.refs_0_), channel_id=1, source_target_pairs={{0,2},{1,3},{2,0},{3,1},{4,6},{5,7},{6,4},{7,5},{8,10},{9,11},{10,... | collective-permute-start | bytes 98312 | tf_op jit(solution)/shard_map/ppermute | solution.py:613
  15.9 2.4 %collective-permute-start.2 = (f32[64,128]{1,0:T(8,128)S(1)}, f32[64,128]{1,0:T(8,128)S(1)}, u32[]{:S(2)}, u32[]{:S(2)}) collective-permute-start(f32[64,128]{1,0:T(8,128)S(1)} %get-tuple-element.54.refs_0_), channel_id=1, source_target_pairs={{0,1},{1,0},{2,3},{3,2},{4,5},{5,4},{6,7},{7,6},{8,9},{9,8},{10,11... | collective-permute-start | bytes 98312 | tf_op jit(solution)/shard_map/ppermute | solution.py:613
  19.6 11.3 %collective-permute-start.5 = (bf16[4,3,64,128]{3,2,1,0:T(8,128)(2,1)S(1)}, bf16[4,3,64,128]{3,2,1,0:T(8,128)(2,1)S(1)}, u32[]{:S(2)}, u32[]{:S(2)}) collective-permute-start(bf16[4,3,64,128]{3,2,1,0:T(8,128)(2,1)S(1)} %get-tuple-element.60), channel_id=1, source_target_pairs={{0,4},{4,0},{8,12},{12,8},{16,20},{20,16},{24,28},{28,24},{1,5},{5... | collective-permute-start | bytes 589832 | tf_op jit(solution)/shard_map/ppermute | solution.py:568
  22.0 8.9 %collective-permute-start.6 = (bf16[4,3,64,128]{3,2,1,0:T(8,128)(2,1)S(1)}, bf16[4,3,64,128]{3,2,1,0:T(8,128)(2,1)S(1)}, u32[]{:S(2)}, u32[]{:S(2)}) collective-permute-start(bf16[4,3,64,128]{3,2,1,0:T(8,128)(2,1)S(1)} %get-tuple-element.61), channel_id=1, source_target_pairs={{4,8},{8,4},{12,16},{16,12},{20,24},{24,20},{5,9},{9,5},{13,17},{1... | collective-permute-start | bytes 589832 | tf_op jit(solution)/shard_map/ppermute | solution.py:567
  26.5 7.2 %copy-start.3 = (s32[128,2]{0,1:T(2,128)S(1)}, s32[128,2]{0,1:T(2,128)}, u32[]{:S(2)}) copy-start(s32[128,2]{0,1:T(2,128)} %param.17) | copy-start | bytes 3076
  26.5 7.1 %copy-start.4 = (s32[128,2,2]{0,2,1:T(2,128)S(1)}, s32[128,2,2]{0,2,1:T(2,128)}, u32[]{:S(2)}) copy-start(s32[128,2,2]{0,2,1:T(2,128)} %param.18) | copy-start | bytes 6148
  31.7 3.7 %collective-permute-start.9 = (f32[64,128]{1,0:T(8,128)S(1)}, f32[64,128]{1,0:T(8,128)S(1)}, u32[]{:S(2)}, u32[]{:S(2)}) collective-permute-start(f32[64,128]{1,0:T(8,128)S(1)} %get-tuple-element.78.refs_0_), channel_id=1, source_target_pairs={{0,3},{1,2},{2,1},{3,0},{4,7},{5,6},{6,5},{7,4},{8,11},{9,10},{10,... | collective-permute-start | bytes 98312 | tf_op jit(solution)/shard_map/ppermute | solution.py:613
  31.8 4.2 %collective-permute-start.8 = (f32[64,128]{1,0:T(8,128)S(1)}, f32[64,128]{1,0:T(8,128)S(1)}, u32[]{:S(2)}, u32[]{:S(2)}) collective-permute-start(f32[64,128]{1,0:T(8,128)S(1)} %get-tuple-element.78.refs_0_), channel_id=1, source_target_pairs={{0,2},{1,3},{2,0},{3,1},{4,6},{5,7},{6,4},{7,5},{8,10},{9,11},{10,... | collective-permute-start | bytes 98312 | tf_op jit(solution)/shard_map/ppermute | solution.py:613
  32.9 3.2 %collective-permute-start.7 = (f32[64,128]{1,0:T(8,128)S(1)}, f32[64,128]{1,0:T(8,128)S(1)}, u32[]{:S(2)}, u32[]{:S(2)}) collective-permute-start(f32[64,128]{1,0:T(8,128)S(1)} %get-tuple-element.78.refs_0_), channel_id=1, source_target_pairs={{0,1},{1,0},{2,3},{3,2},{4,5},{5,4},{6,7},{7,6},{8,9},{9,8},{10,11... | collective-permute-start | bytes 98312 | tf_op jit(solution)/shard_map/ppermute | solution.py:613
  37.4 11.0 %collective-permute-start.10 = (bf16[4,3,64,128]{3,2,1,0:T(8,128)(2,1)S(1)}, bf16[4,3,64,128]{3,2,1,0:T(8,128)(2,1)S(1)}, u32[]{:S(2)}, u32[]{:S(2)}) collective-permute-start(bf16[4,3,64,128]{3,2,1,0:T(8,128)(2,1)S(1)} %get-tuple-element.80), channel_id=1, source_target_pairs={{0,4},{4,0},{8,12},{12,8},{16,20},{20,16},{24,28},{28,24},{1,5},{5... | collective-permute-start | bytes 589832 | tf_op jit(solution)/shard_map/ppermute | solution.py:568
  39.7 8.7 %collective-permute-start.11 = (bf16[4,3,64,128]{3,2,1,0:T(8,128)(2,1)S(1)}, bf16[4,3,64,128]{3,2,1,0:T(8,128)(2,1)S(1)}, u32[]{:S(2)}, u32[]{:S(2)}) collective-permute-start(bf16[4,3,64,128]{3,2,1,0:T(8,128)(2,1)S(1)} %get-tuple-element.81), channel_id=1, source_target_pairs={{4,8},{8,4},{12,16},{16,12},{20,24},{24,20},{5,9},{9,5},{13,17},{1... | collective-permute-start | bytes 589832 | tf_op jit(solution)/shard_map/ppermute | solution.py:567
  42.2 8.4 %collective-permute-start.17 = (f32[64,128]{1,0:T(8,128)S(1)}, f32[64,128]{1,0:T(8,128)S(1)}, u32[]{:S(2)}, u32[]{:S(2)}) collective-permute-start(f32[64,128]{1,0:T(8,128)S(1)} %shard_map.127.refs_0_), channel_id=1, source_target_pairs={{0,3},{1,2},{2,1},{3,0},{4,7},{5,6},{6,5},{7,4},{8,11},{9,10},{10,... | collective-permute-start | bytes 98312 | tf_op jit(solution)/shard_map/ppermute | solution.py:613
  42.8 8.3 %collective-permute-start.16 = (f32[64,128]{1,0:T(8,128)S(1)}, f32[64,128]{1,0:T(8,128)S(1)}, u32[]{:S(2)}, u32[]{:S(2)}) collective-permute-start(f32[64,128]{1,0:T(8,128)S(1)} %shard_map.127.refs_0_), channel_id=1, source_target_pairs={{0,2},{1,3},{2,0},{3,1},{4,6},{5,7},{6,4},{7,5},{8,10},{9,11},{10,... | collective-permute-start | bytes 98312 | tf_op jit(solution)/shard_map/ppermute | solution.py:613
  43.7 7.5 %collective-permute-start.15 = (f32[64,128]{1,0:T(8,128)S(1)}, f32[64,128]{1,0:T(8,128)S(1)}, u32[]{:S(2)}, u32[]{:S(2)}) collective-permute-start(f32[64,128]{1,0:T(8,128)S(1)} %shard_map.127.refs_0_), channel_id=1, source_target_pairs={{0,1},{1,0},{2,3},{3,2},{4,5},{5,4},{6,7},{7,6},{8,9},{9,8},{10,11... | collective-permute-start | bytes 98312 | tf_op jit(solution)/shard_map/ppermute | solution.py:613
  49.2 4.7 %collective-permute-start.14 = (f32[64,128]{1,0:T(8,128)S(1)}, f32[64,128]{1,0:T(8,128)S(1)}, u32[]{:S(2)}, u32[]{:S(2)}) collective-permute-start(f32[64,128]{1,0:T(8,128)S(1)} %get-tuple-element.83.refs_0_), channel_id=1, source_target_pairs={{0,3},{1,2},{2,1},{3,0},{4,7},{5,6},{6,5},{7,4},{8,11},{9,10},{10,... | collective-permute-start | bytes 98312 | tf_op jit(solution)/shard_map/ppermute | solution.py:613
  49.3 4.7 %collective-permute-start.13 = (f32[64,128]{1,0:T(8,128)S(1)}, f32[64,128]{1,0:T(8,128)S(1)}, u32[]{:S(2)}, u32[]{:S(2)}) collective-permute-start(f32[64,128]{1,0:T(8,128)S(1)} %get-tuple-element.83.refs_0_), channel_id=1, source_target_pairs={{0,2},{1,3},{2,0},{3,1},{4,6},{5,7},{6,4},{7,5},{8,10},{9,11},{10,... | collective-permute-start | bytes 98312 | tf_op jit(solution)/shard_map/ppermute | solution.py:613
  50.6 3.4 %collective-permute-start.12 = (f32[64,128]{1,0:T(8,128)S(1)}, f32[64,128]{1,0:T(8,128)S(1)}, u32[]{:S(2)}, u32[]{:S(2)}) collective-permute-start(f32[64,128]{1,0:T(8,128)S(1)} %get-tuple-element.83.refs_0_), channel_id=1, source_target_pairs={{0,1},{1,0},{2,3},{3,2},{4,5},{5,4},{6,7},{7,6},{8,9},{9,8},{10,11... | collective-permute-start | bytes 98312 | tf_op jit(solution)/shard_map/ppermute | solution.py:613
  54.0 17.0 %copy-start.1 = (bf16[1,3,256,256]{3,2,1,0:T(8,128)(2,1)S(1)}, bf16[1,3,256,256]{3,2,1,0:T(8,128)(2,1)}, u32[]{:S(2)}) copy-start(bf16[1,3,256,256]{3,2,1,0:T(8,128)(2,1)} %pixels_ref.1) | copy-start | bytes 1179652

commit v6 on v5

--- a/solution.py
+++ b/solution.py
@@ -268,7 +268,7 @@
         return tuple(new_sigma), tuple(new_drive)
 
     zero = jnp.zeros((8, LANES), f32)
-    sigma, drive = lax.fori_loop(0, graph[1, i], slot, ((zero,) * len(parts), rhs))
+    sigma, drive = lax.fori_loop(1, graph[1, i], slot, slot(0, ((zero,) * len(parts), rhs)))
     for k, (b, j) in enumerate(parts):
         first, second = (
             diag_ref[at, b, pl.ds(2 * j + c, 8, stride=8), :] + sigma[k] for c in range(2)
@@ -329,11 +329,11 @@
 
 def last_sweep(interior, offset_ref, count_ref, *refs):
     shares, state, place_ref = refs[:4], refs[4:9], refs[9]
-    weights, graph, solved, sems = refs[-4:]
+    weights, graph = refs[-2:]
     if interior:
-        out_ref, windows = refs[10:12]
+        solved, windows = refs[10:12]
     else:
-        out_ref, send_ref, windows = refs[12:15]
+        solved, send_ref, windows = refs[12:15]
     granules, bands = solved.shape[:2]
     read_graph(offset_ref, count_ref, graph)
     if interior:
@@ -351,29 +351,32 @@
         return carry
 
     lax.fori_loop(*((REACH, granules - REACH) if interior else (0, 2 * REACH)), step, 0)
-    parts = ((REACH, granules - 2 * REACH),) if interior else ((0, REACH), (granules - REACH, REACH))
-    copies = []
-    for n, (first, size) in enumerate(parts):
-        part = pl.ds(first, size)
-        copies.append(pltpu.make_async_copy(solved.at[part], out_ref.at[part], sems.at[n]))
-        copies[n].start()
     lane = lax.broadcasted_iota(jnp.int32, (8, LANES), 1) // SPAN
+    seats = LANES // SPAN
     places = place_ref[...]
     for i in visits(granules, interior):
         for r in range(2):
             owner, rank, top, turn = (places[k, r * granules + i] for k in range(4))
-            here = lane == rank
+            here = [lane == jnp.bitwise_and(rank + half * (KN // SPAN), seats - 1) for half in (0, 1)]
             for b in range(bands):
                 for c in range(2):
                     rows = solved[i, b, pl.ds(2 * top + c, 8, stride=2), :]
+                    moved = pltpu.roll(rows, jnp.bitwise_and(turn, LANES - 1), 1)
                     for half in (0, 1):
                         at = 16 * (2 * b + c) + 8 * half
-                        moved = pltpu.roll(rows, jnp.bitwise_and(turn + KN * half, LANES - 1), 1)
-                        pltpu.store(windows.at[owner, at : at + 8, :], moved, mask=here)
+                        pltpu.store(windows.at[owner, at : at + 8, :], moved, mask=here[half])
     if not interior:
-        send_ref[...] = windows[...].astype(bf16)
-    for copy in copies:
-        copy.wait()
+        for owner in range(windows.shape[0]):
+            for at in range(0, windows.shape[1], 16):
+                odd = pltpu.roll(windows[owner, at + 8 : at + 16, :], KN, 1)
+                both = jnp.concatenate([windows[owner, at : at + 8, :], odd], axis=0)
+                send_ref[owner, at : at + 16, :] = both.astype(bf16)
+
+
+def copy_out(solved, out_ref, sem):
+    copy = pltpu.make_async_copy(solved, out_ref, sem)
+    copy.start()
+    copy.wait()
 
 
 def earlier(first, second, granules):
@@ -665,28 +668,24 @@
                 aliases={len(inputs): 0},
             )
     windows = (device_total, 2 * bands * SPAN, LANES)
-    scratch = [
-        weights,
-        scalars,
-        pltpu.VMEM(own, f32),
-        pltpu.SemaphoreType.DMA((2,)),
-    ]
+    scratch = [weights, scalars]
     inputs = graph + inner_shares + [("v", extended)] + inner_state + [("v", places)]
     balanced, gathered_windows = call(
         functools.partial(last_sweep, True),
         inputs,
-        [("h", own, f32), ("v", windows, f32)],
+        [("v", own, f32), ("v", windows, f32)],
         scratch,
     )
-    inputs = graph + shares + edge_state_now + [("v", places)] + [("h", balanced), ("v", gathered_windows)]
+    inputs = graph + shares + edge_state_now + [("v", places)] + [("v", balanced), ("v", gathered_windows)]
     balanced, payload, _ = call(
         functools.partial(last_sweep, False),
         inputs,
-        [("h", own, f32), ("v", windows, bf16), ("v", windows, f32)],
+        [("v", own, f32), ("v", windows, bf16), ("v", windows, f32)],
         scratch,
         aliases={len(inputs) - 2: 0, len(inputs) - 1: 2},
     )
     received = lax.all_to_all(payload, "gran", split_axis=0, concat_axis=0, tiled=True)
+    (balanced,) = call(copy_out, [("v", balanced)], [("h", own, f32)], [pltpu.SemaphoreType.DMA])
     (corrected,) = call(
         compose,
         [tiles[0], ("v", received), ("v", row_weights), ("v", col_weights), ("v", tile_pixels)],

time: 73.4 us -> 72.7 us (level)
  blocking collectives: 14.1 us -> 0 us
  waiting for transfers between devices: 13.2 us -> 21.2 us
  starting transfers between devices: 17.4 us -> 23.6 us
  Pallas kernels: 28 us -> 26.9 us
    all_to_all x1 -> x0, blocking collectives: 14.1 us -> none  [per_device(): lax.all_to_all(payload, 'gran', split_axis=0, concat_axis=0, tiled=True)]
    all_to_all x0 -> x1, waiting for transfers between devices: none -> 7.08 us  [per_device(): lax.all_to_all(payload, 'gran', split_axis=0, concat_axis=0, tiled=True)]
    all_to_all x0 -> x1, starting transfers between devices: none -> 6.48 us  [per_device(): lax.all_to_all(payload, 'gran', split_axis=0, concat_axis=0, tiled=True)]
    pallas_call x18 -> x19, Pallas kernels: 28 us -> 26.9 us  [call(): pl.pallas_call(body, in_specs=[ON_CHIP if kind == 'v' else ANYWHERE for k...]
    ppermute x12, waiting for transfers between devices: 2.79 us -> 3.65 us  [over_band(): lax.ppermute(partial, 'band', [(i, i ^ flip) for i in range(band_total)])]
  transfers between devices with their start and end apart: 18 -> 19, of which waited for: 6 -> 9; matrix products, arithmetic and copies ran while one was open for 0% -> 0% of each run, Pallas kernels for 23% -> 23%
where the time goes in v6:
time: 72.7 us; the launch traced here: 72.6 us
  Pallas kernels  26.9 us (37%)
  starting transfers between devices  23.6 us (32%)
  waiting for transfers between devices  21.2 us (29%)
  between operations  0.87 us (1%)
    pallas_call x19, Pallas kernels, call(): pl.pallas_call(body, in_specs=[ON_CHIP if kind == 'v' else ANYWHERE for k...  26.9 us
    ppermute x3, waiting for transfers between devices, exchange(): near = lax.ppermute(near, 'gran', near_pairs)  10.5 us
    ppermute x12, starting transfers between devices, over_band(): lax.ppermute(partial, 'band', [(i, i ^ flip) for i in range(band_total)])  7.68 us
    ppermute x3, starting transfers between devices, exchange(): near = lax.ppermute(near, 'gran', near_pairs)  7.41 us
    all_to_all x1, waiting for transfers between devices, per_device(): lax.all_to_all(payload, 'gran', split_axis=0, concat_axis=0, tiled=True)  7.08 us
    all_to_all x1, starting transfers between devices, per_device(): lax.all_to_all(payload, 'gran', split_axis=0, concat_axis=0, tiled=True)  6.48 us
    ppermute x12, waiting for transfers between devices, over_band(): lax.ppermute(partial, 'band', [(i, i ^ flip) for i in range(band_total)])  3.65 us
    ppermute x3, starting transfers between devices, exchange(): far = lax.ppermute(far, 'gran', far_pairs)  1.98 us
  transfers between devices with their start and end apart: 19, of which 9 were waited for; matrix products, arithmetic and copies ran while one was open for 0% of the time, Pallas kernels for 23%

profile of v6, /device:TPU:0, one launch (start us, length us, event | category | flops | bytes accessed | tf_op | source)
XLA Modules:
  0.0 72.6 jit_solution(1124238712730518425)
XLA Ops:
  0.6 1.3 %shard_map.113 = (bf16[4,3,64,128]{3,2,1,0:T(8,128)(2,1)S(1)}, bf16[4,3,64,128]{3,2,1,0:T(8,128)(2,1)S(1)}) custom-call(f32[16,3,64,128]{3,2,1,0:T(8,128)} %bitcast.71), custom_call_target="tpu_custom_call" | custom-call | tf_op jit(solution)/shard_map/pallas_call | solution.py:31
  2.0 0.0 copy-start.2
  2.0 3.0 %collective-permute-start = (bf16[4,3,64,128]{3,2,1,0:T(8,128)(2,1)S(1)}, bf16[4,3,64,128]{3,2,1,0:T(8,128)(2,1)S(1)}, u32[]{:S(2)}, u32[]{:S(2)}) collective-permute-start(bf16[4,3,64,128]{3,2,1,0:T(8,128)(2,1)S(1)} %get-tuple-element.47), channel_id=1, source_target_pairs={{0,4},{4,0},{8,12},{12,8},{16,20},{20,16},{24,28},{28,24},{1,5},{5... | collective-permute-start | bytes 589832 | tf_op jit(solution)/shard_map/ppermute | solution.py:571
  5.0 0.7 collective-permute-start.1
  5.6 1.5 %shard_map.114.ext_ref.refs_0_ = f32[24,3,64,128]{3,2,1,0:T(8,128)S(1)} custom-call(f32[16,3,64,128]{3,2,1,0:T(8,128)} %bitcast.72), custom_call_target="tpu_custom_call" | custom-call | tf_op jit(solution)/shard_map/pallas_call | solution.py:31
  7.1 0.7 shard_map.115.refs_1_
  7.8 3.0 %shard_map.116 = (f32[8,3,64,128]{3,2,1,0:T(8,128)S(1)}, f32[8,3,64,128]{3,2,1,0:T(8,128)S(1)}, f32[8,3,32,128]{3,2,1,0:T(8,128)S(1)}, f32[8,8,3,32,128]{4,3,2,1,0:T(8,128)S(1)}) custom-call(s32[8,16]{1,0:T(8,128)S(1)} %bitcast.39, s32[1,16]{1,0:T(1,128)S(1)} %bitcast.53, f32[16,3,64,128]{3,2,1,0:T(8,128)} %bitcast.73, f32[16,3,64,128]{3,2,1,0:T(8,128)} %bitcast.75, ...), custom_call_target="tpu_custom_call" | custom-call | tf_op jit(solution)/shard_map/pallas_call | solution.py:31
  10.9 2.5 %collective-permute-done.near_ref = bf16[4,3,64,128]{3,2,1,0:T(8,128)(2,1)S(1)} collective-permute-done((bf16[4,3,64,128]{3,2,1,0:T(8,128)(2,1)S(1)}, bf16[4,3,64,128]{3,2,1,0:T(8,128)(2,1)S(1)}, u32[]{:S(2)}, u32[]{:S(2)}) %collective-permute-start) | collective-permute-done | bytes 196640 | tf_op jit(solution)/shard_map/ppermute | solution.py:571
  13.4 0.9 %shard_map.117 = (f32[24,3,64,128]{3,2,1,0:T(8,128)S(1)}, f32[64,128]{1,0:T(8,128)S(1)}) custom-call(s32[8,16]{1,0:T(8,128)S(1)} %bitcast.40, s32[1,16]{1,0:T(1,128)S(1)} %bitcast.54, bf16[4,3,64,128]{3,2,1,0:T(8,128)(2,1)S(1)} %collective-permute-done.near_ref, ...), custom_call_target="tpu_custom_call", output_to_operand_aliasing={{0}: (4, {})} | custom-call | tf_op jit(solution)/shard_map/pallas_call | solution.py:31
  14.2 0.1 collective-permute-start.4
  14.3 1.6 %collective-permute-start.3 = (f32[64,128]{1,0:T(8,128)S(1)}, f32[64,128]{1,0:T(8,128)S(1)}, u32[]{:S(2)}, u32[]{:S(2)}) collective-permute-start(f32[64,128]{1,0:T(8,128)S(1)} %get-tuple-element.54.refs_0_), channel_id=1, source_target_pairs={{0,2},{1,3},{2,0},{3,1},{4,6},{5,7},{6,4},{7,5},{8,10},{9,11},{10,... | collective-permute-start | bytes 98312 | tf_op jit(solution)/shard_map/ppermute | solution.py:616
  15.9 0.3 collective-permute-start.2
  16.1 1.8 %collective-permute-done.4.refs_3_ = f32[64,128]{1,0:T(8,128)S(1)} collective-permute-done((f32[64,128]{1,0:T(8,128)S(1)}, f32[64,128]{1,0:T(8,128)S(1)}, u32[]{:S(2)}, u32[]{:S(2)}) %collective-permute-start.4) | collective-permute-done | bytes 32800 | tf_op jit(solution)/shard_map/ppermute | solution.py:616
  17.9 0.4 collective-permute-done.3.refs_2_
  18.3 1.2 %shard_map.118 = (f32[24,3,64,128]{3,2,1,0:T(8,128)S(1)}, bf16[4,3,64,128]{3,2,1,0:T(8,128)(2,1)S(1)}, bf16[4,3,64,128]{3,2,1,0:T(8,128)(2,1)S(1)}) custom-call(s32[8,16]{1,0:T(8,128)S(1)} %bitcast.41, s32[1,16]{1,0:T(1,128)S(1)} %bitcast.55, f32[64,128]{1,0:T(8,128)S(1)} %get-tuple-element.54.refs_0_, f32[64,128]{1,0:T(8,128)S(1)} %collective-permute-done.2.refs_1_, ...), custom_call_target="tpu_custom_call" | custom-call | tf_op jit(solution)/shard_map/pallas_call | solution.py:31
  19.6 2.2 %collective-permute-start.5 = (bf16[4,3,64,128]{3,2,1,0:T(8,128)(2,1)S(1)}, bf16[4,3,64,128]{3,2,1,0:T(8,128)(2,1)S(1)}, u32[]{:S(2)}, u32[]{:S(2)}) collective-permute-start(bf16[4,3,64,128]{3,2,1,0:T(8,128)(2,1)S(1)} %get-tuple-element.60), channel_id=1, source_target_pairs={{0,4},{4,0},{8,12},{12,8},{16,20},{20,16},{24,28},{28,24},{1,5},{5... | collective-permute-start | bytes 589832 | tf_op jit(solution)/shard_map/ppermute | solution.py:571
  21.8 0.7 collective-permute-start.6
  22.4 2.8 %shard_map.119 = (f32[8,3,64,128]{3,2,1,0:T(8,128)S(1)}, f32[8,3,64,128]{3,2,1,0:T(8,128)S(1)}, f32[8,3,32,128]{3,2,1,0:T(8,128)S(1)}, f32[8,8,3,32,128]{4,3,2,1,0:T(8,128)S(1)}) custom-call(s32[8,16]{1,0:T(8,128)S(1)} %bitcast.42, s32[1,16]{1,0:T(1,128)S(1)} %bitcast.56, f32[16,3,64,128]{3,2,1,0:T(8,128)} %bitcast.74, f32[16,3,64,128]{3,2,1,0:T(8,128)} %bitcast.76, ...), custom_call_target="tpu_custom_call" | custom-call | tf_op jit(solution)/shard_map/pallas_call | solution.py:31
  25.2 1.0 %shard_map.120.ext_ref.refs_0_ = f32[24,3,64,128]{3,2,1,0:T(8,128)S(1)} custom-call(s32[8,16]{1,0:T(8,128)S(1)} %bitcast.43, s32[1,16]{1,0:T(1,128)S(1)} %bitcast.57, f32[64,128]{1,0:T(8,128)S(1)} %get-tuple-element.54.refs_0_, f32[64,128]{1,0:T(8,128)S(1)} %collective-permute-done.2.refs_1_, ...), custom_call_target="tpu_custom_call", output_to_operand_aliasing={{}: (11, {})} | custom-call | tf_op jit(solution)/shard_map/pallas_call | solution.py:31
  26.3 0.7 shard_map.121.refs_1_
  27.0 3.7 %collective-permute-done.5.near_ref = bf16[4,3,64,128]{3,2,1,0:T(8,128)(2,1)S(1)} collective-permute-done((bf16[4,3,64,128]{3,2,1,0:T(8,128)(2,1)S(1)}, bf16[4,3,64,128]{3,2,1,0:T(8,128)(2,1)S(1)}, u32[]{:S(2)}, u32[]{:S(2)}) %collective-permute-start.5) | collective-permute-done | bytes 196640 | tf_op jit(solution)/shard_map/ppermute | solution.py:571
  30.7 0.9 %shard_map.122 = (f32[24,3,64,128]{3,2,1,0:T(8,128)S(1)}, f32[64,128]{1,0:T(8,128)S(1)}) custom-call(s32[8,16]{1,0:T(8,128)S(1)} %bitcast.45, s32[1,16]{1,0:T(1,128)S(1)} %bitcast.59, bf16[4,3,64,128]{3,2,1,0:T(8,128)(2,1)S(1)} %collective-permute-done.5.near_ref, ...), custom_call_target="tpu_custom_call", output_to_operand_aliasing={{0}: (4, {})} | custom-call | tf_op jit(solution)/shard_map/pallas_call | solution.py:31
  31.5 0.1 collective-permute-start.9
  31.6 1.1 %collective-permute-start.8 = (f32[64,128]{1,0:T(8,128)S(1)}, f32[64,128]{1,0:T(8,128)S(1)}, u32[]{:S(2)}, u32[]{:S(2)}) collective-permute-start(f32[64,128]{1,0:T(8,128)S(1)} %get-tuple-element.78.refs_0_), channel_id=1, source_target_pairs={{0,2},{1,3},{2,0},{3,1},{4,6},{5,7},{6,4},{7,5},{8,10},{9,11},{10,... | collective-permute-start | bytes 98312 | tf_op jit(solution)/shard_map/ppermute | solution.py:616
  32.7 0.8 %collective-permute-start.7 = (f32[64,128]{1,0:T(8,128)S(1)}, f32[64,128]{1,0:T(8,128)S(1)}, u32[]{:S(2)}, u32[]{:S(2)}) collective-permute-start(f32[64,128]{1,0:T(8,128)S(1)} %get-tuple-element.78.refs_0_), channel_id=1, source_target_pairs={{0,1},{1,0},{2,3},{3,2},{4,5},{5,4},{6,7},{7,6},{8,9},{9,8},{10,11... | collective-permute-start | bytes 98312 | tf_op jit(solution)/shard_map/ppermute | solution.py:616
  33.4 1.8 %shard_map.123 = (bf16[256,1024]{1,0:T(8,128)(2,1)S(1)}, bf16[256,1024]{1,0:T(8,128)(2,1)S(1)}, s32[8,128]{1,0:T(8,128)S(1)}) custom-call(s32[2,128]{1,0:T(2,128)S(1)} %bitcast.66, s32[2,2,128]{2,1,0:T(2,128)S(1)} %bitcast.68), custom_call_target="tpu_custom_call" | custom-call | tf_op jit(solution)/shard_map/pallas_call | solution.py:31
  35.2 0.6 collective-permute-done.8.refs_2_
  35.8 1.2 %shard_map.124 = (f32[24,3,64,128]{3,2,1,0:T(8,128)S(1)}, bf16[4,3,64,128]{3,2,1,0:T(8,128)(2,1)S(1)}, bf16[4,3,64,128]{3,2,1,0:T(8,128)(2,1)S(1)}) custom-call(s32[8,16]{1,0:T(8,128)S(1)} %bitcast.46, s32[1,16]{1,0:T(1,128)S(1)} %bitcast.60, f32[64,128]{1,0:T(8,128)S(1)} %get-tuple-element.78.refs_0_, f32[64,128]{1,0:T(8,128)S(1)} %collective-permute-done.7.refs_1_, ...), custom_call_target="tpu_custom_call" | custom-call | tf_op jit(solution)/shard_map/pallas_call | solution.py:31
  37.1 2.2 %collective-permute-start.10 = (bf16[4,3,64,128]{3,2,1,0:T(8,128)(2,1)S(1)}, bf16[4,3,64,128]{3,2,1,0:T(8,128)(2,1)S(1)}, u32[]{:S(2)}, u32[]{:S(2)}) collective-permute-start(bf16[4,3,64,128]{3,2,1,0:T(8,128)(2,1)S(1)} %get-tuple-element.80), channel_id=1, source_target_pairs={{0,4},{4,0},{8,12},{12,8},{16,20},{20,16},{24,28},{28,24},{1,5},{5... | collective-permute-start | bytes 589832 | tf_op jit(solution)/shard_map/ppermute | solution.py:571
  39.3 0.7 collective-permute-start.11
  39.9 1.0 %shard_map.125.refs_0_.ext_ref = f32[24,3,64,128]{3,2,1,0:T(8,128)S(1)} custom-call(s32[8,16]{1,0:T(8,128)S(1)} %bitcast.47, s32[1,16]{1,0:T(1,128)S(1)} %bitcast.61, f32[64,128]{1,0:T(8,128)S(1)} %get-tuple-element.78.refs_0_, f32[64,128]{1,0:T(8,128)S(1)} %collective-permute-done.7.refs_1_, ...), custom_call_target="tpu_custom_call", output_to_operand_aliasing={{}: (11, {})} | custom-call | tf_op jit(solution)/shard_map/pallas_call | solution.py:31
  41.0 0.7 shard_map.127.refs_0_
  41.7 0.7 collective-permute-start.17
  42.3 0.9 %collective-permute-start.16 = (f32[64,128]{1,0:T(8,128)S(1)}, f32[64,128]{1,0:T(8,128)S(1)}, u32[]{:S(2)}, u32[]{:S(2)}) collective-permute-start(f32[64,128]{1,0:T(8,128)S(1)} %shard_map.127.refs_0_), channel_id=1, source_target_pairs={{0,2},{1,3},{2,0},{3,1},{4,6},{5,7},{6,4},{7,5},{8,10},{9,11},{10,... | collective-permute-start | bytes 98312 | tf_op jit(solution)/shard_map/ppermute | solution.py:616
  43.2 0.4 collective-permute-start.15
  43.6 4.3 %collective-permute-done.10.near_ref = bf16[4,3,64,128]{3,2,1,0:T(8,128)(2,1)S(1)} collective-permute-done((bf16[4,3,64,128]{3,2,1,0:T(8,128)(2,1)S(1)}, bf16[4,3,64,128]{3,2,1,0:T(8,128)(2,1)S(1)}, u32[]{:S(2)}, u32[]{:S(2)}) %collective-permute-start.10) | collective-permute-done | bytes 196640 | tf_op jit(solution)/shard_map/ppermute | solution.py:571
  47.9 0.8 %shard_map.126 = (f32[24,3,64,128]{3,2,1,0:T(8,128)S(1)}, f32[64,128]{1,0:T(8,128)S(1)}) custom-call(s32[8,16]{1,0:T(8,128)S(1)} %bitcast.49, s32[1,16]{1,0:T(1,128)S(1)} %bitcast.63, bf16[4,3,64,128]{3,2,1,0:T(8,128)(2,1)S(1)} %collective-permute-done.10.near_ref, ...), custom_call_target="tpu_custom_call", output_to_operand_aliasing={{0}: (4, {})} | custom-call | tf_op jit(solution)/shard_map/pallas_call | solution.py:31
  48.8 0.1 collective-permute-start.14
  48.9 1.2 %collective-permute-start.13 = (f32[64,128]{1,0:T(8,128)S(1)}, f32[64,128]{1,0:T(8,128)S(1)}, u32[]{:S(2)}, u32[]{:S(2)}) collective-permute-start(f32[64,128]{1,0:T(8,128)S(1)} %get-tuple-element.83.refs_0_), channel_id=1, source_target_pairs={{0,2},{1,3},{2,0},{3,1},{4,6},{5,7},{6,4},{7,5},{8,10},{9,11},{10,... | collective-permute-start | bytes 98312 | tf_op jit(solution)/shard_map/ppermute | solution.py:616
  50.1 0.6 collective-permute-start.12
  50.7 1.4 %shard_map.128 = (f32[16,3,64,128]{3,2,1,0:T(8,128)S(1)}, f32[8,96,128]{2,1,0:T(8,128)S(1)}) custom-call(s32[8,16]{1,0:T(8,128)S(1)} %bitcast.50, s32[1,16]{1,0:T(1,128)S(1)} %bitcast.64, f32[64,128]{1,0:T(8,128)S(1)} %shard_map.127.refs_0_, f32[64,128]{1,0:T(8,128)S(1)} %collective-permute-done.15.refs_1_, f32[64,128]{1,0:T(8,128)S(1)} %collective-permute-done.16.refs_2_, ...), custom_call_target="tpu_custom_call" | custom-call | tf_op jit(solution)/shard_map/pallas_call | solution.py:31
  52.1 0.2 collective-permute-done.14.refs_3_
  52.3 0.7 collective-permute-done.13.refs_2_
  53.0 2.3 %shard_map.129 = (f32[16,3,64,128]{3,2,1,0:T(8,128)S(1)}, bf16[8,96,128]{2,1,0:T(8,128)(2,1)}, f32[8,96,128]{2,1,0:T(8,128)S(1)}) custom-call(s32[8,16]{1,0:T(8,128)S(1)} %bitcast.51, s32[1,16]{1,0:T(1,128)S(1)} %bitcast.65, f32[64,128]{1,0:T(8,128)S(1)} %get-tuple-element.83.refs_0_, ...), custom_call_target="tpu_custom_call", output_to_operand_aliasing={{0}: (12, {}), {2}: (13, {})} | custom-call | tf_op jit(solution)/shard_map/pallas_call | solution.py:31
  55.3 6.5 %all-to-all-start = ((bf16[8,96,128]{2,1,0:T(8,128)(2,1)}), bf16[8,96,128]{2,1,0:T(8,128)(2,1)S(1)}, u32[]{:S(2)}, u32[]{:S(2)}) async-start(bf16[8,96,128]{2,1,0:T(8,128)(2,1)} %get-tuple-element.89), calls=%async_computation | async-start | bytes 393216 | tf_op jit(solution)/shard_map/all_to_all | solution.py:687
  61.8 1.1 %shard_map.130 = f32[16,3,64,128]{3,2,1,0:T(8,128)} custom-call(f32[16,3,64,128]{3,2,1,0:T(8,128)S(1)} %get-tuple-element.88.solved), custom_call_target="tpu_custom_call" | custom-call | tf_op jit(solution)/shard_map/pallas_call | solution.py:31
  62.9 7.1 %all-to-all-done.received_ref = bf16[8,96,128]{2,1,0:T(8,128)(2,1)S(1)} async-done(((bf16[8,96,128]{2,1,0:T(8,128)(2,1)}), bf16[8,96,128]{2,1,0:T(8,128)(2,1)S(1)}, u32[]{:S(2)}, u32[]{:S(2)}) %all-to-all-start) | async-done | bytes 196640 | tf_op jit(solution)/shard_map/all_to_all | solution.py:687
  70.0 2.6 %shard_map.131 = bf16[1,3,256,256]{3,2,1,0:T(8,128)(2,1)} custom-call(s32[2,128]{1,0:T(2,128)S(1)} %bitcast.67, bf16[8,96,128]{2,1,0:T(8,128)(2,1)S(1)} %all-to-all-done.received_ref, bf16[256,1024]{1,0:T(8,128)(2,1)S(1)} %get-tuple-element.90.row_ref, bf16[256,1024]{1,0:T(8,128)(2,1)S(1)} %get-tuple-element.91.col_ref, bf16[1,3,256,256]{3,2,1,0:T(8,128)(2,1)S(1)} %copy-done.1), custom_call_target="tpu_custom_call" | custom-call | tf_op jit(solution)/shard_map/pallas_call | solution.py:31
  (19 shorter events, 0.1 us)
Async XLA Ops:
  1.9 5.2 %copy-start = (s32[16,8]{0,1:T(8,128)S(1)}, s32[16,8]{0,1:T(8,128)}, u32[]{:S(2)}) copy-start(s32[16,8]{0,1:T(8,128)} %param.15) | copy-start | bytes 1540
  2.0 5.2 %copy-start.2 = (s32[16]{0:T(128)S(1)}, s32[16]{0:T(128)}, u32[]{:S(2)}) copy-start(s32[16]{0:T(128)} %param.16) | copy-start | bytes 196
  2.0 11.4 %collective-permute-start = (bf16[4,3,64,128]{3,2,1,0:T(8,128)(2,1)S(1)}, bf16[4,3,64,128]{3,2,1,0:T(8,128)(2,1)S(1)}, u32[]{:S(2)}, u32[]{:S(2)}) collective-permute-start(bf16[4,3,64,128]{3,2,1,0:T(8,128)(2,1)S(1)} %get-tuple-element.47), channel_id=1, source_target_pairs={{0,4},{4,0},{8,12},{12,8},{16,20},{20,16},{24,28},{28,24},{1,5},{5... | collective-permute-start | bytes 589832 | tf_op jit(solution)/shard_map/ppermute | solution.py:571
  5.0 8.4 %collective-permute-start.1 = (bf16[4,3,64,128]{3,2,1,0:T(8,128)(2,1)S(1)}, bf16[4,3,64,128]{3,2,1,0:T(8,128)(2,1)S(1)}, u32[]{:S(2)}, u32[]{:S(2)}) collective-permute-start(bf16[4,3,64,128]{3,2,1,0:T(8,128)(2,1)S(1)} %get-tuple-element.48), channel_id=1, source_target_pairs={{4,8},{8,4},{12,16},{16,12},{20,24},{24,20},{5,9},{9,5},{13,17},{1... | collective-permute-start | bytes 589832 | tf_op jit(solution)/shard_map/ppermute | solution.py:570
  14.2 3.7 %collective-permute-start.4 = (f32[64,128]{1,0:T(8,128)S(1)}, f32[64,128]{1,0:T(8,128)S(1)}, u32[]{:S(2)}, u32[]{:S(2)}) collective-permute-start(f32[64,128]{1,0:T(8,128)S(1)} %get-tuple-element.54.refs_0_), channel_id=1, source_target_pairs={{0,3},{1,2},{2,1},{3,0},{4,7},{5,6},{6,5},{7,4},{8,11},{9,10},{10,... | collective-permute-start | bytes 98312 | tf_op jit(solution)/shard_map/ppermute | solution.py:616
  14.3 4.0 %collective-permute-start.3 = (f32[64,128]{1,0:T(8,128)S(1)}, f32[64,128]{1,0:T(8,128)S(1)}, u32[]{:S(2)}, u32[]{:S(2)}) collective-permute-start(f32[64,128]{1,0:T(8,128)S(1)} %get-tuple-element.54.refs_0_), channel_id=1, source_target_pairs={{0,2},{1,3},{2,0},{3,1},{4,6},{5,7},{6,4},{7,5},{8,10},{9,11},{10,... | collective-permute-start | bytes 98312 | tf_op jit(solution)/shard_map/ppermute | solution.py:616
  15.9 2.4 %collective-permute-start.2 = (f32[64,128]{1,0:T(8,128)S(1)}, f32[64,128]{1,0:T(8,128)S(1)}, u32[]{:S(2)}, u32[]{:S(2)}) collective-permute-start(f32[64,128]{1,0:T(8,128)S(1)} %get-tuple-element.54.refs_0_), channel_id=1, source_target_pairs={{0,1},{1,0},{2,3},{3,2},{4,5},{5,4},{6,7},{7,6},{8,9},{9,8},{10,11... | collective-permute-start | bytes 98312 | tf_op jit(solution)/shard_map/ppermute | solution.py:616
  19.6 11.1 %collective-permute-start.5 = (bf16[4,3,64,128]{3,2,1,0:T(8,128)(2,1)S(1)}, bf16[4,3,64,128]{3,2,1,0:T(8,128)(2,1)S(1)}, u32[]{:S(2)}, u32[]{:S(2)}) collective-permute-start(bf16[4,3,64,128]{3,2,1,0:T(8,128)(2,1)S(1)} %get-tuple-element.60), channel_id=1, source_target_pairs={{0,4},{4,0},{8,12},{12,8},{16,20},{20,16},{24,28},{28,24},{1,5},{5... | collective-permute-start | bytes 589832 | tf_op jit(solution)/shard_map/ppermute | solution.py:571
  21.8 8.9 %collective-permute-start.6 = (bf16[4,3,64,128]{3,2,1,0:T(8,128)(2,1)S(1)}, bf16[4,3,64,128]{3,2,1,0:T(8,128)(2,1)S(1)}, u32[]{:S(2)}, u32[]{:S(2)}) collective-permute-start(bf16[4,3,64,128]{3,2,1,0:T(8,128)(2,1)S(1)} %get-tuple-element.61), channel_id=1, source_target_pairs={{4,8},{8,4},{12,16},{16,12},{20,24},{24,20},{5,9},{9,5},{13,17},{1... | collective-permute-start | bytes 589832 | tf_op jit(solution)/shard_map/ppermute | solution.py:570
  26.2 7.2 %copy-start.3 = (s32[128,2]{0,1:T(2,128)S(1)}, s32[128,2]{0,1:T(2,128)}, u32[]{:S(2)}) copy-start(s32[128,2]{0,1:T(2,128)} %param.17) | copy-start | bytes 3076
  26.3 7.2 %copy-start.4 = (s32[128,2,2]{0,2,1:T(2,128)S(1)}, s32[128,2,2]{0,2,1:T(2,128)}, u32[]{:S(2)}) copy-start(s32[128,2,2]{0,2,1:T(2,128)} %param.18) | copy-start | bytes 6148
  31.5 3.7 %collective-permute-start.9 = (f32[64,128]{1,0:T(8,128)S(1)}, f32[64,128]{1,0:T(8,128)S(1)}, u32[]{:S(2)}, u32[]{:S(2)}) collective-permute-start(f32[64,128]{1,0:T(8,128)S(1)} %get-tuple-element.78.refs_0_), channel_id=1, source_target_pairs={{0,3},{1,2},{2,1},{3,0},{4,7},{5,6},{6,5},{7,4},{8,11},{9,10},{10,... | collective-permute-start | bytes 98312 | tf_op jit(solution)/shard_map/ppermute | solution.py:616
  31.6 4.2 %collective-permute-start.8 = (f32[64,128]{1,0:T(8,128)S(1)}, f32[64,128]{1,0:T(8,128)S(1)}, u32[]{:S(2)}, u32[]{:S(2)}) collective-permute-start(f32[64,128]{1,0:T(8,128)S(1)} %get-tuple-element.78.refs_0_), channel_id=1, source_target_pairs={{0,2},{1,3},{2,0},{3,1},{4,6},{5,7},{6,4},{7,5},{8,10},{9,11},{10,... | collective-permute-start | bytes 98312 | tf_op jit(solution)/shard_map/ppermute | solution.py:616
  32.7 3.2 %collective-permute-start.7 = (f32[64,128]{1,0:T(8,128)S(1)}, f32[64,128]{1,0:T(8,128)S(1)}, u32[]{:S(2)}, u32[]{:S(2)}) collective-permute-start(f32[64,128]{1,0:T(8,128)S(1)} %get-tuple-element.78.refs_0_), channel_id=1, source_target_pairs={{0,1},{1,0},{2,3},{3,2},{4,5},{5,4},{6,7},{7,6},{8,9},{9,8},{10,11... | collective-permute-start | bytes 98312 | tf_op jit(solution)/shard_map/ppermute | solution.py:616
  37.1 10.8 %collective-permute-start.10 = (bf16[4,3,64,128]{3,2,1,0:T(8,128)(2,1)S(1)}, bf16[4,3,64,128]{3,2,1,0:T(8,128)(2,1)S(1)}, u32[]{:S(2)}, u32[]{:S(2)}) collective-permute-start(bf16[4,3,64,128]{3,2,1,0:T(8,128)(2,1)S(1)} %get-tuple-element.80), channel_id=1, source_target_pairs={{0,4},{4,0},{8,12},{12,8},{16,20},{20,16},{24,28},{28,24},{1,5},{5... | collective-permute-start | bytes 589832 | tf_op jit(solution)/shard_map/ppermute | solution.py:571
  39.3 8.7 %collective-permute-start.11 = (bf16[4,3,64,128]{3,2,1,0:T(8,128)(2,1)S(1)}, bf16[4,3,64,128]{3,2,1,0:T(8,128)(2,1)S(1)}, u32[]{:S(2)}, u32[]{:S(2)}) collective-permute-start(bf16[4,3,64,128]{3,2,1,0:T(8,128)(2,1)S(1)} %get-tuple-element.81), channel_id=1, source_target_pairs={{4,8},{8,4},{12,16},{16,12},{20,24},{24,20},{5,9},{9,5},{13,17},{1... | collective-permute-start | bytes 589832 | tf_op jit(solution)/shard_map/ppermute | solution.py:570
  41.7 8.4 %collective-permute-start.17 = (f32[64,128]{1,0:T(8,128)S(1)}, f32[64,128]{1,0:T(8,128)S(1)}, u32[]{:S(2)}, u32[]{:S(2)}) collective-permute-start(f32[64,128]{1,0:T(8,128)S(1)} %shard_map.127.refs_0_), channel_id=1, source_target_pairs={{0,3},{1,2},{2,1},{3,0},{4,7},{5,6},{6,5},{7,4},{8,11},{9,10},{10,... | collective-permute-start | bytes 98312 | tf_op jit(solution)/shard_map/ppermute | solution.py:616
  42.3 8.4 %collective-permute-start.16 = (f32[64,128]{1,0:T(8,128)S(1)}, f32[64,128]{1,0:T(8,128)S(1)}, u32[]{:S(2)}, u32[]{:S(2)}) collective-permute-start(f32[64,128]{1,0:T(8,128)S(1)} %shard_map.127.refs_0_), channel_id=1, source_target_pairs={{0,2},{1,3},{2,0},{3,1},{4,6},{5,7},{6,4},{7,5},{8,10},{9,11},{10,... | collective-permute-start | bytes 98312 | tf_op jit(solution)/shard_map/ppermute | solution.py:616
  43.2 7.5 %collective-permute-start.15 = (f32[64,128]{1,0:T(8,128)S(1)}, f32[64,128]{1,0:T(8,128)S(1)}, u32[]{:S(2)}, u32[]{:S(2)}) collective-permute-start(f32[64,128]{1,0:T(8,128)S(1)} %shard_map.127.refs_0_), channel_id=1, source_target_pairs={{0,1},{1,0},{2,3},{3,2},{4,5},{5,4},{6,7},{7,6},{8,9},{9,8},{10,11... | collective-permute-start | bytes 98312 | tf_op jit(solution)/shard_map/ppermute | solution.py:616
  48.8 3.5 %collective-permute-start.14 = (f32[64,128]{1,0:T(8,128)S(1)}, f32[64,128]{1,0:T(8,128)S(1)}, u32[]{:S(2)}, u32[]{:S(2)}) collective-permute-start(f32[64,128]{1,0:T(8,128)S(1)} %get-tuple-element.83.refs_0_), channel_id=1, source_target_pairs={{0,3},{1,2},{2,1},{3,0},{4,7},{5,6},{6,5},{7,4},{8,11},{9,10},{10,... | collective-permute-start | bytes 98312 | tf_op jit(solution)/shard_map/ppermute | solution.py:616
  48.9 4.1 %collective-permute-start.13 = (f32[64,128]{1,0:T(8,128)S(1)}, f32[64,128]{1,0:T(8,128)S(1)}, u32[]{:S(2)}, u32[]{:S(2)}) collective-permute-start(f32[64,128]{1,0:T(8,128)S(1)} %get-tuple-element.83.refs_0_), channel_id=1, source_target_pairs={{0,2},{1,3},{2,0},{3,1},{4,6},{5,7},{6,4},{7,5},{8,10},{9,11},{10,... | collective-permute-start | bytes 98312 | tf_op jit(solution)/shard_map/ppermute | solution.py:616
  50.1 2.9 %collective-permute-start.12 = (f32[64,128]{1,0:T(8,128)S(1)}, f32[64,128]{1,0:T(8,128)S(1)}, u32[]{:S(2)}, u32[]{:S(2)}) collective-permute-start(f32[64,128]{1,0:T(8,128)S(1)} %get-tuple-element.83.refs_0_), channel_id=1, source_target_pairs={{0,1},{1,0},{2,3},{3,2},{4,5},{5,4},{6,7},{7,6},{8,9},{9,8},{10,11... | collective-permute-start | bytes 98312 | tf_op jit(solution)/shard_map/ppermute | solution.py:616
  55.3 14.7 %copy-start.1 = (bf16[1,3,256,256]{3,2,1,0:T(8,128)(2,1)S(1)}, bf16[1,3,256,256]{3,2,1,0:T(8,128)(2,1)}, u32[]{:S(2)}) copy-start(bf16[1,3,256,256]{3,2,1,0:T(8,128)(2,1)} %pixels_ref.1) | copy-start | bytes 1179652
  55.3 14.7 %all-to-all-start = ((bf16[8,96,128]{2,1,0:T(8,128)(2,1)}), bf16[8,96,128]{2,1,0:T(8,128)(2,1)S(1)}, u32[]{:S(2)}, u32[]{:S(2)}) async-start(bf16[8,96,128]{2,1,0:T(8,128)(2,1)} %get-tuple-element.89), calls=%async_computation | async-start | bytes 393216 | tf_op jit(solution)/shard_map/all_to_all | solution.py:687

commit v7 on v6

--- a/solution.py
+++ b/solution.py
@@ -371,12 +371,6 @@
                 odd = pltpu.roll(windows[owner, at + 8 : at + 16, :], KN, 1)
                 both = jnp.concatenate([windows[owner, at : at + 8, :], odd], axis=0)
                 send_ref[owner, at : at + 16, :] = both.astype(bf16)
-
-
-def copy_out(solved, out_ref, sem):
-    copy = pltpu.make_async_copy(solved, out_ref, sem)
-    copy.start()
-    copy.wait()
 
 
 def earlier(first, second, granules):
@@ -482,7 +476,9 @@
                     ref[q : q + 16, to] = jnp.concatenate(pair, axis=0).astype(bf16)
 
 
-def compose(route_ref, received_ref, row_ref, col_ref, pixels_ref, out_ref, passed, result, sems):
+def compose(route_ref, received_ref, row_ref, col_ref, pixels_ref, solved, out_ref, grids_out, passed, result, sems):
+    copies = [pltpu.make_async_copy(solved, grids_out, sems.at[result.shape[0]])]
+    copies[0].start()
     senders = received_ref.shape[0]
     bands = result.shape[0]
     lane = lax.broadcasted_iota(jnp.int32, (16, LANES), 1) // SPAN
@@ -509,7 +505,6 @@
         return carry
 
     lax.fori_loop(0, senders // steps, several, 0)
-    copies = []
     for b in range(bands):
         fields = [
             lax.dot_general(
@@ -521,7 +516,7 @@
         pixels = pixels_ref[0, b].astype(f32)
         result[b] = (pixels * (1.0 + fields[0]) + fields[1]).astype(bf16)
         copies.append(pltpu.make_async_copy(result.at[b], out_ref.at[0, b], sems.at[b]))
-        copies[b].start()
+        copies[-1].start()
     for copy in copies:
         copy.wait()
 
@@ -685,15 +680,15 @@
         aliases={len(inputs) - 2: 0, len(inputs) - 1: 2},
     )
     received = lax.all_to_all(payload, "gran", split_axis=0, concat_axis=0, tiled=True)
-    (balanced,) = call(copy_out, [("v", balanced)], [("h", own, f32)], [pltpu.SemaphoreType.DMA])
-    (corrected,) = call(
+    inputs = [tiles[0], ("v", received), ("v", row_weights), ("v", col_weights), ("v", tile_pixels)]
+    corrected, balanced = call(
         compose,
-        [tiles[0], ("v", received), ("v", row_weights), ("v", col_weights), ("v", tile_pixels)],
-        [("h", tile_pixels.shape, bf16)],
+        inputs + [("v", balanced)],
+        [("h", tile_pixels.shape, bf16), ("h", own, f32)],
         [
             pltpu.VMEM((2 * bands, pixel_count, device_total * LANES), bf16),
             pltpu.VMEM(tile_pixels.shape[1:], bf16),
-            pltpu.SemaphoreType.DMA((bands,)),
+            pltpu.SemaphoreType.DMA((bands + 1,)),
         ],
         limit=32,
     )

time: 72.7 us -> 71.8 us (0.988)
  blocking collectives: 0 us -> 13.9 us
  waiting for transfers between devices: 21.2 us -> 13.7 us
  starting transfers between devices: 23.6 us -> 18.8 us
  Pallas kernels: 26.9 us -> 24.3 us
    all_to_all x0 -> x1, blocking collectives: none -> 13.9 us  [per_device(): lax.all_to_all(payload, 'gran', split_axis=0, concat_axis=0, tiled=True)]
    all_to_all x1 -> x0, waiting for transfers between devices: 7.08 us -> none  [per_device(): lax.all_to_all(payload, 'gran', split_axis=0, concat_axis=0, tiled=True)]
    all_to_all x1 -> x0, starting transfers between devices: 6.48 us -> none  [per_device(): lax.all_to_all(payload, 'gran', split_axis=0, concat_axis=0, tiled=True)]
    pallas_call x19 -> x18, Pallas kernels: 26.9 us -> 24.3 us  [call(): pl.pallas_call(body, in_specs=[ON_CHIP if kind == 'v' else ANYWHERE for k...]
    ppermute x3, starting transfers between devices: 7.41 us -> 9.15 us  [exchange(): near = lax.ppermute(near, 'gran', near_pairs)]
  transfers between devices with their start and end apart: 19 -> 18, of which waited for: 9 -> 8; matrix products, arithmetic and copies ran while one was open for 0% -> 0% of each run, Pallas kernels for 23% -> 22%
where the time goes in v7:
time: 71.8 us; the launch traced here: 71.6 us
  Pallas kernels  24.3 us (34%)
  starting transfers between devices  18.8 us (26%)
  blocking collectives  13.9 us (19%)
  waiting for transfers between devices  13.7 us (19%)
  between operations  0.86 us (1%)
    pallas_call x18, Pallas kernels, call(): pl.pallas_call(body, in_specs=[ON_CHIP if kind == 'v' else ANYWHERE for k...  24.3 us
    all_to_all x1, blocking collectives, per_device(): lax.all_to_all(payload, 'gran', split_axis=0, concat_axis=0, tiled=True)  13.9 us
    ppermute x3, waiting for transfers between devices, exchange(): near = lax.ppermute(near, 'gran', near_pairs)  10.2 us
    ppermute x3, starting transfers between devices, exchange(): near = lax.ppermute(near, 'gran', near_pairs)  9.15 us
    ppermute x12, starting transfers between devices, over_band(): lax.ppermute(partial, 'band', [(i, i ^ flip) for i in range(band_total)])  7.68 us
    ppermute x12, waiting for transfers between devices, over_band(): lax.ppermute(partial, 'band', [(i, i ^ flip) for i in range(band_total)])  3.55 us
    ppermute x3, starting transfers between devices, exchange(): far = lax.ppermute(far, 'gran', far_pairs)  1.98 us
  transfers between devices with their start and end apart: 18, of which 8 were waited for; matrix products, arithmetic and copies ran while one was open for 0% of the time, Pallas kernels for 22%

profile of v7, /device:TPU:0, one launch (start us, length us, event | category | flops | bytes accessed | tf_op | source)
XLA Modules:
  0.0 71.6 jit_solution(5756928169606812358)
XLA Ops:
  0.6 1.3 %shard_map.113 = (bf16[4,3,64,128]{3,2,1,0:T(8,128)(2,1)S(1)}, bf16[4,3,64,128]{3,2,1,0:T(8,128)(2,1)S(1)}) custom-call(f32[16,3,64,128]{3,2,1,0:T(8,128)} %bitcast.71), custom_call_target="tpu_custom_call" | custom-call | tf_op jit(solution)/shard_map/pallas_call | solution.py:31
  1.9 0.0 copy-start
  2.0 0.0 copy-start.2
  2.0 3.0 %collective-permute-start = (bf16[4,3,64,128]{3,2,1,0:T(8,128)(2,1)S(1)}, bf16[4,3,64,128]{3,2,1,0:T(8,128)(2,1)S(1)}, u32[]{:S(2)}, u32[]{:S(2)}) collective-permute-start(bf16[4,3,64,128]{3,2,1,0:T(8,128)(2,1)S(1)} %get-tuple-element.49), channel_id=1, source_target_pairs={{0,4},{4,0},{8,12},{12,8},{16,20},{20,16},{24,28},{28,24},{1,5},{5... | collective-permute-start | bytes 589832 | tf_op jit(solution)/shard_map/ppermute | solution.py:566
  5.0 0.7 collective-permute-start.1
  5.6 1.5 %shard_map.114.ext_ref.refs_0_ = f32[24,3,64,128]{3,2,1,0:T(8,128)S(1)} custom-call(f32[16,3,64,128]{3,2,1,0:T(8,128)} %bitcast.72), custom_call_target="tpu_custom_call" | custom-call | tf_op jit(solution)/shard_map/pallas_call | solution.py:31
  7.1 0.8 %shard_map.115.refs_1_ = f32[64,128]{1,0:T(8,128)S(1)} custom-call(s32[8,16]{1,0:T(8,128)S(1)} %bitcast.38, s32[1,16]{1,0:T(1,128)S(1)} %bitcast.52, f32[24,3,64,128]{3,2,1,0:T(8,128)S(1)} %shard_map.114.ext_ref.refs_0_), custom_call_target="tpu_custom_call" | custom-call | tf_op jit(solution)/shard_map/pallas_call | solution.py:31
  7.9 2.7 %shard_map.116 = (f32[8,3,64,128]{3,2,1,0:T(8,128)S(1)}, f32[8,3,64,128]{3,2,1,0:T(8,128)S(1)}, f32[8,3,32,128]{3,2,1,0:T(8,128)S(1)}, f32[8,8,3,32,128]{4,3,2,1,0:T(8,128)S(1)}) custom-call(s32[8,16]{1,0:T(8,128)S(1)} %bitcast.39, s32[1,16]{1,0:T(1,128)S(1)} %bitcast.53, f32[16,3,64,128]{3,2,1,0:T(8,128)} %bitcast.73, f32[16,3,64,128]{3,2,1,0:T(8,128)} %bitcast.75, ...), custom_call_target="tpu_custom_call" | custom-call | tf_op jit(solution)/shard_map/pallas_call | solution.py:31
  10.6 2.7 %collective-permute-done.near_ref = bf16[4,3,64,128]{3,2,1,0:T(8,128)(2,1)S(1)} collective-permute-done((bf16[4,3,64,128]{3,2,1,0:T(8,128)(2,1)S(1)}, bf16[4,3,64,128]{3,2,1,0:T(8,128)(2,1)S(1)}, u32[]{:S(2)}, u32[]{:S(2)}) %collective-permute-start) | collective-permute-done | bytes 196640 | tf_op jit(solution)/shard_map/ppermute | solution.py:566
  13.4 0.7 shard_map.117
  14.0 0.1 collective-permute-start.4
  14.1 1.6 %collective-permute-start.3 = (f32[64,128]{1,0:T(8,128)S(1)}, f32[64,128]{1,0:T(8,128)S(1)}, u32[]{:S(2)}, u32[]{:S(2)}) collective-permute-start(f32[64,128]{1,0:T(8,128)S(1)} %get-tuple-element.56.refs_0_), channel_id=1, source_target_pairs={{0,2},{1,3},{2,0},{3,1},{4,6},{5,7},{6,4},{7,5},{8,10},{9,11},{10,... | collective-permute-start | bytes 98312 | tf_op jit(solution)/shard_map/ppermute | solution.py:611
  15.7 0.3 collective-permute-start.2
  15.9 1.8 %collective-permute-done.4.refs_3_ = f32[64,128]{1,0:T(8,128)S(1)} collective-permute-done((f32[64,128]{1,0:T(8,128)S(1)}, f32[64,128]{1,0:T(8,128)S(1)}, u32[]{:S(2)}, u32[]{:S(2)}) %collective-permute-start.4) | collective-permute-done | bytes 32800 | tf_op jit(solution)/shard_map/ppermute | solution.py:611
  17.7 0.4 collective-permute-done.3.refs_2_
  18.1 1.0 %shard_map.118 = (f32[24,3,64,128]{3,2,1,0:T(8,128)S(1)}, bf16[4,3,64,128]{3,2,1,0:T(8,128)(2,1)S(1)}, bf16[4,3,64,128]{3,2,1,0:T(8,128)(2,1)S(1)}) custom-call(s32[8,16]{1,0:T(8,128)S(1)} %bitcast.41, s32[1,16]{1,0:T(1,128)S(1)} %bitcast.55, f32[64,128]{1,0:T(8,128)S(1)} %get-tuple-element.56.refs_0_, f32[64,128]{1,0:T(8,128)S(1)} %collective-permute-done.2.refs_1_, ...), custom_call_target="tpu_custom_call" | custom-call | tf_op jit(solution)/shard_map/pallas_call | solution.py:31
  19.1 3.1 %collective-permute-start.5 = (bf16[4,3,64,128]{3,2,1,0:T(8,128)(2,1)S(1)}, bf16[4,3,64,128]{3,2,1,0:T(8,128)(2,1)S(1)}, u32[]{:S(2)}, u32[]{:S(2)}) collective-permute-start(bf16[4,3,64,128]{3,2,1,0:T(8,128)(2,1)S(1)} %get-tuple-element.62), channel_id=1, source_target_pairs={{0,4},{4,0},{8,12},{12,8},{16,20},{20,16},{24,28},{28,24},{1,5},{5... | collective-permute-start | bytes 589832 | tf_op jit(solution)/shard_map/ppermute | solution.py:566
  22.2 0.7 collective-permute-start.6
  22.9 2.9 %shard_map.119 = (f32[8,3,64,128]{3,2,1,0:T(8,128)S(1)}, f32[8,3,64,128]{3,2,1,0:T(8,128)S(1)}, f32[8,3,32,128]{3,2,1,0:T(8,128)S(1)}, f32[8,8,3,32,128]{4,3,2,1,0:T(8,128)S(1)}) custom-call(s32[8,16]{1,0:T(8,128)S(1)} %bitcast.42, s32[1,16]{1,0:T(1,128)S(1)} %bitcast.56, f32[16,3,64,128]{3,2,1,0:T(8,128)} %bitcast.74, f32[16,3,64,128]{3,2,1,0:T(8,128)} %bitcast.76, ...), custom_call_target="tpu_custom_call" | custom-call | tf_op jit(solution)/shard_map/pallas_call | solution.py:31
  25.8 1.1 %shard_map.120.ext_ref.refs_0_ = f32[24,3,64,128]{3,2,1,0:T(8,128)S(1)} custom-call(s32[8,16]{1,0:T(8,128)S(1)} %bitcast.43, s32[1,16]{1,0:T(1,128)S(1)} %bitcast.57, f32[64,128]{1,0:T(8,128)S(1)} %get-tuple-element.56.refs_0_, f32[64,128]{1,0:T(8,128)S(1)} %collective-permute-done.2.refs_1_, ...), custom_call_target="tpu_custom_call", output_to_operand_aliasing={{}: (11, {})} | custom-call | tf_op jit(solution)/shard_map/pallas_call | solution.py:31
  27.0 0.0 copy-start.3
  27.0 0.8 %shard_map.121.refs_1_ = f32[64,128]{1,0:T(8,128)S(1)} custom-call(s32[8,16]{1,0:T(8,128)S(1)} %bitcast.44, s32[1,16]{1,0:T(1,128)S(1)} %bitcast.58, f32[24,3,64,128]{3,2,1,0:T(8,128)S(1)} %shard_map.120.ext_ref.refs_0_), custom_call_target="tpu_custom_call" | custom-call | tf_op jit(solution)/shard_map/pallas_call | solution.py:31
  27.8 3.3 %collective-permute-done.5.near_ref = bf16[4,3,64,128]{3,2,1,0:T(8,128)(2,1)S(1)} collective-permute-done((bf16[4,3,64,128]{3,2,1,0:T(8,128)(2,1)S(1)}, bf16[4,3,64,128]{3,2,1,0:T(8,128)(2,1)S(1)}, u32[]{:S(2)}, u32[]{:S(2)}) %collective-permute-start.5) | collective-permute-done | bytes 196640 | tf_op jit(solution)/shard_map/ppermute | solution.py:566
  31.1 0.7 shard_map.122
  31.8 0.1 collective-permute-start.9
  31.8 1.1 %collective-permute-start.8 = (f32[64,128]{1,0:T(8,128)S(1)}, f32[64,128]{1,0:T(8,128)S(1)}, u32[]{:S(2)}, u32[]{:S(2)}) collective-permute-start(f32[64,128]{1,0:T(8,128)S(1)} %get-tuple-element.80.refs_0_), channel_id=1, source_target_pairs={{0,2},{1,3},{2,0},{3,1},{4,6},{5,7},{6,4},{7,5},{8,10},{9,11},{10,... | collective-permute-start | bytes 98312 | tf_op jit(solution)/shard_map/ppermute | solution.py:611
  32.9 0.8 %collective-permute-start.7 = (f32[64,128]{1,0:T(8,128)S(1)}, f32[64,128]{1,0:T(8,128)S(1)}, u32[]{:S(2)}, u32[]{:S(2)}) collective-permute-start(f32[64,128]{1,0:T(8,128)S(1)} %get-tuple-element.80.refs_0_), channel_id=1, source_target_pairs={{0,1},{1,0},{2,3},{3,2},{4,5},{5,4},{6,7},{7,6},{8,9},{9,8},{10,11... | collective-permute-start | bytes 98312 | tf_op jit(solution)/shard_map/ppermute | solution.py:611
  33.7 1.8 %shard_map.123 = (bf16[256,1024]{1,0:T(8,128)(2,1)S(1)}, bf16[256,1024]{1,0:T(8,128)(2,1)S(1)}, s32[8,128]{1,0:T(8,128)S(1)}) custom-call(s32[2,128]{1,0:T(2,128)S(1)} %bitcast.66, s32[2,2,128]{2,1,0:T(2,128)S(1)} %bitcast.68), custom_call_target="tpu_custom_call" | custom-call | tf_op jit(solution)/shard_map/pallas_call | solution.py:31
  35.5 0.6 collective-permute-done.8.refs_2_
  36.1 1.0 %shard_map.124 = (f32[24,3,64,128]{3,2,1,0:T(8,128)S(1)}, bf16[4,3,64,128]{3,2,1,0:T(8,128)(2,1)S(1)}, bf16[4,3,64,128]{3,2,1,0:T(8,128)(2,1)S(1)}) custom-call(s32[8,16]{1,0:T(8,128)S(1)} %bitcast.46, s32[1,16]{1,0:T(1,128)S(1)} %bitcast.60, f32[64,128]{1,0:T(8,128)S(1)} %get-tuple-element.80.refs_0_, f32[64,128]{1,0:T(8,128)S(1)} %collective-permute-done.7.refs_1_, ...), custom_call_target="tpu_custom_call" | custom-call | tf_op jit(solution)/shard_map/pallas_call | solution.py:31
  37.1 3.1 %collective-permute-start.10 = (bf16[4,3,64,128]{3,2,1,0:T(8,128)(2,1)S(1)}, bf16[4,3,64,128]{3,2,1,0:T(8,128)(2,1)S(1)}, u32[]{:S(2)}, u32[]{:S(2)}) collective-permute-start(bf16[4,3,64,128]{3,2,1,0:T(8,128)(2,1)S(1)} %get-tuple-element.82), channel_id=1, source_target_pairs={{0,4},{4,0},{8,12},{12,8},{16,20},{20,16},{24,28},{28,24},{1,5},{5... | collective-permute-start | bytes 589832 | tf_op jit(solution)/shard_map/ppermute | solution.py:566
  40.1 0.7 collective-permute-start.11
  40.8 1.1 %shard_map.125.refs_0_.ext_ref = f32[24,3,64,128]{3,2,1,0:T(8,128)S(1)} custom-call(s32[8,16]{1,0:T(8,128)S(1)} %bitcast.47, s32[1,16]{1,0:T(1,128)S(1)} %bitcast.61, f32[64,128]{1,0:T(8,128)S(1)} %get-tuple-element.80.refs_0_, f32[64,128]{1,0:T(8,128)S(1)} %collective-permute-done.7.refs_1_, ...), custom_call_target="tpu_custom_call", output_to_operand_aliasing={{}: (11, {})} | custom-call | tf_op jit(solution)/shard_map/pallas_call | solution.py:31
  41.9 0.8 %shard_map.127.refs_0_ = f32[64,128]{1,0:T(8,128)S(1)} custom-call(s32[8,16]{1,0:T(8,128)S(1)} %bitcast.48, s32[1,16]{1,0:T(1,128)S(1)} %bitcast.62, f32[24,3,64,128]{3,2,1,0:T(8,128)S(1)} %shard_map.125.refs_0_.ext_ref), custom_call_target="tpu_custom_call" | custom-call | tf_op jit(solution)/shard_map/pallas_call | solution.py:31
  42.7 0.7 collective-permute-start.17
  43.4 0.9 %collective-permute-start.16 = (f32[64,128]{1,0:T(8,128)S(1)}, f32[64,128]{1,0:T(8,128)S(1)}, u32[]{:S(2)}, u32[]{:S(2)}) collective-permute-start(f32[64,128]{1,0:T(8,128)S(1)} %shard_map.127.refs_0_), channel_id=1, source_target_pairs={{0,2},{1,3},{2,0},{3,1},{4,6},{5,7},{6,4},{7,5},{8,10},{9,11},{10,... | collective-permute-start | bytes 98312 | tf_op jit(solution)/shard_map/ppermute | solution.py:611
  44.3 0.4 collective-permute-start.15
  44.7 4.1 %collective-permute-done.10.near_ref = bf16[4,3,64,128]{3,2,1,0:T(8,128)(2,1)S(1)} collective-permute-done((bf16[4,3,64,128]{3,2,1,0:T(8,128)(2,1)S(1)}, bf16[4,3,64,128]{3,2,1,0:T(8,128)(2,1)S(1)}, u32[]{:S(2)}, u32[]{:S(2)}) %collective-permute-start.10) | collective-permute-done | bytes 196640 | tf_op jit(solution)/shard_map/ppermute | solution.py:566
  48.8 0.7 shard_map.126
  49.5 0.1 collective-permute-start.14
  49.5 1.2 %collective-permute-start.13 = (f32[64,128]{1,0:T(8,128)S(1)}, f32[64,128]{1,0:T(8,128)S(1)}, u32[]{:S(2)}, u32[]{:S(2)}) collective-permute-start(f32[64,128]{1,0:T(8,128)S(1)} %get-tuple-element.85.refs_0_), channel_id=1, source_target_pairs={{0,2},{1,3},{2,0},{3,1},{4,6},{5,7},{6,4},{7,5},{8,10},{9,11},{10,... | collective-permute-start | bytes 98312 | tf_op jit(solution)/shard_map/ppermute | solution.py:611
  50.8 0.6 collective-permute-start.12
  51.4 1.5 %shard_map.128 = (f32[16,3,64,128]{3,2,1,0:T(8,128)S(1)}, f32[8,96,128]{2,1,0:T(8,128)S(1)}) custom-call(s32[8,16]{1,0:T(8,128)S(1)} %bitcast.50, s32[1,16]{1,0:T(1,128)S(1)} %bitcast.64, f32[64,128]{1,0:T(8,128)S(1)} %shard_map.127.refs_0_, f32[64,128]{1,0:T(8,128)S(1)} %collective-permute-done.15.refs_1_, f32[64,128]{1,0:T(8,128)S(1)} %collective-permute-done.16.refs_2_, ...), custom_call_target="tpu_custom_call" | custom-call | tf_op jit(solution)/shard_map/pallas_call | solution.py:31
  52.9 0.1 collective-permute-done.14.refs_3_
  52.9 0.7 collective-permute-done.13.refs_2_
  53.6 1.4 %shard_map.129 = (f32[16,3,64,128]{3,2,1,0:T(8,128)S(1)}, bf16[8,96,128]{2,1,0:T(8,128)(2,1)S(1)}, f32[8,96,128]{2,1,0:T(8,128)S(1)}) custom-call(s32[8,16]{1,0:T(8,128)S(1)} %bitcast.51, s32[1,16]{1,0:T(1,128)S(1)} %bitcast.65, f32[64,128]{1,0:T(8,128)S(1)} %get-tuple-element.85.refs_0_, ...), custom_call_target="tpu_custom_call", output_to_operand_aliasing={{0}: (12, {}), {2}: (13, {})} | custom-call | tf_op jit(solution)/shard_map/pallas_call | solution.py:31
  55.1 13.9 %all_to_all.5.received_ref = bf16[8,96,128]{2,1,0:T(8,128)(2,1)S(1)} all-to-all(bf16[8,96,128]{2,1,0:T(8,128)(2,1)S(1)} %get-tuple-element.90), channel_id=1, replica_groups=mesh['gran'=8,'band'=4] {'gran'}, dimensions={0} | all-to-all | bytes 393216 | tf_op jit(solution)/shard_map/all_to_all | solution.py:682
  69.0 2.6 %shard_map.130 = (bf16[1,3,256,256]{3,2,1,0:T(8,128)(2,1)}, f32[16,3,64,128]{3,2,1,0:T(8,128)}) custom-call(s32[2,128]{1,0:T(2,128)S(1)} %bitcast.67, bf16[8,96,128]{2,1,0:T(8,128)(2,1)S(1)} %all_to_all.5.received_ref, bf16[256,1024]{1,0:T(8,128)(2,1)S(1)} %get-tuple-element.91.row_ref, bf16[256,1024]{1,0:T(8,128)(2,1)S(1)} %get-tuple-element.92.col_ref, ...), custom_call_target="tpu_custom_call" | custom-call | tf_op jit(solution)/shard_map/pallas_call | solution.py:31
  (17 shorter events, 0.0 us)
Async XLA Ops:
  1.9 5.2 %copy-start = (s32[16,8]{0,1:T(8,128)S(1)}, s32[16,8]{0,1:T(8,128)}, u32[]{:S(2)}) copy-start(s32[16,8]{0,1:T(8,128)} %param.15) | copy-start | bytes 1540
  2.0 5.2 %copy-start.2 = (s32[16]{0:T(128)S(1)}, s32[16]{0:T(128)}, u32[]{:S(2)}) copy-start(s32[16]{0:T(128)} %param.16) | copy-start | bytes 196
  2.0 11.4 %collective-permute-start = (bf16[4,3,64,128]{3,2,1,0:T(8,128)(2,1)S(1)}, bf16[4,3,64,128]{3,2,1,0:T(8,128)(2,1)S(1)}, u32[]{:S(2)}, u32[]{:S(2)}) collective-permute-start(bf16[4,3,64,128]{3,2,1,0:T(8,128)(2,1)S(1)} %get-tuple-element.49), channel_id=1, source_target_pairs={{0,4},{4,0},{8,12},{12,8},{16,20},{20,16},{24,28},{28,24},{1,5},{5... | collective-permute-start | bytes 589832 | tf_op jit(solution)/shard_map/ppermute | solution.py:566
  5.0 8.4 %collective-permute-start.1 = (bf16[4,3,64,128]{3,2,1,0:T(8,128)(2,1)S(1)}, bf16[4,3,64,128]{3,2,1,0:T(8,128)(2,1)S(1)}, u32[]{:S(2)}, u32[]{:S(2)}) collective-permute-start(bf16[4,3,64,128]{3,2,1,0:T(8,128)(2,1)S(1)} %get-tuple-element.50), channel_id=1, source_target_pairs={{4,8},{8,4},{12,16},{16,12},{20,24},{24,20},{5,9},{9,5},{13,17},{1... | collective-permute-start | bytes 589832 | tf_op jit(solution)/shard_map/ppermute | solution.py:565
  14.0 3.7 %collective-permute-start.4 = (f32[64,128]{1,0:T(8,128)S(1)}, f32[64,128]{1,0:T(8,128)S(1)}, u32[]{:S(2)}, u32[]{:S(2)}) collective-permute-start(f32[64,128]{1,0:T(8,128)S(1)} %get-tuple-element.56.refs_0_), channel_id=1, source_target_pairs={{0,3},{1,2},{2,1},{3,0},{4,7},{5,6},{6,5},{7,4},{8,11},{9,10},{10,... | collective-permute-start | bytes 98312 | tf_op jit(solution)/shard_map/ppermute | solution.py:611
  14.1 4.0 %collective-permute-start.3 = (f32[64,128]{1,0:T(8,128)S(1)}, f32[64,128]{1,0:T(8,128)S(1)}, u32[]{:S(2)}, u32[]{:S(2)}) collective-permute-start(f32[64,128]{1,0:T(8,128)S(1)} %get-tuple-element.56.refs_0_), channel_id=1, source_target_pairs={{0,2},{1,3},{2,0},{3,1},{4,6},{5,7},{6,4},{7,5},{8,10},{9,11},{10,... | collective-permute-start | bytes 98312 | tf_op jit(solution)/shard_map/ppermute | solution.py:611
  15.7 2.4 %collective-permute-start.2 = (f32[64,128]{1,0:T(8,128)S(1)}, f32[64,128]{1,0:T(8,128)S(1)}, u32[]{:S(2)}, u32[]{:S(2)}) collective-permute-start(f32[64,128]{1,0:T(8,128)S(1)} %get-tuple-element.56.refs_0_), channel_id=1, source_target_pairs={{0,1},{1,0},{2,3},{3,2},{4,5},{5,4},{6,7},{7,6},{8,9},{9,8},{10,11... | collective-permute-start | bytes 98312 | tf_op jit(solution)/shard_map/ppermute | solution.py:611
  19.1 12.0 %collective-permute-start.5 = (bf16[4,3,64,128]{3,2,1,0:T(8,128)(2,1)S(1)}, bf16[4,3,64,128]{3,2,1,0:T(8,128)(2,1)S(1)}, u32[]{:S(2)}, u32[]{:S(2)}) collective-permute-start(bf16[4,3,64,128]{3,2,1,0:T(8,128)(2,1)S(1)} %get-tuple-element.62), channel_id=1, source_target_pairs={{0,4},{4,0},{8,12},{12,8},{16,20},{20,16},{24,28},{28,24},{1,5},{5... | collective-permute-start | bytes 589832 | tf_op jit(solution)/shard_map/ppermute | solution.py:566
  22.2 8.9 %collective-permute-start.6 = (bf16[4,3,64,128]{3,2,1,0:T(8,128)(2,1)S(1)}, bf16[4,3,64,128]{3,2,1,0:T(8,128)(2,1)S(1)}, u32[]{:S(2)}, u32[]{:S(2)}) collective-permute-start(bf16[4,3,64,128]{3,2,1,0:T(8,128)(2,1)S(1)} %get-tuple-element.63), channel_id=1, source_target_pairs={{4,8},{8,4},{12,16},{16,12},{20,24},{24,20},{5,9},{9,5},{13,17},{1... | collective-permute-start | bytes 589832 | tf_op jit(solution)/shard_map/ppermute | solution.py:565
  27.0 6.7 %copy-start.3 = (s32[128,2]{0,1:T(2,128)S(1)}, s32[128,2]{0,1:T(2,128)}, u32[]{:S(2)}) copy-start(s32[128,2]{0,1:T(2,128)} %param.17) | copy-start | bytes 3076
  27.0 6.7 %copy-start.4 = (s32[128,2,2]{0,2,1:T(2,128)S(1)}, s32[128,2,2]{0,2,1:T(2,128)}, u32[]{:S(2)}) copy-start(s32[128,2,2]{0,2,1:T(2,128)} %param.18) | copy-start | bytes 6148
  31.8 3.7 %collective-permute-start.9 = (f32[64,128]{1,0:T(8,128)S(1)}, f32[64,128]{1,0:T(8,128)S(1)}, u32[]{:S(2)}, u32[]{:S(2)}) collective-permute-start(f32[64,128]{1,0:T(8,128)S(1)} %get-tuple-element.80.refs_0_), channel_id=1, source_target_pairs={{0,3},{1,2},{2,1},{3,0},{4,7},{5,6},{6,5},{7,4},{8,11},{9,10},{10,... | collective-permute-start | bytes 98312 | tf_op jit(solution)/shard_map/ppermute | solution.py:611
  31.8 4.2 %collective-permute-start.8 = (f32[64,128]{1,0:T(8,128)S(1)}, f32[64,128]{1,0:T(8,128)S(1)}, u32[]{:S(2)}, u32[]{:S(2)}) collective-permute-start(f32[64,128]{1,0:T(8,128)S(1)} %get-tuple-element.80.refs_0_), channel_id=1, source_target_pairs={{0,2},{1,3},{2,0},{3,1},{4,6},{5,7},{6,4},{7,5},{8,10},{9,11},{10,... | collective-permute-start | bytes 98312 | tf_op jit(solution)/shard_map/ppermute | solution.py:611
  32.9 3.2 %collective-permute-start.7 = (f32[64,128]{1,0:T(8,128)S(1)}, f32[64,128]{1,0:T(8,128)S(1)}, u32[]{:S(2)}, u32[]{:S(2)}) collective-permute-start(f32[64,128]{1,0:T(8,128)S(1)} %get-tuple-element.80.refs_0_), channel_id=1, source_target_pairs={{0,1},{1,0},{2,3},{3,2},{4,5},{5,4},{6,7},{7,6},{8,9},{9,8},{10,11... | collective-permute-start | bytes 98312 | tf_op jit(solution)/shard_map/ppermute | solution.py:611
  37.1 11.7 %collective-permute-start.10 = (bf16[4,3,64,128]{3,2,1,0:T(8,128)(2,1)S(1)}, bf16[4,3,64,128]{3,2,1,0:T(8,128)(2,1)S(1)}, u32[]{:S(2)}, u32[]{:S(2)}) collective-permute-start(bf16[4,3,64,128]{3,2,1,0:T(8,128)(2,1)S(1)} %get-tuple-element.82), channel_id=1, source_target_pairs={{0,4},{4,0},{8,12},{12,8},{16,20},{20,16},{24,28},{28,24},{1,5},{5... | collective-permute-start | bytes 589832 | tf_op jit(solution)/shard_map/ppermute | solution.py:566
  40.1 8.7 %collective-permute-start.11 = (bf16[4,3,64,128]{3,2,1,0:T(8,128)(2,1)S(1)}, bf16[4,3,64,128]{3,2,1,0:T(8,128)(2,1)S(1)}, u32[]{:S(2)}, u32[]{:S(2)}) collective-permute-start(bf16[4,3,64,128]{3,2,1,0:T(8,128)(2,1)S(1)} %get-tuple-element.83), channel_id=1, source_target_pairs={{4,8},{8,4},{12,16},{16,12},{20,24},{24,20},{5,9},{9,5},{13,17},{1... | collective-permute-start | bytes 589832 | tf_op jit(solution)/shard_map/ppermute | solution.py:565
  42.7 8.0 %collective-permute-start.17 = (f32[64,128]{1,0:T(8,128)S(1)}, f32[64,128]{1,0:T(8,128)S(1)}, u32[]{:S(2)}, u32[]{:S(2)}) collective-permute-start(f32[64,128]{1,0:T(8,128)S(1)} %shard_map.127.refs_0_), channel_id=1, source_target_pairs={{0,3},{1,2},{2,1},{3,0},{4,7},{5,6},{6,5},{7,4},{8,11},{9,10},{10,... | collective-permute-start | bytes 98312 | tf_op jit(solution)/shard_map/ppermute | solution.py:611
  43.4 8.0 %collective-permute-start.16 = (f32[64,128]{1,0:T(8,128)S(1)}, f32[64,128]{1,0:T(8,128)S(1)}, u32[]{:S(2)}, u32[]{:S(2)}) collective-permute-start(f32[64,128]{1,0:T(8,128)S(1)} %shard_map.127.refs_0_), channel_id=1, source_target_pairs={{0,2},{1,3},{2,0},{3,1},{4,6},{5,7},{6,4},{7,5},{8,10},{9,11},{10,... | collective-permute-start | bytes 98312 | tf_op jit(solution)/shard_map/ppermute | solution.py:611
  44.3 7.1 %collective-permute-start.15 = (f32[64,128]{1,0:T(8,128)S(1)}, f32[64,128]{1,0:T(8,128)S(1)}, u32[]{:S(2)}, u32[]{:S(2)}) collective-permute-start(f32[64,128]{1,0:T(8,128)S(1)} %shard_map.127.refs_0_), channel_id=1, source_target_pairs={{0,1},{1,0},{2,3},{3,2},{4,5},{5,4},{6,7},{7,6},{8,9},{9,8},{10,11... | collective-permute-start | bytes 98312 | tf_op jit(solution)/shard_map/ppermute | solution.py:611
  49.5 3.5 %collective-permute-start.14 = (f32[64,128]{1,0:T(8,128)S(1)}, f32[64,128]{1,0:T(8,128)S(1)}, u32[]{:S(2)}, u32[]{:S(2)}) collective-permute-start(f32[64,128]{1,0:T(8,128)S(1)} %get-tuple-element.85.refs_0_), channel_id=1, source_target_pairs={{0,3},{1,2},{2,1},{3,0},{4,7},{5,6},{6,5},{7,4},{8,11},{9,10},{10,... | collective-permute-start | bytes 98312 | tf_op jit(solution)/shard_map/ppermute | solution.py:611
  49.5 4.1 %collective-permute-start.13 = (f32[64,128]{1,0:T(8,128)S(1)}, f32[64,128]{1,0:T(8,128)S(1)}, u32[]{:S(2)}, u32[]{:S(2)}) collective-permute-start(f32[64,128]{1,0:T(8,128)S(1)} %get-tuple-element.85.refs_0_), channel_id=1, source_target_pairs={{0,2},{1,3},{2,0},{3,1},{4,6},{5,7},{6,4},{7,5},{8,10},{9,11},{10,... | collective-permute-start | bytes 98312 | tf_op jit(solution)/shard_map/ppermute | solution.py:611
  50.8 2.9 %collective-permute-start.12 = (f32[64,128]{1,0:T(8,128)S(1)}, f32[64,128]{1,0:T(8,128)S(1)}, u32[]{:S(2)}, u32[]{:S(2)}) collective-permute-start(f32[64,128]{1,0:T(8,128)S(1)} %get-tuple-element.85.refs_0_), channel_id=1, source_target_pairs={{0,1},{1,0},{2,3},{3,2},{4,5},{5,4},{6,7},{7,6},{8,9},{9,8},{10,11... | collective-permute-start | bytes 98312 | tf_op jit(solution)/shard_map/ppermute | solution.py:611
  53.6 15.3 %copy-start.1 = (bf16[1,3,256,256]{3,2,1,0:T(8,128)(2,1)S(1)}, bf16[1,3,256,256]{3,2,1,0:T(8,128)(2,1)}, u32[]{:S(2)}) copy-start(bf16[1,3,256,256]{3,2,1,0:T(8,128)(2,1)} %pixels_ref.1) | copy-start | bytes 1179652

commit v8 on v7

--- a/solution.py
+++ b/solution.py
@@ -230,9 +230,13 @@
     out_ref[...] = packed + refs[1][...] if len(refs) == 6 else packed
 
 
+def add(one_ref, other_ref, out_ref):
+    out_ref[...] = one_ref[...] + other_ref[...]
+
+
 def spread_weights(shares, interior, weights):
     slots = weights.shape[0]
-    total = (shares[0][...] + shares[1][...]) + (shares[2][...] + shares[3][...])
+    total = shares[0][...] + shares[1][...]
     robust = 1.0 / (1.0 + total * (1.0 / (robust_scale * BANDS * PATCH * PATCH)))
     high = robust.astype(bf16).astype(f32)
     both = jnp.concatenate([high, robust - high], axis=1)
@@ -285,7 +289,7 @@
 
 
 def edge_sweep(offset_ref, count_ref, *refs):
-    shares, state, (new_ref, near_ref, far_ref, weights, graph) = refs[:4], refs[4:9], refs[9:]
+    shares, state, (new_ref, near_ref, far_ref, weights, graph) = refs[:2], refs[2:7], refs[7:]
     read_graph(offset_ref, count_ref, graph)
     spread_weights(shares, False, weights)
     odd = parity()
@@ -305,7 +309,7 @@
 
 
 def interior_sweep(offset_ref, count_ref, *refs):
-    shares, state, (_, new_ref, weights, graph) = refs[:4], refs[4:9], refs[9:]
+    shares, state, (_, new_ref, weights, graph) = refs[:2], refs[2:7], refs[7:]
     read_graph(offset_ref, count_ref, graph)
     spread_weights(shares, True, weights)
 
@@ -328,12 +332,12 @@
 
 
 def last_sweep(interior, offset_ref, count_ref, *refs):
-    shares, state, place_ref = refs[:4], refs[4:9], refs[9]
+    shares, state, place_ref = refs[:2], refs[2:7], refs[7]
     weights, graph = refs[-2:]
     if interior:
-        solved, windows = refs[10:12]
+        solved, windows = refs[8:10]
     else:
-        solved, send_ref, windows = refs[12:15]
+        solved, send_ref, windows = refs[10:13]
     granules, bands = solved.shape[:2]
     read_graph(offset_ref, count_ref, graph)
     if interior:
@@ -607,10 +611,13 @@
     scalars = pltpu.SMEM((2, granules), jnp.int32)
 
     def over_band(partial):
-        return [("v", partial)] + [
-            ("v", lax.ppermute(partial, "band", [(i, i ^ flip) for i in range(band_total)]))
-            for flip in range(1, band_total)
-        ]
+        flip = 1
+        other = lax.ppermute(partial, "band", [(i, i ^ flip) for i in range(band_total)])
+        while 2 * flip + 1 < band_total:
+            flip = 2 * flip + 1
+            (partial,) = call(add, [("v", partial), ("v", other)], [packed])
+            other = lax.ppermute(partial, "band", [(i, i ^ flip) for i in range(band_total)])
+        return [("v", partial), ("v", other)]
 
     for sweep in range(SWEEPS):
         last = sweep == SWEEPS - 1
@@ -632,15 +639,16 @@
         )
         shares = over_band(partial)
         if sweep == 1:
-            routes, starts, _ = lax.optimization_barrier((tiles[0][1], tiles[1][1], partial))
+            summed = shares[0][1]
+            routes, starts, _ = lax.optimization_barrier((tiles[0][1], tiles[1][1], summed))
             weight_shape = ("v", (pixel_count, device_total * LANES), bf16)
             made = call(
                 tile_places,
                 [("v", routes), ("v", starts)],
                 [weight_shape, weight_shape, ("v", (8, LANES), jnp.int32)],
             )
-            partial, row_weights, col_weights, places = lax.optimization_barrier((partial, *made))
-            shares[0] = ("v", partial)
+            summed, row_weights, col_weights, places = lax.optimization_barrier((summed, *made))
+            shares[0] = ("v", summed)
         edge_state_now = [("v", extended)] + [("v", array) for array in edge_state]
         if not last:
             inputs = graph + shares + edge_state_now

time: 71.8 us -> 73.7 us (1.026)
  waiting for transfers between devices: 13.7 us -> 17.4 us
  starting transfers between devices: 18.8 us -> 15.9 us
  Pallas kernels: 24.3 us -> 25.1 us
    ppermute x12 -> x8, waiting for transfers between devices: 3.55 us -> 5.94 us  [over_band(): lax.ppermute(partial, 'band', [(i, i ^ flip) for i in range(band_total)])]
    ppermute x12 -> x8, starting transfers between devices: 7.68 us -> 5.31 us  [over_band(): lax.ppermute(partial, 'band', [(i, i ^ flip) for i in range(band_total)])]
    ppermute x3, waiting for transfers between devices: 10.2 us -> 11.4 us  [exchange(): near = lax.ppermute(near, 'gran', near_pairs)]
    pallas_call x18 -> x22, Pallas kernels: 24.3 us -> 25.1 us  [call(): pl.pallas_call(body, in_specs=[ON_CHIP if kind == 'v' else ANYWHERE for k...]
  transfers between devices with their start and end apart: 18 -> 14, of which waited for: 8 -> 9; matrix products, arithmetic and copies ran while one was open for 0% -> 0% of each run, Pallas kernels for 22% -> 22%
where the time goes in v8:
time: 73.7 us; the launch traced here: 73.5 us
  Pallas kernels  25.1 us (34%)
  waiting for transfers between devices  17.4 us (24%)
  starting transfers between devices  15.9 us (22%)
  blocking collectives  14.2 us (19%)
  between operations  0.88 us (1%)
    pallas_call x22, Pallas kernels, call(): pl.pallas_call(body, in_specs=[ON_CHIP if kind == 'v' else ANYWHERE for k...  25.1 us
    all_to_all x1, blocking collectives, per_device(): lax.all_to_all(payload, 'gran', split_axis=0, concat_axis=0, tiled=True)  14.2 us
    ppermute x3, waiting for transfers between devices, exchange(): near = lax.ppermute(near, 'gran', near_pairs)  11.4 us
    ppermute x3, starting transfers between devices, exchange(): near = lax.ppermute(near, 'gran', near_pairs)  8.6 us
    ppermute x8, waiting for transfers between devices, over_band(): lax.ppermute(partial, 'band', [(i, i ^ flip) for i in range(band_total)])  5.94 us
    ppermute x8, starting transfers between devices, over_band(): lax.ppermute(partial, 'band', [(i, i ^ flip) for i in range(band_total)])  5.31 us
    ppermute x3, starting transfers between devices, exchange(): far = lax.ppermute(far, 'gran', far_pairs)  1.98 us
  transfers between devices with their start and end apart: 14, of which 9 were waited for; matrix products, arithmetic and copies ran while one was open for 0% of the time, Pallas kernels for 22%

profile of v8, /device:TPU:0, one launch (start us, length us, event | category | flops | bytes accessed | tf_op | source)
XLA Modules:
  0.0 73.5 jit_solution(6836446925351470285)
XLA Ops:
  0.6 1.3 %shard_map.113 = (bf16[4,3,64,128]{3,2,1,0:T(8,128)(2,1)S(1)}, bf16[4,3,64,128]{3,2,1,0:T(8,128)(2,1)S(1)}) custom-call(f32[16,3,64,128]{3,2,1,0:T(8,128)} %bitcast.71), custom_call_target="tpu_custom_call" | custom-call | tf_op jit(solution)/shard_map/pallas_call | solution.py:31
  1.9 0.0 copy-start
  2.0 0.0 copy-start.2
  2.0 3.0 %collective-permute-start = (bf16[4,3,64,128]{3,2,1,0:T(8,128)(2,1)S(1)}, bf16[4,3,64,128]{3,2,1,0:T(8,128)(2,1)S(1)}, u32[]{:S(2)}, u32[]{:S(2)}) collective-permute-start(bf16[4,3,64,128]{3,2,1,0:T(8,128)(2,1)S(1)} %get-tuple-element.49), channel_id=1, source_target_pairs={{0,4},{4,0},{8,12},{12,8},{16,20},{20,16},{24,28},{28,24},{1,5},{5... | collective-permute-start | bytes 589832 | tf_op jit(solution)/shard_map/ppermute | solution.py:570
  5.0 0.7 collective-permute-start.1
  5.6 1.5 %shard_map.114.ext_ref.refs_0_ = f32[24,3,64,128]{3,2,1,0:T(8,128)S(1)} custom-call(f32[16,3,64,128]{3,2,1,0:T(8,128)} %bitcast.72), custom_call_target="tpu_custom_call" | custom-call | tf_op jit(solution)/shard_map/pallas_call | solution.py:31
  7.1 0.8 %shard_map.115.refs_1_ = f32[64,128]{1,0:T(8,128)S(1)} custom-call(s32[8,16]{1,0:T(8,128)S(1)} %bitcast.38, s32[1,16]{1,0:T(1,128)S(1)} %bitcast.52, f32[24,3,64,128]{3,2,1,0:T(8,128)S(1)} %shard_map.114.ext_ref.refs_0_), custom_call_target="tpu_custom_call" | custom-call | tf_op jit(solution)/shard_map/pallas_call | solution.py:31
  8.0 2.8 %shard_map.116 = (f32[8,3,64,128]{3,2,1,0:T(8,128)S(1)}, f32[8,3,64,128]{3,2,1,0:T(8,128)S(1)}, f32[8,3,32,128]{3,2,1,0:T(8,128)S(1)}, f32[8,8,3,32,128]{4,3,2,1,0:T(8,128)S(1)}) custom-call(s32[8,16]{1,0:T(8,128)S(1)} %bitcast.39, s32[1,16]{1,0:T(1,128)S(1)} %bitcast.53, f32[16,3,64,128]{3,2,1,0:T(8,128)} %bitcast.73, f32[16,3,64,128]{3,2,1,0:T(8,128)} %bitcast.75, ...), custom_call_target="tpu_custom_call" | custom-call | tf_op jit(solution)/shard_map/pallas_call | solution.py:31
  10.8 2.6 %collective-permute-done.near_ref = bf16[4,3,64,128]{3,2,1,0:T(8,128)(2,1)S(1)} collective-permute-done((bf16[4,3,64,128]{3,2,1,0:T(8,128)(2,1)S(1)}, bf16[4,3,64,128]{3,2,1,0:T(8,128)(2,1)S(1)}, u32[]{:S(2)}, u32[]{:S(2)}) %collective-permute-start) | collective-permute-done | bytes 196640 | tf_op jit(solution)/shard_map/ppermute | solution.py:570
  13.3 0.0 collective-permute-done.1.far_ref
  13.4 0.7 shard_map.117
  14.1 0.1 collective-permute-start.2
  14.1 1.2 %collective-permute-done.2.other_ref = f32[64,128]{1,0:T(8,128)S(1)} collective-permute-done((f32[64,128]{1,0:T(8,128)S(1)}, f32[64,128]{1,0:T(8,128)S(1)}, u32[]{:S(2)}, u32[]{:S(2)}) %collective-permute-start.2) | collective-permute-done | bytes 32800 | tf_op jit(solution)/shard_map/ppermute | solution.py:615
  15.3 1.3 %collective-permute-start.3 = (f32[64,128]{1,0:T(8,128)S(1)}, f32[64,128]{1,0:T(8,128)S(1)}, u32[]{:S(2)}, u32[]{:S(2)}) collective-permute-start(f32[64,128]{1,0:T(8,128)S(1)} %shard_map.118.refs_0_), channel_id=1, source_target_pairs={{0,3},{1,2},{2,1},{3,0},{4,7},{5,6},{6,5},{7,4},{8,11},{9,10},{10,... | collective-permute-start | bytes 98312 | tf_op jit(solution)/shard_map/ppermute | solution.py:619
  16.6 2.1 %collective-permute-done.3.refs_1_ = f32[64,128]{1,0:T(8,128)S(1)} collective-permute-done((f32[64,128]{1,0:T(8,128)S(1)}, f32[64,128]{1,0:T(8,128)S(1)}, u32[]{:S(2)}, u32[]{:S(2)}) %collective-permute-start.3) | collective-permute-done | bytes 32800 | tf_op jit(solution)/shard_map/ppermute | solution.py:619
  18.7 1.0 %shard_map.119 = (f32[24,3,64,128]{3,2,1,0:T(8,128)S(1)}, bf16[4,3,64,128]{3,2,1,0:T(8,128)(2,1)S(1)}, bf16[4,3,64,128]{3,2,1,0:T(8,128)(2,1)S(1)}) custom-call(s32[8,16]{1,0:T(8,128)S(1)} %bitcast.41, s32[1,16]{1,0:T(1,128)S(1)} %bitcast.55, f32[64,128]{1,0:T(8,128)S(1)} %shard_map.118.refs_0_, f32[64,128]{1,0:T(8,128)S(1)} %collective-permute-done.3.refs_1_, ...), custom_call_target="tpu_custom_call" | custom-call | tf_op jit(solution)/shard_map/pallas_call | solution.py:31
  19.7 2.8 %collective-permute-start.4 = (bf16[4,3,64,128]{3,2,1,0:T(8,128)(2,1)S(1)}, bf16[4,3,64,128]{3,2,1,0:T(8,128)(2,1)S(1)}, u32[]{:S(2)}, u32[]{:S(2)}) collective-permute-start(bf16[4,3,64,128]{3,2,1,0:T(8,128)(2,1)S(1)} %get-tuple-element.62), channel_id=1, source_target_pairs={{0,4},{4,0},{8,12},{12,8},{16,20},{20,16},{24,28},{28,24},{1,5},{5... | collective-permute-start | bytes 589832 | tf_op jit(solution)/shard_map/ppermute | solution.py:570
  22.5 0.7 collective-permute-start.5
  23.2 3.0 %shard_map.120 = (f32[8,3,64,128]{3,2,1,0:T(8,128)S(1)}, f32[8,3,64,128]{3,2,1,0:T(8,128)S(1)}, f32[8,3,32,128]{3,2,1,0:T(8,128)S(1)}, f32[8,8,3,32,128]{4,3,2,1,0:T(8,128)S(1)}) custom-call(s32[8,16]{1,0:T(8,128)S(1)} %bitcast.42, s32[1,16]{1,0:T(1,128)S(1)} %bitcast.56, f32[16,3,64,128]{3,2,1,0:T(8,128)} %bitcast.74, f32[16,3,64,128]{3,2,1,0:T(8,128)} %bitcast.76, ...), custom_call_target="tpu_custom_call" | custom-call | tf_op jit(solution)/shard_map/pallas_call | solution.py:31
  26.2 1.2 %shard_map.121.ext_ref.refs_0_ = f32[24,3,64,128]{3,2,1,0:T(8,128)S(1)} custom-call(s32[8,16]{1,0:T(8,128)S(1)} %bitcast.43, s32[1,16]{1,0:T(1,128)S(1)} %bitcast.57, f32[64,128]{1,0:T(8,128)S(1)} %shard_map.118.refs_0_, f32[64,128]{1,0:T(8,128)S(1)} %collective-permute-done.3.refs_1_, ...), custom_call_target="tpu_custom_call", output_to_operand_aliasing={{}: (9, {})} | custom-call | tf_op jit(solution)/shard_map/pallas_call | solution.py:31
  27.5 0.0 copy-start.3
  27.5 0.0 copy-start.4
  27.5 0.8 %shard_map.122.refs_1_ = f32[64,128]{1,0:T(8,128)S(1)} custom-call(s32[8,16]{1,0:T(8,128)S(1)} %bitcast.44, s32[1,16]{1,0:T(1,128)S(1)} %bitcast.58, f32[24,3,64,128]{3,2,1,0:T(8,128)S(1)} %shard_map.121.ext_ref.refs_0_), custom_call_target="tpu_custom_call" | custom-call | tf_op jit(solution)/shard_map/pallas_call | solution.py:31
  28.3 2.9 %collective-permute-done.4.near_ref = bf16[4,3,64,128]{3,2,1,0:T(8,128)(2,1)S(1)} collective-permute-done((bf16[4,3,64,128]{3,2,1,0:T(8,128)(2,1)S(1)}, bf16[4,3,64,128]{3,2,1,0:T(8,128)(2,1)S(1)}, u32[]{:S(2)}, u32[]{:S(2)}) %collective-permute-start.4) | collective-permute-done | bytes 196640 | tf_op jit(solution)/shard_map/ppermute | solution.py:570
  31.2 0.7 shard_map.123
  31.9 0.1 collective-permute-start.6
  32.0 1.2 %collective-permute-done.6.other_ref = f32[64,128]{1,0:T(8,128)S(1)} collective-permute-done((f32[64,128]{1,0:T(8,128)S(1)}, f32[64,128]{1,0:T(8,128)S(1)}, u32[]{:S(2)}, u32[]{:S(2)}) %collective-permute-start.6) | collective-permute-done | bytes 32800 | tf_op jit(solution)/shard_map/ppermute | solution.py:615
  33.2 1.3 %collective-permute-start.7 = (f32[64,128]{1,0:T(8,128)S(1)}, f32[64,128]{1,0:T(8,128)S(1)}, u32[]{:S(2)}, u32[]{:S(2)}) collective-permute-start(f32[64,128]{1,0:T(8,128)S(1)} %shard_map.124.refs_0_), channel_id=1, source_target_pairs={{0,3},{1,2},{2,1},{3,0},{4,7},{5,6},{6,5},{7,4},{8,11},{9,10},{10,... | collective-permute-start | bytes 98312 | tf_op jit(solution)/shard_map/ppermute | solution.py:619
  34.5 1.8 %shard_map.125 = (bf16[256,1024]{1,0:T(8,128)(2,1)S(1)}, bf16[256,1024]{1,0:T(8,128)(2,1)S(1)}, s32[8,128]{1,0:T(8,128)S(1)}) custom-call(s32[2,128]{1,0:T(2,128)S(1)} %bitcast.66, s32[2,2,128]{2,1,0:T(2,128)S(1)} %bitcast.68), custom_call_target="tpu_custom_call" | custom-call | tf_op jit(solution)/shard_map/pallas_call | solution.py:31
  36.3 0.3 collective-permute-done.7.refs_1_
  36.6 1.0 %shard_map.126 = (f32[24,3,64,128]{3,2,1,0:T(8,128)S(1)}, bf16[4,3,64,128]{3,2,1,0:T(8,128)(2,1)S(1)}, bf16[4,3,64,128]{3,2,1,0:T(8,128)(2,1)S(1)}) custom-call(s32[8,16]{1,0:T(8,128)S(1)} %bitcast.46, s32[1,16]{1,0:T(1,128)S(1)} %bitcast.60, f32[64,128]{1,0:T(8,128)S(1)} %shard_map.124.refs_0_, f32[64,128]{1,0:T(8,128)S(1)} %collective-permute-done.7.refs_1_, ...), custom_call_target="tpu_custom_call" | custom-call | tf_op jit(solution)/shard_map/pallas_call | solution.py:31
  37.6 2.8 %collective-permute-start.8 = (bf16[4,3,64,128]{3,2,1,0:T(8,128)(2,1)S(1)}, bf16[4,3,64,128]{3,2,1,0:T(8,128)(2,1)S(1)}, u32[]{:S(2)}, u32[]{:S(2)}) collective-permute-start(bf16[4,3,64,128]{3,2,1,0:T(8,128)(2,1)S(1)} %get-tuple-element.82), channel_id=1, source_target_pairs={{0,4},{4,0},{8,12},{12,8},{16,20},{20,16},{24,28},{28,24},{1,5},{5... | collective-permute-start | bytes 589832 | tf_op jit(solution)/shard_map/ppermute | solution.py:570
  40.4 0.7 collective-permute-start.9
  41.1 1.2 %shard_map.127.refs_0_.ext_ref = f32[24,3,64,128]{3,2,1,0:T(8,128)S(1)} custom-call(s32[8,16]{1,0:T(8,128)S(1)} %bitcast.47, s32[1,16]{1,0:T(1,128)S(1)} %bitcast.61, f32[64,128]{1,0:T(8,128)S(1)} %shard_map.124.refs_0_, f32[64,128]{1,0:T(8,128)S(1)} %collective-permute-done.7.refs_1_, ...), custom_call_target="tpu_custom_call", output_to_operand_aliasing={{}: (9, {})} | custom-call | tf_op jit(solution)/shard_map/pallas_call | solution.py:31
  42.3 0.8 %shard_map.130.one_ref = f32[64,128]{1,0:T(8,128)S(1)} custom-call(s32[8,16]{1,0:T(8,128)S(1)} %bitcast.48, s32[1,16]{1,0:T(1,128)S(1)} %bitcast.62, f32[24,3,64,128]{3,2,1,0:T(8,128)S(1)} %shard_map.127.refs_0_.ext_ref), custom_call_target="tpu_custom_call" | custom-call | tf_op jit(solution)/shard_map/pallas_call | solution.py:31
  43.1 0.1 collective-permute-start.12
  43.2 5.9 %collective-permute-done.8.near_ref = bf16[4,3,64,128]{3,2,1,0:T(8,128)(2,1)S(1)} collective-permute-done((bf16[4,3,64,128]{3,2,1,0:T(8,128)(2,1)S(1)}, bf16[4,3,64,128]{3,2,1,0:T(8,128)(2,1)S(1)}, u32[]{:S(2)}, u32[]{:S(2)}) %collective-permute-start.8) | collective-permute-done | bytes 196640 | tf_op jit(solution)/shard_map/ppermute | solution.py:570
  49.1 0.0 collective-permute-done.9.far_ref
  49.1 0.7 shard_map.128
  49.8 0.1 collective-permute-start.10
  49.9 1.7 %collective-permute-start.13 = (f32[64,128]{1,0:T(8,128)S(1)}, f32[64,128]{1,0:T(8,128)S(1)}, u32[]{:S(2)}, u32[]{:S(2)}) collective-permute-start(f32[64,128]{1,0:T(8,128)S(1)} %shard_map.131.refs_0_), channel_id=1, source_target_pairs={{0,3},{1,2},{2,1},{3,0},{4,7},{5,6},{6,5},{7,4},{8,11},{9,10},{10,... | collective-permute-start | bytes 98312 | tf_op jit(solution)/shard_map/ppermute | solution.py:619
  51.6 0.8 %collective-permute-start.11 = (f32[64,128]{1,0:T(8,128)S(1)}, f32[64,128]{1,0:T(8,128)S(1)}, u32[]{:S(2)}, u32[]{:S(2)}) collective-permute-start(f32[64,128]{1,0:T(8,128)S(1)} %shard_map.129.refs_0_), channel_id=1, source_target_pairs={{0,3},{1,2},{2,1},{3,0},{4,7},{5,6},{6,5},{7,4},{8,11},{9,10},{10,... | collective-permute-start | bytes 98312 | tf_op jit(solution)/shard_map/ppermute | solution.py:619
  52.4 0.9 %collective-permute-done.13.refs_1_ = f32[64,128]{1,0:T(8,128)S(1)} collective-permute-done((f32[64,128]{1,0:T(8,128)S(1)}, f32[64,128]{1,0:T(8,128)S(1)}, u32[]{:S(2)}, u32[]{:S(2)}) %collective-permute-start.13) | collective-permute-done | bytes 32800 | tf_op jit(solution)/shard_map/ppermute | solution.py:619
  53.3 1.5 %shard_map.132 = (f32[16,3,64,128]{3,2,1,0:T(8,128)S(1)}, f32[8,96,128]{2,1,0:T(8,128)S(1)}) custom-call(s32[8,16]{1,0:T(8,128)S(1)} %bitcast.50, s32[1,16]{1,0:T(1,128)S(1)} %bitcast.64, f32[64,128]{1,0:T(8,128)S(1)} %shard_map.131.refs_0_, f32[64,128]{1,0:T(8,128)S(1)} %collective-permute-done.13.refs_1_, ...), custom_call_target="tpu_custom_call" | custom-call | tf_op jit(solution)/shard_map/pallas_call | solution.py:31
  54.9 0.3 collective-permute-done.11.refs_1_
  55.2 1.5 %shard_map.133 = (f32[16,3,64,128]{3,2,1,0:T(8,128)S(1)}, bf16[8,96,128]{2,1,0:T(8,128)(2,1)S(1)}, f32[8,96,128]{2,1,0:T(8,128)S(1)}) custom-call(s32[8,16]{1,0:T(8,128)S(1)} %bitcast.51, s32[1,16]{1,0:T(1,128)S(1)} %bitcast.65, f32[64,128]{1,0:T(8,128)S(1)} %shard_map.129.refs_0_, ...), custom_call_target="tpu_custom_call", output_to_operand_aliasing={{0}: (10, {}), {2}: (11, {})} | custom-call | tf_op jit(solution)/shard_map/pallas_call | solution.py:31
  56.6 14.2 %all_to_all.5.received_ref = bf16[8,96,128]{2,1,0:T(8,128)(2,1)S(1)} all-to-all(bf16[8,96,128]{2,1,0:T(8,128)(2,1)S(1)} %get-tuple-element.90), channel_id=1, replica_groups=mesh['gran'=8,'band'=4] {'gran'}, dimensions={0} | all-to-all | bytes 393216 | tf_op jit(solution)/shard_map/all_to_all | solution.py:690
  70.8 2.6 %shard_map.134 = (bf16[1,3,256,256]{3,2,1,0:T(8,128)(2,1)}, f32[16,3,64,128]{3,2,1,0:T(8,128)}) custom-call(s32[2,128]{1,0:T(2,128)S(1)} %bitcast.67, bf16[8,96,128]{2,1,0:T(8,128)(2,1)S(1)} %all_to_all.5.received_ref, bf16[256,1024]{1,0:T(8,128)(2,1)S(1)} %get-tuple-element.91.row_ref, bf16[256,1024]{1,0:T(8,128)(2,1)S(1)} %get-tuple-element.92.col_ref, ...), custom_call_target="tpu_custom_call" | custom-call | tf_op jit(solution)/shard_map/pallas_call | solution.py:31
  (13 shorter events, 0.0 us)
Async XLA Ops:
  1.9 5.2 %copy-start = (s32[16,8]{0,1:T(8,128)S(1)}, s32[16,8]{0,1:T(8,128)}, u32[]{:S(2)}) copy-start(s32[16,8]{0,1:T(8,128)} %param.15) | copy-start | bytes 1540
  2.0 5.2 %copy-start.2 = (s32[16]{0:T(128)S(1)}, s32[16]{0:T(128)}, u32[]{:S(2)}) copy-start(s32[16]{0:T(128)} %param.16) | copy-start | bytes 196
  2.0 11.4 %collective-permute-start = (bf16[4,3,64,128]{3,2,1,0:T(8,128)(2,1)S(1)}, bf16[4,3,64,128]{3,2,1,0:T(8,128)(2,1)S(1)}, u32[]{:S(2)}, u32[]{:S(2)}) collective-permute-start(bf16[4,3,64,128]{3,2,1,0:T(8,128)(2,1)S(1)} %get-tuple-element.49), channel_id=1, source_target_pairs={{0,4},{4,0},{8,12},{12,8},{16,20},{20,16},{24,28},{28,24},{1,5},{5... | collective-permute-start | bytes 589832 | tf_op jit(solution)/shard_map/ppermute | solution.py:570
  5.0 8.4 %collective-permute-start.1 = (bf16[4,3,64,128]{3,2,1,0:T(8,128)(2,1)S(1)}, bf16[4,3,64,128]{3,2,1,0:T(8,128)(2,1)S(1)}, u32[]{:S(2)}, u32[]{:S(2)}) collective-permute-start(bf16[4,3,64,128]{3,2,1,0:T(8,128)(2,1)S(1)} %get-tuple-element.50), channel_id=1, source_target_pairs={{4,8},{8,4},{12,16},{16,12},{20,24},{24,20},{5,9},{9,5},{13,17},{1... | collective-permute-start | bytes 589832 | tf_op jit(solution)/shard_map/ppermute | solution.py:569
  14.1 1.3 %collective-permute-start.2 = (f32[64,128]{1,0:T(8,128)S(1)}, f32[64,128]{1,0:T(8,128)S(1)}, u32[]{:S(2)}, u32[]{:S(2)}) collective-permute-start(f32[64,128]{1,0:T(8,128)S(1)} %get-tuple-element.56.one_ref), channel_id=1, source_target_pairs={{0,1},{1,0},{2,3},{3,2},{4,5},{5,4},{6,7},{7,6},{8,9},{9,8},{10,11... | collective-permute-start | bytes 98312 | tf_op jit(solution)/shard_map/ppermute | solution.py:615
  15.3 3.3 %collective-permute-start.3 = (f32[64,128]{1,0:T(8,128)S(1)}, f32[64,128]{1,0:T(8,128)S(1)}, u32[]{:S(2)}, u32[]{:S(2)}) collective-permute-start(f32[64,128]{1,0:T(8,128)S(1)} %shard_map.118.refs_0_), channel_id=1, source_target_pairs={{0,3},{1,2},{2,1},{3,0},{4,7},{5,6},{6,5},{7,4},{8,11},{9,10},{10,... | collective-permute-start | bytes 98312 | tf_op jit(solution)/shard_map/ppermute | solution.py:619
  19.7 11.5 %collective-permute-start.4 = (bf16[4,3,64,128]{3,2,1,0:T(8,128)(2,1)S(1)}, bf16[4,3,64,128]{3,2,1,0:T(8,128)(2,1)S(1)}, u32[]{:S(2)}, u32[]{:S(2)}) collective-permute-start(bf16[4,3,64,128]{3,2,1,0:T(8,128)(2,1)S(1)} %get-tuple-element.62), channel_id=1, source_target_pairs={{0,4},{4,0},{8,12},{12,8},{16,20},{20,16},{24,28},{28,24},{1,5},{5... | collective-permute-start | bytes 589832 | tf_op jit(solution)/shard_map/ppermute | solution.py:570
  22.5 8.7 %collective-permute-start.5 = (bf16[4,3,64,128]{3,2,1,0:T(8,128)(2,1)S(1)}, bf16[4,3,64,128]{3,2,1,0:T(8,128)(2,1)S(1)}, u32[]{:S(2)}, u32[]{:S(2)}) collective-permute-start(bf16[4,3,64,128]{3,2,1,0:T(8,128)(2,1)S(1)} %get-tuple-element.63), channel_id=1, source_target_pairs={{4,8},{8,4},{12,16},{16,12},{20,24},{24,20},{5,9},{9,5},{13,17},{1... | collective-permute-start | bytes 589832 | tf_op jit(solution)/shard_map/ppermute | solution.py:569
  27.5 7.1 %copy-start.3 = (s32[128,2]{0,1:T(2,128)S(1)}, s32[128,2]{0,1:T(2,128)}, u32[]{:S(2)}) copy-start(s32[128,2]{0,1:T(2,128)} %param.17) | copy-start | bytes 3076
  27.5 7.0 %copy-start.4 = (s32[128,2,2]{0,2,1:T(2,128)S(1)}, s32[128,2,2]{0,2,1:T(2,128)}, u32[]{:S(2)}) copy-start(s32[128,2,2]{0,2,1:T(2,128)} %param.18) | copy-start | bytes 6148
  31.9 1.3 %collective-permute-start.6 = (f32[64,128]{1,0:T(8,128)S(1)}, f32[64,128]{1,0:T(8,128)S(1)}, u32[]{:S(2)}, u32[]{:S(2)}) collective-permute-start(f32[64,128]{1,0:T(8,128)S(1)} %get-tuple-element.74.one_ref), channel_id=1, source_target_pairs={{0,1},{1,0},{2,3},{3,2},{4,5},{5,4},{6,7},{7,6},{8,9},{9,8},{10,11... | collective-permute-start | bytes 98312 | tf_op jit(solution)/shard_map/ppermute | solution.py:615
  33.2 3.3 %collective-permute-start.7 = (f32[64,128]{1,0:T(8,128)S(1)}, f32[64,128]{1,0:T(8,128)S(1)}, u32[]{:S(2)}, u32[]{:S(2)}) collective-permute-start(f32[64,128]{1,0:T(8,128)S(1)} %shard_map.124.refs_0_), channel_id=1, source_target_pairs={{0,3},{1,2},{2,1},{3,0},{4,7},{5,6},{6,5},{7,4},{8,11},{9,10},{10,... | collective-permute-start | bytes 98312 | tf_op jit(solution)/shard_map/ppermute | solution.py:619
  37.6 11.5 %collective-permute-start.8 = (bf16[4,3,64,128]{3,2,1,0:T(8,128)(2,1)S(1)}, bf16[4,3,64,128]{3,2,1,0:T(8,128)(2,1)S(1)}, u32[]{:S(2)}, u32[]{:S(2)}) collective-permute-start(bf16[4,3,64,128]{3,2,1,0:T(8,128)(2,1)S(1)} %get-tuple-element.82), channel_id=1, source_target_pairs={{0,4},{4,0},{8,12},{12,8},{16,20},{20,16},{24,28},{28,24},{1,5},{5... | collective-permute-start | bytes 589832 | tf_op jit(solution)/shard_map/ppermute | solution.py:570
  40.4 8.7 %collective-permute-start.9 = (bf16[4,3,64,128]{3,2,1,0:T(8,128)(2,1)S(1)}, bf16[4,3,64,128]{3,2,1,0:T(8,128)(2,1)S(1)}, u32[]{:S(2)}, u32[]{:S(2)}) collective-permute-start(bf16[4,3,64,128]{3,2,1,0:T(8,128)(2,1)S(1)} %get-tuple-element.83), channel_id=1, source_target_pairs={{4,8},{8,4},{12,16},{16,12},{20,24},{24,20},{5,9},{9,5},{13,17},{1... | collective-permute-start | bytes 589832 | tf_op jit(solution)/shard_map/ppermute | solution.py:569
  43.1 6.8 %collective-permute-start.12 = (f32[64,128]{1,0:T(8,128)S(1)}, f32[64,128]{1,0:T(8,128)S(1)}, u32[]{:S(2)}, u32[]{:S(2)}) collective-permute-start(f32[64,128]{1,0:T(8,128)S(1)} %shard_map.130.one_ref), channel_id=1, source_target_pairs={{0,1},{1,0},{2,3},{3,2},{4,5},{5,4},{6,7},{7,6},{8,9},{9,8},{10,11... | collective-permute-start | bytes 98312 | tf_op jit(solution)/shard_map/ppermute | solution.py:615
  49.8 1.8 %collective-permute-start.10 = (f32[64,128]{1,0:T(8,128)S(1)}, f32[64,128]{1,0:T(8,128)S(1)}, u32[]{:S(2)}, u32[]{:S(2)}) collective-permute-start(f32[64,128]{1,0:T(8,128)S(1)} %get-tuple-element.85.one_ref), channel_id=1, source_target_pairs={{0,1},{1,0},{2,3},{3,2},{4,5},{5,4},{6,7},{7,6},{8,9},{9,8},{10,11... | collective-permute-start | bytes 98312 | tf_op jit(solution)/shard_map/ppermute | solution.py:615
  49.9 3.4 %collective-permute-start.13 = (f32[64,128]{1,0:T(8,128)S(1)}, f32[64,128]{1,0:T(8,128)S(1)}, u32[]{:S(2)}, u32[]{:S(2)}) collective-permute-start(f32[64,128]{1,0:T(8,128)S(1)} %shard_map.131.refs_0_), channel_id=1, source_target_pairs={{0,3},{1,2},{2,1},{3,0},{4,7},{5,6},{6,5},{7,4},{8,11},{9,10},{10,... | collective-permute-start | bytes 98312 | tf_op jit(solution)/shard_map/ppermute | solution.py:619
  51.6 3.5 %collective-permute-start.11 = (f32[64,128]{1,0:T(8,128)S(1)}, f32[64,128]{1,0:T(8,128)S(1)}, u32[]{:S(2)}, u32[]{:S(2)}) collective-permute-start(f32[64,128]{1,0:T(8,128)S(1)} %shard_map.129.refs_0_), channel_id=1, source_target_pairs={{0,3},{1,2},{2,1},{3,0},{4,7},{5,6},{6,5},{7,4},{8,11},{9,10},{10,... | collective-permute-start | bytes 98312 | tf_op jit(solution)/shard_map/ppermute | solution.py:619
  55.2 15.7 %copy-start.1 = (bf16[1,3,256,256]{3,2,1,0:T(8,128)(2,1)S(1)}, bf16[1,3,256,256]{3,2,1,0:T(8,128)(2,1)}, u32[]{:S(2)}) copy-start(bf16[1,3,256,256]{3,2,1,0:T(8,128)(2,1)} %pixels_ref.1) | copy-start | bytes 1179652

commit v9 on v7

--- a/solution.py
+++ b/solution.py
@@ -14,6 +14,7 @@
 SP = 32
 LANES = 128
 SPAN = 16
+FIRST = 3
 
 robust_scale = 0.3
 
@@ -195,15 +196,21 @@
             continue
         own = response(i + REACH)
 
-        def slot(s, carry, i=i, own=own):
+        def slot(s, i=i, own=own):
             total = None
             for a, o in zip(own, response(neighbour(graph, i, s))):
                 d = a - o
                 total = d * d if total is None else total + d * d
             gathered[s, 8 * (i % 8) : 8 * (i % 8) + 8, :] = total
-            return carry
-
-        lax.fori_loop(0, graph[1, i], slot, 0)
+
+        for s in range(FIRST):
+            slot(s)
+
+        @pl.when(graph[1, i] > FIRST)
+        def _(slot=slot):
+            for s in range(FIRST, slots):
+                slot(s)
+
     sums = jnp.dot(
         gathered[...].reshape(slots * 64, LANES).astype(bf16), lane_sums(), preferred_element_type=f32
     )
@@ -214,12 +221,14 @@
     return packed
 
 
-def interior_disparities(offset_ref, count_ref, ext_ref, out_ref, gathered, graph):
-    out_ref[...] = disparities(True, offset_ref, count_ref, ext_ref, gathered, graph)
+def interior_disparities(offset_ref, count_ref, ext_ref, out_ref, send_ref, gathered, graph):
+    packed = disparities(True, offset_ref, count_ref, ext_ref, gathered, graph)
+    out_ref[...] = packed
+    send_ref[...] = packed.astype(bf16)
 
 
 def edge_disparities(offset_ref, count_ref, near_ref, far_ref, *refs):
-    ext_ref, out_ref, gathered, graph = refs[-4:]
+    ext_ref, out_ref, send_ref, gathered, graph = refs[-5:]
     odd = parity()
     right = ext_ref.shape[0] - REACH
     for ref, base in ((near_ref, (1 - odd) * right), (far_ref, odd * right)):
@@ -227,12 +236,17 @@
             for b in range(ref.shape[1]):
                 ext_ref[base + g, b] = ref[g, b].astype(f32)
     packed = disparities(False, offset_ref, count_ref, ext_ref, gathered, graph)
-    out_ref[...] = packed + refs[1][...] if len(refs) == 6 else packed
+    if len(refs) == 7:
+        packed = packed + refs[1][...]
+    out_ref[...] = packed
+    send_ref[...] = packed.astype(bf16)
 
 
 def spread_weights(shares, interior, weights):
     slots = weights.shape[0]
-    total = (shares[0][...] + shares[1][...]) + (shares[2][...] + shares[3][...])
+    total = shares[0][...]
+    for share in shares[1:]:
+        total = total + share[...].astype(f32)
     robust = 1.0 / (1.0 + total * (1.0 / (robust_scale * BANDS * PATCH * PATCH)))
     high = robust.astype(bf16).astype(f32)
     both = jnp.concatenate([high, robust - high], axis=1)
@@ -249,12 +263,16 @@
 def balance(i, at, ext_ref, rhs_ref, diag_ref, cross_ref, coupling_ref, weights, graph, store):
     bands = rhs_ref.shape[1]
     row = pl.multiple_of(lax.rem(i, 8) * 8, 8)
+    slots = weights.shape[0]
     parts = [(b, j) for b in range(bands) for j in range(4)]
     rhs = tuple(rhs_ref[at, b, pl.ds(2 * j + c, 8, stride=8), :] for b, j in parts for c in range(2))
 
-    def slot(s, sums):
+    count = graph[1, i]
+
+    def slot(slot_index, sums):
         sigma, drive = sums
-        weight = weights[s, pl.ds(row, 8), :]
+        s = jnp.minimum(slot_index, count - 1)
+        weight = jnp.where(slot_index < count, weights[s, pl.ds(row, 8), :], 0.0)
         n = neighbour(graph, i, s)
         new_sigma, new_drive = [], []
         for b in range(bands):
@@ -268,7 +286,16 @@
         return tuple(new_sigma), tuple(new_drive)
 
     zero = jnp.zeros((8, LANES), f32)
-    sigma, drive = lax.fori_loop(1, graph[1, i], slot, slot(0, ((zero,) * len(parts), rhs)))
+    sums = ((zero,) * len(parts), rhs)
+    for s in range(FIRST):
+        sums = slot(s, sums)
+
+    def others(_, sums):
+        for s in range(FIRST, slots):
+            sums = slot(s, sums)
+        return sums
+
+    sigma, drive = lax.fori_loop(0, (count > FIRST).astype(jnp.int32), others, sums)
     for k, (b, j) in enumerate(parts):
         first, second = (
             diag_ref[at, b, pl.ds(2 * j + c, 8, stride=8), :] + sigma[k] for c in range(2)
@@ -504,7 +531,10 @@
             sender(n * steps + k, carry)
         return carry
 
-    lax.fori_loop(0, senders // steps, several, 0)
+    if senders == steps:
+        several(0, 0)
+    else:
+        lax.fori_loop(0, senders // steps, several, 0)
     for b in range(bands):
         fields = [
             lax.dot_general(
@@ -553,7 +583,7 @@
     edge = (REACH, bands, 64, LANES)
     own = (granules, bands, 64, LANES)
     ext = (granules + 2 * REACH, bands, 64, LANES)
-    packed = ("v", (64, LANES), f32)
+    packed = [("v", (64, LANES), f32), ("v", (64, LANES), bf16)]
     chunks = 4
 
     near_pairs = [(i, i ^ 1) for i in range(device_total)]
@@ -606,31 +636,31 @@
     weights = pltpu.VMEM((slots, 64, LANES), f32)
     scalars = pltpu.SMEM((2, granules), jnp.int32)
 
-    def over_band(partial):
+    def over_band(partial, rounded):
         return [("v", partial)] + [
-            ("v", lax.ppermute(partial, "band", [(i, i ^ flip) for i in range(band_total)]))
+            ("v", lax.ppermute(rounded, "band", [(i, i ^ flip) for i in range(band_total)]))
             for flip in range(1, band_total)
         ]
 
     for sweep in range(SWEEPS):
         last = sweep == SWEEPS - 1
-        (inner,) = call(
-            interior_disparities, graph + [("v", extended)], [packed], [gathered, scalars]
+        inner, inner_rounded = call(
+            interior_disparities, graph + [("v", extended)], packed, [gathered, scalars]
         )
         if sweep == 0:
             inner, *edge_state = lax.optimization_barrier((inner, *arranged(False, sources)))
         if last:
-            inner_shares = over_band(inner)
+            inner_shares = over_band(inner, inner_rounded)
         inputs = graph + [("v", near), ("v", far), ("v", extended)]
         inputs += [] if last else [("v", inner)]
-        extended, partial = call(
+        extended, partial, rounded = call(
             edge_disparities,
             inputs,
-            [("v", ext, f32), packed],
+            [("v", ext, f32)] + packed,
             [gathered, scalars],
             aliases={4: 0},
         )
-        shares = over_band(partial)
+        shares = over_band(partial, rounded)
         if sweep == 1:
             routes, starts, _ = lax.optimization_barrier((tiles[0][1], tiles[1][1], partial))
             weight_shape = ("v", (pixel_count, device_total * LANES), bf16)

time: 71.8 us -> 70 us (0.975)
  waiting for transfers between devices: 13.7 us -> 12.1 us
    ppermute x12, waiting for transfers between devices: 3.55 us -> 2.75 us  [over_band(): lax.ppermute(rounded, 'band', [(i, i ^ flip) for i in range(band_total)])]
    ppermute x3, waiting for transfers between devices: 10.2 us -> 9.38 us  [exchange(): near = lax.ppermute(near, 'gran', near_pairs)]
    ppermute x3, starting transfers between devices: 9.15 us -> 8.4 us  [exchange(): near = lax.ppermute(near, 'gran', near_pairs)]
  transfers between devices with their start and end apart: 18 -> 18, of which waited for: 8 -> 7; matrix products, arithmetic and copies ran while one was open for 0% -> 0% of each run, Pallas kernels for 22% -> 23%
where the time goes in v9:
time: 70 us; the launch traced here: 69.8 us
  Pallas kernels  24.5 us (35%)
  starting transfers between devices  18.1 us (26%)
  blocking collectives  14.1 us (20%)
  waiting for transfers between devices  12.1 us (17%)
  between operations  0.84 us (1%)
    pallas_call x18, Pallas kernels, call(): pl.pallas_call(body, in_specs=[ON_CHIP if kind == 'v' else ANYWHERE for k...  24.5 us
    all_to_all x1, blocking collectives, per_device(): lax.all_to_all(payload, 'gran', split_axis=0, concat_axis=0, tiled=True)  14.1 us
    ppermute x3, waiting for transfers between devices, exchange(): near = lax.ppermute(near, 'gran', near_pairs)  9.38 us
    ppermute x3, starting transfers between devices, exchange(): near = lax.ppermute(near, 'gran', near_pairs)  8.4 us
    ppermute x12, starting transfers between devices, over_band(): lax.ppermute(rounded, 'band', [(i, i ^ flip) for i in range(band_total)])  7.69 us
    ppermute x12, waiting for transfers between devices, over_band(): lax.ppermute(rounded, 'band', [(i, i ^ flip) for i in range(band_total)])  2.75 us
    ppermute x3, starting transfers between devices, exchange(): far = lax.ppermute(far, 'gran', far_pairs)  1.98 us
  transfers between devices with their start and end apart: 18, of which 7 were waited for; matrix products, arithmetic and copies ran while one was open for 0% of the time, Pallas kernels for 23%

profile of v9, /device:TPU:0, one launch (start us, length us, event | category | flops | bytes accessed | tf_op | source)
XLA Modules:
  0.0 69.8 jit_solution(2653324879075816222)
XLA Ops:
  0.6 1.3 %shard_map.113 = (bf16[4,3,64,128]{3,2,1,0:T(8,128)(2,1)S(1)}, bf16[4,3,64,128]{3,2,1,0:T(8,128)(2,1)S(1)}) custom-call(f32[16,3,64,128]{3,2,1,0:T(8,128)} %bitcast.71), custom_call_target="tpu_custom_call" | custom-call | tf_op jit(solution)/shard_map/pallas_call | solution.py:32
  1.9 0.0 copy-start
  2.0 0.0 copy-start.2
  2.0 3.0 %collective-permute-start = (bf16[4,3,64,128]{3,2,1,0:T(8,128)(2,1)S(1)}, bf16[4,3,64,128]{3,2,1,0:T(8,128)(2,1)S(1)}, u32[]{:S(2)}, u32[]{:S(2)}) collective-permute-start(bf16[4,3,64,128]{3,2,1,0:T(8,128)(2,1)S(1)} %get-tuple-element.56), channel_id=1, source_target_pairs={{0,4},{4,0},{8,12},{12,8},{16,20},{20,16},{24,28},{28,24},{1,5},{5... | collective-permute-start | bytes 589832 | tf_op jit(solution)/shard_map/ppermute | solution.py:596
  5.0 0.7 collective-permute-start.1
  5.6 1.5 %shard_map.114.ext_ref.refs_0_ = f32[24,3,64,128]{3,2,1,0:T(8,128)S(1)} custom-call(f32[16,3,64,128]{3,2,1,0:T(8,128)} %bitcast.72), custom_call_target="tpu_custom_call" | custom-call | tf_op jit(solution)/shard_map/pallas_call | solution.py:32
  7.1 1.2 %shard_map.115 = (f32[64,128]{1,0:T(8,128)S(1)}, bf16[64,128]{1,0:T(8,128)(2,1)}) custom-call(s32[8,16]{1,0:T(8,128)S(1)} %bitcast.38, s32[1,16]{1,0:T(1,128)S(1)} %bitcast.52, f32[24,3,64,128]{3,2,1,0:T(8,128)S(1)} %shard_map.114.ext_ref.refs_0_), custom_call_target="tpu_custom_call" | custom-call | tf_op jit(solution)/shard_map/pallas_call | solution.py:32
  8.3 2.7 %shard_map.116 = (f32[8,3,64,128]{3,2,1,0:T(8,128)S(1)}, f32[8,3,64,128]{3,2,1,0:T(8,128)S(1)}, f32[8,3,32,128]{3,2,1,0:T(8,128)S(1)}, f32[8,8,3,32,128]{4,3,2,1,0:T(8,128)S(1)}) custom-call(s32[8,16]{1,0:T(8,128)S(1)} %bitcast.39, s32[1,16]{1,0:T(1,128)S(1)} %bitcast.53, f32[16,3,64,128]{3,2,1,0:T(8,128)} %bitcast.73, f32[16,3,64,128]{3,2,1,0:T(8,128)} %bitcast.75, ...), custom_call_target="tpu_custom_call" | custom-call | tf_op jit(solution)/shard_map/pallas_call | solution.py:32
  11.1 2.3 %collective-permute-done.near_ref = bf16[4,3,64,128]{3,2,1,0:T(8,128)(2,1)S(1)} collective-permute-done((bf16[4,3,64,128]{3,2,1,0:T(8,128)(2,1)S(1)}, bf16[4,3,64,128]{3,2,1,0:T(8,128)(2,1)S(1)}, u32[]{:S(2)}, u32[]{:S(2)}) %collective-permute-start) | collective-permute-done | bytes 196640 | tf_op jit(solution)/shard_map/ppermute | solution.py:596
  13.4 0.6 shard_map.117
  13.9 0.1 collective-permute-start.4
  14.0 1.6 %collective-permute-start.3 = (bf16[64,128]{1,0:T(8,128)(2,1)S(1)}, bf16[64,128]{1,0:T(8,128)(2,1)S(1)}, u32[]{:S(2)}, u32[]{:S(2)}) collective-permute-start(bf16[64,128]{1,0:T(8,128)(2,1)S(1)} %get-tuple-element.65), channel_id=1, source_target_pairs={{0,2},{1,3},{2,0},{3,1},{4,6},{5,7},{6,4},{7,5},{8,10},{9,11},{10,... | collective-permute-start | bytes 49160 | tf_op jit(solution)/shard_map/ppermute | solution.py:641
  15.6 0.3 collective-permute-start.2
  15.9 1.4 %collective-permute-done.4.refs_3_ = bf16[64,128]{1,0:T(8,128)(2,1)S(1)} collective-permute-done((bf16[64,128]{1,0:T(8,128)(2,1)S(1)}, bf16[64,128]{1,0:T(8,128)(2,1)S(1)}, u32[]{:S(2)}, u32[]{:S(2)}) %collective-permute-start.4) | collective-permute-done | bytes 16416 | tf_op jit(solution)/shard_map/ppermute | solution.py:641
  17.3 0.6 collective-permute-done.3.refs_2_
  17.8 1.0 %shard_map.118 = (f32[24,3,64,128]{3,2,1,0:T(8,128)S(1)}, bf16[4,3,64,128]{3,2,1,0:T(8,128)(2,1)S(1)}, bf16[4,3,64,128]{3,2,1,0:T(8,128)(2,1)S(1)}) custom-call(s32[8,16]{1,0:T(8,128)S(1)} %bitcast.41, s32[1,16]{1,0:T(1,128)S(1)} %bitcast.55, f32[64,128]{1,0:T(8,128)S(1)} %get-tuple-element.64.refs_0_, bf16[64,128]{1,0:T(8,128)(2,1)S(1)} %collective-permute-done.2.refs_1_, ...), custom_call_target="tpu_custom_call" | custom-call | tf_op jit(solution)/shard_map/pallas_call | solution.py:32
  18.8 2.8 %collective-permute-start.5 = (bf16[4,3,64,128]{3,2,1,0:T(8,128)(2,1)S(1)}, bf16[4,3,64,128]{3,2,1,0:T(8,128)(2,1)S(1)}, u32[]{:S(2)}, u32[]{:S(2)}) collective-permute-start(bf16[4,3,64,128]{3,2,1,0:T(8,128)(2,1)S(1)} %get-tuple-element.71), channel_id=1, source_target_pairs={{0,4},{4,0},{8,12},{12,8},{16,20},{20,16},{24,28},{28,24},{1,5},{5... | collective-permute-start | bytes 589832 | tf_op jit(solution)/shard_map/ppermute | solution.py:596
  21.6 0.7 collective-permute-start.6
  22.3 3.0 %shard_map.119 = (f32[8,3,64,128]{3,2,1,0:T(8,128)S(1)}, f32[8,3,64,128]{3,2,1,0:T(8,128)S(1)}, f32[8,3,32,128]{3,2,1,0:T(8,128)S(1)}, f32[8,8,3,32,128]{4,3,2,1,0:T(8,128)S(1)}) custom-call(s32[8,16]{1,0:T(8,128)S(1)} %bitcast.42, s32[1,16]{1,0:T(1,128)S(1)} %bitcast.56, f32[16,3,64,128]{3,2,1,0:T(8,128)} %bitcast.74, f32[16,3,64,128]{3,2,1,0:T(8,128)} %bitcast.76, ...), custom_call_target="tpu_custom_call" | custom-call | tf_op jit(solution)/shard_map/pallas_call | solution.py:32
  25.3 1.0 %shard_map.120.ext_ref.refs_0_ = f32[24,3,64,128]{3,2,1,0:T(8,128)S(1)} custom-call(s32[8,16]{1,0:T(8,128)S(1)} %bitcast.43, s32[1,16]{1,0:T(1,128)S(1)} %bitcast.57, f32[64,128]{1,0:T(8,128)S(1)} %get-tuple-element.64.refs_0_, bf16[64,128]{1,0:T(8,128)(2,1)S(1)} %collective-permute-done.2.refs_1_, ...), custom_call_target="tpu_custom_call", output_to_operand_aliasing={{}: (11, {})} | custom-call | tf_op jit(solution)/shard_map/pallas_call | solution.py:32
  26.3 0.0 copy-start.4
  26.3 1.2 %shard_map.121 = (f32[64,128]{1,0:T(8,128)S(1)}, bf16[64,128]{1,0:T(8,128)(2,1)}) custom-call(s32[8,16]{1,0:T(8,128)S(1)} %bitcast.44, s32[1,16]{1,0:T(1,128)S(1)} %bitcast.58, f32[24,3,64,128]{3,2,1,0:T(8,128)S(1)} %shard_map.120.ext_ref.refs_0_), custom_call_target="tpu_custom_call" | custom-call | tf_op jit(solution)/shard_map/pallas_call | solution.py:32
  27.5 2.9 %collective-permute-done.5.near_ref = bf16[4,3,64,128]{3,2,1,0:T(8,128)(2,1)S(1)} collective-permute-done((bf16[4,3,64,128]{3,2,1,0:T(8,128)(2,1)S(1)}, bf16[4,3,64,128]{3,2,1,0:T(8,128)(2,1)S(1)}, u32[]{:S(2)}, u32[]{:S(2)}) %collective-permute-start.5) | collective-permute-done | bytes 196640 | tf_op jit(solution)/shard_map/ppermute | solution.py:596
  30.4 0.6 shard_map.122
  31.0 0.1 collective-permute-start.9
  31.1 1.0 %collective-permute-start.8 = (bf16[64,128]{1,0:T(8,128)(2,1)S(1)}, bf16[64,128]{1,0:T(8,128)(2,1)S(1)}, u32[]{:S(2)}, u32[]{:S(2)}) collective-permute-start(bf16[64,128]{1,0:T(8,128)(2,1)S(1)} %get-tuple-element.91), channel_id=1, source_target_pairs={{0,2},{1,3},{2,0},{3,1},{4,6},{5,7},{6,4},{7,5},{8,10},{9,11},{10,... | collective-permute-start | bytes 49160 | tf_op jit(solution)/shard_map/ppermute | solution.py:641
  32.1 0.9 %collective-permute-start.7 = (bf16[64,128]{1,0:T(8,128)(2,1)S(1)}, bf16[64,128]{1,0:T(8,128)(2,1)S(1)}, u32[]{:S(2)}, u32[]{:S(2)}) collective-permute-start(bf16[64,128]{1,0:T(8,128)(2,1)S(1)} %get-tuple-element.91), channel_id=1, source_target_pairs={{0,1},{1,0},{2,3},{3,2},{4,5},{5,4},{6,7},{7,6},{8,9},{9,8},{10,11... | collective-permute-start | bytes 49160 | tf_op jit(solution)/shard_map/ppermute | solution.py:641
  33.0 1.8 %shard_map.123 = (bf16[256,1024]{1,0:T(8,128)(2,1)S(1)}, bf16[256,1024]{1,0:T(8,128)(2,1)S(1)}, s32[8,128]{1,0:T(8,128)S(1)}) custom-call(s32[2,128]{1,0:T(2,128)S(1)} %bitcast.66, s32[2,2,128]{2,1,0:T(2,128)S(1)} %bitcast.68), custom_call_target="tpu_custom_call" | custom-call | tf_op jit(solution)/shard_map/pallas_call | solution.py:32
  34.8 0.1 collective-permute-done.8.refs_2_
  34.9 1.0 %shard_map.124 = (f32[24,3,64,128]{3,2,1,0:T(8,128)S(1)}, bf16[4,3,64,128]{3,2,1,0:T(8,128)(2,1)S(1)}, bf16[4,3,64,128]{3,2,1,0:T(8,128)(2,1)S(1)}) custom-call(s32[8,16]{1,0:T(8,128)S(1)} %bitcast.46, s32[1,16]{1,0:T(1,128)S(1)} %bitcast.60, f32[64,128]{1,0:T(8,128)S(1)} %get-tuple-element.90.refs_0_, bf16[64,128]{1,0:T(8,128)(2,1)S(1)} %collective-permute-done.7.refs_1_, ...), custom_call_target="tpu_custom_call" | custom-call | tf_op jit(solution)/shard_map/pallas_call | solution.py:32
  35.9 2.6 %collective-permute-start.10 = (bf16[4,3,64,128]{3,2,1,0:T(8,128)(2,1)S(1)}, bf16[4,3,64,128]{3,2,1,0:T(8,128)(2,1)S(1)}, u32[]{:S(2)}, u32[]{:S(2)}) collective-permute-start(bf16[4,3,64,128]{3,2,1,0:T(8,128)(2,1)S(1)} %get-tuple-element.93), channel_id=1, source_target_pairs={{0,4},{4,0},{8,12},{12,8},{16,20},{20,16},{24,28},{28,24},{1,5},{5... | collective-permute-start | bytes 589832 | tf_op jit(solution)/shard_map/ppermute | solution.py:596
  38.6 0.7 collective-permute-start.11
  39.2 1.0 %shard_map.125.refs_0_.ext_ref = f32[24,3,64,128]{3,2,1,0:T(8,128)S(1)} custom-call(s32[8,16]{1,0:T(8,128)S(1)} %bitcast.47, s32[1,16]{1,0:T(1,128)S(1)} %bitcast.61, f32[64,128]{1,0:T(8,128)S(1)} %get-tuple-element.90.refs_0_, bf16[64,128]{1,0:T(8,128)(2,1)S(1)} %collective-permute-done.7.refs_1_, ...), custom_call_target="tpu_custom_call", output_to_operand_aliasing={{}: (11, {})} | custom-call | tf_op jit(solution)/shard_map/pallas_call | solution.py:32
  40.3 0.6 shard_map.127
  40.9 0.7 collective-permute-start.17
  41.5 0.6 collective-permute-start.16
  42.2 0.6 collective-permute-start.15
  42.8 4.2 %collective-permute-done.10.near_ref = bf16[4,3,64,128]{3,2,1,0:T(8,128)(2,1)S(1)} collective-permute-done((bf16[4,3,64,128]{3,2,1,0:T(8,128)(2,1)S(1)}, bf16[4,3,64,128]{3,2,1,0:T(8,128)(2,1)S(1)}, u32[]{:S(2)}, u32[]{:S(2)}) %collective-permute-start.10) | collective-permute-done | bytes 196640 | tf_op jit(solution)/shard_map/ppermute | solution.py:596
  47.0 0.6 shard_map.126
  47.6 0.2 collective-permute-start.14
  47.8 1.3 %collective-permute-start.13 = (bf16[64,128]{1,0:T(8,128)(2,1)S(1)}, bf16[64,128]{1,0:T(8,128)(2,1)S(1)}, u32[]{:S(2)}, u32[]{:S(2)}) collective-permute-start(bf16[64,128]{1,0:T(8,128)(2,1)S(1)} %get-tuple-element.97), channel_id=1, source_target_pairs={{0,2},{1,3},{2,0},{3,1},{4,6},{5,7},{6,4},{7,5},{8,10},{9,11},{10,... | collective-permute-start | bytes 49160 | tf_op jit(solution)/shard_map/ppermute | solution.py:641
  49.1 0.4 collective-permute-start.12
  49.5 1.4 %shard_map.128 = (f32[16,3,64,128]{3,2,1,0:T(8,128)S(1)}, f32[8,96,128]{2,1,0:T(8,128)S(1)}) custom-call(s32[8,16]{1,0:T(8,128)S(1)} %bitcast.50, s32[1,16]{1,0:T(1,128)S(1)} %bitcast.64, f32[64,128]{1,0:T(8,128)S(1)} %get-tuple-element.100.refs_0_, bf16[64,128]{1,0:T(8,128)(2,1)S(1)} %collective-permute-done.15.refs_1_, ...), custom_call_target="tpu_custom_call" | custom-call | tf_op jit(solution)/shard_map/pallas_call | solution.py:32
  50.9 0.0 collective-permute-done.14.refs_3_
  50.9 0.6 collective-permute-done.13.refs_2_
  51.5 1.4 %shard_map.129 = (f32[16,3,64,128]{3,2,1,0:T(8,128)S(1)}, bf16[8,96,128]{2,1,0:T(8,128)(2,1)S(1)}, f32[8,96,128]{2,1,0:T(8,128)S(1)}) custom-call(s32[8,16]{1,0:T(8,128)S(1)} %bitcast.51, s32[1,16]{1,0:T(1,128)S(1)} %bitcast.65, f32[64,128]{1,0:T(8,128)S(1)} %get-tuple-element.96.refs_0_, ...), custom_call_target="tpu_custom_call", output_to_operand_aliasing={{0}: (12, {}), {2}: (13, {})} | custom-call | tf_op jit(solution)/shard_map/pallas_call | solution.py:32
  53.0 14.1 %all_to_all.5.received_ref = bf16[8,96,128]{2,1,0:T(8,128)(2,1)S(1)} all-to-all(bf16[8,96,128]{2,1,0:T(8,128)(2,1)S(1)} %get-tuple-element.104), channel_id=1, replica_groups=mesh['gran'=8,'band'=4] {'gran'}, dimensions={0} | all-to-all | bytes 393216 | tf_op jit(solution)/shard_map/all_to_all | solution.py:712
  67.1 2.6 %shard_map.130 = (bf16[1,3,256,256]{3,2,1,0:T(8,128)(2,1)}, f32[16,3,64,128]{3,2,1,0:T(8,128)}) custom-call(s32[2,128]{1,0:T(2,128)S(1)} %bitcast.67, bf16[8,96,128]{2,1,0:T(8,128)(2,1)S(1)} %all_to_all.5.received_ref, bf16[256,1024]{1,0:T(8,128)(2,1)S(1)} %get-tuple-element.105.row_ref, bf16[256,1024]{1,0:T(8,128)(2,1)S(1)} %get-tuple-element.106.col_ref, ...), custom_call_target="tpu_custom_call" | custom-call | tf_op jit(solution)/shard_map/pallas_call | solution.py:32
  (17 shorter events, 0.0 us)
Async XLA Ops:
  1.9 5.2 %copy-start = (s32[16,8]{0,1:T(8,128)S(1)}, s32[16,8]{0,1:T(8,128)}, u32[]{:S(2)}) copy-start(s32[16,8]{0,1:T(8,128)} %param.15) | copy-start | bytes 1540
  2.0 5.2 %copy-start.2 = (s32[16]{0:T(128)S(1)}, s32[16]{0:T(128)}, u32[]{:S(2)}) copy-start(s32[16]{0:T(128)} %param.16) | copy-start | bytes 196
  2.0 11.4 %collective-permute-start = (bf16[4,3,64,128]{3,2,1,0:T(8,128)(2,1)S(1)}, bf16[4,3,64,128]{3,2,1,0:T(8,128)(2,1)S(1)}, u32[]{:S(2)}, u32[]{:S(2)}) collective-permute-start(bf16[4,3,64,128]{3,2,1,0:T(8,128)(2,1)S(1)} %get-tuple-element.56), channel_id=1, source_target_pairs={{0,4},{4,0},{8,12},{12,8},{16,20},{20,16},{24,28},{28,24},{1,5},{5... | collective-permute-start | bytes 589832 | tf_op jit(solution)/shard_map/ppermute | solution.py:596
  5.0 8.4 %collective-permute-start.1 = (bf16[4,3,64,128]{3,2,1,0:T(8,128)(2,1)S(1)}, bf16[4,3,64,128]{3,2,1,0:T(8,128)(2,1)S(1)}, u32[]{:S(2)}, u32[]{:S(2)}) collective-permute-start(bf16[4,3,64,128]{3,2,1,0:T(8,128)(2,1)S(1)} %get-tuple-element.57), channel_id=1, source_target_pairs={{4,8},{8,4},{12,16},{16,12},{20,24},{24,20},{5,9},{9,5},{13,17},{1... | collective-permute-start | bytes 589832 | tf_op jit(solution)/shard_map/ppermute | solution.py:595
  13.9 3.3 %collective-permute-start.4 = (bf16[64,128]{1,0:T(8,128)(2,1)S(1)}, bf16[64,128]{1,0:T(8,128)(2,1)S(1)}, u32[]{:S(2)}, u32[]{:S(2)}) collective-permute-start(bf16[64,128]{1,0:T(8,128)(2,1)S(1)} %get-tuple-element.65), channel_id=1, source_target_pairs={{0,3},{1,2},{2,1},{3,0},{4,7},{5,6},{6,5},{7,4},{8,11},{9,10},{10,... | collective-permute-start | bytes 49160 | tf_op jit(solution)/shard_map/ppermute | solution.py:641
  14.0 3.8 %collective-permute-start.3 = (bf16[64,128]{1,0:T(8,128)(2,1)S(1)}, bf16[64,128]{1,0:T(8,128)(2,1)S(1)}, u32[]{:S(2)}, u32[]{:S(2)}) collective-permute-start(bf16[64,128]{1,0:T(8,128)(2,1)S(1)} %get-tuple-element.65), channel_id=1, source_target_pairs={{0,2},{1,3},{2,0},{3,1},{4,6},{5,7},{6,4},{7,5},{8,10},{9,11},{10,... | collective-permute-start | bytes 49160 | tf_op jit(solution)/shard_map/ppermute | solution.py:641
  15.6 2.2 %collective-permute-start.2 = (bf16[64,128]{1,0:T(8,128)(2,1)S(1)}, bf16[64,128]{1,0:T(8,128)(2,1)S(1)}, u32[]{:S(2)}, u32[]{:S(2)}) collective-permute-start(bf16[64,128]{1,0:T(8,128)(2,1)S(1)} %get-tuple-element.65), channel_id=1, source_target_pairs={{0,1},{1,0},{2,3},{3,2},{4,5},{5,4},{6,7},{7,6},{8,9},{9,8},{10,11... | collective-permute-start | bytes 49160 | tf_op jit(solution)/shard_map/ppermute | solution.py:641
  18.8 11.6 %collective-permute-start.5 = (bf16[4,3,64,128]{3,2,1,0:T(8,128)(2,1)S(1)}, bf16[4,3,64,128]{3,2,1,0:T(8,128)(2,1)S(1)}, u32[]{:S(2)}, u32[]{:S(2)}) collective-permute-start(bf16[4,3,64,128]{3,2,1,0:T(8,128)(2,1)S(1)} %get-tuple-element.71), channel_id=1, source_target_pairs={{0,4},{4,0},{8,12},{12,8},{16,20},{20,16},{24,28},{28,24},{1,5},{5... | collective-permute-start | bytes 589832 | tf_op jit(solution)/shard_map/ppermute | solution.py:596
  21.6 8.8 %collective-permute-start.6 = (bf16[4,3,64,128]{3,2,1,0:T(8,128)(2,1)S(1)}, bf16[4,3,64,128]{3,2,1,0:T(8,128)(2,1)S(1)}, u32[]{:S(2)}, u32[]{:S(2)}) collective-permute-start(bf16[4,3,64,128]{3,2,1,0:T(8,128)(2,1)S(1)} %get-tuple-element.72), channel_id=1, source_target_pairs={{4,8},{8,4},{12,16},{16,12},{20,24},{24,20},{5,9},{9,5},{13,17},{1... | collective-permute-start | bytes 589832 | tf_op jit(solution)/shard_map/ppermute | solution.py:595
  26.3 6.6 %copy-start.3 = (s32[128,2]{0,1:T(2,128)S(1)}, s32[128,2]{0,1:T(2,128)}, u32[]{:S(2)}) copy-start(s32[128,2]{0,1:T(2,128)} %param.17) | copy-start | bytes 3076
  26.3 6.6 %copy-start.4 = (s32[128,2,2]{0,2,1:T(2,128)S(1)}, s32[128,2,2]{0,2,1:T(2,128)}, u32[]{:S(2)}) copy-start(s32[128,2,2]{0,2,1:T(2,128)} %param.18) | copy-start | bytes 6148
  31.0 3.7 %collective-permute-start.9 = (bf16[64,128]{1,0:T(8,128)(2,1)S(1)}, bf16[64,128]{1,0:T(8,128)(2,1)S(1)}, u32[]{:S(2)}, u32[]{:S(2)}) collective-permute-start(bf16[64,128]{1,0:T(8,128)(2,1)S(1)} %get-tuple-element.91), channel_id=1, source_target_pairs={{0,3},{1,2},{2,1},{3,0},{4,7},{5,6},{6,5},{7,4},{8,11},{9,10},{10,... | collective-permute-start | bytes 49160 | tf_op jit(solution)/shard_map/ppermute | solution.py:641
  31.1 3.8 %collective-permute-start.8 = (bf16[64,128]{1,0:T(8,128)(2,1)S(1)}, bf16[64,128]{1,0:T(8,128)(2,1)S(1)}, u32[]{:S(2)}, u32[]{:S(2)}) collective-permute-start(bf16[64,128]{1,0:T(8,128)(2,1)S(1)} %get-tuple-element.91), channel_id=1, source_target_pairs={{0,2},{1,3},{2,0},{3,1},{4,6},{5,7},{6,4},{7,5},{8,10},{9,11},{10,... | collective-permute-start | bytes 49160 | tf_op jit(solution)/shard_map/ppermute | solution.py:641
  32.1 2.8 %collective-permute-start.7 = (bf16[64,128]{1,0:T(8,128)(2,1)S(1)}, bf16[64,128]{1,0:T(8,128)(2,1)S(1)}, u32[]{:S(2)}, u32[]{:S(2)}) collective-permute-start(bf16[64,128]{1,0:T(8,128)(2,1)S(1)} %get-tuple-element.91), channel_id=1, source_target_pairs={{0,1},{1,0},{2,3},{3,2},{4,5},{5,4},{6,7},{7,6},{8,9},{9,8},{10,11... | collective-permute-start | bytes 49160 | tf_op jit(solution)/shard_map/ppermute | solution.py:641
  35.9 11.1 %collective-permute-start.10 = (bf16[4,3,64,128]{3,2,1,0:T(8,128)(2,1)S(1)}, bf16[4,3,64,128]{3,2,1,0:T(8,128)(2,1)S(1)}, u32[]{:S(2)}, u32[]{:S(2)}) collective-permute-start(bf16[4,3,64,128]{3,2,1,0:T(8,128)(2,1)S(1)} %get-tuple-element.93), channel_id=1, source_target_pairs={{0,4},{4,0},{8,12},{12,8},{16,20},{20,16},{24,28},{28,24},{1,5},{5... | collective-permute-start | bytes 589832 | tf_op jit(solution)/shard_map/ppermute | solution.py:596
  38.6 8.4 %collective-permute-start.11 = (bf16[4,3,64,128]{3,2,1,0:T(8,128)(2,1)S(1)}, bf16[4,3,64,128]{3,2,1,0:T(8,128)(2,1)S(1)}, u32[]{:S(2)}, u32[]{:S(2)}) collective-permute-start(bf16[4,3,64,128]{3,2,1,0:T(8,128)(2,1)S(1)} %get-tuple-element.94), channel_id=1, source_target_pairs={{4,8},{8,4},{12,16},{16,12},{20,24},{24,20},{5,9},{9,5},{13,17},{1... | collective-permute-start | bytes 589832 | tf_op jit(solution)/shard_map/ppermute | solution.py:595
  40.9 8.3 %collective-permute-start.17 = (bf16[64,128]{1,0:T(8,128)(2,1)S(1)}, bf16[64,128]{1,0:T(8,128)(2,1)S(1)}, u32[]{:S(2)}, u32[]{:S(2)}) collective-permute-start(bf16[64,128]{1,0:T(8,128)(2,1)S(1)} %get-tuple-element.101), channel_id=1, source_target_pairs={{0,3},{1,2},{2,1},{3,0},{4,7},{5,6},{6,5},{7,4},{8,11},{9,10},{10,... | collective-permute-start | bytes 49160 | tf_op jit(solution)/shard_map/ppermute | solution.py:641
  41.5 8.0 %collective-permute-start.16 = (bf16[64,128]{1,0:T(8,128)(2,1)S(1)}, bf16[64,128]{1,0:T(8,128)(2,1)S(1)}, u32[]{:S(2)}, u32[]{:S(2)}) collective-permute-start(bf16[64,128]{1,0:T(8,128)(2,1)S(1)} %get-tuple-element.101), channel_id=1, source_target_pairs={{0,2},{1,3},{2,0},{3,1},{4,6},{5,7},{6,4},{7,5},{8,10},{9,11},{10,... | collective-permute-start | bytes 49160 | tf_op jit(solution)/shard_map/ppermute | solution.py:641
  42.2 7.3 %collective-permute-start.15 = (bf16[64,128]{1,0:T(8,128)(2,1)S(1)}, bf16[64,128]{1,0:T(8,128)(2,1)S(1)}, u32[]{:S(2)}, u32[]{:S(2)}) collective-permute-start(bf16[64,128]{1,0:T(8,128)(2,1)S(1)} %get-tuple-element.101), channel_id=1, source_target_pairs={{0,1},{1,0},{2,3},{3,2},{4,5},{5,4},{6,7},{7,6},{8,9},{9,8},{10,11... | collective-permute-start | bytes 49160 | tf_op jit(solution)/shard_map/ppermute | solution.py:641
  47.6 3.4 %collective-permute-start.14 = (bf16[64,128]{1,0:T(8,128)(2,1)S(1)}, bf16[64,128]{1,0:T(8,128)(2,1)S(1)}, u32[]{:S(2)}, u32[]{:S(2)}) collective-permute-start(bf16[64,128]{1,0:T(8,128)(2,1)S(1)} %get-tuple-element.97), channel_id=1, source_target_pairs={{0,3},{1,2},{2,1},{3,0},{4,7},{5,6},{6,5},{7,4},{8,11},{9,10},{10,... | collective-permute-start | bytes 49160 | tf_op jit(solution)/shard_map/ppermute | solution.py:641
  47.8 3.7 %collective-permute-start.13 = (bf16[64,128]{1,0:T(8,128)(2,1)S(1)}, bf16[64,128]{1,0:T(8,128)(2,1)S(1)}, u32[]{:S(2)}, u32[]{:S(2)}) collective-permute-start(bf16[64,128]{1,0:T(8,128)(2,1)S(1)} %get-tuple-element.97), channel_id=1, source_target_pairs={{0,2},{1,3},{2,0},{3,1},{4,6},{5,7},{6,4},{7,5},{8,10},{9,11},{10,... | collective-permute-start | bytes 49160 | tf_op jit(solution)/shard_map/ppermute | solution.py:641
  49.1 2.4 %collective-permute-start.12 = (bf16[64,128]{1,0:T(8,128)(2,1)S(1)}, bf16[64,128]{1,0:T(8,128)(2,1)S(1)}, u32[]{:S(2)}, u32[]{:S(2)}) collective-permute-start(bf16[64,128]{1,0:T(8,128)(2,1)S(1)} %get-tuple-element.97), channel_id=1, source_target_pairs={{0,1},{1,0},{2,3},{3,2},{4,5},{5,4},{6,7},{7,6},{8,9},{9,8},{10,11... | collective-permute-start | bytes 49160 | tf_op jit(solution)/shard_map/ppermute | solution.py:641
  51.5 15.6 %copy-start.1 = (bf16[1,3,256,256]{3,2,1,0:T(8,128)(2,1)S(1)}, bf16[1,3,256,256]{3,2,1,0:T(8,128)(2,1)}, u32[]{:S(2)}) copy-start(bf16[1,3,256,256]{3,2,1,0:T(8,128)(2,1)} %pixels_ref.1) | copy-start | bytes 1179652

commit v10 on v9

--- a/solution.py
+++ b/solution.py
@@ -92,7 +92,7 @@
     return inner if interior else [i for i in range(granules) if i not in inner]
 
 
-def arrange(interior, offset_ref, count_ref, rhs_ref, diag_ref, cross_ref, coupling_ref, rhs_out, diag_out, cross_out, coupling_out, cross_raw, coupling_raw, wide, graph, sems):
+def arrange(interior, count_ref, rhs_ref, diag_ref, cross_ref, coupling_ref, rhs_out, diag_out, cross_out, coupling_out, rhs_raw, diag_raw, cross_raw, coupling_raw, wide, graph, sems):
     granules, bands = rhs_ref.shape[:2]
     own = visits(granules, interior)
     size = REACH
@@ -100,23 +100,22 @@
     copies = []
     for n in range(chunks):
         source, target = pl.ds(own[n * size], size), pl.ds(n * size, size)
-        moves = ((coupling_ref, coupling_raw), (diag_ref, diag_out), (rhs_ref, rhs_out))
+        moves = ((coupling_ref, coupling_raw), (diag_ref, diag_raw), (rhs_ref, rhs_raw))
         copies.append(
             [
                 pltpu.make_async_copy(here.at[source], there.at[target], sems.at[k, n])
                 for k, (here, there) in enumerate(moves)
             ]
         )
-        for copy in copies[n][:2]:
+        for copy in copies[n]:
             copy.start()
         if n == 0:
             whole = pltpu.make_async_copy(cross_ref, cross_raw, sems.at[3, 0])
             whole.start()
+    for i, count in enumerate(visits(granules, interior)):
+        graph[i] = count_ref[...][0, count]
     for n in range(chunks):
-        copies[n][2].start()
-    read_graph(offset_ref, count_ref, graph)
-    for n in range(chunks):
-        for copy in copies[n][:2]:
+        for copy in copies[n]:
             copy.wait()
         if n == 0:
             whole.wait()
@@ -127,7 +126,13 @@
             for b in range(bands):
                 wide[b] = coupling_raw[at, b].astype(f32)
                 for j in range(4):
-                    d = [diag_out[at, b, pl.ds(2 * j + c, 8, stride=8), :] for c in range(2)]
+                    d = []
+                    for c in range(2):
+                        rows = pl.ds(2 * j + c, 8, stride=8)
+                        to = slice(16 * j + 8 * c, 16 * j + 8 * c + 8)
+                        rhs_out[at, b, to, :] = rhs_raw[at, b, rows, :]
+                        d.append(diag_raw[at, b, rows, :])
+                        diag_out[at, b, to, :] = d[c]
                     pick = cross_raw[b, i // 8, pl.ds(8 * j + i % 8, 8, stride=32), :]
                     cross_out[at, b, 8 * j : 8 * j + 8, :] = pick * jnp.sqrt(d[0] * d[1])
 
@@ -138,11 +143,9 @@
                         coupling_out[at, s, b, 8 * j : 8 * j + 8, :] = pick
                 return carry
 
-            return lax.fori_loop(0, graph[1, i], slot, carry)
+            return lax.fori_loop(0, graph[at], slot, carry)
 
         lax.fori_loop(0, size, step, 0)
-    for n in range(chunks):
-        copies[n][2].wait()
 
 
 def lane_sums():
@@ -157,18 +160,19 @@
     return ((col % KN) // PATCH == row % PATCH).astype(f32).astype(bf16)
 
 
-def read_graph(offset_ref, count_ref, graph):
-    slots, granules = offset_ref.shape
+def graph_codes(offset_ref):
     slot = lax.broadcasted_iota(jnp.int32, offset_ref.shape, 0)
-    codes = jnp.sum(jnp.left_shift(offset_ref[...] + REACH, 4 * slot), axis=0, keepdims=True)
-    counts = count_ref[...]
-    for i in range(granules):
-        graph[0, i] = codes[0, i]
-        graph[1, i] = counts[0, i]
-
-
-def neighbour(graph, i, s):
-    return i + jnp.bitwise_and(jnp.right_shift(graph[0, i], 4 * s), 15)
+    return jnp.sum(jnp.left_shift(offset_ref[...] + REACH, 4 * slot), axis=0, keepdims=True)
+
+
+def read_graph(offset_ref, graph):
+    codes = graph_codes(offset_ref)
+    for i in range(offset_ref.shape[1]):
+        graph[i] = codes[0, i]
+
+
+def step_to(code, s):
+    return jnp.bitwise_and(jnp.right_shift(code, 4 * s), 15)
 
 
 def group_mask(interior, slots):
@@ -177,12 +181,12 @@
     return lane - slots * (1 - row if interior else row)
 
 
-def disparities(interior, offset_ref, count_ref, ext_ref, gathered, graph):
+def disparities(interior, offset_ref, ext_ref, gathered):
     bands = ext_ref.shape[1]
     granules = ext_ref.shape[0] - 2 * REACH
     slots = gathered.shape[0]
     gathered[...] = jnp.zeros_like(gathered)
-    read_graph(offset_ref, count_ref, graph)
+    codes = graph_codes(offset_ref)
 
     def response(g):
         return [
@@ -195,10 +199,11 @@
         if (REACH <= i < granules - REACH) != interior:
             continue
         own = response(i + REACH)
-
-        def slot(s, i=i, own=own):
+        code = codes[0, i]
+
+        def slot(s, i=i, own=own, code=code):
             total = None
-            for a, o in zip(own, response(neighbour(graph, i, s))):
+            for a, o in zip(own, response(i + step_to(code, s))):
                 d = a - o
                 total = d * d if total is None else total + d * d
             gathered[s, 8 * (i % 8) : 8 * (i % 8) + 8, :] = total
@@ -206,7 +211,7 @@
         for s in range(FIRST):
             slot(s)
 
-        @pl.when(graph[1, i] > FIRST)
+        @pl.when(step_to(code, FIRST) != REACH)
         def _(slot=slot):
             for s in range(FIRST, slots):
                 slot(s)
@@ -221,22 +226,23 @@
     return packed
 
 
-def interior_disparities(offset_ref, count_ref, ext_ref, out_ref, send_ref, gathered, graph):
-    packed = disparities(True, offset_ref, count_ref, ext_ref, gathered, graph)
+def interior_disparities(offset_ref, ext_ref, out_ref, *refs):
+    packed = disparities(True, offset_ref, ext_ref, refs[-1])
     out_ref[...] = packed
-    send_ref[...] = packed.astype(bf16)
-
-
-def edge_disparities(offset_ref, count_ref, near_ref, far_ref, *refs):
-    ext_ref, out_ref, send_ref, gathered, graph = refs[-5:]
+    if len(refs) == 2:
+        refs[0][...] = packed.astype(bf16)
+
+
+def edge_disparities(offset_ref, near_ref, far_ref, *refs):
+    ext_ref, out_ref, send_ref, gathered = refs[-4:]
     odd = parity()
     right = ext_ref.shape[0] - REACH
     for ref, base in ((near_ref, (1 - odd) * right), (far_ref, odd * right)):
         for g in range(REACH):
             for b in range(ref.shape[1]):
                 ext_ref[base + g, b] = ref[g, b].astype(f32)
-    packed = disparities(False, offset_ref, count_ref, ext_ref, gathered, graph)
-    if len(refs) == 7:
+    packed = disparities(False, offset_ref, ext_ref, gathered)
+    if len(refs) == 6:
         packed = packed + refs[1][...]
     out_ref[...] = packed
     send_ref[...] = packed.astype(bf16)
@@ -265,15 +271,17 @@
     row = pl.multiple_of(lax.rem(i, 8) * 8, 8)
     slots = weights.shape[0]
     parts = [(b, j) for b in range(bands) for j in range(4)]
-    rhs = tuple(rhs_ref[at, b, pl.ds(2 * j + c, 8, stride=8), :] for b, j in parts for c in range(2))
-
-    count = graph[1, i]
+    rows = [slice(8 * q, 8 * q + 8) for q in range(8)]
+    rhs = tuple(rhs_ref[at, b, rows[2 * j + c], :] for b, j in parts for c in range(2))
+
+    code = graph[i]
 
     def slot(slot_index, sums):
         sigma, drive = sums
-        s = jnp.minimum(slot_index, count - 1)
-        weight = jnp.where(slot_index < count, weights[s, pl.ds(row, 8), :], 0.0)
-        n = neighbour(graph, i, s)
+        used = step_to(code, slot_index) != REACH
+        s = jnp.where(used, slot_index, 0)
+        weight = jnp.where(used, weights[s, pl.ds(row, 8), :], 0.0)
+        n = i + step_to(code, s)
         new_sigma, new_drive = [], []
         for b in range(bands):
             for j in range(4):
@@ -295,10 +303,10 @@
             sums = slot(s, sums)
         return sums
 
-    sigma, drive = lax.fori_loop(0, (count > FIRST).astype(jnp.int32), others, sums)
+    sigma, drive = lax.fori_loop(0, (step_to(code, FIRST) != REACH).astype(jnp.int32), others, sums)
     for k, (b, j) in enumerate(parts):
         first, second = (
-            diag_ref[at, b, pl.ds(2 * j + c, 8, stride=8), :] + sigma[k] for c in range(2)
+            diag_ref[at, b, rows[2 * j + c], :] + sigma[k] for c in range(2)
         )
         cross = cross_ref[at, b, 8 * j : 8 * j + 8, :]
         inverse = 1.0 / (first * second - cross * cross)
@@ -311,9 +319,9 @@
         )
 
 
-def edge_sweep(offset_ref, count_ref, *refs):
+def edge_sweep(offset_ref, *refs):
     shares, state, (new_ref, near_ref, far_ref, weights, graph) = refs[:4], refs[4:9], refs[9:]
-    read_graph(offset_ref, count_ref, graph)
+    read_graph(offset_ref, graph)
     spread_weights(shares, False, weights)
     odd = parity()
     last = new_ref.shape[0] - 3 * REACH
@@ -331,9 +339,9 @@
         lax.fori_loop(0, REACH, step, 0)
 
 
-def interior_sweep(offset_ref, count_ref, *refs):
+def interior_sweep(offset_ref, *refs):
     shares, state, (_, new_ref, weights, graph) = refs[:4], refs[4:9], refs[9:]
-    read_graph(offset_ref, count_ref, graph)
+    read_graph(offset_ref, graph)
     spread_weights(shares, True, weights)
 
     def step(i, carry):
@@ -354,7 +362,7 @@
     return pltpu.roll(ref[at + (pl.ds(base, LANES),)], turn, 1)
 
 
-def last_sweep(interior, offset_ref, count_ref, *refs):
+def last_sweep(interior, offset_ref, *refs):
     shares, state, place_ref = refs[:4], refs[4:9], refs[9]
     weights, graph = refs[-2:]
     if interior:
@@ -362,7 +370,7 @@
     else:
         solved, send_ref, windows = refs[12:15]
     granules, bands = solved.shape[:2]
-    read_graph(offset_ref, count_ref, graph)
+    read_graph(offset_ref, graph)
     if interior:
         windows[...] = jnp.zeros_like(windows)
     spread_weights(shares, interior, weights)
@@ -578,7 +586,7 @@
     diagonal = by_lane_tile(pif_diagonal)
     cross = by_lane_tile(pif_cross.transpose(1, 0, 2).reshape(bands, granules // 8, 8, KN * KN))
     coupling = by_lane_tile(pif_coupling.transpose(0, 2, 1, 3))
-    graph = [("v", neighbour_offset.T), ("v", neighbour_count[None, :])]
+    graph = [("v", neighbour_offset.T)]
     tiles = [("v", tile_route.T), ("v", tile_window.transpose(1, 2, 0))]
     edge = (REACH, bands, 64, LANES)
     own = (granules, bands, 64, LANES)
@@ -616,7 +624,7 @@
         some = (part, bands, 64, LANES)
         return call(
             functools.partial(arrange, interior),
-            graph + [("h", source) for source in sources],
+            [("v", neighbour_count[None, :])] + [("h", source) for source in sources],
             [
                 ("v", some, f32),
                 ("v", some, f32),
@@ -624,17 +632,19 @@
                 ("v", (part, slots, bands, 32, LANES), f32),
             ],
             [
+                pltpu.VMEM(some, f32),
+                pltpu.VMEM(some, f32),
                 pltpu.VMEM(cross.shape, f32),
                 pltpu.VMEM((part,) + coupling.shape[1:], bf16),
                 pltpu.VMEM(coupling.shape[1:], f32),
-                pltpu.SMEM((2, granules), jnp.int32),
+                pltpu.SMEM((part,), jnp.int32),
                 pltpu.SemaphoreType.DMA((4, chunks)),
             ],
         )
 
     gathered = pltpu.VMEM((slots, 64, LANES), f32)
     weights = pltpu.VMEM((slots, 64, LANES), f32)
-    scalars = pltpu.SMEM((2, granules), jnp.int32)
+    scalars = pltpu.SMEM((granules,), jnp.int32)
 
     def over_band(partial, rounded):
         return [("v", partial)] + [
@@ -644,21 +654,24 @@
 
     for sweep in range(SWEEPS):
         last = sweep == SWEEPS - 1
-        inner, inner_rounded = call(
-            interior_disparities, graph + [("v", extended)], packed, [gathered, scalars]
+        inner, *inner_rounded = call(
+            interior_disparities,
+            graph + [("v", extended)],
+            packed if last else packed[:1],
+            [gathered],
         )
         if sweep == 0:
             inner, *edge_state = lax.optimization_barrier((inner, *arranged(False, sources)))
         if last:
-            inner_shares = over_band(inner, inner_rounded)
+            inner_shares = over_band(inner, *inner_rounded)
         inputs = graph + [("v", near), ("v", far), ("v", extended)]
         inputs += [] if last else [("v", inner)]
         extended, partial, rounded = call(
             edge_disparities,
             inputs,
             [("v", ext, f32)] + packed,
-            [gathered, scalars],
-            aliases={4: 0},
+            [gathered],
+            aliases={3: 0},
         )
         shares = over_band(partial, rounded)
         if sweep == 1:

time: 70 us -> 71.5 us (1.021)
  Pallas kernels: 24.5 us -> 26.8 us
  waiting for transfers between devices: 12.1 us -> 11.2 us
    pallas_call x18, Pallas kernels: 24.5 us -> 26.8 us  [call(): pl.pallas_call(body, in_specs=[ON_CHIP if kind == 'v' else ANYWHERE for k...]
    ppermute x3, waiting for transfers between devices: 9.38 us -> 8.24 us  [exchange(): near = lax.ppermute(near, 'gran', near_pairs)]
  transfers between devices with their start and end apart: 18 -> 18, of which waited for: 7 -> 8; matrix products, arithmetic and copies ran while one was open for 0% -> 0% of each run, Pallas kernels for 23% -> 24%
where the time goes in v10:
time: 71.5 us; the launch traced here: 71.2 us
  Pallas kernels  26.8 us (37%)
  starting transfers between devices  18.1 us (25%)
  blocking collectives  14.2 us (20%)
  waiting for transfers between devices  11.2 us (16%)
  between operations  0.86 us (1%)
    pallas_call x18, Pallas kernels, call(): pl.pallas_call(body, in_specs=[ON_CHIP if kind == 'v' else ANYWHERE for k...  26.8 us
    all_to_all x1, blocking collectives, per_device(): lax.all_to_all(payload, 'gran', split_axis=0, concat_axis=0, tiled=True)  14.2 us
    ppermute x3, starting transfers between devices, exchange(): near = lax.ppermute(near, 'gran', near_pairs)  8.29 us
    ppermute x3, waiting for transfers between devices, exchange(): near = lax.ppermute(near, 'gran', near_pairs)  8.24 us
    ppermute x12, starting transfers between devices, over_band(): lax.ppermute(rounded, 'band', [(i, i ^ flip) for i in range(band_total)])  7.68 us
    ppermute x12, waiting for transfers between devices, over_band(): lax.ppermute(rounded, 'band', [(i, i ^ flip) for i in range(band_total)])  2.96 us
    ppermute x3, starting transfers between devices, exchange(): far = lax.ppermute(far, 'gran', far_pairs)  2.11 us
  transfers between devices with their start and end apart: 18, of which 8 were waited for; matrix products, arithmetic and copies ran while one was open for 0% of the time, Pallas kernels for 24%

profile of v10, /device:TPU:0, one launch (start us, length us, event | category | flops | bytes accessed | tf_op | source)
XLA Modules:
  0.0 71.2 jit_solution(11222306830153868872)
XLA Ops:
  0.6 1.3 %shard_map.113 = (bf16[4,3,64,128]{3,2,1,0:T(8,128)(2,1)S(1)}, bf16[4,3,64,128]{3,2,1,0:T(8,128)(2,1)S(1)}) custom-call(f32[16,3,64,128]{3,2,1,0:T(8,128)} %bitcast.61), custom_call_target="tpu_custom_call" | custom-call | tf_op jit(solution)/shard_map/pallas_call | solution.py:32
  1.9 0.0 copy-start
  2.0 3.0 %collective-permute-start = (bf16[4,3,64,128]{3,2,1,0:T(8,128)(2,1)S(1)}, bf16[4,3,64,128]{3,2,1,0:T(8,128)(2,1)S(1)}, u32[]{:S(2)}, u32[]{:S(2)}) collective-permute-start(bf16[4,3,64,128]{3,2,1,0:T(8,128)(2,1)S(1)} %get-tuple-element.54), channel_id=1, source_target_pairs={{0,4},{4,0},{8,12},{12,8},{16,20},{20,16},{24,28},{28,24},{1,5},{5... | collective-permute-start | bytes 589832 | tf_op jit(solution)/shard_map/ppermute | solution.py:604
  5.0 0.8 %collective-permute-start.1 = (bf16[4,3,64,128]{3,2,1,0:T(8,128)(2,1)S(1)}, bf16[4,3,64,128]{3,2,1,0:T(8,128)(2,1)S(1)}, u32[]{:S(2)}, u32[]{:S(2)}) collective-permute-start(bf16[4,3,64,128]{3,2,1,0:T(8,128)(2,1)S(1)} %get-tuple-element.55), channel_id=1, source_target_pairs={{4,8},{8,4},{12,16},{16,12},{20,24},{24,20},{5,9},{9,5},{13,17},{1... | collective-permute-start | bytes 589832 | tf_op jit(solution)/shard_map/ppermute | solution.py:603
  5.8 1.5 %shard_map.114.ext_ref.refs_0_ = f32[24,3,64,128]{3,2,1,0:T(8,128)S(1)} custom-call(f32[16,3,64,128]{3,2,1,0:T(8,128)} %bitcast.62), custom_call_target="tpu_custom_call" | custom-call | tf_op jit(solution)/shard_map/pallas_call | solution.py:32
  7.3 1.2 %shard_map.115.refs_1_ = f32[64,128]{1,0:T(8,128)S(1)} custom-call(s32[8,16]{1,0:T(8,128)S(1)} %bitcast.38, f32[24,3,64,128]{3,2,1,0:T(8,128)S(1)} %shard_map.114.ext_ref.refs_0_), custom_call_target="tpu_custom_call" | custom-call | tf_op jit(solution)/shard_map/pallas_call | solution.py:32
  8.5 3.2 %shard_map.116 = (f32[8,3,64,128]{3,2,1,0:T(8,128)S(1)}, f32[8,3,64,128]{3,2,1,0:T(8,128)S(1)}, f32[8,3,32,128]{3,2,1,0:T(8,128)S(1)}, f32[8,8,3,32,128]{4,3,2,1,0:T(8,128)S(1)}) custom-call(s32[1,16]{1,0:T(1,128)S(1)} %bitcast.52, f32[16,3,64,128]{3,2,1,0:T(8,128)} %bitcast.57, f32[16,3,64,128]{3,2,1,0:T(8,128)} %bitcast.59, f32[3,2,256,128]{3,2,1,0:T(8,128)} %bitcast.63, ...), custom_call_target="tpu_custom_call" | custom-call | tf_op jit(solution)/shard_map/pallas_call | solution.py:32
  11.8 1.6 %collective-permute-done.near_ref = bf16[4,3,64,128]{3,2,1,0:T(8,128)(2,1)S(1)} collective-permute-done((bf16[4,3,64,128]{3,2,1,0:T(8,128)(2,1)S(1)}, bf16[4,3,64,128]{3,2,1,0:T(8,128)(2,1)S(1)}, u32[]{:S(2)}, u32[]{:S(2)}) %collective-permute-start) | collective-permute-done | bytes 196640 | tf_op jit(solution)/shard_map/ppermute | solution.py:604
  13.3 1.3 %shard_map.117 = (f32[24,3,64,128]{3,2,1,0:T(8,128)S(1)}, f32[64,128]{1,0:T(8,128)S(1)}, bf16[64,128]{1,0:T(8,128)(2,1)S(1)}) custom-call(s32[8,16]{1,0:T(8,128)S(1)} %bitcast.39, bf16[4,3,64,128]{3,2,1,0:T(8,128)(2,1)S(1)} %collective-permute-done.near_ref, ...), custom_call_target="tpu_custom_call", output_to_operand_aliasing={{0}: (3, {})} | custom-call | tf_op jit(solution)/shard_map/pallas_call | solution.py:32
  14.6 0.1 collective-permute-start.4
  14.7 1.6 %collective-permute-start.3 = (bf16[64,128]{1,0:T(8,128)(2,1)S(1)}, bf16[64,128]{1,0:T(8,128)(2,1)S(1)}, u32[]{:S(2)}, u32[]{:S(2)}) collective-permute-start(bf16[64,128]{1,0:T(8,128)(2,1)S(1)} %get-tuple-element.62), channel_id=1, source_target_pairs={{0,2},{1,3},{2,0},{3,1},{4,6},{5,7},{6,4},{7,5},{8,10},{9,11},{10,... | collective-permute-start | bytes 49160 | tf_op jit(solution)/shard_map/ppermute | solution.py:651
  16.3 0.3 collective-permute-start.2
  16.5 1.4 %collective-permute-done.4.refs_3_ = bf16[64,128]{1,0:T(8,128)(2,1)S(1)} collective-permute-done((bf16[64,128]{1,0:T(8,128)(2,1)S(1)}, bf16[64,128]{1,0:T(8,128)(2,1)S(1)}, u32[]{:S(2)}, u32[]{:S(2)}) %collective-permute-start.4) | collective-permute-done | bytes 16416 | tf_op jit(solution)/shard_map/ppermute | solution.py:651
  17.9 0.6 collective-permute-done.3.refs_2_
  18.5 0.9 %shard_map.118 = (f32[24,3,64,128]{3,2,1,0:T(8,128)S(1)}, bf16[4,3,64,128]{3,2,1,0:T(8,128)(2,1)S(1)}, bf16[4,3,64,128]{3,2,1,0:T(8,128)(2,1)S(1)}) custom-call(s32[8,16]{1,0:T(8,128)S(1)} %bitcast.40, f32[64,128]{1,0:T(8,128)S(1)} %get-tuple-element.61.refs_0_, bf16[64,128]{1,0:T(8,128)(2,1)S(1)} %collective-permute-done.2.refs_1_, ...), custom_call_target="tpu_custom_call" | custom-call | tf_op jit(solution)/shard_map/pallas_call | solution.py:32
  19.4 2.8 %collective-permute-start.5 = (bf16[4,3,64,128]{3,2,1,0:T(8,128)(2,1)S(1)}, bf16[4,3,64,128]{3,2,1,0:T(8,128)(2,1)S(1)}, u32[]{:S(2)}, u32[]{:S(2)}) collective-permute-start(bf16[4,3,64,128]{3,2,1,0:T(8,128)(2,1)S(1)} %get-tuple-element.68), channel_id=1, source_target_pairs={{0,4},{4,0},{8,12},{12,8},{16,20},{20,16},{24,28},{28,24},{1,5},{5... | collective-permute-start | bytes 589832 | tf_op jit(solution)/shard_map/ppermute | solution.py:604
  22.2 0.7 collective-permute-start.6
  22.9 3.0 %shard_map.119 = (f32[8,3,64,128]{3,2,1,0:T(8,128)S(1)}, f32[8,3,64,128]{3,2,1,0:T(8,128)S(1)}, f32[8,3,32,128]{3,2,1,0:T(8,128)S(1)}, f32[8,8,3,32,128]{4,3,2,1,0:T(8,128)S(1)}) custom-call(s32[1,16]{1,0:T(1,128)S(1)} %bitcast.53, f32[16,3,64,128]{3,2,1,0:T(8,128)} %bitcast.58, f32[16,3,64,128]{3,2,1,0:T(8,128)} %bitcast.60, f32[3,2,256,128]{3,2,1,0:T(8,128)} %bitcast.64, ...), custom_call_target="tpu_custom_call" | custom-call | tf_op jit(solution)/shard_map/pallas_call | solution.py:32
  26.0 0.8 %shard_map.120.ext_ref.refs_0_ = f32[24,3,64,128]{3,2,1,0:T(8,128)S(1)} custom-call(s32[8,16]{1,0:T(8,128)S(1)} %bitcast.41, f32[64,128]{1,0:T(8,128)S(1)} %get-tuple-element.61.refs_0_, bf16[64,128]{1,0:T(8,128)(2,1)S(1)} %collective-permute-done.2.refs_1_, bf16[64,128]{1,0:T(8,128)(2,1)S(1)} %collective-permute-done.3.refs_2_, ...), custom_call_target="tpu_custom_call", output_to_operand_aliasing={{}: (10, {})} | custom-call | tf_op jit(solution)/shard_map/pallas_call | solution.py:32
  26.7 0.0 copy-start.2
  26.8 0.0 copy-start.4
  26.8 1.2 %shard_map.121.refs_1_ = f32[64,128]{1,0:T(8,128)S(1)} custom-call(s32[8,16]{1,0:T(8,128)S(1)} %bitcast.42, f32[24,3,64,128]{3,2,1,0:T(8,128)S(1)} %shard_map.120.ext_ref.refs_0_), custom_call_target="tpu_custom_call" | custom-call | tf_op jit(solution)/shard_map/pallas_call | solution.py:32
  28.0 2.9 %collective-permute-done.5.near_ref = bf16[4,3,64,128]{3,2,1,0:T(8,128)(2,1)S(1)} collective-permute-done((bf16[4,3,64,128]{3,2,1,0:T(8,128)(2,1)S(1)}, bf16[4,3,64,128]{3,2,1,0:T(8,128)(2,1)S(1)}, u32[]{:S(2)}, u32[]{:S(2)}) %collective-permute-start.5) | collective-permute-done | bytes 196640 | tf_op jit(solution)/shard_map/ppermute | solution.py:604
  30.9 1.3 %shard_map.122 = (f32[24,3,64,128]{3,2,1,0:T(8,128)S(1)}, f32[64,128]{1,0:T(8,128)S(1)}, bf16[64,128]{1,0:T(8,128)(2,1)S(1)}) custom-call(s32[8,16]{1,0:T(8,128)S(1)} %bitcast.43, bf16[4,3,64,128]{3,2,1,0:T(8,128)(2,1)S(1)} %collective-permute-done.5.near_ref, ...), custom_call_target="tpu_custom_call", output_to_operand_aliasing={{0}: (3, {})} | custom-call | tf_op jit(solution)/shard_map/pallas_call | solution.py:32
  32.2 0.1 collective-permute-start.9
  32.2 0.6 collective-permute-start.8
  32.8 1.2 %collective-permute-start.7 = (bf16[64,128]{1,0:T(8,128)(2,1)S(1)}, bf16[64,128]{1,0:T(8,128)(2,1)S(1)}, u32[]{:S(2)}, u32[]{:S(2)}) collective-permute-start(bf16[64,128]{1,0:T(8,128)(2,1)S(1)} %get-tuple-element.87), channel_id=1, source_target_pairs={{0,1},{1,0},{2,3},{3,2},{4,5},{5,4},{6,7},{7,6},{8,9},{9,8},{10,11... | collective-permute-start | bytes 49160 | tf_op jit(solution)/shard_map/ppermute | solution.py:651
  34.1 1.8 %shard_map.123 = (bf16[256,1024]{1,0:T(8,128)(2,1)S(1)}, bf16[256,1024]{1,0:T(8,128)(2,1)S(1)}, s32[8,128]{1,0:T(8,128)S(1)}) custom-call(s32[2,128]{1,0:T(2,128)S(1)} %bitcast.50, s32[2,2,128]{2,1,0:T(2,128)S(1)} %bitcast.54), custom_call_target="tpu_custom_call" | custom-call | tf_op jit(solution)/shard_map/pallas_call | solution.py:32
  35.9 0.1 collective-permute-done.8.refs_2_
  36.0 0.9 %shard_map.124 = (f32[24,3,64,128]{3,2,1,0:T(8,128)S(1)}, bf16[4,3,64,128]{3,2,1,0:T(8,128)(2,1)S(1)}, bf16[4,3,64,128]{3,2,1,0:T(8,128)(2,1)S(1)}) custom-call(s32[8,16]{1,0:T(8,128)S(1)} %bitcast.44, f32[64,128]{1,0:T(8,128)S(1)} %get-tuple-element.86.refs_0_, bf16[64,128]{1,0:T(8,128)(2,1)S(1)} %collective-permute-done.7.refs_1_, ...), custom_call_target="tpu_custom_call" | custom-call | tf_op jit(solution)/shard_map/pallas_call | solution.py:32
  37.0 2.4 %collective-permute-start.10 = (bf16[4,3,64,128]{3,2,1,0:T(8,128)(2,1)S(1)}, bf16[4,3,64,128]{3,2,1,0:T(8,128)(2,1)S(1)}, u32[]{:S(2)}, u32[]{:S(2)}) collective-permute-start(bf16[4,3,64,128]{3,2,1,0:T(8,128)(2,1)S(1)} %get-tuple-element.89), channel_id=1, source_target_pairs={{0,4},{4,0},{8,12},{12,8},{16,20},{20,16},{24,28},{28,24},{1,5},{5... | collective-permute-start | bytes 589832 | tf_op jit(solution)/shard_map/ppermute | solution.py:604
  39.4 0.7 collective-permute-start.11
  40.1 0.8 %shard_map.125.refs_0_.ext_ref = f32[24,3,64,128]{3,2,1,0:T(8,128)S(1)} custom-call(s32[8,16]{1,0:T(8,128)S(1)} %bitcast.45, f32[64,128]{1,0:T(8,128)S(1)} %get-tuple-element.86.refs_0_, bf16[64,128]{1,0:T(8,128)(2,1)S(1)} %collective-permute-done.7.refs_1_, bf16[64,128]{1,0:T(8,128)(2,1)S(1)} %collective-permute-done.8.refs_2_, ...), custom_call_target="tpu_custom_call", output_to_operand_aliasing={{}: (10, {})} | custom-call | tf_op jit(solution)/shard_map/pallas_call | solution.py:32
  40.9 1.2 %shard_map.127 = (f32[64,128]{1,0:T(8,128)S(1)}, bf16[64,128]{1,0:T(8,128)(2,1)S(1)}) custom-call(s32[8,16]{1,0:T(8,128)S(1)} %bitcast.46, f32[24,3,64,128]{3,2,1,0:T(8,128)S(1)} %shard_map.125.refs_0_.ext_ref), custom_call_target="tpu_custom_call" | custom-call | tf_op jit(solution)/shard_map/pallas_call | solution.py:32
  42.1 0.3 collective-permute-start.17
  42.5 1.0 %collective-permute-start.16 = (bf16[64,128]{1,0:T(8,128)(2,1)S(1)}, bf16[64,128]{1,0:T(8,128)(2,1)S(1)}, u32[]{:S(2)}, u32[]{:S(2)}) collective-permute-start(bf16[64,128]{1,0:T(8,128)(2,1)S(1)} %get-tuple-element.97), channel_id=1, source_target_pairs={{0,2},{1,3},{2,0},{3,1},{4,6},{5,7},{6,4},{7,5},{8,10},{9,11},{10,... | collective-permute-start | bytes 49160 | tf_op jit(solution)/shard_map/ppermute | solution.py:651
  43.4 0.6 collective-permute-start.15
  44.0 3.8 %collective-permute-done.10.near_ref = bf16[4,3,64,128]{3,2,1,0:T(8,128)(2,1)S(1)} collective-permute-done((bf16[4,3,64,128]{3,2,1,0:T(8,128)(2,1)S(1)}, bf16[4,3,64,128]{3,2,1,0:T(8,128)(2,1)S(1)}, u32[]{:S(2)}, u32[]{:S(2)}) %collective-permute-start.10) | collective-permute-done | bytes 196640 | tf_op jit(solution)/shard_map/ppermute | solution.py:604
  47.8 1.3 %shard_map.126 = (f32[24,3,64,128]{3,2,1,0:T(8,128)S(1)}, f32[64,128]{1,0:T(8,128)S(1)}, bf16[64,128]{1,0:T(8,128)(2,1)S(1)}) custom-call(s32[8,16]{1,0:T(8,128)S(1)} %bitcast.47, bf16[4,3,64,128]{3,2,1,0:T(8,128)(2,1)S(1)} %collective-permute-done.10.near_ref, ...), custom_call_target="tpu_custom_call", output_to_operand_aliasing={{0}: (3, {})} | custom-call | tf_op jit(solution)/shard_map/pallas_call | solution.py:32
  49.1 0.1 collective-permute-start.14
  49.2 1.1 %collective-permute-start.13 = (bf16[64,128]{1,0:T(8,128)(2,1)S(1)}, bf16[64,128]{1,0:T(8,128)(2,1)S(1)}, u32[]{:S(2)}, u32[]{:S(2)}) collective-permute-start(bf16[64,128]{1,0:T(8,128)(2,1)S(1)} %get-tuple-element.93), channel_id=1, source_target_pairs={{0,2},{1,3},{2,0},{3,1},{4,6},{5,7},{6,4},{7,5},{8,10},{9,11},{10,... | collective-permute-start | bytes 49160 | tf_op jit(solution)/shard_map/ppermute | solution.py:651
  50.3 0.7 %collective-permute-start.12 = (bf16[64,128]{1,0:T(8,128)(2,1)S(1)}, bf16[64,128]{1,0:T(8,128)(2,1)S(1)}, u32[]{:S(2)}, u32[]{:S(2)}) collective-permute-start(bf16[64,128]{1,0:T(8,128)(2,1)S(1)} %get-tuple-element.93), channel_id=1, source_target_pairs={{0,1},{1,0},{2,3},{3,2},{4,5},{5,4},{6,7},{7,6},{8,9},{9,8},{10,11... | collective-permute-start | bytes 49160 | tf_op jit(solution)/shard_map/ppermute | solution.py:651
  51.0 1.1 %shard_map.128 = (f32[16,3,64,128]{3,2,1,0:T(8,128)S(1)}, f32[8,96,128]{2,1,0:T(8,128)S(1)}) custom-call(s32[8,16]{1,0:T(8,128)S(1)} %bitcast.48, f32[64,128]{1,0:T(8,128)S(1)} %get-tuple-element.96.refs_0_, bf16[64,128]{1,0:T(8,128)(2,1)S(1)} %collective-permute-done.15.refs_1_, bf16[64,128]{1,0:T(8,128)(2,1)S(1)} %collective-permute-done.16.refs_2_, ...), custom_call_target="tpu_custom_call" | custom-call | tf_op jit(solution)/shard_map/pallas_call | solution.py:32
  52.2 0.1 collective-permute-done.14.refs_3_
  52.3 0.7 collective-permute-done.13.refs_2_
  53.0 1.3 %shard_map.129 = (f32[16,3,64,128]{3,2,1,0:T(8,128)S(1)}, bf16[8,96,128]{2,1,0:T(8,128)(2,1)S(1)}, f32[8,96,128]{2,1,0:T(8,128)S(1)}) custom-call(s32[8,16]{1,0:T(8,128)S(1)} %bitcast.49, f32[64,128]{1,0:T(8,128)S(1)} %get-tuple-element.92.refs_0_, ...), custom_call_target="tpu_custom_call", output_to_operand_aliasing={{0}: (11, {}), {2}: (12, {})} | custom-call | tf_op jit(solution)/shard_map/pallas_call | solution.py:32
  54.4 14.2 %all_to_all.5.received_ref = bf16[8,96,128]{2,1,0:T(8,128)(2,1)S(1)} all-to-all(bf16[8,96,128]{2,1,0:T(8,128)(2,1)S(1)} %get-tuple-element.100), channel_id=1, replica_groups=mesh['gran'=8,'band'=4] {'gran'}, dimensions={0} | all-to-all | bytes 393216 | tf_op jit(solution)/shard_map/all_to_all | solution.py:725
  68.6 2.6 %shard_map.130 = (bf16[1,3,256,256]{3,2,1,0:T(8,128)(2,1)}, f32[16,3,64,128]{3,2,1,0:T(8,128)}) custom-call(s32[2,128]{1,0:T(2,128)S(1)} %bitcast.51, bf16[8,96,128]{2,1,0:T(8,128)(2,1)S(1)} %all_to_all.5.received_ref, bf16[256,1024]{1,0:T(8,128)(2,1)S(1)} %get-tuple-element.101.row_ref, bf16[256,1024]{1,0:T(8,128)(2,1)S(1)} %get-tuple-element.102.col_ref, ...), custom_call_target="tpu_custom_call" | custom-call | tf_op jit(solution)/shard_map/pallas_call | solution.py:32
  (17 shorter events, 0.0 us)
Async XLA Ops:
  1.9 5.3 %copy-start = (s32[16,8]{0,1:T(8,128)S(1)}, s32[16,8]{0,1:T(8,128)}, u32[]{:S(2)}) copy-start(s32[16,8]{0,1:T(8,128)} %param.15) | copy-start | bytes 1540
  2.0 11.4 %collective-permute-start = (bf16[4,3,64,128]{3,2,1,0:T(8,128)(2,1)S(1)}, bf16[4,3,64,128]{3,2,1,0:T(8,128)(2,1)S(1)}, u32[]{:S(2)}, u32[]{:S(2)}) collective-permute-start(bf16[4,3,64,128]{3,2,1,0:T(8,128)(2,1)S(1)} %get-tuple-element.54), channel_id=1, source_target_pairs={{0,4},{4,0},{8,12},{12,8},{16,20},{20,16},{24,28},{28,24},{1,5},{5... | collective-permute-start | bytes 589832 | tf_op jit(solution)/shard_map/ppermute | solution.py:604
  5.0 3.5 %copy-start.3 = (s32[16]{0:T(128)S(1)}, s32[16]{0:T(128)}, u32[]{:S(2)}) copy-start(s32[16]{0:T(128)} %param.16) | copy-start | bytes 196
  5.0 8.4 %collective-permute-start.1 = (bf16[4,3,64,128]{3,2,1,0:T(8,128)(2,1)S(1)}, bf16[4,3,64,128]{3,2,1,0:T(8,128)(2,1)S(1)}, u32[]{:S(2)}, u32[]{:S(2)}) collective-permute-start(bf16[4,3,64,128]{3,2,1,0:T(8,128)(2,1)S(1)} %get-tuple-element.55), channel_id=1, source_target_pairs={{4,8},{8,4},{12,16},{16,12},{20,24},{24,20},{5,9},{9,5},{13,17},{1... | collective-permute-start | bytes 589832 | tf_op jit(solution)/shard_map/ppermute | solution.py:603
  14.6 3.3 %collective-permute-start.4 = (bf16[64,128]{1,0:T(8,128)(2,1)S(1)}, bf16[64,128]{1,0:T(8,128)(2,1)S(1)}, u32[]{:S(2)}, u32[]{:S(2)}) collective-permute-start(bf16[64,128]{1,0:T(8,128)(2,1)S(1)} %get-tuple-element.62), channel_id=1, source_target_pairs={{0,3},{1,2},{2,1},{3,0},{4,7},{5,6},{6,5},{7,4},{8,11},{9,10},{10,... | collective-permute-start | bytes 49160 | tf_op jit(solution)/shard_map/ppermute | solution.py:651
  14.7 3.8 %collective-permute-start.3 = (bf16[64,128]{1,0:T(8,128)(2,1)S(1)}, bf16[64,128]{1,0:T(8,128)(2,1)S(1)}, u32[]{:S(2)}, u32[]{:S(2)}) collective-permute-start(bf16[64,128]{1,0:T(8,128)(2,1)S(1)} %get-tuple-element.62), channel_id=1, source_target_pairs={{0,2},{1,3},{2,0},{3,1},{4,6},{5,7},{6,4},{7,5},{8,10},{9,11},{10,... | collective-permute-start | bytes 49160 | tf_op jit(solution)/shard_map/ppermute | solution.py:651
  16.3 2.2 %collective-permute-start.2 = (bf16[64,128]{1,0:T(8,128)(2,1)S(1)}, bf16[64,128]{1,0:T(8,128)(2,1)S(1)}, u32[]{:S(2)}, u32[]{:S(2)}) collective-permute-start(bf16[64,128]{1,0:T(8,128)(2,1)S(1)} %get-tuple-element.62), channel_id=1, source_target_pairs={{0,1},{1,0},{2,3},{3,2},{4,5},{5,4},{6,7},{7,6},{8,9},{9,8},{10,11... | collective-permute-start | bytes 49160 | tf_op jit(solution)/shard_map/ppermute | solution.py:651
  19.4 11.5 %collective-permute-start.5 = (bf16[4,3,64,128]{3,2,1,0:T(8,128)(2,1)S(1)}, bf16[4,3,64,128]{3,2,1,0:T(8,128)(2,1)S(1)}, u32[]{:S(2)}, u32[]{:S(2)}) collective-permute-start(bf16[4,3,64,128]{3,2,1,0:T(8,128)(2,1)S(1)} %get-tuple-element.68), channel_id=1, source_target_pairs={{0,4},{4,0},{8,12},{12,8},{16,20},{20,16},{24,28},{28,24},{1,5},{5... | collective-permute-start | bytes 589832 | tf_op jit(solution)/shard_map/ppermute | solution.py:604
  22.2 8.7 %collective-permute-start.6 = (bf16[4,3,64,128]{3,2,1,0:T(8,128)(2,1)S(1)}, bf16[4,3,64,128]{3,2,1,0:T(8,128)(2,1)S(1)}, u32[]{:S(2)}, u32[]{:S(2)}) collective-permute-start(bf16[4,3,64,128]{3,2,1,0:T(8,128)(2,1)S(1)} %get-tuple-element.69), channel_id=1, source_target_pairs={{4,8},{8,4},{12,16},{16,12},{20,24},{24,20},{5,9},{9,5},{13,17},{1... | collective-permute-start | bytes 589832 | tf_op jit(solution)/shard_map/ppermute | solution.py:603
  26.7 7.3 %copy-start.2 = (s32[128,2]{0,1:T(2,128)S(1)}, s32[128,2]{0,1:T(2,128)}, u32[]{:S(2)}) copy-start(s32[128,2]{0,1:T(2,128)} %param.17) | copy-start | bytes 3076
  26.8 7.3 %copy-start.4 = (s32[128,2,2]{0,2,1:T(2,128)S(1)}, s32[128,2,2]{0,2,1:T(2,128)}, u32[]{:S(2)}) copy-start(s32[128,2,2]{0,2,1:T(2,128)} %param.18) | copy-start | bytes 6148
  32.2 3.7 %collective-permute-start.9 = (bf16[64,128]{1,0:T(8,128)(2,1)S(1)}, bf16[64,128]{1,0:T(8,128)(2,1)S(1)}, u32[]{:S(2)}, u32[]{:S(2)}) collective-permute-start(bf16[64,128]{1,0:T(8,128)(2,1)S(1)} %get-tuple-element.87), channel_id=1, source_target_pairs={{0,3},{1,2},{2,1},{3,0},{4,7},{5,6},{6,5},{7,4},{8,11},{9,10},{10,... | collective-permute-start | bytes 49160 | tf_op jit(solution)/shard_map/ppermute | solution.py:651
  32.2 3.8 %collective-permute-start.8 = (bf16[64,128]{1,0:T(8,128)(2,1)S(1)}, bf16[64,128]{1,0:T(8,128)(2,1)S(1)}, u32[]{:S(2)}, u32[]{:S(2)}) collective-permute-start(bf16[64,128]{1,0:T(8,128)(2,1)S(1)} %get-tuple-element.87), channel_id=1, source_target_pairs={{0,2},{1,3},{2,0},{3,1},{4,6},{5,7},{6,4},{7,5},{8,10},{9,11},{10,... | collective-permute-start | bytes 49160 | tf_op jit(solution)/shard_map/ppermute | solution.py:651
  32.8 3.2 %collective-permute-start.7 = (bf16[64,128]{1,0:T(8,128)(2,1)S(1)}, bf16[64,128]{1,0:T(8,128)(2,1)S(1)}, u32[]{:S(2)}, u32[]{:S(2)}) collective-permute-start(bf16[64,128]{1,0:T(8,128)(2,1)S(1)} %get-tuple-element.87), channel_id=1, source_target_pairs={{0,1},{1,0},{2,3},{3,2},{4,5},{5,4},{6,7},{7,6},{8,9},{9,8},{10,11... | collective-permute-start | bytes 49160 | tf_op jit(solution)/shard_map/ppermute | solution.py:651
  37.0 10.9 %collective-permute-start.10 = (bf16[4,3,64,128]{3,2,1,0:T(8,128)(2,1)S(1)}, bf16[4,3,64,128]{3,2,1,0:T(8,128)(2,1)S(1)}, u32[]{:S(2)}, u32[]{:S(2)}) collective-permute-start(bf16[4,3,64,128]{3,2,1,0:T(8,128)(2,1)S(1)} %get-tuple-element.89), channel_id=1, source_target_pairs={{0,4},{4,0},{8,12},{12,8},{16,20},{20,16},{24,28},{28,24},{1,5},{5... | collective-permute-start | bytes 589832 | tf_op jit(solution)/shard_map/ppermute | solution.py:604
  39.4 8.4 %collective-permute-start.11 = (bf16[4,3,64,128]{3,2,1,0:T(8,128)(2,1)S(1)}, bf16[4,3,64,128]{3,2,1,0:T(8,128)(2,1)S(1)}, u32[]{:S(2)}, u32[]{:S(2)}) collective-permute-start(bf16[4,3,64,128]{3,2,1,0:T(8,128)(2,1)S(1)} %get-tuple-element.90), channel_id=1, source_target_pairs={{4,8},{8,4},{12,16},{16,12},{20,24},{24,20},{5,9},{9,5},{13,17},{1... | collective-permute-start | bytes 589832 | tf_op jit(solution)/shard_map/ppermute | solution.py:603
  42.1 8.2 %collective-permute-start.17 = (bf16[64,128]{1,0:T(8,128)(2,1)S(1)}, bf16[64,128]{1,0:T(8,128)(2,1)S(1)}, u32[]{:S(2)}, u32[]{:S(2)}) collective-permute-start(bf16[64,128]{1,0:T(8,128)(2,1)S(1)} %get-tuple-element.97), channel_id=1, source_target_pairs={{0,3},{1,2},{2,1},{3,0},{4,7},{5,6},{6,5},{7,4},{8,11},{9,10},{10,... | collective-permute-start | bytes 49160 | tf_op jit(solution)/shard_map/ppermute | solution.py:651
  42.5 8.6 %collective-permute-start.16 = (bf16[64,128]{1,0:T(8,128)(2,1)S(1)}, bf16[64,128]{1,0:T(8,128)(2,1)S(1)}, u32[]{:S(2)}, u32[]{:S(2)}) collective-permute-start(bf16[64,128]{1,0:T(8,128)(2,1)S(1)} %get-tuple-element.97), channel_id=1, source_target_pairs={{0,2},{1,3},{2,0},{3,1},{4,6},{5,7},{6,4},{7,5},{8,10},{9,11},{10,... | collective-permute-start | bytes 49160 | tf_op jit(solution)/shard_map/ppermute | solution.py:651
  43.4 7.6 %collective-permute-start.15 = (bf16[64,128]{1,0:T(8,128)(2,1)S(1)}, bf16[64,128]{1,0:T(8,128)(2,1)S(1)}, u32[]{:S(2)}, u32[]{:S(2)}) collective-permute-start(bf16[64,128]{1,0:T(8,128)(2,1)S(1)} %get-tuple-element.97), channel_id=1, source_target_pairs={{0,1},{1,0},{2,3},{3,2},{4,5},{5,4},{6,7},{7,6},{8,9},{9,8},{10,11... | collective-permute-start | bytes 49160 | tf_op jit(solution)/shard_map/ppermute | solution.py:651
  49.1 3.2 %collective-permute-start.14 = (bf16[64,128]{1,0:T(8,128)(2,1)S(1)}, bf16[64,128]{1,0:T(8,128)(2,1)S(1)}, u32[]{:S(2)}, u32[]{:S(2)}) collective-permute-start(bf16[64,128]{1,0:T(8,128)(2,1)S(1)} %get-tuple-element.93), channel_id=1, source_target_pairs={{0,3},{1,2},{2,1},{3,0},{4,7},{5,6},{6,5},{7,4},{8,11},{9,10},{10,... | collective-permute-start | bytes 49160 | tf_op jit(solution)/shard_map/ppermute | solution.py:651
  49.2 3.8 %collective-permute-start.13 = (bf16[64,128]{1,0:T(8,128)(2,1)S(1)}, bf16[64,128]{1,0:T(8,128)(2,1)S(1)}, u32[]{:S(2)}, u32[]{:S(2)}) collective-permute-start(bf16[64,128]{1,0:T(8,128)(2,1)S(1)} %get-tuple-element.93), channel_id=1, source_target_pairs={{0,2},{1,3},{2,0},{3,1},{4,6},{5,7},{6,4},{7,5},{8,10},{9,11},{10,... | collective-permute-start | bytes 49160 | tf_op jit(solution)/shard_map/ppermute | solution.py:651
  50.3 2.7 %collective-permute-start.12 = (bf16[64,128]{1,0:T(8,128)(2,1)S(1)}, bf16[64,128]{1,0:T(8,128)(2,1)S(1)}, u32[]{:S(2)}, u32[]{:S(2)}) collective-permute-start(bf16[64,128]{1,0:T(8,128)(2,1)S(1)} %get-tuple-element.93), channel_id=1, source_target_pairs={{0,1},{1,0},{2,3},{3,2},{4,5},{5,4},{6,7},{7,6},{8,9},{9,8},{10,11... | collective-permute-start | bytes 49160 | tf_op jit(solution)/shard_map/ppermute | solution.py:651
  53.0 15.5 %copy-start.1 = (bf16[1,3,256,256]{3,2,1,0:T(8,128)(2,1)S(1)}, bf16[1,3,256,256]{3,2,1,0:T(8,128)(2,1)}, u32[]{:S(2)}) copy-start(bf16[1,3,256,256]{3,2,1,0:T(8,128)(2,1)} %pixels_ref.1) | copy-start | bytes 1179652

commit v11 on v10

--- a/solution.py
+++ b/solution.py
@@ -160,13 +160,9 @@
     return ((col % KN) // PATCH == row % PATCH).astype(f32).astype(bf16)
 
 
-def graph_codes(offset_ref):
+def read_graph(offset_ref, graph):
     slot = lax.broadcasted_iota(jnp.int32, offset_ref.shape, 0)
-    return jnp.sum(jnp.left_shift(offset_ref[...] + REACH, 4 * slot), axis=0, keepdims=True)
-
-
-def read_graph(offset_ref, graph):
-    codes = graph_codes(offset_ref)
+    codes = jnp.sum(jnp.left_shift(offset_ref[...] + REACH, 4 * slot), axis=0, keepdims=True)
     for i in range(offset_ref.shape[1]):
         graph[i] = codes[0, i]
 
@@ -181,12 +177,12 @@
     return lane - slots * (1 - row if interior else row)
 
 
-def disparities(interior, offset_ref, ext_ref, gathered):
+def disparities(interior, offset_ref, ext_ref, gathered, graph):
     bands = ext_ref.shape[1]
     granules = ext_ref.shape[0] - 2 * REACH
     slots = gathered.shape[0]
     gathered[...] = jnp.zeros_like(gathered)
-    codes = graph_codes(offset_ref)
+    read_graph(offset_ref, graph)
 
     def response(g):
         return [
@@ -199,7 +195,7 @@
         if (REACH <= i < granules - REACH) != interior:
             continue
         own = response(i + REACH)
-        code = codes[0, i]
+        code = graph[i]
 
         def slot(s, i=i, own=own, code=code):
             total = None
@@ -227,22 +223,22 @@
 
 
 def interior_disparities(offset_ref, ext_ref, out_ref, *refs):
-    packed = disparities(True, offset_ref, ext_ref, refs[-1])
+    packed = disparities(True, offset_ref, ext_ref, *refs[-2:])
     out_ref[...] = packed
-    if len(refs) == 2:
+    if len(refs) == 3:
         refs[0][...] = packed.astype(bf16)
 
 
 def edge_disparities(offset_ref, near_ref, far_ref, *refs):
-    ext_ref, out_ref, send_ref, gathered = refs[-4:]
+    ext_ref, out_ref, send_ref, gathered, graph = refs[-5:]
     odd = parity()
     right = ext_ref.shape[0] - REACH
     for ref, base in ((near_ref, (1 - odd) * right), (far_ref, odd * right)):
         for g in range(REACH):
             for b in range(ref.shape[1]):
                 ext_ref[base + g, b] = ref[g, b].astype(f32)
-    packed = disparities(False, offset_ref, ext_ref, gathered)
-    if len(refs) == 6:
+    packed = disparities(False, offset_ref, ext_ref, gathered, graph)
+    if len(refs) == 7:
         packed = packed + refs[1][...]
     out_ref[...] = packed
     send_ref[...] = packed.astype(bf16)
@@ -658,7 +654,7 @@
             interior_disparities,
             graph + [("v", extended)],
             packed if last else packed[:1],
-            [gathered],
+            [gathered, scalars],
         )
         if sweep == 0:
             inner, *edge_state = lax.optimization_barrier((inner, *arranged(False, sources)))
@@ -670,7 +666,7 @@
             edge_disparities,
             inputs,
             [("v", ext, f32)] + packed,
-            [gathered],
+            [gathered, scalars],
             aliases={3: 0},
         )
         shares = over_band(partial, rounded)

time: 71.5 us -> 69.1 us (0.966)
  Pallas kernels: 26.8 us -> 22.9 us
  waiting for transfers between devices: 11.2 us -> 13.4 us
    pallas_call x18, Pallas kernels: 26.8 us -> 22.9 us  [call(): pl.pallas_call(body, in_specs=[ON_CHIP if kind == 'v' else ANYWHERE for k...]
    ppermute x3, waiting for transfers between devices: 8.24 us -> 10.5 us  [exchange(): near = lax.ppermute(near, 'gran', near_pairs)]
  transfers between devices with their start and end apart: 18 -> 18, of which waited for: 8 -> 8; matrix products, arithmetic and copies ran while one was open for 0% -> 0% of each run, Pallas kernels for 24% -> 21%
where the time goes in v11:
time: 69.1 us; the launch traced here: 68.9 us
  Pallas kernels  22.9 us (33%)
  starting transfers between devices  17.9 us (26%)
  blocking collectives  13.8 us (20%)
  waiting for transfers between devices  13.4 us (19%)
  between operations  0.86 us (1%)
    pallas_call x18, Pallas kernels, call(): pl.pallas_call(body, in_specs=[ON_CHIP if kind == 'v' else ANYWHERE for k...  22.9 us
    all_to_all x1, blocking collectives, per_device(): lax.all_to_all(payload, 'gran', split_axis=0, concat_axis=0, tiled=True)  13.8 us
    ppermute x3, waiting for transfers between devices, exchange(): near = lax.ppermute(near, 'gran', near_pairs)  10.5 us
    ppermute x3, starting transfers between devices, exchange(): near = lax.ppermute(near, 'gran', near_pairs)  8.1 us
    ppermute x12, starting transfers between devices, over_band(): lax.ppermute(rounded, 'band', [(i, i ^ flip) for i in range(band_total)])  7.68 us
    ppermute x12, waiting for transfers between devices, over_band(): lax.ppermute(rounded, 'band', [(i, i ^ flip) for i in range(band_total)])  2.92 us
    ppermute x3, starting transfers between devices, exchange(): far = lax.ppermute(far, 'gran', far_pairs)  2.11 us
  transfers between devices with their start and end apart: 18, of which 8 were waited for; matrix products, arithmetic and copies ran while one was open for 0% of the time, Pallas kernels for 21%

profile of v11, /device:TPU:0, one launch (start us, length us, event | category | flops | bytes accessed | tf_op | source)
XLA Modules:
  0.0 68.9 jit_solution(3942668553063936198)
XLA Ops:
  0.6 1.3 %shard_map.113 = (bf16[4,3,64,128]{3,2,1,0:T(8,128)(2,1)S(1)}, bf16[4,3,64,128]{3,2,1,0:T(8,128)(2,1)S(1)}) custom-call(f32[16,3,64,128]{3,2,1,0:T(8,128)} %bitcast.61), custom_call_target="tpu_custom_call" | custom-call | tf_op jit(solution)/shard_map/pallas_call | solution.py:32
  1.9 0.0 copy-start
  2.0 3.0 %collective-permute-start = (bf16[4,3,64,128]{3,2,1,0:T(8,128)(2,1)S(1)}, bf16[4,3,64,128]{3,2,1,0:T(8,128)(2,1)S(1)}, u32[]{:S(2)}, u32[]{:S(2)}) collective-permute-start(bf16[4,3,64,128]{3,2,1,0:T(8,128)(2,1)S(1)} %get-tuple-element.54), channel_id=1, source_target_pairs={{0,4},{4,0},{8,12},{12,8},{16,20},{20,16},{24,28},{28,24},{1,5},{5... | collective-permute-start | bytes 589832 | tf_op jit(solution)/shard_map/ppermute | solution.py:600
  5.0 0.8 %collective-permute-start.1 = (bf16[4,3,64,128]{3,2,1,0:T(8,128)(2,1)S(1)}, bf16[4,3,64,128]{3,2,1,0:T(8,128)(2,1)S(1)}, u32[]{:S(2)}, u32[]{:S(2)}) collective-permute-start(bf16[4,3,64,128]{3,2,1,0:T(8,128)(2,1)S(1)} %get-tuple-element.55), channel_id=1, source_target_pairs={{4,8},{8,4},{12,16},{16,12},{20,24},{24,20},{5,9},{9,5},{13,17},{1... | collective-permute-start | bytes 589832 | tf_op jit(solution)/shard_map/ppermute | solution.py:599
  5.8 1.5 %shard_map.114.ext_ref.refs_0_ = f32[24,3,64,128]{3,2,1,0:T(8,128)S(1)} custom-call(f32[16,3,64,128]{3,2,1,0:T(8,128)} %bitcast.62), custom_call_target="tpu_custom_call" | custom-call | tf_op jit(solution)/shard_map/pallas_call | solution.py:32
  7.3 0.6 shard_map.115.refs_1_
  7.8 3.3 %shard_map.116 = (f32[8,3,64,128]{3,2,1,0:T(8,128)S(1)}, f32[8,3,64,128]{3,2,1,0:T(8,128)S(1)}, f32[8,3,32,128]{3,2,1,0:T(8,128)S(1)}, f32[8,8,3,32,128]{4,3,2,1,0:T(8,128)S(1)}) custom-call(s32[1,16]{1,0:T(1,128)S(1)} %bitcast.52, f32[16,3,64,128]{3,2,1,0:T(8,128)} %bitcast.57, f32[16,3,64,128]{3,2,1,0:T(8,128)} %bitcast.59, f32[3,2,256,128]{3,2,1,0:T(8,128)} %bitcast.63, ...), custom_call_target="tpu_custom_call" | custom-call | tf_op jit(solution)/shard_map/pallas_call | solution.py:32
  11.1 2.2 %collective-permute-done.near_ref = bf16[4,3,64,128]{3,2,1,0:T(8,128)(2,1)S(1)} collective-permute-done((bf16[4,3,64,128]{3,2,1,0:T(8,128)(2,1)S(1)}, bf16[4,3,64,128]{3,2,1,0:T(8,128)(2,1)S(1)}, u32[]{:S(2)}, u32[]{:S(2)}) %collective-permute-start) | collective-permute-done | bytes 196640 | tf_op jit(solution)/shard_map/ppermute | solution.py:600
  13.3 0.6 shard_map.117
  13.9 0.1 collective-permute-start.4
  14.0 1.6 %collective-permute-start.3 = (bf16[64,128]{1,0:T(8,128)(2,1)S(1)}, bf16[64,128]{1,0:T(8,128)(2,1)S(1)}, u32[]{:S(2)}, u32[]{:S(2)}) collective-permute-start(bf16[64,128]{1,0:T(8,128)(2,1)S(1)} %get-tuple-element.62), channel_id=1, source_target_pairs={{0,2},{1,3},{2,0},{3,1},{4,6},{5,7},{6,4},{7,5},{8,10},{9,11},{10,... | collective-permute-start | bytes 49160 | tf_op jit(solution)/shard_map/ppermute | solution.py:647
  15.6 0.3 collective-permute-start.2
  15.9 1.4 %collective-permute-done.4.refs_3_ = bf16[64,128]{1,0:T(8,128)(2,1)S(1)} collective-permute-done((bf16[64,128]{1,0:T(8,128)(2,1)S(1)}, bf16[64,128]{1,0:T(8,128)(2,1)S(1)}, u32[]{:S(2)}, u32[]{:S(2)}) %collective-permute-start.4) | collective-permute-done | bytes 16416 | tf_op jit(solution)/shard_map/ppermute | solution.py:647
  17.3 0.6 collective-permute-done.3.refs_2_
  17.8 0.9 %shard_map.118 = (f32[24,3,64,128]{3,2,1,0:T(8,128)S(1)}, bf16[4,3,64,128]{3,2,1,0:T(8,128)(2,1)S(1)}, bf16[4,3,64,128]{3,2,1,0:T(8,128)(2,1)S(1)}) custom-call(s32[8,16]{1,0:T(8,128)S(1)} %bitcast.40, f32[64,128]{1,0:T(8,128)S(1)} %get-tuple-element.61.refs_0_, bf16[64,128]{1,0:T(8,128)(2,1)S(1)} %collective-permute-done.2.refs_1_, ...), custom_call_target="tpu_custom_call" | custom-call | tf_op jit(solution)/shard_map/pallas_call | solution.py:32
  18.7 2.5 %collective-permute-start.5 = (bf16[4,3,64,128]{3,2,1,0:T(8,128)(2,1)S(1)}, bf16[4,3,64,128]{3,2,1,0:T(8,128)(2,1)S(1)}, u32[]{:S(2)}, u32[]{:S(2)}) collective-permute-start(bf16[4,3,64,128]{3,2,1,0:T(8,128)(2,1)S(1)} %get-tuple-element.68), channel_id=1, source_target_pairs={{0,4},{4,0},{8,12},{12,8},{16,20},{20,16},{24,28},{28,24},{1,5},{5... | collective-permute-start | bytes 589832 | tf_op jit(solution)/shard_map/ppermute | solution.py:600
  21.3 0.7 collective-permute-start.6
  21.9 3.1 %shard_map.119 = (f32[8,3,64,128]{3,2,1,0:T(8,128)S(1)}, f32[8,3,64,128]{3,2,1,0:T(8,128)S(1)}, f32[8,3,32,128]{3,2,1,0:T(8,128)S(1)}, f32[8,8,3,32,128]{4,3,2,1,0:T(8,128)S(1)}) custom-call(s32[1,16]{1,0:T(1,128)S(1)} %bitcast.53, f32[16,3,64,128]{3,2,1,0:T(8,128)} %bitcast.58, f32[16,3,64,128]{3,2,1,0:T(8,128)} %bitcast.60, f32[3,2,256,128]{3,2,1,0:T(8,128)} %bitcast.64, ...), custom_call_target="tpu_custom_call" | custom-call | tf_op jit(solution)/shard_map/pallas_call | solution.py:32
  25.1 0.8 %shard_map.120.ext_ref.refs_0_ = f32[24,3,64,128]{3,2,1,0:T(8,128)S(1)} custom-call(s32[8,16]{1,0:T(8,128)S(1)} %bitcast.41, f32[64,128]{1,0:T(8,128)S(1)} %get-tuple-element.61.refs_0_, bf16[64,128]{1,0:T(8,128)(2,1)S(1)} %collective-permute-done.2.refs_1_, bf16[64,128]{1,0:T(8,128)(2,1)S(1)} %collective-permute-done.3.refs_2_, ...), custom_call_target="tpu_custom_call", output_to_operand_aliasing={{}: (10, {})} | custom-call | tf_op jit(solution)/shard_map/pallas_call | solution.py:32
  25.9 0.0 copy-start.2
  25.9 0.0 copy-start.4
  25.9 0.6 shard_map.121.refs_1_
  26.4 3.8 %collective-permute-done.5.near_ref = bf16[4,3,64,128]{3,2,1,0:T(8,128)(2,1)S(1)} collective-permute-done((bf16[4,3,64,128]{3,2,1,0:T(8,128)(2,1)S(1)}, bf16[4,3,64,128]{3,2,1,0:T(8,128)(2,1)S(1)}, u32[]{:S(2)}, u32[]{:S(2)}) %collective-permute-start.5) | collective-permute-done | bytes 196640 | tf_op jit(solution)/shard_map/ppermute | solution.py:600
  30.3 0.6 shard_map.122
  30.8 0.1 collective-permute-start.9
  30.9 1.1 %collective-permute-start.8 = (bf16[64,128]{1,0:T(8,128)(2,1)S(1)}, bf16[64,128]{1,0:T(8,128)(2,1)S(1)}, u32[]{:S(2)}, u32[]{:S(2)}) collective-permute-start(bf16[64,128]{1,0:T(8,128)(2,1)S(1)} %get-tuple-element.87), channel_id=1, source_target_pairs={{0,2},{1,3},{2,0},{3,1},{4,6},{5,7},{6,4},{7,5},{8,10},{9,11},{10,... | collective-permute-start | bytes 49160 | tf_op jit(solution)/shard_map/ppermute | solution.py:647
  32.0 0.7 %collective-permute-start.7 = (bf16[64,128]{1,0:T(8,128)(2,1)S(1)}, bf16[64,128]{1,0:T(8,128)(2,1)S(1)}, u32[]{:S(2)}, u32[]{:S(2)}) collective-permute-start(bf16[64,128]{1,0:T(8,128)(2,1)S(1)} %get-tuple-element.87), channel_id=1, source_target_pairs={{0,1},{1,0},{2,3},{3,2},{4,5},{5,4},{6,7},{7,6},{8,9},{9,8},{10,11... | collective-permute-start | bytes 49160 | tf_op jit(solution)/shard_map/ppermute | solution.py:647
  32.8 1.8 %shard_map.123 = (bf16[256,1024]{1,0:T(8,128)(2,1)S(1)}, bf16[256,1024]{1,0:T(8,128)(2,1)S(1)}, s32[8,128]{1,0:T(8,128)S(1)}) custom-call(s32[2,128]{1,0:T(2,128)S(1)} %bitcast.50, s32[2,2,128]{2,1,0:T(2,128)S(1)} %bitcast.54), custom_call_target="tpu_custom_call" | custom-call | tf_op jit(solution)/shard_map/pallas_call | solution.py:32
  34.6 0.1 collective-permute-done.8.refs_2_
  34.7 0.9 %shard_map.124 = (f32[24,3,64,128]{3,2,1,0:T(8,128)S(1)}, bf16[4,3,64,128]{3,2,1,0:T(8,128)(2,1)S(1)}, bf16[4,3,64,128]{3,2,1,0:T(8,128)(2,1)S(1)}) custom-call(s32[8,16]{1,0:T(8,128)S(1)} %bitcast.44, f32[64,128]{1,0:T(8,128)S(1)} %get-tuple-element.86.refs_0_, bf16[64,128]{1,0:T(8,128)(2,1)S(1)} %collective-permute-done.7.refs_1_, ...), custom_call_target="tpu_custom_call" | custom-call | tf_op jit(solution)/shard_map/pallas_call | solution.py:32
  35.6 2.5 %collective-permute-start.10 = (bf16[4,3,64,128]{3,2,1,0:T(8,128)(2,1)S(1)}, bf16[4,3,64,128]{3,2,1,0:T(8,128)(2,1)S(1)}, u32[]{:S(2)}, u32[]{:S(2)}) collective-permute-start(bf16[4,3,64,128]{3,2,1,0:T(8,128)(2,1)S(1)} %get-tuple-element.89), channel_id=1, source_target_pairs={{0,4},{4,0},{8,12},{12,8},{16,20},{20,16},{24,28},{28,24},{1,5},{5... | collective-permute-start | bytes 589832 | tf_op jit(solution)/shard_map/ppermute | solution.py:600
  38.2 0.7 collective-permute-start.11
  38.9 0.8 %shard_map.125.refs_0_.ext_ref = f32[24,3,64,128]{3,2,1,0:T(8,128)S(1)} custom-call(s32[8,16]{1,0:T(8,128)S(1)} %bitcast.45, f32[64,128]{1,0:T(8,128)S(1)} %get-tuple-element.86.refs_0_, bf16[64,128]{1,0:T(8,128)(2,1)S(1)} %collective-permute-done.7.refs_1_, bf16[64,128]{1,0:T(8,128)(2,1)S(1)} %collective-permute-done.8.refs_2_, ...), custom_call_target="tpu_custom_call", output_to_operand_aliasing={{}: (10, {})} | custom-call | tf_op jit(solution)/shard_map/pallas_call | solution.py:32
  39.6 0.6 shard_map.127
  40.2 0.7 collective-permute-start.17
  40.9 0.7 %collective-permute-start.16 = (bf16[64,128]{1,0:T(8,128)(2,1)S(1)}, bf16[64,128]{1,0:T(8,128)(2,1)S(1)}, u32[]{:S(2)}, u32[]{:S(2)}) collective-permute-start(bf16[64,128]{1,0:T(8,128)(2,1)S(1)} %get-tuple-element.97), channel_id=1, source_target_pairs={{0,2},{1,3},{2,0},{3,1},{4,6},{5,7},{6,4},{7,5},{8,10},{9,11},{10,... | collective-permute-start | bytes 49160 | tf_op jit(solution)/shard_map/ppermute | solution.py:647
  41.6 0.5 collective-permute-start.15
  42.1 4.5 %collective-permute-done.10.near_ref = bf16[4,3,64,128]{3,2,1,0:T(8,128)(2,1)S(1)} collective-permute-done((bf16[4,3,64,128]{3,2,1,0:T(8,128)(2,1)S(1)}, bf16[4,3,64,128]{3,2,1,0:T(8,128)(2,1)S(1)}, u32[]{:S(2)}, u32[]{:S(2)}) %collective-permute-start.10) | collective-permute-done | bytes 196640 | tf_op jit(solution)/shard_map/ppermute | solution.py:600
  46.6 0.6 shard_map.126
  47.2 0.1 collective-permute-start.14
  47.3 1.5 %collective-permute-start.13 = (bf16[64,128]{1,0:T(8,128)(2,1)S(1)}, bf16[64,128]{1,0:T(8,128)(2,1)S(1)}, u32[]{:S(2)}, u32[]{:S(2)}) collective-permute-start(bf16[64,128]{1,0:T(8,128)(2,1)S(1)} %get-tuple-element.93), channel_id=1, source_target_pairs={{0,2},{1,3},{2,0},{3,1},{4,6},{5,7},{6,4},{7,5},{8,10},{9,11},{10,... | collective-permute-start | bytes 49160 | tf_op jit(solution)/shard_map/ppermute | solution.py:647
  48.8 0.4 collective-permute-start.12
  49.1 1.1 %shard_map.128 = (f32[16,3,64,128]{3,2,1,0:T(8,128)S(1)}, f32[8,96,128]{2,1,0:T(8,128)S(1)}) custom-call(s32[8,16]{1,0:T(8,128)S(1)} %bitcast.48, f32[64,128]{1,0:T(8,128)S(1)} %get-tuple-element.96.refs_0_, bf16[64,128]{1,0:T(8,128)(2,1)S(1)} %collective-permute-done.15.refs_1_, bf16[64,128]{1,0:T(8,128)(2,1)S(1)} %collective-permute-done.16.refs_2_, ...), custom_call_target="tpu_custom_call" | custom-call | tf_op jit(solution)/shard_map/pallas_call | solution.py:32
  50.3 0.3 collective-permute-done.14.refs_3_
  50.6 0.5 collective-permute-done.13.refs_2_
  51.1 1.3 %shard_map.129 = (f32[16,3,64,128]{3,2,1,0:T(8,128)S(1)}, bf16[8,96,128]{2,1,0:T(8,128)(2,1)S(1)}, f32[8,96,128]{2,1,0:T(8,128)S(1)}) custom-call(s32[8,16]{1,0:T(8,128)S(1)} %bitcast.49, f32[64,128]{1,0:T(8,128)S(1)} %get-tuple-element.92.refs_0_, ...), custom_call_target="tpu_custom_call", output_to_operand_aliasing={{0}: (11, {}), {2}: (12, {})} | custom-call | tf_op jit(solution)/shard_map/pallas_call | solution.py:32
  52.4 13.8 %all_to_all.5.received_ref = bf16[8,96,128]{2,1,0:T(8,128)(2,1)S(1)} all-to-all(bf16[8,96,128]{2,1,0:T(8,128)(2,1)S(1)} %get-tuple-element.100), channel_id=1, replica_groups=mesh['gran'=8,'band'=4] {'gran'}, dimensions={0} | all-to-all | bytes 393216 | tf_op jit(solution)/shard_map/all_to_all | solution.py:721
  66.2 2.6 %shard_map.130 = (bf16[1,3,256,256]{3,2,1,0:T(8,128)(2,1)}, f32[16,3,64,128]{3,2,1,0:T(8,128)}) custom-call(s32[2,128]{1,0:T(2,128)S(1)} %bitcast.51, bf16[8,96,128]{2,1,0:T(8,128)(2,1)S(1)} %all_to_all.5.received_ref, bf16[256,1024]{1,0:T(8,128)(2,1)S(1)} %get-tuple-element.101.row_ref, bf16[256,1024]{1,0:T(8,128)(2,1)S(1)} %get-tuple-element.102.col_ref, ...), custom_call_target="tpu_custom_call" | custom-call | tf_op jit(solution)/shard_map/pallas_call | solution.py:32
  (17 shorter events, 0.0 us)
Async XLA Ops:
  1.9 5.3 %copy-start = (s32[16,8]{0,1:T(8,128)S(1)}, s32[16,8]{0,1:T(8,128)}, u32[]{:S(2)}) copy-start(s32[16,8]{0,1:T(8,128)} %param.15) | copy-start | bytes 1540
  2.0 11.4 %collective-permute-start = (bf16[4,3,64,128]{3,2,1,0:T(8,128)(2,1)S(1)}, bf16[4,3,64,128]{3,2,1,0:T(8,128)(2,1)S(1)}, u32[]{:S(2)}, u32[]{:S(2)}) collective-permute-start(bf16[4,3,64,128]{3,2,1,0:T(8,128)(2,1)S(1)} %get-tuple-element.54), channel_id=1, source_target_pairs={{0,4},{4,0},{8,12},{12,8},{16,20},{20,16},{24,28},{28,24},{1,5},{5... | collective-permute-start | bytes 589832 | tf_op jit(solution)/shard_map/ppermute | solution.py:600
  5.0 2.9 %copy-start.3 = (s32[16]{0:T(128)S(1)}, s32[16]{0:T(128)}, u32[]{:S(2)}) copy-start(s32[16]{0:T(128)} %param.16) | copy-start | bytes 196
  5.0 8.4 %collective-permute-start.1 = (bf16[4,3,64,128]{3,2,1,0:T(8,128)(2,1)S(1)}, bf16[4,3,64,128]{3,2,1,0:T(8,128)(2,1)S(1)}, u32[]{:S(2)}, u32[]{:S(2)}) collective-permute-start(bf16[4,3,64,128]{3,2,1,0:T(8,128)(2,1)S(1)} %get-tuple-element.55), channel_id=1, source_target_pairs={{4,8},{8,4},{12,16},{16,12},{20,24},{24,20},{5,9},{9,5},{13,17},{1... | collective-permute-start | bytes 589832 | tf_op jit(solution)/shard_map/ppermute | solution.py:599
  13.9 3.3 %collective-permute-start.4 = (bf16[64,128]{1,0:T(8,128)(2,1)S(1)}, bf16[64,128]{1,0:T(8,128)(2,1)S(1)}, u32[]{:S(2)}, u32[]{:S(2)}) collective-permute-start(bf16[64,128]{1,0:T(8,128)(2,1)S(1)} %get-tuple-element.62), channel_id=1, source_target_pairs={{0,3},{1,2},{2,1},{3,0},{4,7},{5,6},{6,5},{7,4},{8,11},{9,10},{10,... | collective-permute-start | bytes 49160 | tf_op jit(solution)/shard_map/ppermute | solution.py:647
  14.0 3.8 %collective-permute-start.3 = (bf16[64,128]{1,0:T(8,128)(2,1)S(1)}, bf16[64,128]{1,0:T(8,128)(2,1)S(1)}, u32[]{:S(2)}, u32[]{:S(2)}) collective-permute-start(bf16[64,128]{1,0:T(8,128)(2,1)S(1)} %get-tuple-element.62), channel_id=1, source_target_pairs={{0,2},{1,3},{2,0},{3,1},{4,6},{5,7},{6,4},{7,5},{8,10},{9,11},{10,... | collective-permute-start | bytes 49160 | tf_op jit(solution)/shard_map/ppermute | solution.py:647
  15.6 2.2 %collective-permute-start.2 = (bf16[64,128]{1,0:T(8,128)(2,1)S(1)}, bf16[64,128]{1,0:T(8,128)(2,1)S(1)}, u32[]{:S(2)}, u32[]{:S(2)}) collective-permute-start(bf16[64,128]{1,0:T(8,128)(2,1)S(1)} %get-tuple-element.62), channel_id=1, source_target_pairs={{0,1},{1,0},{2,3},{3,2},{4,5},{5,4},{6,7},{7,6},{8,9},{9,8},{10,11... | collective-permute-start | bytes 49160 | tf_op jit(solution)/shard_map/ppermute | solution.py:647
  18.7 11.5 %collective-permute-start.5 = (bf16[4,3,64,128]{3,2,1,0:T(8,128)(2,1)S(1)}, bf16[4,3,64,128]{3,2,1,0:T(8,128)(2,1)S(1)}, u32[]{:S(2)}, u32[]{:S(2)}) collective-permute-start(bf16[4,3,64,128]{3,2,1,0:T(8,128)(2,1)S(1)} %get-tuple-element.68), channel_id=1, source_target_pairs={{0,4},{4,0},{8,12},{12,8},{16,20},{20,16},{24,28},{28,24},{1,5},{5... | collective-permute-start | bytes 589832 | tf_op jit(solution)/shard_map/ppermute | solution.py:600
  21.3 9.0 %collective-permute-start.6 = (bf16[4,3,64,128]{3,2,1,0:T(8,128)(2,1)S(1)}, bf16[4,3,64,128]{3,2,1,0:T(8,128)(2,1)S(1)}, u32[]{:S(2)}, u32[]{:S(2)}) collective-permute-start(bf16[4,3,64,128]{3,2,1,0:T(8,128)(2,1)S(1)} %get-tuple-element.69), channel_id=1, source_target_pairs={{4,8},{8,4},{12,16},{16,12},{20,24},{24,20},{5,9},{9,5},{13,17},{1... | collective-permute-start | bytes 589832 | tf_op jit(solution)/shard_map/ppermute | solution.py:599
  25.9 6.9 %copy-start.2 = (s32[128,2]{0,1:T(2,128)S(1)}, s32[128,2]{0,1:T(2,128)}, u32[]{:S(2)}) copy-start(s32[128,2]{0,1:T(2,128)} %param.17) | copy-start | bytes 3076
  25.9 6.9 %copy-start.4 = (s32[128,2,2]{0,2,1:T(2,128)S(1)}, s32[128,2,2]{0,2,1:T(2,128)}, u32[]{:S(2)}) copy-start(s32[128,2,2]{0,2,1:T(2,128)} %param.18) | copy-start | bytes 6148
  30.8 3.7 %collective-permute-start.9 = (bf16[64,128]{1,0:T(8,128)(2,1)S(1)}, bf16[64,128]{1,0:T(8,128)(2,1)S(1)}, u32[]{:S(2)}, u32[]{:S(2)}) collective-permute-start(bf16[64,128]{1,0:T(8,128)(2,1)S(1)} %get-tuple-element.87), channel_id=1, source_target_pairs={{0,3},{1,2},{2,1},{3,0},{4,7},{5,6},{6,5},{7,4},{8,11},{9,10},{10,... | collective-permute-start | bytes 49160 | tf_op jit(solution)/shard_map/ppermute | solution.py:647
  30.9 3.8 %collective-permute-start.8 = (bf16[64,128]{1,0:T(8,128)(2,1)S(1)}, bf16[64,128]{1,0:T(8,128)(2,1)S(1)}, u32[]{:S(2)}, u32[]{:S(2)}) collective-permute-start(bf16[64,128]{1,0:T(8,128)(2,1)S(1)} %get-tuple-element.87), channel_id=1, source_target_pairs={{0,2},{1,3},{2,0},{3,1},{4,6},{5,7},{6,4},{7,5},{8,10},{9,11},{10,... | collective-permute-start | bytes 49160 | tf_op jit(solution)/shard_map/ppermute | solution.py:647
  32.0 2.7 %collective-permute-start.7 = (bf16[64,128]{1,0:T(8,128)(2,1)S(1)}, bf16[64,128]{1,0:T(8,128)(2,1)S(1)}, u32[]{:S(2)}, u32[]{:S(2)}) collective-permute-start(bf16[64,128]{1,0:T(8,128)(2,1)S(1)} %get-tuple-element.87), channel_id=1, source_target_pairs={{0,1},{1,0},{2,3},{3,2},{4,5},{5,4},{6,7},{7,6},{8,9},{9,8},{10,11... | collective-permute-start | bytes 49160 | tf_op jit(solution)/shard_map/ppermute | solution.py:647
  35.6 11.0 %collective-permute-start.10 = (bf16[4,3,64,128]{3,2,1,0:T(8,128)(2,1)S(1)}, bf16[4,3,64,128]{3,2,1,0:T(8,128)(2,1)S(1)}, u32[]{:S(2)}, u32[]{:S(2)}) collective-permute-start(bf16[4,3,64,128]{3,2,1,0:T(8,128)(2,1)S(1)} %get-tuple-element.89), channel_id=1, source_target_pairs={{0,4},{4,0},{8,12},{12,8},{16,20},{20,16},{24,28},{28,24},{1,5},{5... | collective-permute-start | bytes 589832 | tf_op jit(solution)/shard_map/ppermute | solution.py:600
  38.2 8.4 %collective-permute-start.11 = (bf16[4,3,64,128]{3,2,1,0:T(8,128)(2,1)S(1)}, bf16[4,3,64,128]{3,2,1,0:T(8,128)(2,1)S(1)}, u32[]{:S(2)}, u32[]{:S(2)}) collective-permute-start(bf16[4,3,64,128]{3,2,1,0:T(8,128)(2,1)S(1)} %get-tuple-element.90), channel_id=1, source_target_pairs={{4,8},{8,4},{12,16},{16,12},{20,24},{24,20},{5,9},{9,5},{13,17},{1... | collective-permute-start | bytes 589832 | tf_op jit(solution)/shard_map/ppermute | solution.py:599
  40.2 8.5 %collective-permute-start.17 = (bf16[64,128]{1,0:T(8,128)(2,1)S(1)}, bf16[64,128]{1,0:T(8,128)(2,1)S(1)}, u32[]{:S(2)}, u32[]{:S(2)}) collective-permute-start(bf16[64,128]{1,0:T(8,128)(2,1)S(1)} %get-tuple-element.97), channel_id=1, source_target_pairs={{0,3},{1,2},{2,1},{3,0},{4,7},{5,6},{6,5},{7,4},{8,11},{9,10},{10,... | collective-permute-start | bytes 49160 | tf_op jit(solution)/shard_map/ppermute | solution.py:647
  40.9 8.2 %collective-permute-start.16 = (bf16[64,128]{1,0:T(8,128)(2,1)S(1)}, bf16[64,128]{1,0:T(8,128)(2,1)S(1)}, u32[]{:S(2)}, u32[]{:S(2)}) collective-permute-start(bf16[64,128]{1,0:T(8,128)(2,1)S(1)} %get-tuple-element.97), channel_id=1, source_target_pairs={{0,2},{1,3},{2,0},{3,1},{4,6},{5,7},{6,4},{7,5},{8,10},{9,11},{10,... | collective-permute-start | bytes 49160 | tf_op jit(solution)/shard_map/ppermute | solution.py:647
  41.6 7.5 %collective-permute-start.15 = (bf16[64,128]{1,0:T(8,128)(2,1)S(1)}, bf16[64,128]{1,0:T(8,128)(2,1)S(1)}, u32[]{:S(2)}, u32[]{:S(2)}) collective-permute-start(bf16[64,128]{1,0:T(8,128)(2,1)S(1)} %get-tuple-element.97), channel_id=1, source_target_pairs={{0,1},{1,0},{2,3},{3,2},{4,5},{5,4},{6,7},{7,6},{8,9},{9,8},{10,11... | collective-permute-start | bytes 49160 | tf_op jit(solution)/shard_map/ppermute | solution.py:647
  47.2 3.4 %collective-permute-start.14 = (bf16[64,128]{1,0:T(8,128)(2,1)S(1)}, bf16[64,128]{1,0:T(8,128)(2,1)S(1)}, u32[]{:S(2)}, u32[]{:S(2)}) collective-permute-start(bf16[64,128]{1,0:T(8,128)(2,1)S(1)} %get-tuple-element.93), channel_id=1, source_target_pairs={{0,3},{1,2},{2,1},{3,0},{4,7},{5,6},{6,5},{7,4},{8,11},{9,10},{10,... | collective-permute-start | bytes 49160 | tf_op jit(solution)/shard_map/ppermute | solution.py:647
  47.3 3.8 %collective-permute-start.13 = (bf16[64,128]{1,0:T(8,128)(2,1)S(1)}, bf16[64,128]{1,0:T(8,128)(2,1)S(1)}, u32[]{:S(2)}, u32[]{:S(2)}) collective-permute-start(bf16[64,128]{1,0:T(8,128)(2,1)S(1)} %get-tuple-element.93), channel_id=1, source_target_pairs={{0,2},{1,3},{2,0},{3,1},{4,6},{5,7},{6,4},{7,5},{8,10},{9,11},{10,... | collective-permute-start | bytes 49160 | tf_op jit(solution)/shard_map/ppermute | solution.py:647
  48.8 2.3 %collective-permute-start.12 = (bf16[64,128]{1,0:T(8,128)(2,1)S(1)}, bf16[64,128]{1,0:T(8,128)(2,1)S(1)}, u32[]{:S(2)}, u32[]{:S(2)}) collective-permute-start(bf16[64,128]{1,0:T(8,128)(2,1)S(1)} %get-tuple-element.93), channel_id=1, source_target_pairs={{0,1},{1,0},{2,3},{3,2},{4,5},{5,4},{6,7},{7,6},{8,9},{9,8},{10,11... | collective-permute-start | bytes 49160 | tf_op jit(solution)/shard_map/ppermute | solution.py:647
  51.1 15.1 %copy-start.1 = (bf16[1,3,256,256]{3,2,1,0:T(8,128)(2,1)S(1)}, bf16[1,3,256,256]{3,2,1,0:T(8,128)(2,1)}, u32[]{:S(2)}) copy-start(bf16[1,3,256,256]{3,2,1,0:T(8,128)(2,1)} %pixels_ref.1) | copy-start | bytes 1179652

commit v12 on v11

--- a/solution.py
+++ b/solution.py
@@ -14,6 +14,7 @@
 SP = 32
 LANES = 128
 SPAN = 16
+PARTED = 0
 FIRST = 3
 
 robust_scale = 0.3
@@ -236,7 +237,12 @@
     for ref, base in ((near_ref, (1 - odd) * right), (far_ref, odd * right)):
         for g in range(REACH):
             for b in range(ref.shape[1]):
-                ext_ref[base + g, b] = ref[g, b].astype(f32)
+                if ref.shape[2] == ext_ref.shape[2]:
+                    ext_ref[base + g, b] = ref[g, b].astype(f32)
+                    continue
+                for j in range(4):
+                    ext_ref[base + g, b, 16 * j : 16 * j + 8, :] = ref[g, b, 8 * j : 8 * j + 8, :].astype(f32)
+                    ext_ref[base + g, b, 16 * j + 8 : 16 * j + 16, :] = jnp.zeros((8, LANES), f32)
     packed = disparities(False, offset_ref, ext_ref, gathered, graph)
     if len(refs) == 7:
         packed = packed + refs[1][...]
@@ -315,19 +321,40 @@
         )
 
 
-def edge_sweep(offset_ref, *refs):
-    shares, state, (new_ref, near_ref, far_ref, weights, graph) = refs[:4], refs[4:9], refs[9:]
+def edge_sweep(split, parted, offset_ref, *refs):
+    shares, state, refs = refs[:4], refs[4:9], refs[9:]
+    weights, graph = refs[-2:]
+    odd = parity()
+    if split:
+        response_ref, gain_ref, kept_ref = refs[0], refs[1], refs[2]
+        refs = refs[3:]
+        state = (kept_ref,) + state[1:]
+        base = (1 - odd) * (kept_ref.shape[0] - REACH)
+        for g in range(REACH):
+            for b in range(gain_ref.shape[1]):
+                for j in range(4):
+                    rows = slice(8 * j, 8 * j + 8)
+                    gain = gain_ref[g, b, rows, :].astype(f32)
+                    kept_ref[base + g, b, 16 * j : 16 * j + 8, :] = gain
+                    offset = response_ref[g, b, rows, :].astype(f32) - gain
+                    kept_ref[base + g, b, 16 * j + 8 : 16 * j + 16, :] = offset
+    new_ref, far_ref = refs[:2]
+    near_refs = refs[2:-2]
     read_graph(offset_ref, graph)
     spread_weights(shares, False, weights)
-    odd = parity()
     last = new_ref.shape[0] - 3 * REACH
-    for ref, base in ((far_ref, odd * last), (near_ref, (1 - odd) * last)):
-
-        def step(g, carry, ref=ref, base=base):
+    for near, base in ((False, odd * last), (True, (1 - odd) * last)):
+
+        def step(g, carry, near=near, base=base):
             def store(b, j, gain, offset):
                 both = jnp.concatenate([gain, offset], axis=0)
                 new_ref[base + g + REACH, b, 16 * j : 16 * j + 16, :] = both
-                ref[g, b, 16 * j : 16 * j + 16, :] = both.astype(bf16)
+                if near and parted:
+                    near_refs[0][g, b, 8 * j : 8 * j + 8, :] = (gain + offset).astype(bf16)
+                    near_refs[1][g, b, 8 * j : 8 * j + 8, :] = gain.astype(bf16)
+                else:
+                    ref = near_refs[0] if near else far_ref
+                    ref[g, b, 16 * j : 16 * j + 16, :] = both.astype(bf16)
 
             balance(base + g, lax.div(base, 2 * REACH) * REACH + g, *state, weights, graph, store)
             return carry
@@ -656,6 +683,8 @@
             packed if last else packed[:1],
             [gathered, scalars],
         )
+        if sweep == PARTED + 1:
+            inner, *gains = lax.optimization_barrier((inner, *gains))
         if sweep == 0:
             inner, *edge_state = lax.optimization_barrier((inner, *arranged(False, sources)))
         if last:
@@ -670,6 +699,8 @@
             aliases={3: 0},
         )
         shares = over_band(partial, rounded)
+        if sweep == PARTED + 1:
+            near_gain = lax.ppermute(gains[0], "gran", near_pairs)
         if sweep == 1:
             routes, starts, _ = lax.optimization_barrier((tiles[0][1], tiles[1][1], partial))
             weight_shape = ("v", (pixel_count, device_total * LANES), bf16)
@@ -683,12 +714,25 @@
         edge_state_now = [("v", extended)] + [("v", array) for array in edge_state]
         if not last:
             inputs = graph + shares + edge_state_now
-            updated, near, far = call(
-                edge_sweep,
+            parted = sweep == PARTED
+            split = sweep == PARTED + 1
+            half = ("v", (REACH, bands, 32, LANES), bf16)
+            outputs = [("v", ext, f32), ("v", edge, bf16)] + ([half] * 2 if parted else [("v", edge, bf16)])
+            aliases = {}
+            if split:
+                inputs = inputs + [("v", near), ("v", near_gain)]
+                outputs = [("v", ext, f32)] + outputs
+                aliases = {len(graph + shares): 0}
+            made = call(
+                functools.partial(edge_sweep, split, parted),
                 inputs,
-                [("v", ext, f32), ("v", edge, bf16), ("v", edge, bf16)],
+                outputs,
                 [weights, scalars],
+                aliases=aliases,
             )
+            if split:
+                extended, *made = made
+            updated, far, near, *gains = made
             near, far = exchange(near, far)
             if sweep == 0:
                 *later, updated = lax.optimization_barrier((*sources, updated))

time: 69.1 us -> 69.9 us (1.012)
  starting transfers between devices: 17.9 us -> 20.8 us
  waiting for transfers between devices: 13.4 us -> 11.3 us
    ppermute x3, starting transfers between devices: 8.1 us -> 10.9 us  [exchange(): near = lax.ppermute(near, 'gran', near_pairs)]
    ppermute x3, waiting for transfers between devices: 10.5 us -> 8.38 us  [exchange(): near = lax.ppermute(near, 'gran', near_pairs)]
  transfers between devices with their start and end apart: 18 -> 19, of which waited for: 8 -> 8; matrix products, arithmetic and copies ran while one was open for 0% -> 0% of each run, Pallas kernels for 21% -> 22%
where the time goes in v12:
time: 69.9 us; the launch traced here: 69.5 us
  Pallas kernels  22.8 us (33%)
  starting transfers between devices  20.8 us (30%)
  blocking collectives  13.7 us (20%)
  waiting for transfers between devices  11.3 us (16%)
  between operations  0.87 us (1%)
    pallas_call x18, Pallas kernels, call(): pl.pallas_call(body, in_specs=[ON_CHIP if kind == 'v' else ANYWHERE for k...  22.8 us
    all_to_all x1, blocking collectives, per_device(): lax.all_to_all(payload, 'gran', split_axis=0, concat_axis=0, tiled=True)  13.7 us
    ppermute x3, starting transfers between devices, exchange(): near = lax.ppermute(near, 'gran', near_pairs)  10.9 us
    ppermute x3, waiting for transfers between devices, exchange(): near = lax.ppermute(near, 'gran', near_pairs)  8.38 us
    ppermute x12, starting transfers between devices, over_band(): lax.ppermute(rounded, 'band', [(i, i ^ flip) for i in range(band_total)])  7.69 us
    ppermute x12, waiting for transfers between devices, over_band(): lax.ppermute(rounded, 'band', [(i, i ^ flip) for i in range(band_total)])  2.89 us
    ppermute x3, starting transfers between devices, exchange(): far = lax.ppermute(far, 'gran', far_pairs)  2.13 us
  transfers between devices with their start and end apart: 19, of which 8 were waited for; matrix products, arithmetic and copies ran while one was open for 0% of the time, Pallas kernels for 22%

profile of v12, /device:TPU:0, one launch (start us, length us, event | category | flops | bytes accessed | tf_op | source)
XLA Modules:
  0.0 69.5 jit_solution(8518882606086788110)
XLA Ops:
  0.6 1.3 %shard_map.113 = (bf16[4,3,64,128]{3,2,1,0:T(8,128)(2,1)S(1)}, bf16[4,3,64,128]{3,2,1,0:T(8,128)(2,1)S(1)}) custom-call(f32[16,3,64,128]{3,2,1,0:T(8,128)} %bitcast.61), custom_call_target="tpu_custom_call" | custom-call | tf_op jit(solution)/shard_map/pallas_call | solution.py:33
  2.0 3.0 %collective-permute-start = (bf16[4,3,64,128]{3,2,1,0:T(8,128)(2,1)S(1)}, bf16[4,3,64,128]{3,2,1,0:T(8,128)(2,1)S(1)}, u32[]{:S(2)}, u32[]{:S(2)}) collective-permute-start(bf16[4,3,64,128]{3,2,1,0:T(8,128)(2,1)S(1)} %get-tuple-element.58), channel_id=1, source_target_pairs={{0,4},{4,0},{8,12},{12,8},{16,20},{20,16},{24,28},{28,24},{1,5},{5... | collective-permute-start | bytes 589832 | tf_op jit(solution)/shard_map/ppermute | solution.py:627
  5.0 0.8 %collective-permute-start.1 = (bf16[4,3,64,128]{3,2,1,0:T(8,128)(2,1)S(1)}, bf16[4,3,64,128]{3,2,1,0:T(8,128)(2,1)S(1)}, u32[]{:S(2)}, u32[]{:S(2)}) collective-permute-start(bf16[4,3,64,128]{3,2,1,0:T(8,128)(2,1)S(1)} %get-tuple-element.59), channel_id=1, source_target_pairs={{4,8},{8,4},{12,16},{16,12},{20,24},{24,20},{5,9},{9,5},{13,17},{1... | collective-permute-start | bytes 589832 | tf_op jit(solution)/shard_map/ppermute | solution.py:626
  5.8 1.5 %shard_map.114.ext_ref.refs_0_ = f32[24,3,64,128]{3,2,1,0:T(8,128)S(1)} custom-call(f32[16,3,64,128]{3,2,1,0:T(8,128)} %bitcast.62), custom_call_target="tpu_custom_call" | custom-call | tf_op jit(solution)/shard_map/pallas_call | solution.py:33
  7.3 0.6 shard_map.115.refs_1_
  7.8 3.0 %shard_map.116 = (f32[8,3,64,128]{3,2,1,0:T(8,128)S(1)}, f32[8,3,64,128]{3,2,1,0:T(8,128)S(1)}, f32[8,3,32,128]{3,2,1,0:T(8,128)S(1)}, f32[8,8,3,32,128]{4,3,2,1,0:T(8,128)S(1)}) custom-call(s32[1,16]{1,0:T(1,128)S(1)} %bitcast.52, f32[16,3,64,128]{3,2,1,0:T(8,128)} %bitcast.57, f32[16,3,64,128]{3,2,1,0:T(8,128)} %bitcast.59, f32[3,2,256,128]{3,2,1,0:T(8,128)} %bitcast.63, ...), custom_call_target="tpu_custom_call" | custom-call | tf_op jit(solution)/shard_map/pallas_call | solution.py:33
  10.9 2.4 %collective-permute-done.near_ref = bf16[4,3,64,128]{3,2,1,0:T(8,128)(2,1)S(1)} collective-permute-done((bf16[4,3,64,128]{3,2,1,0:T(8,128)(2,1)S(1)}, bf16[4,3,64,128]{3,2,1,0:T(8,128)(2,1)S(1)}, u32[]{:S(2)}, u32[]{:S(2)}) %collective-permute-start) | collective-permute-done | bytes 196640 | tf_op jit(solution)/shard_map/ppermute | solution.py:627
  13.3 0.6 shard_map.117
  13.9 0.1 collective-permute-start.4
  14.0 1.6 %collective-permute-start.3 = (bf16[64,128]{1,0:T(8,128)(2,1)S(1)}, bf16[64,128]{1,0:T(8,128)(2,1)S(1)}, u32[]{:S(2)}, u32[]{:S(2)}) collective-permute-start(bf16[64,128]{1,0:T(8,128)(2,1)S(1)} %get-tuple-element.66), channel_id=1, source_target_pairs={{0,2},{1,3},{2,0},{3,1},{4,6},{5,7},{6,4},{7,5},{8,10},{9,11},{10,... | collective-permute-start | bytes 49160 | tf_op jit(solution)/shard_map/ppermute | solution.py:674
  15.6 0.3 collective-permute-start.2
  15.8 1.4 %collective-permute-done.4.refs_3_ = bf16[64,128]{1,0:T(8,128)(2,1)S(1)} collective-permute-done((bf16[64,128]{1,0:T(8,128)(2,1)S(1)}, bf16[64,128]{1,0:T(8,128)(2,1)S(1)}, u32[]{:S(2)}, u32[]{:S(2)}) %collective-permute-start.4) | collective-permute-done | bytes 16416 | tf_op jit(solution)/shard_map/ppermute | solution.py:674
  17.2 0.6 collective-permute-done.3.refs_2_
  17.8 0.9 %shard_map.118 = (f32[24,3,64,128]{3,2,1,0:T(8,128)S(1)}, bf16[4,3,64,128]{3,2,1,0:T(8,128)(2,1)S(1)}, bf16[4,3,32,128]{3,2,1,0:T(8,128)(2,1)S(1)}, bf16[4,3,32,128]{3,2,1,0:T(8,128)(2,1)S(1)}) custom-call(s32[8,16]{1,0:T(8,128)S(1)} %bitcast.40, f32[64,128]{1,0:T(8,128)S(1)} %get-tuple-element.65.refs_0_, ...), custom_call_target="tpu_custom_call" | custom-call | tf_op jit(solution)/shard_map/pallas_call | solution.py:33
  18.7 0.7 collective-permute-start.6
  19.3 5.3 %collective-permute-start.5 = (bf16[4,3,32,128]{3,2,1,0:T(8,128)(2,1)S(1)}, bf16[4,3,32,128]{3,2,1,0:T(8,128)(2,1)S(1)}, u32[]{:S(2)}, u32[]{:S(2)}) collective-permute-start(bf16[4,3,32,128]{3,2,1,0:T(8,128)(2,1)S(1)} %get-tuple-element.72), channel_id=1, source_target_pairs={{0,4},{4,0},{8,12},{12,8},{16,20},{20,16},{24,28},{28,24},{1,5},{5... | collective-permute-start | bytes 294920 | tf_op jit(solution)/shard_map/ppermute | solution.py:627
  24.7 3.3 %shard_map.119 = (f32[8,3,64,128]{3,2,1,0:T(8,128)S(1)}, f32[8,3,64,128]{3,2,1,0:T(8,128)S(1)}, f32[8,3,32,128]{3,2,1,0:T(8,128)S(1)}, f32[8,8,3,32,128]{4,3,2,1,0:T(8,128)S(1)}) custom-call(s32[1,16]{1,0:T(1,128)S(1)} %bitcast.53, f32[16,3,64,128]{3,2,1,0:T(8,128)} %bitcast.58, f32[16,3,64,128]{3,2,1,0:T(8,128)} %bitcast.60, f32[3,2,256,128]{3,2,1,0:T(8,128)} %bitcast.64, ...), custom_call_target="tpu_custom_call" | custom-call | tf_op jit(solution)/shard_map/pallas_call | solution.py:33
  28.0 0.8 %shard_map.120.ext_ref.refs_0_ = f32[24,3,64,128]{3,2,1,0:T(8,128)S(1)} custom-call(s32[8,16]{1,0:T(8,128)S(1)} %bitcast.41, f32[64,128]{1,0:T(8,128)S(1)} %get-tuple-element.65.refs_0_, bf16[64,128]{1,0:T(8,128)(2,1)S(1)} %collective-permute-done.2.refs_1_, bf16[64,128]{1,0:T(8,128)(2,1)S(1)} %collective-permute-done.3.refs_2_, ...), custom_call_target="tpu_custom_call", output_to_operand_aliasing={{}: (10, {})} | custom-call | tf_op jit(solution)/shard_map/pallas_call | solution.py:33
  28.8 0.0 copy-start.2
  28.8 0.0 copy-start.4
  28.9 0.6 shard_map.121.refs_1_
  29.4 0.1 collective-permute-start.10
  29.5 1.3 %collective-permute-done.5.near_ref.refs_9_ = bf16[4,3,32,128]{3,2,1,0:T(8,128)(2,1)S(1)} collective-permute-done((bf16[4,3,32,128]{3,2,1,0:T(8,128)(2,1)S(1)}, bf16[4,3,32,128]{3,2,1,0:T(8,128)(2,1)S(1)}, u32[]{:S(2)}, u32[]{:S(2)}) %collective-permute-start.5) | collective-permute-done | bytes 98336 | tf_op jit(solution)/shard_map/ppermute | solution.py:627
  30.9 0.6 shard_map.122
  31.4 0.2 collective-permute-start.9
  31.6 1.5 %collective-permute-start.8 = (bf16[64,128]{1,0:T(8,128)(2,1)S(1)}, bf16[64,128]{1,0:T(8,128)(2,1)S(1)}, u32[]{:S(2)}, u32[]{:S(2)}) collective-permute-start(bf16[64,128]{1,0:T(8,128)(2,1)S(1)} %get-tuple-element.93), channel_id=1, source_target_pairs={{0,2},{1,3},{2,0},{3,1},{4,6},{5,7},{6,4},{7,5},{8,10},{9,11},{10,... | collective-permute-start | bytes 49160 | tf_op jit(solution)/shard_map/ppermute | solution.py:674
  33.1 0.3 collective-permute-start.7
  33.4 1.8 %shard_map.123 = (bf16[256,1024]{1,0:T(8,128)(2,1)S(1)}, bf16[256,1024]{1,0:T(8,128)(2,1)S(1)}, s32[8,128]{1,0:T(8,128)S(1)}) custom-call(s32[2,128]{1,0:T(2,128)S(1)} %bitcast.50, s32[2,2,128]{2,1,0:T(2,128)S(1)} %bitcast.54), custom_call_target="tpu_custom_call" | custom-call | tf_op jit(solution)/shard_map/pallas_call | solution.py:33
  35.2 0.2 collective-permute-done.8.refs_2_
  35.3 0.8 %shard_map.124 = (f32[24,3,64,128]{3,2,1,0:T(8,128)S(1)}, f32[24,3,64,128]{3,2,1,0:T(8,128)S(1)}, bf16[4,3,64,128]{3,2,1,0:T(8,128)(2,1)S(1)}, bf16[4,3,64,128]{3,2,1,0:T(8,128)(2,1)S(1)}) custom-call(s32[8,16]{1,0:T(8,128)S(1)} %bitcast.44, f32[64,128]{1,0:T(8,128)S(1)} %get-tuple-element.92.refs_0_, ...), custom_call_target="tpu_custom_call", output_to_operand_aliasing={{0}: (5, {})} | custom-call | tf_op jit(solution)/shard_map/pallas_call | solution.py:33
  36.2 2.5 %collective-permute-start.11 = (bf16[4,3,64,128]{3,2,1,0:T(8,128)(2,1)S(1)}, bf16[4,3,64,128]{3,2,1,0:T(8,128)(2,1)S(1)}, u32[]{:S(2)}, u32[]{:S(2)}) collective-permute-start(bf16[4,3,64,128]{3,2,1,0:T(8,128)(2,1)S(1)} %get-tuple-element.96), channel_id=1, source_target_pairs={{0,4},{4,0},{8,12},{12,8},{16,20},{20,16},{24,28},{28,24},{1,5},{5... | collective-permute-start | bytes 589832 | tf_op jit(solution)/shard_map/ppermute | solution.py:627
  38.7 0.7 collective-permute-start.12
  39.4 0.9 %shard_map.125.refs_0_.ext_ref = f32[24,3,64,128]{3,2,1,0:T(8,128)S(1)} custom-call(s32[8,16]{1,0:T(8,128)S(1)} %bitcast.45, f32[64,128]{1,0:T(8,128)S(1)} %get-tuple-element.92.refs_0_, bf16[64,128]{1,0:T(8,128)(2,1)S(1)} %collective-permute-done.7.refs_1_, bf16[64,128]{1,0:T(8,128)(2,1)S(1)} %collective-permute-done.8.refs_2_, ...), custom_call_target="tpu_custom_call", output_to_operand_aliasing={{}: (10, {})} | custom-call | tf_op jit(solution)/shard_map/pallas_call | solution.py:33
  40.3 0.6 shard_map.127
  40.9 0.3 collective-permute-start.18
  41.1 1.4 %collective-permute-start.17 = (bf16[64,128]{1,0:T(8,128)(2,1)S(1)}, bf16[64,128]{1,0:T(8,128)(2,1)S(1)}, u32[]{:S(2)}, u32[]{:S(2)}) collective-permute-start(bf16[64,128]{1,0:T(8,128)(2,1)S(1)} %get-tuple-element.105), channel_id=1, source_target_pairs={{0,2},{1,3},{2,0},{3,1},{4,6},{5,7},{6,4},{7,5},{8,10},{9,11},{10,... | collective-permute-start | bytes 49160 | tf_op jit(solution)/shard_map/ppermute | solution.py:674
  42.5 0.3 collective-permute-start.16
  42.8 4.6 %collective-permute-done.11.near_ref = bf16[4,3,64,128]{3,2,1,0:T(8,128)(2,1)S(1)} collective-permute-done((bf16[4,3,64,128]{3,2,1,0:T(8,128)(2,1)S(1)}, bf16[4,3,64,128]{3,2,1,0:T(8,128)(2,1)S(1)}, u32[]{:S(2)}, u32[]{:S(2)}) %collective-permute-start.11) | collective-permute-done | bytes 196640 | tf_op jit(solution)/shard_map/ppermute | solution.py:627
  47.4 0.6 shard_map.126
  47.9 0.1 collective-permute-start.15
  48.0 0.8 %collective-permute-start.14 = (bf16[64,128]{1,0:T(8,128)(2,1)S(1)}, bf16[64,128]{1,0:T(8,128)(2,1)S(1)}, u32[]{:S(2)}, u32[]{:S(2)}) collective-permute-start(bf16[64,128]{1,0:T(8,128)(2,1)S(1)} %get-tuple-element.101), channel_id=1, source_target_pairs={{0,2},{1,3},{2,0},{3,1},{4,6},{5,7},{6,4},{7,5},{8,10},{9,11},{10,... | collective-permute-start | bytes 49160 | tf_op jit(solution)/shard_map/ppermute | solution.py:674
  48.9 1.0 %collective-permute-start.13 = (bf16[64,128]{1,0:T(8,128)(2,1)S(1)}, bf16[64,128]{1,0:T(8,128)(2,1)S(1)}, u32[]{:S(2)}, u32[]{:S(2)}) collective-permute-start(bf16[64,128]{1,0:T(8,128)(2,1)S(1)} %get-tuple-element.101), channel_id=1, source_target_pairs={{0,1},{1,0},{2,3},{3,2},{4,5},{5,4},{6,7},{7,6},{8,9},{9,8},{10,11... | collective-permute-start | bytes 49160 | tf_op jit(solution)/shard_map/ppermute | solution.py:674
  49.9 1.2 %shard_map.128 = (f32[16,3,64,128]{3,2,1,0:T(8,128)S(1)}, f32[8,96,128]{2,1,0:T(8,128)S(1)}) custom-call(s32[8,16]{1,0:T(8,128)S(1)} %bitcast.48, f32[64,128]{1,0:T(8,128)S(1)} %get-tuple-element.104.refs_0_, bf16[64,128]{1,0:T(8,128)(2,1)S(1)} %collective-permute-done.16.refs_1_, bf16[64,128]{1,0:T(8,128)(2,1)S(1)} %collective-permute-done.17.refs_2_, ...), custom_call_target="tpu_custom_call" | custom-call | tf_op jit(solution)/shard_map/pallas_call | solution.py:33
  51.1 0.1 collective-permute-done.15.refs_3_
  51.2 0.7 collective-permute-done.14.refs_2_
  51.9 1.3 %shard_map.129 = (f32[16,3,64,128]{3,2,1,0:T(8,128)S(1)}, bf16[8,96,128]{2,1,0:T(8,128)(2,1)S(1)}, f32[8,96,128]{2,1,0:T(8,128)S(1)}) custom-call(s32[8,16]{1,0:T(8,128)S(1)} %bitcast.49, f32[64,128]{1,0:T(8,128)S(1)} %get-tuple-element.100.refs_0_, ...), custom_call_target="tpu_custom_call", output_to_operand_aliasing={{0}: (11, {}), {2}: (12, {})} | custom-call | tf_op jit(solution)/shard_map/pallas_call | solution.py:33
  53.1 13.7 %all_to_all.5.received_ref = bf16[8,96,128]{2,1,0:T(8,128)(2,1)S(1)} all-to-all(bf16[8,96,128]{2,1,0:T(8,128)(2,1)S(1)} %get-tuple-element.108), channel_id=1, replica_groups=mesh['gran'=8,'band'=4] {'gran'}, dimensions={0} | all-to-all | bytes 393216 | tf_op jit(solution)/shard_map/all_to_all | solution.py:765
  66.9 2.6 %shard_map.130 = (bf16[1,3,256,256]{3,2,1,0:T(8,128)(2,1)}, f32[16,3,64,128]{3,2,1,0:T(8,128)}) custom-call(s32[2,128]{1,0:T(2,128)S(1)} %bitcast.51, bf16[8,96,128]{2,1,0:T(8,128)(2,1)S(1)} %all_to_all.5.received_ref, bf16[256,1024]{1,0:T(8,128)(2,1)S(1)} %get-tuple-element.109.row_ref, bf16[256,1024]{1,0:T(8,128)(2,1)S(1)} %get-tuple-element.110.col_ref, ...), custom_call_target="tpu_custom_call" | custom-call | tf_op jit(solution)/shard_map/pallas_call | solution.py:33
  (19 shorter events, 0.0 us)
Async XLA Ops:
  1.9 5.3 %copy-start = (s32[16,8]{0,1:T(8,128)S(1)}, s32[16,8]{0,1:T(8,128)}, u32[]{:S(2)}) copy-start(s32[16,8]{0,1:T(8,128)} %param.15) | copy-start | bytes 1540
  2.0 11.4 %collective-permute-start = (bf16[4,3,64,128]{3,2,1,0:T(8,128)(2,1)S(1)}, bf16[4,3,64,128]{3,2,1,0:T(8,128)(2,1)S(1)}, u32[]{:S(2)}, u32[]{:S(2)}) collective-permute-start(bf16[4,3,64,128]{3,2,1,0:T(8,128)(2,1)S(1)} %get-tuple-element.58), channel_id=1, source_target_pairs={{0,4},{4,0},{8,12},{12,8},{16,20},{20,16},{24,28},{28,24},{1,5},{5... | collective-permute-start | bytes 589832 | tf_op jit(solution)/shard_map/ppermute | solution.py:627
  5.0 2.9 %copy-start.3 = (s32[16]{0:T(128)S(1)}, s32[16]{0:T(128)}, u32[]{:S(2)}) copy-start(s32[16]{0:T(128)} %param.16) | copy-start | bytes 196
  5.0 8.4 %collective-permute-start.1 = (bf16[4,3,64,128]{3,2,1,0:T(8,128)(2,1)S(1)}, bf16[4,3,64,128]{3,2,1,0:T(8,128)(2,1)S(1)}, u32[]{:S(2)}, u32[]{:S(2)}) collective-permute-start(bf16[4,3,64,128]{3,2,1,0:T(8,128)(2,1)S(1)} %get-tuple-element.59), channel_id=1, source_target_pairs={{4,8},{8,4},{12,16},{16,12},{20,24},{24,20},{5,9},{9,5},{13,17},{1... | collective-permute-start | bytes 589832 | tf_op jit(solution)/shard_map/ppermute | solution.py:626
  13.9 3.3 %collective-permute-start.4 = (bf16[64,128]{1,0:T(8,128)(2,1)S(1)}, bf16[64,128]{1,0:T(8,128)(2,1)S(1)}, u32[]{:S(2)}, u32[]{:S(2)}) collective-permute-start(bf16[64,128]{1,0:T(8,128)(2,1)S(1)} %get-tuple-element.66), channel_id=1, source_target_pairs={{0,3},{1,2},{2,1},{3,0},{4,7},{5,6},{6,5},{7,4},{8,11},{9,10},{10,... | collective-permute-start | bytes 49160 | tf_op jit(solution)/shard_map/ppermute | solution.py:674
  14.0 3.8 %collective-permute-start.3 = (bf16[64,128]{1,0:T(8,128)(2,1)S(1)}, bf16[64,128]{1,0:T(8,128)(2,1)S(1)}, u32[]{:S(2)}, u32[]{:S(2)}) collective-permute-start(bf16[64,128]{1,0:T(8,128)(2,1)S(1)} %get-tuple-element.66), channel_id=1, source_target_pairs={{0,2},{1,3},{2,0},{3,1},{4,6},{5,7},{6,4},{7,5},{8,10},{9,11},{10,... | collective-permute-start | bytes 49160 | tf_op jit(solution)/shard_map/ppermute | solution.py:674
  15.6 2.2 %collective-permute-start.2 = (bf16[64,128]{1,0:T(8,128)(2,1)S(1)}, bf16[64,128]{1,0:T(8,128)(2,1)S(1)}, u32[]{:S(2)}, u32[]{:S(2)}) collective-permute-start(bf16[64,128]{1,0:T(8,128)(2,1)S(1)} %get-tuple-element.66), channel_id=1, source_target_pairs={{0,1},{1,0},{2,3},{3,2},{4,5},{5,4},{6,7},{7,6},{8,9},{9,8},{10,11... | collective-permute-start | bytes 49160 | tf_op jit(solution)/shard_map/ppermute | solution.py:674
  18.7 12.2 %collective-permute-start.6 = (bf16[4,3,64,128]{3,2,1,0:T(8,128)(2,1)S(1)}, bf16[4,3,64,128]{3,2,1,0:T(8,128)(2,1)S(1)}, u32[]{:S(2)}, u32[]{:S(2)}) collective-permute-start(bf16[4,3,64,128]{3,2,1,0:T(8,128)(2,1)S(1)} %get-tuple-element.73), channel_id=1, source_target_pairs={{4,8},{8,4},{12,16},{16,12},{20,24},{24,20},{5,9},{9,5},{13,17},{1... | collective-permute-start | bytes 589832 | tf_op jit(solution)/shard_map/ppermute | solution.py:626
  19.3 11.5 %collective-permute-start.5 = (bf16[4,3,32,128]{3,2,1,0:T(8,128)(2,1)S(1)}, bf16[4,3,32,128]{3,2,1,0:T(8,128)(2,1)S(1)}, u32[]{:S(2)}, u32[]{:S(2)}) collective-permute-start(bf16[4,3,32,128]{3,2,1,0:T(8,128)(2,1)S(1)} %get-tuple-element.72), channel_id=1, source_target_pairs={{0,4},{4,0},{8,12},{12,8},{16,20},{20,16},{24,28},{28,24},{1,5},{5... | collective-permute-start | bytes 294920 | tf_op jit(solution)/shard_map/ppermute | solution.py:627
  28.8 4.5 %copy-start.2 = (s32[128,2]{0,1:T(2,128)S(1)}, s32[128,2]{0,1:T(2,128)}, u32[]{:S(2)}) copy-start(s32[128,2]{0,1:T(2,128)} %param.17) | copy-start | bytes 3076
  28.8 4.5 %copy-start.4 = (s32[128,2,2]{0,2,1:T(2,128)S(1)}, s32[128,2,2]{0,2,1:T(2,128)}, u32[]{:S(2)}) copy-start(s32[128,2,2]{0,2,1:T(2,128)} %param.18) | copy-start | bytes 6148
  29.4 5.7 %collective-permute-start.10 = (bf16[4,3,32,128]{3,2,1,0:T(8,128)(2,1)S(1)}, bf16[4,3,32,128]{3,2,1,0:T(8,128)(2,1)S(1)}, u32[]{:S(2)}, u32[]{:S(2)}) collective-permute-start(bf16[4,3,32,128]{3,2,1,0:T(8,128)(2,1)S(1)} %get-tuple-element.95), channel_id=1, source_target_pairs={{0,4},{4,0},{8,12},{12,8},{16,20},{20,16},{24,28},{28,24},{1,5},{5... | collective-permute-start | bytes 294920 | tf_op jit(solution)/shard_map/ppermute | solution.py:703
  31.4 3.7 %collective-permute-start.9 = (bf16[64,128]{1,0:T(8,128)(2,1)S(1)}, bf16[64,128]{1,0:T(8,128)(2,1)S(1)}, u32[]{:S(2)}, u32[]{:S(2)}) collective-permute-start(bf16[64,128]{1,0:T(8,128)(2,1)S(1)} %get-tuple-element.93), channel_id=1, source_target_pairs={{0,3},{1,2},{2,1},{3,0},{4,7},{5,6},{6,5},{7,4},{8,11},{9,10},{10,... | collective-permute-start | bytes 49160 | tf_op jit(solution)/shard_map/ppermute | solution.py:674
  31.6 3.7 %collective-permute-start.8 = (bf16[64,128]{1,0:T(8,128)(2,1)S(1)}, bf16[64,128]{1,0:T(8,128)(2,1)S(1)}, u32[]{:S(2)}, u32[]{:S(2)}) collective-permute-start(bf16[64,128]{1,0:T(8,128)(2,1)S(1)} %get-tuple-element.93), channel_id=1, source_target_pairs={{0,2},{1,3},{2,0},{3,1},{4,6},{5,7},{6,4},{7,5},{8,10},{9,11},{10,... | collective-permute-start | bytes 49160 | tf_op jit(solution)/shard_map/ppermute | solution.py:674
  33.1 2.2 %collective-permute-start.7 = (bf16[64,128]{1,0:T(8,128)(2,1)S(1)}, bf16[64,128]{1,0:T(8,128)(2,1)S(1)}, u32[]{:S(2)}, u32[]{:S(2)}) collective-permute-start(bf16[64,128]{1,0:T(8,128)(2,1)S(1)} %get-tuple-element.93), channel_id=1, source_target_pairs={{0,1},{1,0},{2,3},{3,2},{4,5},{5,4},{6,7},{7,6},{8,9},{9,8},{10,11... | collective-permute-start | bytes 49160 | tf_op jit(solution)/shard_map/ppermute | solution.py:674
  36.2 11.2 %collective-permute-start.11 = (bf16[4,3,64,128]{3,2,1,0:T(8,128)(2,1)S(1)}, bf16[4,3,64,128]{3,2,1,0:T(8,128)(2,1)S(1)}, u32[]{:S(2)}, u32[]{:S(2)}) collective-permute-start(bf16[4,3,64,128]{3,2,1,0:T(8,128)(2,1)S(1)} %get-tuple-element.96), channel_id=1, source_target_pairs={{0,4},{4,0},{8,12},{12,8},{16,20},{20,16},{24,28},{28,24},{1,5},{5... | collective-permute-start | bytes 589832 | tf_op jit(solution)/shard_map/ppermute | solution.py:627
  38.7 8.7 %collective-permute-start.12 = (bf16[4,3,64,128]{3,2,1,0:T(8,128)(2,1)S(1)}, bf16[4,3,64,128]{3,2,1,0:T(8,128)(2,1)S(1)}, u32[]{:S(2)}, u32[]{:S(2)}) collective-permute-start(bf16[4,3,64,128]{3,2,1,0:T(8,128)(2,1)S(1)} %get-tuple-element.97), channel_id=1, source_target_pairs={{4,8},{8,4},{12,16},{16,12},{20,24},{24,20},{5,9},{9,5},{13,17},{1... | collective-permute-start | bytes 589832 | tf_op jit(solution)/shard_map/ppermute | solution.py:626
  40.9 8.0 %collective-permute-start.18 = (bf16[64,128]{1,0:T(8,128)(2,1)S(1)}, bf16[64,128]{1,0:T(8,128)(2,1)S(1)}, u32[]{:S(2)}, u32[]{:S(2)}) collective-permute-start(bf16[64,128]{1,0:T(8,128)(2,1)S(1)} %get-tuple-element.105), channel_id=1, source_target_pairs={{0,3},{1,2},{2,1},{3,0},{4,7},{5,6},{6,5},{7,4},{8,11},{9,10},{10,... | collective-permute-start | bytes 49160 | tf_op jit(solution)/shard_map/ppermute | solution.py:674
  41.1 8.7 %collective-permute-start.17 = (bf16[64,128]{1,0:T(8,128)(2,1)S(1)}, bf16[64,128]{1,0:T(8,128)(2,1)S(1)}, u32[]{:S(2)}, u32[]{:S(2)}) collective-permute-start(bf16[64,128]{1,0:T(8,128)(2,1)S(1)} %get-tuple-element.105), channel_id=1, source_target_pairs={{0,2},{1,3},{2,0},{3,1},{4,6},{5,7},{6,4},{7,5},{8,10},{9,11},{10,... | collective-permute-start | bytes 49160 | tf_op jit(solution)/shard_map/ppermute | solution.py:674
  42.5 7.4 %collective-permute-start.16 = (bf16[64,128]{1,0:T(8,128)(2,1)S(1)}, bf16[64,128]{1,0:T(8,128)(2,1)S(1)}, u32[]{:S(2)}, u32[]{:S(2)}) collective-permute-start(bf16[64,128]{1,0:T(8,128)(2,1)S(1)} %get-tuple-element.105), channel_id=1, source_target_pairs={{0,1},{1,0},{2,3},{3,2},{4,5},{5,4},{6,7},{7,6},{8,9},{9,8},{10,11... | collective-permute-start | bytes 49160 | tf_op jit(solution)/shard_map/ppermute | solution.py:674
  47.9 3.2 %collective-permute-start.15 = (bf16[64,128]{1,0:T(8,128)(2,1)S(1)}, bf16[64,128]{1,0:T(8,128)(2,1)S(1)}, u32[]{:S(2)}, u32[]{:S(2)}) collective-permute-start(bf16[64,128]{1,0:T(8,128)(2,1)S(1)} %get-tuple-element.101), channel_id=1, source_target_pairs={{0,3},{1,2},{2,1},{3,0},{4,7},{5,6},{6,5},{7,4},{8,11},{9,10},{10,... | collective-permute-start | bytes 49160 | tf_op jit(solution)/shard_map/ppermute | solution.py:674
  48.0 3.8 %collective-permute-start.14 = (bf16[64,128]{1,0:T(8,128)(2,1)S(1)}, bf16[64,128]{1,0:T(8,128)(2,1)S(1)}, u32[]{:S(2)}, u32[]{:S(2)}) collective-permute-start(bf16[64,128]{1,0:T(8,128)(2,1)S(1)} %get-tuple-element.101), channel_id=1, source_target_pairs={{0,2},{1,3},{2,0},{3,1},{4,6},{5,7},{6,4},{7,5},{8,10},{9,11},{10,... | collective-permute-start | bytes 49160 | tf_op jit(solution)/shard_map/ppermute | solution.py:674
  48.9 3.0 %collective-permute-start.13 = (bf16[64,128]{1,0:T(8,128)(2,1)S(1)}, bf16[64,128]{1,0:T(8,128)(2,1)S(1)}, u32[]{:S(2)}, u32[]{:S(2)}) collective-permute-start(bf16[64,128]{1,0:T(8,128)(2,1)S(1)} %get-tuple-element.101), channel_id=1, source_target_pairs={{0,1},{1,0},{2,3},{3,2},{4,5},{5,4},{6,7},{7,6},{8,9},{9,8},{10,11... | collective-permute-start | bytes 49160 | tf_op jit(solution)/shard_map/ppermute | solution.py:674
  51.9 15.0 %copy-start.1 = (bf16[1,3,256,256]{3,2,1,0:T(8,128)(2,1)S(1)}, bf16[1,3,256,256]{3,2,1,0:T(8,128)(2,1)}, u32[]{:S(2)}) copy-start(bf16[1,3,256,256]{3,2,1,0:T(8,128)(2,1)} %pixels_ref.1) | copy-start | bytes 1179652

commit v13 on v12

--- a/solution.py
+++ b/solution.py
@@ -329,7 +329,7 @@
         response_ref, gain_ref, kept_ref = refs[0], refs[1], refs[2]
         refs = refs[3:]
         state = (kept_ref,) + state[1:]
-        base = (1 - odd) * (kept_ref.shape[0] - REACH)
+        base = odd * (kept_ref.shape[0] - REACH)
         for g in range(REACH):
             for b in range(gain_ref.shape[1]):
                 for j in range(4):
@@ -338,8 +338,8 @@
                     kept_ref[base + g, b, 16 * j : 16 * j + 8, :] = gain
                     offset = response_ref[g, b, rows, :].astype(f32) - gain
                     kept_ref[base + g, b, 16 * j + 8 : 16 * j + 16, :] = offset
-    new_ref, far_ref = refs[:2]
-    near_refs = refs[2:-2]
+    new_ref, near_ref = refs[:2]
+    far_refs = refs[2:-2]
     read_graph(offset_ref, graph)
     spread_weights(shares, False, weights)
     last = new_ref.shape[0] - 3 * REACH
@@ -349,11 +349,11 @@
             def store(b, j, gain, offset):
                 both = jnp.concatenate([gain, offset], axis=0)
                 new_ref[base + g + REACH, b, 16 * j : 16 * j + 16, :] = both
-                if near and parted:
-                    near_refs[0][g, b, 8 * j : 8 * j + 8, :] = (gain + offset).astype(bf16)
-                    near_refs[1][g, b, 8 * j : 8 * j + 8, :] = gain.astype(bf16)
+                if parted and not near:
+                    far_refs[0][g, b, 8 * j : 8 * j + 8, :] = (gain + offset).astype(bf16)
+                    far_refs[1][g, b, 8 * j : 8 * j + 8, :] = gain.astype(bf16)
                 else:
-                    ref = near_refs[0] if near else far_ref
+                    ref = near_ref if near else far_refs[0]
                     ref[g, b, 16 * j : 16 * j + 16, :] = both.astype(bf16)
 
             balance(base + g, lax.div(base, 2 * REACH) * REACH + g, *state, weights, graph, store)
@@ -700,7 +700,7 @@
         )
         shares = over_band(partial, rounded)
         if sweep == PARTED + 1:
-            near_gain = lax.ppermute(gains[0], "gran", near_pairs)
+            far_gain = lax.ppermute(gains[0], "gran", far_pairs)
         if sweep == 1:
             routes, starts, _ = lax.optimization_barrier((tiles[0][1], tiles[1][1], partial))
             weight_shape = ("v", (pixel_count, device_total * LANES), bf16)
@@ -720,7 +720,7 @@
             outputs = [("v", ext, f32), ("v", edge, bf16)] + ([half] * 2 if parted else [("v", edge, bf16)])
             aliases = {}
             if split:
-                inputs = inputs + [("v", near), ("v", near_gain)]
+                inputs = inputs + [("v", far), ("v", far_gain)]
                 outputs = [("v", ext, f32)] + outputs
                 aliases = {len(graph + shares): 0}
             made = call(
@@ -732,7 +732,7 @@
             )
             if split:
                 extended, *made = made
-            updated, far, near, *gains = made
+            updated, near, far, *gains = made
             near, far = exchange(near, far)
             if sweep == 0:
                 *later, updated = lax.optimization_barrier((*sources, updated))

time: 69.9 us -> 70.4 us (level)
  starting transfers between devices: 20.8 us -> 21.7 us
  waiting for transfers between devices: 11.3 us -> 10.5 us
    ppermute x3, waiting for transfers between devices: 8.38 us -> 7.59 us  [exchange(): near = lax.ppermute(near, 'gran', near_pairs)]
where the time goes in v13:
time: 70.4 us; the launch traced here: 70.1 us
  Pallas kernels  22.8 us (32%)
  starting transfers between devices  21.7 us (31%)
  blocking collectives  14.2 us (20%)
  waiting for transfers between devices  10.5 us (15%)
  between operations  0.89 us (1%)
    pallas_call x18, Pallas kernels, call(): pl.pallas_call(body, in_specs=[ON_CHIP if kind == 'v' else ANYWHERE for k...  22.8 us
    all_to_all x1, blocking collectives, per_device(): lax.all_to_all(payload, 'gran', split_axis=0, concat_axis=0, tiled=True)  14.2 us
    ppermute x3, starting transfers between devices, exchange(): near = lax.ppermute(near, 'gran', near_pairs)  11.2 us
    ppermute x12, starting transfers between devices, over_band(): lax.ppermute(rounded, 'band', [(i, i ^ flip) for i in range(band_total)])  7.68 us
    ppermute x3, waiting for transfers between devices, exchange(): near = lax.ppermute(near, 'gran', near_pairs)  7.59 us
    ppermute x12, waiting for transfers between devices, over_band(): lax.ppermute(rounded, 'band', [(i, i ^ flip) for i in range(band_total)])  2.91 us
    ppermute x3, starting transfers between devices, exchange(): far = lax.ppermute(far, 'gran', far_pairs)  2.11 us
  transfers between devices with their start and end apart: 19, of which 8 were waited for; matrix products, arithmetic and copies ran while one was open for 0% of the time, Pallas kernels for 22%

profile of v13, /device:TPU:0, one launch (start us, length us, event | category | flops | bytes accessed | tf_op | source)
XLA Modules:
  0.0 70.1 jit_solution(14280107845032923066)
XLA Ops:
  0.6 1.3 %shard_map.113 = (bf16[4,3,64,128]{3,2,1,0:T(8,128)(2,1)S(1)}, bf16[4,3,64,128]{3,2,1,0:T(8,128)(2,1)S(1)}) custom-call(f32[16,3,64,128]{3,2,1,0:T(8,128)} %bitcast.61), custom_call_target="tpu_custom_call" | custom-call | tf_op jit(solution)/shard_map/pallas_call | solution.py:33
  1.9 0.0 copy-start
  2.0 3.0 %collective-permute-start = (bf16[4,3,64,128]{3,2,1,0:T(8,128)(2,1)S(1)}, bf16[4,3,64,128]{3,2,1,0:T(8,128)(2,1)S(1)}, u32[]{:S(2)}, u32[]{:S(2)}) collective-permute-start(bf16[4,3,64,128]{3,2,1,0:T(8,128)(2,1)S(1)} %get-tuple-element.58), channel_id=1, source_target_pairs={{0,4},{4,0},{8,12},{12,8},{16,20},{20,16},{24,28},{28,24},{1,5},{5... | collective-permute-start | bytes 589832 | tf_op jit(solution)/shard_map/ppermute | solution.py:627
  5.0 0.8 %collective-permute-start.1 = (bf16[4,3,64,128]{3,2,1,0:T(8,128)(2,1)S(1)}, bf16[4,3,64,128]{3,2,1,0:T(8,128)(2,1)S(1)}, u32[]{:S(2)}, u32[]{:S(2)}) collective-permute-start(bf16[4,3,64,128]{3,2,1,0:T(8,128)(2,1)S(1)} %get-tuple-element.59), channel_id=1, source_target_pairs={{4,8},{8,4},{12,16},{16,12},{20,24},{24,20},{5,9},{9,5},{13,17},{1... | collective-permute-start | bytes 589832 | tf_op jit(solution)/shard_map/ppermute | solution.py:626
  5.8 1.5 %shard_map.114.ext_ref.refs_0_ = f32[24,3,64,128]{3,2,1,0:T(8,128)S(1)} custom-call(f32[16,3,64,128]{3,2,1,0:T(8,128)} %bitcast.62), custom_call_target="tpu_custom_call" | custom-call | tf_op jit(solution)/shard_map/pallas_call | solution.py:33
  7.3 0.6 shard_map.115.refs_1_
  7.8 3.2 %shard_map.116 = (f32[8,3,64,128]{3,2,1,0:T(8,128)S(1)}, f32[8,3,64,128]{3,2,1,0:T(8,128)S(1)}, f32[8,3,32,128]{3,2,1,0:T(8,128)S(1)}, f32[8,8,3,32,128]{4,3,2,1,0:T(8,128)S(1)}) custom-call(s32[1,16]{1,0:T(1,128)S(1)} %bitcast.52, f32[16,3,64,128]{3,2,1,0:T(8,128)} %bitcast.57, f32[16,3,64,128]{3,2,1,0:T(8,128)} %bitcast.59, f32[3,2,256,128]{3,2,1,0:T(8,128)} %bitcast.63, ...), custom_call_target="tpu_custom_call" | custom-call | tf_op jit(solution)/shard_map/pallas_call | solution.py:33
  11.0 2.3 %collective-permute-done.near_ref = bf16[4,3,64,128]{3,2,1,0:T(8,128)(2,1)S(1)} collective-permute-done((bf16[4,3,64,128]{3,2,1,0:T(8,128)(2,1)S(1)}, bf16[4,3,64,128]{3,2,1,0:T(8,128)(2,1)S(1)}, u32[]{:S(2)}, u32[]{:S(2)}) %collective-permute-start) | collective-permute-done | bytes 196640 | tf_op jit(solution)/shard_map/ppermute | solution.py:627
  13.3 0.6 shard_map.117
  13.9 0.1 collective-permute-start.4
  14.0 1.6 %collective-permute-start.3 = (bf16[64,128]{1,0:T(8,128)(2,1)S(1)}, bf16[64,128]{1,0:T(8,128)(2,1)S(1)}, u32[]{:S(2)}, u32[]{:S(2)}) collective-permute-start(bf16[64,128]{1,0:T(8,128)(2,1)S(1)} %get-tuple-element.66), channel_id=1, source_target_pairs={{0,2},{1,3},{2,0},{3,1},{4,6},{5,7},{6,4},{7,5},{8,10},{9,11},{10,... | collective-permute-start | bytes 49160 | tf_op jit(solution)/shard_map/ppermute | solution.py:674
  15.6 0.3 collective-permute-start.2
  15.9 1.4 %collective-permute-done.4.refs_3_ = bf16[64,128]{1,0:T(8,128)(2,1)S(1)} collective-permute-done((bf16[64,128]{1,0:T(8,128)(2,1)S(1)}, bf16[64,128]{1,0:T(8,128)(2,1)S(1)}, u32[]{:S(2)}, u32[]{:S(2)}) %collective-permute-start.4) | collective-permute-done | bytes 16416 | tf_op jit(solution)/shard_map/ppermute | solution.py:674
  17.3 0.6 collective-permute-done.3.refs_2_
  17.8 0.9 %shard_map.118 = (f32[24,3,64,128]{3,2,1,0:T(8,128)S(1)}, bf16[4,3,64,128]{3,2,1,0:T(8,128)(2,1)S(1)}, bf16[4,3,32,128]{3,2,1,0:T(8,128)(2,1)S(1)}, bf16[4,3,32,128]{3,2,1,0:T(8,128)(2,1)S(1)}) custom-call(s32[8,16]{1,0:T(8,128)S(1)} %bitcast.40, f32[64,128]{1,0:T(8,128)S(1)} %get-tuple-element.65.refs_0_, ...), custom_call_target="tpu_custom_call" | custom-call | tf_op jit(solution)/shard_map/pallas_call | solution.py:33
  18.8 2.5 %collective-permute-start.5 = (bf16[4,3,64,128]{3,2,1,0:T(8,128)(2,1)S(1)}, bf16[4,3,64,128]{3,2,1,0:T(8,128)(2,1)S(1)}, u32[]{:S(2)}, u32[]{:S(2)}) collective-permute-start(bf16[4,3,64,128]{3,2,1,0:T(8,128)(2,1)S(1)} %get-tuple-element.72), channel_id=1, source_target_pairs={{0,4},{4,0},{8,12},{12,8},{16,20},{20,16},{24,28},{28,24},{1,5},{5... | collective-permute-start | bytes 589832 | tf_op jit(solution)/shard_map/ppermute | solution.py:627
  21.2 0.7 collective-permute-start.6
  21.9 3.1 %shard_map.119 = (f32[8,3,64,128]{3,2,1,0:T(8,128)S(1)}, f32[8,3,64,128]{3,2,1,0:T(8,128)S(1)}, f32[8,3,32,128]{3,2,1,0:T(8,128)S(1)}, f32[8,8,3,32,128]{4,3,2,1,0:T(8,128)S(1)}) custom-call(s32[1,16]{1,0:T(1,128)S(1)} %bitcast.53, f32[16,3,64,128]{3,2,1,0:T(8,128)} %bitcast.58, f32[16,3,64,128]{3,2,1,0:T(8,128)} %bitcast.60, f32[3,2,256,128]{3,2,1,0:T(8,128)} %bitcast.64, ...), custom_call_target="tpu_custom_call" | custom-call | tf_op jit(solution)/shard_map/pallas_call | solution.py:33
  25.0 0.8 %shard_map.120.ext_ref.refs_0_ = f32[24,3,64,128]{3,2,1,0:T(8,128)S(1)} custom-call(s32[8,16]{1,0:T(8,128)S(1)} %bitcast.41, f32[64,128]{1,0:T(8,128)S(1)} %get-tuple-element.65.refs_0_, bf16[64,128]{1,0:T(8,128)(2,1)S(1)} %collective-permute-done.2.refs_1_, bf16[64,128]{1,0:T(8,128)(2,1)S(1)} %collective-permute-done.3.refs_2_, ...), custom_call_target="tpu_custom_call", output_to_operand_aliasing={{}: (10, {})} | custom-call | tf_op jit(solution)/shard_map/pallas_call | solution.py:33
  25.8 0.0 copy-start.2
  25.8 0.6 shard_map.121.refs_1_
  26.4 0.7 collective-permute-start.10
  27.1 1.0 %collective-permute-done.5.near_ref = bf16[4,3,64,128]{3,2,1,0:T(8,128)(2,1)S(1)} collective-permute-done((bf16[4,3,64,128]{3,2,1,0:T(8,128)(2,1)S(1)}, bf16[4,3,64,128]{3,2,1,0:T(8,128)(2,1)S(1)}, u32[]{:S(2)}, u32[]{:S(2)}) %collective-permute-start.5) | collective-permute-done | bytes 196640 | tf_op jit(solution)/shard_map/ppermute | solution.py:627
  28.1 0.6 shard_map.122
  28.7 0.1 collective-permute-start.9
  28.8 1.1 %collective-permute-start.8 = (bf16[64,128]{1,0:T(8,128)(2,1)S(1)}, bf16[64,128]{1,0:T(8,128)(2,1)S(1)}, u32[]{:S(2)}, u32[]{:S(2)}) collective-permute-start(bf16[64,128]{1,0:T(8,128)(2,1)S(1)} %get-tuple-element.93), channel_id=1, source_target_pairs={{0,2},{1,3},{2,0},{3,1},{4,6},{5,7},{6,4},{7,5},{8,10},{9,11},{10,... | collective-permute-start | bytes 49160 | tf_op jit(solution)/shard_map/ppermute | solution.py:674
  29.9 0.7 %collective-permute-start.7 = (bf16[64,128]{1,0:T(8,128)(2,1)S(1)}, bf16[64,128]{1,0:T(8,128)(2,1)S(1)}, u32[]{:S(2)}, u32[]{:S(2)}) collective-permute-start(bf16[64,128]{1,0:T(8,128)(2,1)S(1)} %get-tuple-element.93), channel_id=1, source_target_pairs={{0,1},{1,0},{2,3},{3,2},{4,5},{5,4},{6,7},{7,6},{8,9},{9,8},{10,11... | collective-permute-start | bytes 49160 | tf_op jit(solution)/shard_map/ppermute | solution.py:674
  30.6 1.8 %shard_map.123 = (bf16[256,1024]{1,0:T(8,128)(2,1)S(1)}, bf16[256,1024]{1,0:T(8,128)(2,1)S(1)}, s32[8,128]{1,0:T(8,128)S(1)}) custom-call(s32[2,128]{1,0:T(2,128)S(1)} %bitcast.50, s32[2,2,128]{2,1,0:T(2,128)S(1)} %bitcast.54), custom_call_target="tpu_custom_call" | custom-call | tf_op jit(solution)/shard_map/pallas_call | solution.py:33
  32.4 0.1 collective-permute-done.8.refs_2_
  32.6 0.9 %shard_map.124 = (f32[24,3,64,128]{3,2,1,0:T(8,128)S(1)}, f32[24,3,64,128]{3,2,1,0:T(8,128)S(1)}, bf16[4,3,64,128]{3,2,1,0:T(8,128)(2,1)S(1)}, bf16[4,3,64,128]{3,2,1,0:T(8,128)(2,1)S(1)}) custom-call(s32[8,16]{1,0:T(8,128)S(1)} %bitcast.44, f32[64,128]{1,0:T(8,128)S(1)} %get-tuple-element.92.refs_0_, ...), custom_call_target="tpu_custom_call", output_to_operand_aliasing={{0}: (5, {})} | custom-call | tf_op jit(solution)/shard_map/pallas_call | solution.py:33
  33.5 5.7 %collective-permute-start.11 = (bf16[4,3,64,128]{3,2,1,0:T(8,128)(2,1)S(1)}, bf16[4,3,64,128]{3,2,1,0:T(8,128)(2,1)S(1)}, u32[]{:S(2)}, u32[]{:S(2)}) collective-permute-start(bf16[4,3,64,128]{3,2,1,0:T(8,128)(2,1)S(1)} %get-tuple-element.96), channel_id=1, source_target_pairs={{0,4},{4,0},{8,12},{12,8},{16,20},{20,16},{24,28},{28,24},{1,5},{5... | collective-permute-start | bytes 589832 | tf_op jit(solution)/shard_map/ppermute | solution.py:627
  39.2 0.7 collective-permute-start.12
  39.9 0.8 %shard_map.125.refs_0_.ext_ref = f32[24,3,64,128]{3,2,1,0:T(8,128)S(1)} custom-call(s32[8,16]{1,0:T(8,128)S(1)} %bitcast.45, f32[64,128]{1,0:T(8,128)S(1)} %get-tuple-element.92.refs_0_, bf16[64,128]{1,0:T(8,128)(2,1)S(1)} %collective-permute-done.7.refs_1_, bf16[64,128]{1,0:T(8,128)(2,1)S(1)} %collective-permute-done.8.refs_2_, ...), custom_call_target="tpu_custom_call", output_to_operand_aliasing={{}: (10, {})} | custom-call | tf_op jit(solution)/shard_map/pallas_call | solution.py:33
  40.7 0.6 shard_map.127
  41.2 0.1 collective-permute-start.18
  41.3 1.6 %collective-permute-start.17 = (bf16[64,128]{1,0:T(8,128)(2,1)S(1)}, bf16[64,128]{1,0:T(8,128)(2,1)S(1)}, u32[]{:S(2)}, u32[]{:S(2)}) collective-permute-start(bf16[64,128]{1,0:T(8,128)(2,1)S(1)} %get-tuple-element.105), channel_id=1, source_target_pairs={{0,2},{1,3},{2,0},{3,1},{4,6},{5,7},{6,4},{7,5},{8,10},{9,11},{10,... | collective-permute-start | bytes 49160 | tf_op jit(solution)/shard_map/ppermute | solution.py:674
  42.9 0.3 collective-permute-start.16
  43.2 4.3 %collective-permute-done.11.near_ref = bf16[4,3,64,128]{3,2,1,0:T(8,128)(2,1)S(1)} collective-permute-done((bf16[4,3,64,128]{3,2,1,0:T(8,128)(2,1)S(1)}, bf16[4,3,64,128]{3,2,1,0:T(8,128)(2,1)S(1)}, u32[]{:S(2)}, u32[]{:S(2)}) %collective-permute-start.11) | collective-permute-done | bytes 196640 | tf_op jit(solution)/shard_map/ppermute | solution.py:627
  47.5 0.6 shard_map.126
  48.0 0.1 collective-permute-start.15
  48.1 0.8 %collective-permute-start.14 = (bf16[64,128]{1,0:T(8,128)(2,1)S(1)}, bf16[64,128]{1,0:T(8,128)(2,1)S(1)}, u32[]{:S(2)}, u32[]{:S(2)}) collective-permute-start(bf16[64,128]{1,0:T(8,128)(2,1)S(1)} %get-tuple-element.101), channel_id=1, source_target_pairs={{0,2},{1,3},{2,0},{3,1},{4,6},{5,7},{6,4},{7,5},{8,10},{9,11},{10,... | collective-permute-start | bytes 49160 | tf_op jit(solution)/shard_map/ppermute | solution.py:674
  48.9 1.1 %collective-permute-start.13 = (bf16[64,128]{1,0:T(8,128)(2,1)S(1)}, bf16[64,128]{1,0:T(8,128)(2,1)S(1)}, u32[]{:S(2)}, u32[]{:S(2)}) collective-permute-start(bf16[64,128]{1,0:T(8,128)(2,1)S(1)} %get-tuple-element.101), channel_id=1, source_target_pairs={{0,1},{1,0},{2,3},{3,2},{4,5},{5,4},{6,7},{7,6},{8,9},{9,8},{10,11... | collective-permute-start | bytes 49160 | tf_op jit(solution)/shard_map/ppermute | solution.py:674
  50.0 1.1 %shard_map.128 = (f32[16,3,64,128]{3,2,1,0:T(8,128)S(1)}, f32[8,96,128]{2,1,0:T(8,128)S(1)}) custom-call(s32[8,16]{1,0:T(8,128)S(1)} %bitcast.48, f32[64,128]{1,0:T(8,128)S(1)} %get-tuple-element.104.refs_0_, bf16[64,128]{1,0:T(8,128)(2,1)S(1)} %collective-permute-done.16.refs_1_, bf16[64,128]{1,0:T(8,128)(2,1)S(1)} %collective-permute-done.17.refs_2_, ...), custom_call_target="tpu_custom_call" | custom-call | tf_op jit(solution)/shard_map/pallas_call | solution.py:33
  51.1 0.1 collective-permute-done.15.refs_3_
  51.3 0.7 collective-permute-done.14.refs_2_
  51.9 1.3 %shard_map.129 = (f32[16,3,64,128]{3,2,1,0:T(8,128)S(1)}, bf16[8,96,128]{2,1,0:T(8,128)(2,1)S(1)}, f32[8,96,128]{2,1,0:T(8,128)S(1)}) custom-call(s32[8,16]{1,0:T(8,128)S(1)} %bitcast.49, f32[64,128]{1,0:T(8,128)S(1)} %get-tuple-element.100.refs_0_, ...), custom_call_target="tpu_custom_call", output_to_operand_aliasing={{0}: (11, {}), {2}: (12, {})} | custom-call | tf_op jit(solution)/shard_map/pallas_call | solution.py:33
  53.3 14.2 %all_to_all.5.received_ref = bf16[8,96,128]{2,1,0:T(8,128)(2,1)S(1)} all-to-all(bf16[8,96,128]{2,1,0:T(8,128)(2,1)S(1)} %get-tuple-element.108), channel_id=1, replica_groups=mesh['gran'=8,'band'=4] {'gran'}, dimensions={0} | all-to-all | bytes 393216 | tf_op jit(solution)/shard_map/all_to_all | solution.py:765
  67.5 2.6 %shard_map.130 = (bf16[1,3,256,256]{3,2,1,0:T(8,128)(2,1)}, f32[16,3,64,128]{3,2,1,0:T(8,128)}) custom-call(s32[2,128]{1,0:T(2,128)S(1)} %bitcast.51, bf16[8,96,128]{2,1,0:T(8,128)(2,1)S(1)} %all_to_all.5.received_ref, bf16[256,1024]{1,0:T(8,128)(2,1)S(1)} %get-tuple-element.109.row_ref, bf16[256,1024]{1,0:T(8,128)(2,1)S(1)} %get-tuple-element.110.col_ref, ...), custom_call_target="tpu_custom_call" | custom-call | tf_op jit(solution)/shard_map/pallas_call | solution.py:33
  (19 shorter events, 0.0 us)
Async XLA Ops:
  1.9 5.3 %copy-start = (s32[16,8]{0,1:T(8,128)S(1)}, s32[16,8]{0,1:T(8,128)}, u32[]{:S(2)}) copy-start(s32[16,8]{0,1:T(8,128)} %param.15) | copy-start | bytes 1540
  2.0 11.4 %collective-permute-start = (bf16[4,3,64,128]{3,2,1,0:T(8,128)(2,1)S(1)}, bf16[4,3,64,128]{3,2,1,0:T(8,128)(2,1)S(1)}, u32[]{:S(2)}, u32[]{:S(2)}) collective-permute-start(bf16[4,3,64,128]{3,2,1,0:T(8,128)(2,1)S(1)} %get-tuple-element.58), channel_id=1, source_target_pairs={{0,4},{4,0},{8,12},{12,8},{16,20},{20,16},{24,28},{28,24},{1,5},{5... | collective-permute-start | bytes 589832 | tf_op jit(solution)/shard_map/ppermute | solution.py:627
  5.0 2.9 %copy-start.3 = (s32[16]{0:T(128)S(1)}, s32[16]{0:T(128)}, u32[]{:S(2)}) copy-start(s32[16]{0:T(128)} %param.16) | copy-start | bytes 196
  5.0 8.4 %collective-permute-start.1 = (bf16[4,3,64,128]{3,2,1,0:T(8,128)(2,1)S(1)}, bf16[4,3,64,128]{3,2,1,0:T(8,128)(2,1)S(1)}, u32[]{:S(2)}, u32[]{:S(2)}) collective-permute-start(bf16[4,3,64,128]{3,2,1,0:T(8,128)(2,1)S(1)} %get-tuple-element.59), channel_id=1, source_target_pairs={{4,8},{8,4},{12,16},{16,12},{20,24},{24,20},{5,9},{9,5},{13,17},{1... | collective-permute-start | bytes 589832 | tf_op jit(solution)/shard_map/ppermute | solution.py:626
  13.9 3.3 %collective-permute-start.4 = (bf16[64,128]{1,0:T(8,128)(2,1)S(1)}, bf16[64,128]{1,0:T(8,128)(2,1)S(1)}, u32[]{:S(2)}, u32[]{:S(2)}) collective-permute-start(bf16[64,128]{1,0:T(8,128)(2,1)S(1)} %get-tuple-element.66), channel_id=1, source_target_pairs={{0,3},{1,2},{2,1},{3,0},{4,7},{5,6},{6,5},{7,4},{8,11},{9,10},{10,... | collective-permute-start | bytes 49160 | tf_op jit(solution)/shard_map/ppermute | solution.py:674
  14.0 3.8 %collective-permute-start.3 = (bf16[64,128]{1,0:T(8,128)(2,1)S(1)}, bf16[64,128]{1,0:T(8,128)(2,1)S(1)}, u32[]{:S(2)}, u32[]{:S(2)}) collective-permute-start(bf16[64,128]{1,0:T(8,128)(2,1)S(1)} %get-tuple-element.66), channel_id=1, source_target_pairs={{0,2},{1,3},{2,0},{3,1},{4,6},{5,7},{6,4},{7,5},{8,10},{9,11},{10,... | collective-permute-start | bytes 49160 | tf_op jit(solution)/shard_map/ppermute | solution.py:674
  15.6 2.2 %collective-permute-start.2 = (bf16[64,128]{1,0:T(8,128)(2,1)S(1)}, bf16[64,128]{1,0:T(8,128)(2,1)S(1)}, u32[]{:S(2)}, u32[]{:S(2)}) collective-permute-start(bf16[64,128]{1,0:T(8,128)(2,1)S(1)} %get-tuple-element.66), channel_id=1, source_target_pairs={{0,1},{1,0},{2,3},{3,2},{4,5},{5,4},{6,7},{7,6},{8,9},{9,8},{10,11... | collective-permute-start | bytes 49160 | tf_op jit(solution)/shard_map/ppermute | solution.py:674
  18.8 9.3 %collective-permute-start.5 = (bf16[4,3,64,128]{3,2,1,0:T(8,128)(2,1)S(1)}, bf16[4,3,64,128]{3,2,1,0:T(8,128)(2,1)S(1)}, u32[]{:S(2)}, u32[]{:S(2)}) collective-permute-start(bf16[4,3,64,128]{3,2,1,0:T(8,128)(2,1)S(1)} %get-tuple-element.72), channel_id=1, source_target_pairs={{0,4},{4,0},{8,12},{12,8},{16,20},{20,16},{24,28},{28,24},{1,5},{5... | collective-permute-start | bytes 589832 | tf_op jit(solution)/shard_map/ppermute | solution.py:627
  21.2 5.8 %collective-permute-start.6 = (bf16[4,3,32,128]{3,2,1,0:T(8,128)(2,1)S(1)}, bf16[4,3,32,128]{3,2,1,0:T(8,128)(2,1)S(1)}, u32[]{:S(2)}, u32[]{:S(2)}) collective-permute-start(bf16[4,3,32,128]{3,2,1,0:T(8,128)(2,1)S(1)} %get-tuple-element.73), channel_id=1, source_target_pairs={{4,8},{8,4},{12,16},{16,12},{20,24},{24,20},{5,9},{9,5},{13,17},{1... | collective-permute-start | bytes 294920 | tf_op jit(solution)/shard_map/ppermute | solution.py:626
  25.8 4.8 %copy-start.2 = (s32[128,2]{0,1:T(2,128)S(1)}, s32[128,2]{0,1:T(2,128)}, u32[]{:S(2)}) copy-start(s32[128,2]{0,1:T(2,128)} %param.17) | copy-start | bytes 3076
  25.8 4.8 %copy-start.4 = (s32[128,2,2]{0,2,1:T(2,128)S(1)}, s32[128,2,2]{0,2,1:T(2,128)}, u32[]{:S(2)}) copy-start(s32[128,2,2]{0,2,1:T(2,128)} %param.18) | copy-start | bytes 6148
  26.4 6.0 %collective-permute-start.10 = (bf16[4,3,32,128]{3,2,1,0:T(8,128)(2,1)S(1)}, bf16[4,3,32,128]{3,2,1,0:T(8,128)(2,1)S(1)}, u32[]{:S(2)}, u32[]{:S(2)}) collective-permute-start(bf16[4,3,32,128]{3,2,1,0:T(8,128)(2,1)S(1)} %get-tuple-element.95), channel_id=1, source_target_pairs={{4,8},{8,4},{12,16},{16,12},{20,24},{24,20},{5,9},{9,5},{13,17},{1... | collective-permute-start | bytes 294920 | tf_op jit(solution)/shard_map/ppermute | solution.py:703
  28.7 3.7 %collective-permute-start.9 = (bf16[64,128]{1,0:T(8,128)(2,1)S(1)}, bf16[64,128]{1,0:T(8,128)(2,1)S(1)}, u32[]{:S(2)}, u32[]{:S(2)}) collective-permute-start(bf16[64,128]{1,0:T(8,128)(2,1)S(1)} %get-tuple-element.93), channel_id=1, source_target_pairs={{0,3},{1,2},{2,1},{3,0},{4,7},{5,6},{6,5},{7,4},{8,11},{9,10},{10,... | collective-permute-start | bytes 49160 | tf_op jit(solution)/shard_map/ppermute | solution.py:674
  28.8 3.8 %collective-permute-start.8 = (bf16[64,128]{1,0:T(8,128)(2,1)S(1)}, bf16[64,128]{1,0:T(8,128)(2,1)S(1)}, u32[]{:S(2)}, u32[]{:S(2)}) collective-permute-start(bf16[64,128]{1,0:T(8,128)(2,1)S(1)} %get-tuple-element.93), channel_id=1, source_target_pairs={{0,2},{1,3},{2,0},{3,1},{4,6},{5,7},{6,4},{7,5},{8,10},{9,11},{10,... | collective-permute-start | bytes 49160 | tf_op jit(solution)/shard_map/ppermute | solution.py:674
  29.9 2.7 %collective-permute-start.7 = (bf16[64,128]{1,0:T(8,128)(2,1)S(1)}, bf16[64,128]{1,0:T(8,128)(2,1)S(1)}, u32[]{:S(2)}, u32[]{:S(2)}) collective-permute-start(bf16[64,128]{1,0:T(8,128)(2,1)S(1)} %get-tuple-element.93), channel_id=1, source_target_pairs={{0,1},{1,0},{2,3},{3,2},{4,5},{5,4},{6,7},{7,6},{8,9},{9,8},{10,11... | collective-permute-start | bytes 49160 | tf_op jit(solution)/shard_map/ppermute | solution.py:674
  33.5 14.0 %collective-permute-start.11 = (bf16[4,3,64,128]{3,2,1,0:T(8,128)(2,1)S(1)}, bf16[4,3,64,128]{3,2,1,0:T(8,128)(2,1)S(1)}, u32[]{:S(2)}, u32[]{:S(2)}) collective-permute-start(bf16[4,3,64,128]{3,2,1,0:T(8,128)(2,1)S(1)} %get-tuple-element.96), channel_id=1, source_target_pairs={{0,4},{4,0},{8,12},{12,8},{16,20},{20,16},{24,28},{28,24},{1,5},{5... | collective-permute-start | bytes 589832 | tf_op jit(solution)/shard_map/ppermute | solution.py:627
  39.2 8.2 %collective-permute-start.12 = (bf16[4,3,64,128]{3,2,1,0:T(8,128)(2,1)S(1)}, bf16[4,3,64,128]{3,2,1,0:T(8,128)(2,1)S(1)}, u32[]{:S(2)}, u32[]{:S(2)}) collective-permute-start(bf16[4,3,64,128]{3,2,1,0:T(8,128)(2,1)S(1)} %get-tuple-element.97), channel_id=1, source_target_pairs={{4,8},{8,4},{12,16},{16,12},{20,24},{24,20},{5,9},{9,5},{13,17},{1... | collective-permute-start | bytes 589832 | tf_op jit(solution)/shard_map/ppermute | solution.py:626
  41.2 7.7 %collective-permute-start.18 = (bf16[64,128]{1,0:T(8,128)(2,1)S(1)}, bf16[64,128]{1,0:T(8,128)(2,1)S(1)}, u32[]{:S(2)}, u32[]{:S(2)}) collective-permute-start(bf16[64,128]{1,0:T(8,128)(2,1)S(1)} %get-tuple-element.105), channel_id=1, source_target_pairs={{0,3},{1,2},{2,1},{3,0},{4,7},{5,6},{6,5},{7,4},{8,11},{9,10},{10,... | collective-permute-start | bytes 49160 | tf_op jit(solution)/shard_map/ppermute | solution.py:674
  41.3 8.7 %collective-permute-start.17 = (bf16[64,128]{1,0:T(8,128)(2,1)S(1)}, bf16[64,128]{1,0:T(8,128)(2,1)S(1)}, u32[]{:S(2)}, u32[]{:S(2)}) collective-permute-start(bf16[64,128]{1,0:T(8,128)(2,1)S(1)} %get-tuple-element.105), channel_id=1, source_target_pairs={{0,2},{1,3},{2,0},{3,1},{4,6},{5,7},{6,4},{7,5},{8,10},{9,11},{10,... | collective-permute-start | bytes 49160 | tf_op jit(solution)/shard_map/ppermute | solution.py:674
  42.9 7.1 %collective-permute-start.16 = (bf16[64,128]{1,0:T(8,128)(2,1)S(1)}, bf16[64,128]{1,0:T(8,128)(2,1)S(1)}, u32[]{:S(2)}, u32[]{:S(2)}) collective-permute-start(bf16[64,128]{1,0:T(8,128)(2,1)S(1)} %get-tuple-element.105), channel_id=1, source_target_pairs={{0,1},{1,0},{2,3},{3,2},{4,5},{5,4},{6,7},{7,6},{8,9},{9,8},{10,11... | collective-permute-start | bytes 49160 | tf_op jit(solution)/shard_map/ppermute | solution.py:674
  48.0 3.2 %collective-permute-start.15 = (bf16[64,128]{1,0:T(8,128)(2,1)S(1)}, bf16[64,128]{1,0:T(8,128)(2,1)S(1)}, u32[]{:S(2)}, u32[]{:S(2)}) collective-permute-start(bf16[64,128]{1,0:T(8,128)(2,1)S(1)} %get-tuple-element.101), channel_id=1, source_target_pairs={{0,3},{1,2},{2,1},{3,0},{4,7},{5,6},{6,5},{7,4},{8,11},{9,10},{10,... | collective-permute-start | bytes 49160 | tf_op jit(solution)/shard_map/ppermute | solution.py:674
  48.1 3.8 %collective-permute-start.14 = (bf16[64,128]{1,0:T(8,128)(2,1)S(1)}, bf16[64,128]{1,0:T(8,128)(2,1)S(1)}, u32[]{:S(2)}, u32[]{:S(2)}) collective-permute-start(bf16[64,128]{1,0:T(8,128)(2,1)S(1)} %get-tuple-element.101), channel_id=1, source_target_pairs={{0,2},{1,3},{2,0},{3,1},{4,6},{5,7},{6,4},{7,5},{8,10},{9,11},{10,... | collective-permute-start | bytes 49160 | tf_op jit(solution)/shard_map/ppermute | solution.py:674
  48.9 3.0 %collective-permute-start.13 = (bf16[64,128]{1,0:T(8,128)(2,1)S(1)}, bf16[64,128]{1,0:T(8,128)(2,1)S(1)}, u32[]{:S(2)}, u32[]{:S(2)}) collective-permute-start(bf16[64,128]{1,0:T(8,128)(2,1)S(1)} %get-tuple-element.101), channel_id=1, source_target_pairs={{0,1},{1,0},{2,3},{3,2},{4,5},{5,4},{6,7},{7,6},{8,9},{9,8},{10,11... | collective-permute-start | bytes 49160 | tf_op jit(solution)/shard_map/ppermute | solution.py:674
  51.9 15.5 %copy-start.1 = (bf16[1,3,256,256]{3,2,1,0:T(8,128)(2,1)S(1)}, bf16[1,3,256,256]{3,2,1,0:T(8,128)(2,1)}, u32[]{:S(2)}) copy-start(bf16[1,3,256,256]{3,2,1,0:T(8,128)(2,1)} %pixels_ref.1) | copy-start | bytes 1179652
